TPU v7x, 32 devices: a whole 2x2x4 slice. The times are simulated.
32 devices in a mesh: layer: 4 (over x, core), feat: 8 (over z, y).
Axes of the slice: x: 2, y: 2, z: 4, core: 2. Of those that a mesh axis runs over, the one named last changes fastest.
Arguments:
- activations: bfloat16 [64, 4, 2304], P('feat', 'layer'), may hold values from -6 to 6
- enc_weight: bfloat16 [4, 2304, 8192], P('layer', None, 'feat'), may hold values from -0.0625 to 0.0625
- dec_weight: bfloat16 [4, 8192, 2304], P('layer', 'feat'), may hold values from -0.09375 to 0.09375
- enc_bias: float32 [8192], P('feat'), may hold values from -3 to 3
- threshold: float32 [8192], P('feat'), may hold values from 0.1 to 1
- dec_bias: float32 [4, 2304], P('layer'), may hold values from -3 to 3
- token_mask: int32 [64], replicated, may hold values 0 or 1
Outputs:
- squared_error: float32 [64, 4], P('feat', 'layer')
- latent_grad: float32 [64, 8192], P(None, 'feat')
- input_grad: bfloat16 [64, 4, 2304], P('feat', 'layer')
All inputs are finite; a program needn't handle non-finite values.
Results may differ from a plain program's by a relative error of at most 0.015.
Values may be sent and summed in bfloat16 or wider, within the bound.
No kernel may reach another device: no remote copies, remote signals or barrier semaphores. Data moves between devices by JAX's collectives and lax.ppermute only.
A program may use at most 64 MiB of HBM per device.

v0:
```python
import jax
import jax.numpy as jnp
from jax import lax
from jax.sharding import PartitionSpec as P

jump_scale = 0.25


def shards(activations, enc_weight, dec_weight, enc_bias, threshold, dec_bias, token_mask):
    tok_dev = activations.shape[0]
    whole_acts = lax.all_gather(activations, "feat", axis=0, tiled=True)
    partial_value = jnp.einsum(
        "tld,ldf->tf", whole_acts, enc_weight, preferred_element_type=jnp.float32
    )
    preact = lax.psum(partial_value.astype(jnp.bfloat16), "layer").astype(jnp.float32) + enc_bias
    gating = jax.nn.sigmoid((preact - threshold) / jump_scale)
    latent = (preact * gating).astype(jnp.bfloat16)
    gate_slope = gating + preact * gating * (1.0 - gating) / jump_scale
    first_row = lax.axis_index("feat") * tok_dev
    decoded = jnp.einsum("tf,lfd->tld", latent, dec_weight, preferred_element_type=jnp.float32)
    rebuilt = lax.psum(decoded, "feat")
    full_mask = token_mask.astype(jnp.float32)[:, None, None]
    error_all = full_mask * (rebuilt + dec_bias[None, :, :] - whole_acts.astype(jnp.float32))
    error = lax.dynamic_slice_in_dim(error_all, first_row, tok_dev, 0)
    grad_part = jnp.einsum(
        "tld,lfd->tf",
        error_all.astype(jnp.bfloat16),
        dec_weight,
        preferred_element_type=jnp.float32,
    )
    squared_error = jnp.mean(error * error, axis=-1)
    latent_grad = lax.psum(grad_part.astype(jnp.bfloat16), "layer").astype(jnp.float32)
    preact_grad = (latent_grad * gate_slope).astype(jnp.bfloat16)
    grad_terms = lax.psum_scatter(
        jnp.einsum("tf,ldf->tld", preact_grad, enc_weight, preferred_element_type=jnp.float32),
        "feat",
        scatter_dimension=0,
        tiled=True,
    )
    input_grad = (grad_terms - error).astype(jnp.bfloat16)
    return (squared_error, latent_grad, input_grad)


def solution(mesh):
    return jax.shard_map(
        shards,
        mesh=mesh,
        in_specs=(
            P("feat", "layer", None),
            P("layer", None, "feat"),
            P("layer", "feat", None),
            P("feat"),
            P("feat"),
            P("layer", None),
            P(),
        ),
        out_specs=(P("feat", "layer"), P(None, "feat"), P("feat", "layer", None)),
        check_vma=False,
    )
```

profile of v0, /device:TPU:0, one launch (start us, length us, event | category | flops | bytes accessed | tf_op | source)
XLA Modules:
  0.0 266.7 jit_solution(14334651617059155627)
XLA Ops:
  7.2 0.0 copy-start.3
  7.2 0.0 copy-start.2
  7.2 0.0 all-reduce.4.cloned.1.call-start
  7.2 32.8 %all_gather.3 = bf16[64,1,2304]{2,0,1:T(8,128)(2,1)S(1)} all-gather(bf16[8,1,2304]{2,0,1:T(8,128)(2,1)} %param.7), channel_id=1, replica_groups=mesh['layer'=4,'feat'=8] {'feat'}, dimensions={0}, use_global_device_ids=true | all-gather | bytes 331776 | tf_op jit(solution)/shard_map/all_gather | solution.py:11
  40.0 0.0 copy-start.5
  40.0 0.0 copy-start.4
  40.0 4.0 %fusion.14 = bf16[64,1024]{1,0:T(8,128)(2,1)} fusion(bf16[1,2304,1024]{2,1,0:T(8,128)(2,1)} %param.8, bf16[64,1,2304]{2,0,1:T(8,128)(2,1)S(1)} %all_gather.3), kind=kOutput, calls=%fused_computation.10 | convolution fusion | flops 302055424 | bytes 5144576 | tf_op jit(solution)/shard_map/tld,ldf->tf/dot_general | solution.py:12
  44.0 0.0 all-reduce.4.cloned.1.call-update
  44.0 0.0 all-reduce.6.cloned.1.call-start
  44.1 32.5 %all-reduce.4.cloned.1.call-done = bf16[64,1024]{1,0:T(8,128)(2,1)} async-done(((bf16[64,1024]{1,0:T(8,128)(2,1)}), bf16[64,1024]{1,0:T(8,128)(2,1)}) %all-reduce.4.cloned.1.call-update) | async-done | bytes 131088 | tf_op jit(solution)/shard_map/psum | solution.py:15
  76.6 0.0 copy-done.3
  76.6 0.0 copy-done.2
  76.6 4.2 %fusion.11 = f32[64,1,2304]{2,0,1:T(8,128)} fusion(bf16[1,1024,2304]{2,1,0:T(8,128)(2,1)} %param.9, bf16[64,1024]{1,0:T(8,128)(2,1)} %all-reduce.4.cloned.1.call-done, f32[1024]{0:T(1024)S(1)} %copy-done.2, f32[1024]{0:T(1024)S(1)} %copy-done.3), kind=kOutput, calls=%fused_computation.9 | convolution fusion | flops 302579712 | bytes 5447680 | tf_op jit(solution)/shard_map/tf,lfd->tld/dot_general | solution.py:20
  80.7 0.0 copy-start.1
  80.7 0.0 all-reduce.6.cloned.1.call-update
  80.8 0.0 all-reduce.8.cloned.1.call-start
  80.8 0.0 copy-done.5
  80.8 0.0 copy-done.4
  80.9 72.9 %all-reduce.6.cloned.1.call-done = f32[64,1,2304]{2,0,1:T(8,128)} async-done(((f32[64,1,2304]{2,0,1:T(8,128)}), f32[64,1,2304]{2,0,1:T(8,128)}) %all-reduce.6.cloned.1.call-update) | async-done | bytes 589840 | tf_op jit(solution)/shard_map/psum | solution.py:21
  153.8 1.2 subtract_multiply_fusion
  155.0 4.5 %fusion.17 = bf16[64,1024]{1,0:T(8,128)(2,1)} fusion(bf16[1,1024,2304]{2,1,0:T(8,128)(2,1)} %param.9, f32[64,1,2304]{2,0,1:T(8,128)S(1)} %subtract_multiply_fusion), kind=kOutput, calls=%fused_computation.11 | convolution fusion | flops 302202880 | bytes 5439488 | tf_op jit(solution)/shard_map/tld,lfd->tf/dot_general | solution.py:25
  159.5 0.0 all-reduce.8.cloned.1.call-update
  159.5 0.0 reduce-scatter.2.cloned.1.call-start
  159.6 30.4 %all-reduce.8.cloned.1.call-done = bf16[64,1024]{1,0:T(8,128)(2,1)} async-done(((bf16[64,1024]{1,0:T(8,128)(2,1)}), bf16[64,1024]{1,0:T(8,128)(2,1)}) %all-reduce.8.cloned.1.call-update) | async-done | bytes 131088 | tf_op jit(solution)/shard_map/psum | solution.py:32
  190.0 0.9 convert_element_type.37
  190.9 0.0 copy-done.1
  190.9 0.0 copy-start
  190.9 4.8 %fusion.8 = f32[64,1,2304]{2,0,1:T(8,128)} fusion(bf16[1,2304,1024]{2,1,0:T(8,128)(2,1)} %param.8, f32[64,1024]{1,0:T(8,128)S(1)} %convert_element_type.37, bf16[64,1024]{1,0:T(8,128)(2,1)S(1)} %copy-done.1, f32[1024]{0:T(1024)S(1)} %copy-done.2, f32[1024]{0:T(1024)S(1)} %copy-done.3), kind=kOutput, calls=%fused_computation.8 | convolution fusion | flops 302907392 | bytes 5709824 | tf_op jit(solution)/shard_map/tf,ldf->tld/dot_general | solution.py:35
  195.8 0.0 reduce-scatter.2.cloned.1.call-update
  195.8 62.3 %reduce-scatter.2.cloned.1.call-done = f32[8,1,2304]{2,0,1:T(8,128)} async-done(((f32[64,1,2304]{2,0,1:T(8,128)}), f32[8,1,2304]{2,0,1:T(8,128)}) %reduce-scatter.2.cloned.1.call-update) | async-done | bytes 73744 | tf_op jit(solution)/shard_map/reduce_scatter | solution.py:34
  258.1 1.6 subtract_convert_fusion
  259.7 0.5 multiply_bitcast_fusion
  260.2 0.0 copy-done
  (2 shorter events, 0.0 us)
Async XLA Ops:
  7.2 69.4 %copy-start.3 = (f32[1024]{0:T(1024)S(1)}, f32[1024]{0:T(1024)}, u32[]{:S(2)}) copy-start(f32[1024]{0:T(1024)} %param.10) | copy-start | bytes 12292
  7.2 69.4 %copy-start.2 = (f32[1024]{0:T(1024)S(1)}, f32[1024]{0:T(1024)}, u32[]{:S(2)}) copy-start(f32[1024]{0:T(1024)} %param.11) | copy-start | bytes 12292
  7.2 69.4 %all-reduce.4.cloned.1.call-start = ((), (), s32[]{:S(2)}) async-start(), calls=%async_computation.1 | async-start | bytes 262144 | tf_op jit(solution)/shard_map/psum | solution.py:15
  40.0 40.8 %copy-start.5 = (s32[64]{0:T(128)S(1)}, s32[64]{0:T(128)}, u32[]{:S(2)}) copy-start(s32[64]{0:T(128)} %param.13) | copy-start | bytes 772
  40.0 40.8 %copy-start.4 = (f32[1,2304]{1,0:T(1,128)S(1)}, f32[1,2304]{1,0:T(1,128)}, u32[]{:S(2)}) copy-start(f32[1,2304]{1,0:T(1,128)} %param.12) | copy-start | bytes 27652
  44.0 109.8 %all-reduce.6.cloned.1.call-start = ((), (), s32[]{:S(2)}) async-start(), calls=%async_computation.2 | async-start | bytes 1179648 | tf_op jit(solution)/shard_map/psum | solution.py:21
  80.7 110.2 %copy-start.1 = (bf16[64,1024]{1,0:T(8,128)(2,1)S(1)}, bf16[64,1024]{1,0:T(8,128)(2,1)}, u32[]{:S(2)}) copy-start(bf16[64,1024]{1,0:T(8,128)(2,1)} %all-reduce.4.cloned.1.call-done) | copy-start | bytes 393220
  80.8 109.2 %all-reduce.8.cloned.1.call-start = ((), (), s32[]{:S(2)}) async-start(), calls=%async_computation.3 | async-start | bytes 262144 | tf_op jit(solution)/shard_map/psum | solution.py:32
  159.5 98.5 %reduce-scatter.2.cloned.1.call-start = ((), (), s32[]{:S(2)}) async-start(), calls=%async_computation.4 | async-start | bytes 663552 | tf_op jit(solution)/shard_map/reduce_scatter | solution.py:34
  190.9 69.3 %copy-start = (f32[64,1024]{1,0:T(8,128)}, f32[64,1024]{1,0:T(8,128)S(1)}, u32[]{:S(2)}) copy-start(f32[64,1024]{1,0:T(8,128)S(1)} %convert_element_type.37) | copy-start | bytes 786436
Sparse Core Ops, SparseCore 0:
  44.1 32.4 all-reduce.3
  80.9 72.8 all-reduce.5
  159.7 30.2 all-reduce.7
  195.9 62.1 reduce-scatter.1
where the time goes:
time: 267 us
  waiting for transfers between devices  198 us (74%)
  blocking collectives  32.8 us (12%)
  matrix products  17.5 us (7%)
  between operations  13.8 us (5%)
  other arithmetic  4.27 us (2%)
    psum x1, waiting for transfers between devices, shards(): rebuilt = lax.psum(decoded, 'feat')  72.9 us
    reduce_scatter x1, waiting for transfers between devices, shards(): lax.psum_scatter(jnp.einsum('tf,ldf->tld', preact_grad, enc_weight, prefe...  62.3 us
    all_gather x1, blocking collectives, shards(): whole_acts = lax.all_gather(activations, 'feat', axis=0, tiled=True)  32.8 us
    psum x1, waiting for transfers between devices, shards(): lax.psum(partial_value.astype(jnp.bfloat16), 'layer').astype(jnp.float32)  32.5 us
    psum x1, waiting for transfers between devices, shards(): lax.psum(grad_part.astype(jnp.bfloat16), 'layer').astype(jnp.float32)  30.4 us
  transfers between devices with their start and end apart: 4, of which 4 were waited for; matrix products, arithmetic and copies ran while one was open for 0% of the time, Pallas kernels for 0%

commit v1 on v0

v1 whole, which is shorter than its diff:
```python
import jax
import jax.numpy as jnp
from jax import lax
from jax.sharding import PartitionSpec as P

jump_scale = 0.25


def spread(block, axis):
    n = lax.axis_size(axis)
    pieces = lax.all_to_all(jnp.broadcast_to(block[None], (n, *block.shape)), axis, 0, 0)
    return pieces.reshape(n * block.shape[0], *block.shape[1:])


def sum_scatter(terms, axis):
    n = lax.axis_size(axis)
    pieces = lax.all_to_all(terms.astype(jnp.bfloat16).reshape(n, -1, terms.shape[-1]), axis, 0, 0)
    return jnp.sum(pieces.astype(jnp.float32), axis=0)


def sum_all(terms, axis):
    return jnp.sum(lax.all_gather(terms.astype(jnp.bfloat16), axis).astype(jnp.float32), axis=0)


def dot(a, b, dims):
    return lax.dot_general(a, b, (dims, ((), ())), preferred_element_type=jnp.float32)


def shards(activations, enc_weight, dec_weight, enc_bias, threshold, dec_bias, token_mask):
    tok_dev = activations.shape[0]
    enc, dec = enc_weight[0], dec_weight[0]
    acts = activations[:, 0]
    whole_acts = spread(acts, "feat")
    preact = sum_all(dot(whole_acts, enc, ((1,), (0,))), "layer") + enc_bias
    gating = jax.nn.sigmoid((preact - threshold) / jump_scale)
    latent = (preact * gating).astype(jnp.bfloat16)
    gate_slope = gating + preact * gating * (1.0 - gating) / jump_scale
    rebuilt = sum_scatter(dot(latent, dec, ((1,), (0,))), "feat")
    mask = lax.dynamic_slice_in_dim(token_mask, lax.axis_index("feat") * tok_dev, tok_dev)
    error = mask.astype(jnp.float32)[:, None] * (rebuilt + dec_bias - acts.astype(jnp.float32))
    error_all = spread(error.astype(jnp.bfloat16), "feat")
    squared_error = jnp.mean(error * error, axis=-1, keepdims=True)
    latent_grad = sum_all(dot(error_all, dec, ((1,), (1,))), "layer")
    preact_grad = (latent_grad * gate_slope).astype(jnp.bfloat16)
    grad_terms = sum_scatter(dot(preact_grad, enc, ((1,), (1,))), "feat")
    input_grad = (grad_terms - error).astype(jnp.bfloat16)
    return (squared_error, latent_grad, input_grad[:, None])


def solution(mesh):
    return jax.shard_map(
        shards,
        mesh=mesh,
        in_specs=(
            P("feat", "layer", None),
            P("layer", None, "feat"),
            P("layer", "feat", None),
            P("feat"),
            P("feat"),
            P("layer", None),
            P(),
        ),
        out_specs=(P("feat", "layer"), P(None, "feat"), P("feat", "layer", None)),
        check_vma=False,
    )
```

time: 267 us -> 89.6 us (0.34)
  waiting for transfers between devices: 198 us -> 19.9 us
  between operations: 13.8 us -> 0.79 us
  blocking collectives: 32.8 us -> 45.2 us
  starting transfers between devices: 0.16 us -> 6.84 us
  matrix products: 17.5 us -> 13.5 us
    psum x3 -> x0, waiting for transfers between devices: 136 us -> none  [the longest x1 72.9 us: shards(): rebuilt = lax.psum(decoded, 'feat')]
    reduce_scatter x1 -> x0, waiting for transfers between devices: 62.3 us -> none  [shards(): lax.psum_scatter(jnp.einsum('tf,ldf->tld', preact_grad, enc_weight, prefe...]
    all_to_all x0 -> x2, blocking collectives: none -> 31.5 us  [spread(): lax.all_to_all(jnp.broadcast_to(block[None], (n, *block.shape)), axis, 0, 0)]
    all_to_all x0 -> x2, waiting for transfers between devices: none -> 19.9 us  [sum_scatter(): lax.all_to_all(terms.astype(jnp.bfloat16).reshape(n, -1, terms.shape[-1])...]
    all_gather x1 -> x2, blocking collectives: 32.8 us -> 13.7 us  [sum_all(): lax.all_gather(terms.astype(jnp.bfloat16), axis).astype(jnp.float32)]
    all_to_all x0 -> x2, starting transfers between devices: none -> 6.84 us  [sum_scatter(): lax.all_to_all(terms.astype(jnp.bfloat16).reshape(n, -1, terms.shape[-1])...]
    dot_general x4, matrix products: 17.5 us -> 13.5 us  [dot(): lax.dot_general(a, b, (dims, ((), ())), preferred_element_type=jnp.float32)]
  transfers between devices with their start and end apart: 4 -> 2, of which waited for: 4 -> 2; matrix products, arithmetic and copies ran while one was open for 0% -> 1% of each run, Pallas kernels for 0% -> 0%
where the time goes in v1:
time: 89.6 us; the launch traced here: 89 us
  blocking collectives  45.2 us (50%)
  waiting for transfers between devices  19.9 us (22%)
  matrix products  13.5 us (15%)
  starting transfers between devices  6.84 us (8%)
  other arithmetic  1.76 us (2%)
  local copies, waits for them, and re-layouts  1 us (1%)
    all_to_all x2, blocking collectives, spread(): lax.all_to_all(jnp.broadcast_to(block[None], (n, *block.shape)), axis, 0, 0)  31.5 us
    all_to_all x2, waiting for transfers between devices, sum_scatter(): lax.all_to_all(terms.astype(jnp.bfloat16).reshape(n, -1, terms.shape[-1])...  19.9 us
    all_gather x2, blocking collectives, sum_all(): lax.all_gather(terms.astype(jnp.bfloat16), axis).astype(jnp.float32)  13.7 us
    dot_general x4, matrix products, dot(): lax.dot_general(a, b, (dims, ((), ())), preferred_element_type=jnp.float32)  13.5 us
    all_to_all x2, starting transfers between devices, sum_scatter(): lax.all_to_all(terms.astype(jnp.bfloat16).reshape(n, -1, terms.shape[-1])...  6.84 us
  transfers between devices with their start and end apart: 2, of which 2 were waited for; matrix products, arithmetic and copies ran while one was open for 1% of the time, Pallas kernels for 0%

profile of v1, /device:TPU:0, one launch (start us, length us, event | category | flops | bytes accessed | tf_op | source)
XLA Modules:
  0.0 89.0 jit_solution(9051582174126854341)
XLA Ops:
  0.6 0.0 copy-start.3
  0.6 0.0 copy-start.4
  0.7 0.0 copy-start
  0.7 0.9 %broadcast_in_dim.7 = bf16[8,8,2304]{2,1,0:T(8,128)(2,1)S(1)} broadcast(bf16[8,2304]{1,0:T(8,128)(2,1)} %bitcast.55), dimensions={1,2} | broadcast | bytes 331776 | tf_op jit(solution)/shard_map/broadcast_in_dim | solution.py:11
  1.6 17.5 %all_to_all.20 = bf16[8,8,2304]{2,1,0:T(8,128)(2,1)S(1)} all-to-all(bf16[8,8,2304]{2,1,0:T(8,128)(2,1)S(1)} %broadcast_in_dim.7), channel_id=1, replica_groups=mesh['layer'=4,'feat'=8] {'feat'}, dimensions={0} | all-to-all | bytes 589824 | tf_op jit(solution)/shard_map/all_to_all | solution.py:11
  19.2 3.3 %fusion.20 = bf16[64,1024]{1,0:T(8,128)(2,1)S(1)} fusion(bf16[1,2304,1024]{2,1,0:T(8,128)(2,1)} %param.8, bf16[8,8,2304]{2,1,0:T(8,128)(2,1)S(1)} %all_to_all.20), kind=kOutput, calls=%fused_computation.12 | convolution fusion | flops 302055424 | bytes 5144576 | tf_op jit(solution)/shard_map/dot_general | solution.py:26
  22.4 0.0 copy-start.5
  22.5 0.0 copy-start.6
  22.5 0.0 copy-start.2
  22.5 7.2 %all-gather = bf16[256,1024]{1,0:T(8,128)(2,1)S(1)} all-gather(bf16[64,1024]{1,0:T(8,128)(2,1)S(1)} %fusion.20), channel_id=2, replica_groups=mesh['layer'=4,'feat'=8] {'layer'}, dimensions={0}, use_global_device_ids=true | all-gather | bytes 655360 | tf_op jit(solution)/shard_map/all_gather | solution.py:22
  29.7 0.1 convert_reduce_fusion.1
  29.7 0.0 copy-done.3
  29.7 0.0 copy-done.4
  29.8 0.0 copy-done
  29.8 1.6 %fusion.14 = bf16[8,8,2304]{2,1,0:T(8,128)(2,1)} fusion(bf16[1,1024,2304]{2,1,0:T(8,128)(2,1)S(1)} %copy-done, f32[64,1024]{1,0:T(8,128)S(1)} %convert_reduce_fusion.1, f32[1024]{0:T(1024)S(1)} %copy-done.3, f32[1024]{0:T(1024)S(1)} %copy-done.4), kind=kOutput, calls=%fused_computation.10 | convolution fusion | flops 302661632 | bytes 5283840 | tf_op jit(solution)/shard_map/dot_general | solution.py:26
  31.4 3.4 %all-to-all-start.1 = ((bf16[8,8,2304]{2,1,0:T(8,128)(2,1)}), bf16[8,8,2304]{2,1,0:T(8,128)(2,1)S(1)}, u32[]{:S(2)}, u32[]{:S(2)}) async-start(bf16[8,8,2304]{2,1,0:T(8,128)(2,1)} %fusion.14), calls=%async_computation.1 | async-start | bytes 589824 | tf_op jit(solution)/shard_map/all_to_all | solution.py:17
  34.8 0.0 copy-done.5
  34.9 0.0 copy-done.6
  34.9 0.1 dynamic-slice_convert_fusion
  35.0 10.1 %all-to-all-done.1 = bf16[8,8,2304]{2,1,0:T(8,128)(2,1)S(1)} async-done(((bf16[8,8,2304]{2,1,0:T(8,128)(2,1)}), bf16[8,8,2304]{2,1,0:T(8,128)(2,1)S(1)}, u32[]{:S(2)}, u32[]{:S(2)}) %all-to-all-start.1) | async-done | bytes 294944 | tf_op jit(solution)/shard_map/all_to_all | solution.py:17
  45.2 0.0 copy-done.2
  45.2 0.2 fusion.42
  45.4 14.0 %all_to_all.21 = bf16[8,8,2304]{2,1,0:T(8,128)(2,1)S(1)} all-to-all(bf16[8,8,2304]{2,1,0:T(8,128)(2,1)S(1)} %broadcast_in_dim.8), channel_id=1, replica_groups=mesh['layer'=4,'feat'=8] {'feat'}, dimensions={0} | all-to-all | bytes 589824 | tf_op jit(solution)/shard_map/all_to_all | solution.py:11
  59.4 3.9 %fusion.23 = bf16[64,1024]{1,0:T(8,128)(2,1)S(1)} fusion(bf16[1,1024,2304]{2,1,0:T(8,128)(2,1)} %param.9, bf16[8,8,2304]{2,1,0:T(8,128)(2,1)S(1)} %all_to_all.21), kind=kOutput, calls=%fused_computation.13 | convolution fusion | flops 302055424 | bytes 5144576 | tf_op jit(solution)/shard_map/dot_general | solution.py:26
  63.2 6.5 %all-gather.1 = bf16[256,1024]{1,0:T(8,128)(2,1)S(1)} all-gather(bf16[64,1024]{1,0:T(8,128)(2,1)S(1)} %fusion.23), channel_id=3, replica_groups=mesh['layer'=4,'feat'=8] {'layer'}, dimensions={0}, use_global_device_ids=true | all-gather | bytes 655360 | tf_op jit(solution)/shard_map/all_gather | solution.py:22
  69.8 0.1 convert_reduce_fusion
  69.8 0.0 copy-start.1
  69.8 4.7 %fusion.17 = bf16[8,8,2304]{2,1,0:T(8,128)(2,1)} fusion(bf16[1,2304,1024]{2,1,0:T(8,128)(2,1)} %param.8, f32[64,1024]{1,0:T(8,128)S(1)} %convert_reduce_fusion, f32[64,1024]{1,0:T(8,128)S(1)} %convert_reduce_fusion.1, f32[1024]{0:T(1024)S(1)} %copy-done.3, f32[1024]{0:T(1024)S(1)} %copy-done.4), kind=kOutput, calls=%fused_computation.11 | convolution fusion | flops 302989312 | bytes 5545984 | tf_op jit(solution)/shard_map/dot_general | solution.py:26
  74.6 3.4 %all-to-all-start.3 = ((bf16[8,8,2304]{2,1,0:T(8,128)(2,1)}), bf16[8,8,2304]{2,1,0:T(8,128)(2,1)S(1)}, u32[]{:S(2)}, u32[]{:S(2)}) async-start(bf16[8,8,2304]{2,1,0:T(8,128)(2,1)} %fusion.17), calls=%async_computation.3 | async-start | bytes 589824 | tf_op jit(solution)/shard_map/all_to_all | solution.py:17
  78.0 0.5 multiply_bitcast_fusion
  78.5 9.8 %all-to-all-done.3 = bf16[8,8,2304]{2,1,0:T(8,128)(2,1)S(1)} async-done(((bf16[8,8,2304]{2,1,0:T(8,128)(2,1)}), bf16[8,8,2304]{2,1,0:T(8,128)(2,1)S(1)}, u32[]{:S(2)}, u32[]{:S(2)}) %all-to-all-start.3) | async-done | bytes 294944 | tf_op jit(solution)/shard_map/all_to_all | solution.py:17
  88.3 0.7 fusion.41
  89.0 0.0 copy-done.1
  (4 shorter events, 0.1 us)
Async XLA Ops:
  0.6 29.1 %copy-start.3 = (f32[1024]{0:T(1024)S(1)}, f32[1024]{0:T(1024)}, u32[]{:S(2)}) copy-start(f32[1024]{0:T(1024)} %param.11) | copy-start | bytes 12292
  0.6 29.1 %copy-start.4 = (f32[1024]{0:T(1024)S(1)}, f32[1024]{0:T(1024)}, u32[]{:S(2)}) copy-start(f32[1024]{0:T(1024)} %param.10) | copy-start | bytes 12292
  0.7 29.1 %copy-start = (bf16[1,1024,2304]{2,1,0:T(8,128)(2,1)S(1)}, bf16[1,1024,2304]{2,1,0:T(8,128)(2,1)}, u32[]{:S(2)}) copy-start(bf16[1,1024,2304]{2,1,0:T(8,128)(2,1)} %param.9) | copy-start | bytes 14155780
  22.4 12.4 %copy-start.5 = (f32[1,2304]{1,0:T(1,128)S(1)}, f32[1,2304]{1,0:T(1,128)}, u32[]{:S(2)}) copy-start(f32[1,2304]{1,0:T(1,128)} %param.12) | copy-start | bytes 27652
  22.5 12.4 %copy-start.6 = (s32[64]{0:T(128)S(1)}, s32[64]{0:T(128)}, u32[]{:S(2)}) copy-start(s32[64]{0:T(128)} %param.13) | copy-start | bytes 772
  22.5 22.7 %copy-start.2 = (bf16[8,1,2304]{2,0,1:T(8,128)(2,1)S(1)}, bf16[8,1,2304]{2,0,1:T(8,128)(2,1)}, u32[]{:S(2)}) copy-start(bf16[8,1,2304]{2,0,1:T(8,128)(2,1)} %param.7) | copy-start | bytes 110596
  31.4 13.7 %all-to-all-start.1 = ((bf16[8,8,2304]{2,1,0:T(8,128)(2,1)}), bf16[8,8,2304]{2,1,0:T(8,128)(2,1)S(1)}, u32[]{:S(2)}, u32[]{:S(2)}) async-start(bf16[8,8,2304]{2,1,0:T(8,128)(2,1)} %fusion.14), calls=%async_computation.1 | async-start | bytes 589824 | tf_op jit(solution)/shard_map/all_to_all | solution.py:17
  69.8 19.2 %copy-start.1 = (f32[64,1024]{1,0:T(8,128)}, f32[64,1024]{1,0:T(8,128)S(1)}, u32[]{:S(2)}) copy-start(f32[64,1024]{1,0:T(8,128)S(1)} %convert_reduce_fusion) | copy-start | bytes 786436
  74.6 13.7 %all-to-all-start.3 = ((bf16[8,8,2304]{2,1,0:T(8,128)(2,1)}), bf16[8,8,2304]{2,1,0:T(8,128)(2,1)S(1)}, u32[]{:S(2)}, u32[]{:S(2)}) async-start(bf16[8,8,2304]{2,1,0:T(8,128)(2,1)} %fusion.17), calls=%async_computation.3 | async-start | bytes 589824 | tf_op jit(solution)/shard_map/all_to_all | solution.py:17

commit v2 on v1

v2 whole, which is shorter than its diff:
```python
import functools

import jax
import jax.numpy as jnp
from jax import lax
from jax.experimental import pallas as pl
from jax.experimental.pallas import tpu as pltpu
from jax.sharding import PartitionSpec as P

jump_scale = 0.25
columns = 256
half, wide = jnp.bfloat16, jnp.float32


def near(shape, dtype):
    return pltpu.VMEM(shape, dtype)


def free(shape, dtype):
    return jax.ShapeDtypeStruct(shape, dtype)


def call(body, outs, *args, scratch=(), fetched=0, sent=0):
    here, away = pl.BlockSpec(memory_space=pltpu.VMEM), pl.BlockSpec(memory_space=pl.ANY)
    spaces = [pltpu.HBM] * fetched + [pltpu.VMEM] * (len(args) - fetched)
    return pl.pallas_call(
        body,
        out_shape=outs,
        in_specs=[away] * fetched + [here] * (len(args) - fetched),
        out_specs=[here] * (len(outs) - sent) + [away] * sent,
        scratch_shapes=scratch,
        compiler_params=pltpu.CompilerParams(vmem_limit_bytes=16 << 20),
    )(*map(pltpu.with_memory_space_constraint, args, spaces))


def rows_of(ref):
    return ref[...].reshape(-1, ref.shape[-1])


def begin(block, enc_bias, threshold, enc, dec, copies, bias_near, threshold_near, done):
    n = copies.shape[0]
    moves = [(block, copies.at[i]) for i in range(n)] + [(enc_bias, bias_near), (threshold, threshold_near)]
    moves = [pltpu.make_async_copy(here, there, done.at[i]) for i, (here, there) in enumerate(moves)]
    for move in moves:
        move.start()
    for move in moves:
        move.wait()


def encode(acts, weight, out):
    x = rows_of(acts)
    for at in range(0, out.shape[1], columns):
        out[:, at : at + columns] = jnp.dot(
            x, weight[:, at : at + columns], preferred_element_type=wide
        ).astype(half)


def encode_turned(rows, weight, out):
    x = rows_of(rows)
    for at in range(0, out.shape[1], columns):
        out[:, at : at + columns] = lax.dot_general(
            x, weight[at : at + columns, :], (((1,), (1,)), ((), ())), preferred_element_type=wide
        ).astype(half)


def decode(terms, enc_bias, threshold, weight, out, slope):
    preact = jnp.sum(terms[...].astype(wide), axis=0) + enc_bias[...]
    gating = jax.nn.sigmoid((preact - threshold[...]) / jump_scale)
    slope[...] = gating + preact * gating * (1.0 - gating) / jump_scale
    latent = (preact * gating).astype(half)
    for at in range(0, out.shape[1], columns):
        out[:, at : at + columns] = jnp.dot(
            latent, weight[:, at : at + columns], preferred_element_type=wide
        ).astype(half)


def decode_turned(terms, slope, weight, out, result, total, done):
    latent_grad = jnp.sum(terms[...].astype(wide), axis=0)
    total[...] = latent_grad
    move = pltpu.make_async_copy(total, result, done)
    move.start()
    x = (latent_grad * slope[...]).astype(half)
    for at in range(0, out.shape[1], columns):
        out[:, at : at + columns] = lax.dot_general(
            x, weight[at : at + columns, :], (((1,), (1,)), ((), ())), preferred_element_type=wide
        ).astype(half)
    move.wait()


def compare(terms, dec_bias, acts, token_mask, error, copies, squared):
    rows, tokens = error.shape[0], token_mask.shape[1]
    token = lax.axis_index("feat") * rows + lax.broadcasted_iota(jnp.int32, (rows, tokens), 0)
    own = token == lax.broadcasted_iota(jnp.int32, (rows, tokens), 1)
    mask = jnp.sum(jnp.where(own, token_mask[...].astype(wide), 0.0), axis=1, keepdims=True)
    rebuilt = jnp.sum(terms[...].astype(wide), axis=0)
    found = mask * (rebuilt + dec_bias[...] - acts[...].astype(wide))
    error[...] = found
    copies[...] = jnp.broadcast_to(found.astype(half)[None], copies.shape)
    means = jnp.mean(found * found, axis=1, keepdims=True)
    one = lax.broadcasted_iota(jnp.int32, (rows, rows), 0) == lax.broadcasted_iota(jnp.int32, (rows, rows), 1)
    squared[...] = jnp.sum(jnp.where(one, means, 0.0), axis=0, keepdims=True)


def finish(terms, error, squared, out, squared_out):
    squared_out[...] = squared[...]
    out[...] = (jnp.sum(terms[...].astype(wide), axis=0) - error[...]).astype(half)


def shards(activations, enc_weight, dec_weight, enc_bias, threshold, dec_bias, token_mask):
    n_feat = lax.axis_size("feat")
    tok_dev, _, depth = activations.shape
    tokens, width = n_feat * tok_dev, enc_bias.shape[0]
    enc, dec = enc_weight[0], dec_weight[0]
    acts = activations[:, 0]
    exchange = functools.partial(lax.all_to_all, axis_name="feat", split_axis=0, concat_axis=0)
    by_owner = (n_feat, tok_dev, depth)

    copies, enc_bias, threshold = call(
        begin,
        [near(by_owner, half), near((1, width), wide), near((1, width), wide)],
        acts,
        enc_bias[None],
        threshold[None],
        enc,
        dec,
        scratch=[pltpu.SemaphoreType.DMA((n_feat + 2,))],
        fetched=5,
    )
    whole_acts = exchange(copies)
    [terms] = call(encode, [near((tokens, width), half)], whole_acts, enc)
    terms = lax.all_gather(terms, "layer")
    decoded, slope = call(
        decode,
        [near((tokens, depth), half), near((tokens, width), wide)],
        terms,
        enc_bias,
        threshold,
        dec,
    )
    pieces = exchange(decoded.reshape(by_owner))
    error, copies, squared = call(
        compare,
        [near((tok_dev, depth), wide), near(by_owner, half), near((1, tok_dev), wide)],
        pieces,
        dec_bias,
        acts,
        token_mask[None],
    )
    error_all = exchange(copies)
    [terms] = call(encode_turned, [near((tokens, width), half)], error_all, dec)
    terms = lax.all_gather(terms, "layer")
    grads, latent_grad = call(
        decode_turned,
        [near((tokens, depth), half), free((tokens, width), wide)],
        terms,
        slope,
        enc,
        scratch=[pltpu.VMEM((tokens, width), wide), pltpu.SemaphoreType.DMA],
        sent=1,
    )
    pieces = exchange(grads.reshape(by_owner))
    input_grad, squared = call(
        finish, [free((tok_dev, depth), half), free((1, tok_dev), wide)], pieces, error, squared
    )
    return (squared.T, latent_grad, input_grad[:, None])


def solution(mesh):
    return jax.shard_map(
        shards,
        mesh=mesh,
        in_specs=(
            P("feat", "layer", None),
            P("layer", None, "feat"),
            P("layer", "feat", None),
            P("feat"),
            P("feat"),
            P("layer", None),
            P(),
        ),
        out_specs=(P("feat", "layer"), P(None, "feat"), P("feat", "layer", None)),
        check_vma=False,
    )
```

time: 89.6 us -> 80.3 us (0.90)
  blocking collectives: 45.2 us -> 71.6 us
  waiting for transfers between devices: 19.9 us -> 0 us
  matrix products: 13.5 us -> 0 us
  Pallas kernels: 0 us -> 7.68 us
  starting transfers between devices: 6.84 us -> 0 us
  other arithmetic: 1.76 us -> 0.01 us
  local copies, waits for them, and re-layouts: 1 us -> 0.02 us
    all_to_all x2 -> x4, blocking collectives: 31.5 us -> 57.8 us  [the longest x1 17.7 us: shards(): whole_acts = exchange(copies)]
    all_to_all x2 -> x0, waiting for transfers between devices: 19.9 us -> none  [sum_scatter(): lax.all_to_all(terms.astype(jnp.bfloat16).reshape(n, -1, terms.shape[-1])...]
    dot_general x4 -> x0, matrix products: 13.5 us -> none  [dot(): lax.dot_general(a, b, (dims, ((), ())), preferred_element_type=jnp.float32)]
    pallas_call x0 -> x7, Pallas kernels: none -> 7.68 us  [call(): pl.pallas_call(body, out_shape=outs, in_specs=[away] * fetched + [here] *...]
    all_to_all x2 -> x0, starting transfers between devices: 6.84 us -> none  [sum_scatter(): lax.all_to_all(terms.astype(jnp.bfloat16).reshape(n, -1, terms.shape[-1])...]
    convert_element_type x3 -> x0, other arithmetic: 0.98 us -> none  [the longest x1 0.69 us: shards(): input_grad = (grad_terms - error).astype(jnp.bfloat16)]
    broadcast_in_dim x2 -> x0, local copies, waits for them, and re-layouts: 0.96 us -> none  [spread(): jnp.broadcast_to(block[None], (n, *block.shape))]
  transfers between devices with their start and end apart: 2 -> 0, of which waited for: 2 -> 0; matrix products, arithmetic and copies ran while one was open for 1% -> 0% of each run, Pallas kernels for 0% -> 0%
where the time goes in v2:
time: 80.3 us; the launch traced here: 80 us
  blocking collectives  71.6 us (89%)
  Pallas kernels  7.68 us (10%)
    all_to_all x1, blocking collectives, shards(): whole_acts = exchange(copies)  17.7 us
    all_gather x2, blocking collectives, shards(): terms = lax.all_gather(terms, 'layer')  13.8 us
    all_to_all x1, blocking collectives, shards(): pieces = exchange(grads.reshape(by_owner))  13.5 us
    all_to_all x1, blocking collectives, shards(): pieces = exchange(decoded.reshape(by_owner))  13.5 us
    all_to_all x1, blocking collectives, shards(): error_all = exchange(copies)  13.1 us
    pallas_call x7, Pallas kernels, call(): pl.pallas_call(body, out_shape=outs, in_specs=[away] * fetched + [here] *...  7.68 us

profile of v2, /device:TPU:0, one launch (start us, length us, event | category | flops | bytes accessed | tf_op | source)
XLA Modules:
  0.0 80.0 jit_solution(16689782746858786963)
XLA Ops:
  0.6 0.0 slice-start
  0.6 0.0 copy-start
  0.7 0.0 slice-start.1
  0.7 1.3 %shard_map.94 = (bf16[8,8,2304]{2,1,0:T(8,128)(2,1)S(1)}, f32[1,1024]{1,0:T(1,128)S(1)}, f32[1,1024]{1,0:T(1,128)S(1)}) custom-call(bf16[8,2304]{1,0:T(8,128)(2,1)} %bitcast.24, f32[1,1024]{1,0:T(1,128)} %bitcast.27, f32[1,1024]{1,0:T(1,128)} %bitcast.28, bf16[2304,1024]{1,0:T(8,128)(2,1)} %bitcast.17, bf16[1024,2304]{1,0:T(8,128)(2,1)} %bitcast.12), custom_call_target="tpu_custom_call" | custom-call | tf_op jit(solution)/shard_map/pallas_call | solution.py:26
  2.0 17.7 %all_to_all.20.acts = bf16[8,8,2304]{2,1,0:T(8,128)(2,1)S(1)} all-to-all(bf16[8,8,2304]{2,1,0:T(8,128)(2,1)S(1)} %get-tuple-element.15), channel_id=1, replica_groups=mesh['layer'=4,'feat'=8] {'feat'}, dimensions={0} | all-to-all | bytes 589824 | tf_op jit(solution)/shard_map/all_to_all | solution.py:129
  19.6 0.0 copy-done
  19.6 0.0 copy-start.1
  19.6 0.0 copy-start.2
  19.6 0.0 copy-start.3
  19.6 0.9 %shard_map.95 = bf16[64,1024]{1,0:T(8,128)(2,1)S(1)} custom-call(bf16[8,8,2304]{2,1,0:T(8,128)(2,1)S(1)} %all_to_all.20.acts, bf16[2304,1024]{1,0:T(8,128)(2,1)S(1)} %bitcast.18), custom_call_target="tpu_custom_call" | custom-call | tf_op jit(solution)/shard_map/pallas_call | solution.py:26
  20.6 7.2 %all-gather = bf16[256,1024]{1,0:T(8,128)(2,1)S(1)} all-gather(bf16[64,1024]{1,0:T(8,128)(2,1)S(1)} %shard_map.95), channel_id=2, replica_groups=mesh['layer'=4,'feat'=8] {'layer'}, dimensions={0}, use_global_device_ids=true | all-gather | bytes 655360 | tf_op jit(solution)/shard_map/all_gather | solution.py:131
  27.8 0.0 slice-done
  27.8 0.0 slice-done.1
  27.8 1.0 %shard_map.96 = (bf16[64,2304]{1,0:T(8,128)(2,1)S(1)}, f32[64,1024]{1,0:T(8,128)S(1)}) custom-call(bf16[4,64,1024]{2,1,0:T(8,128)(2,1)S(1)} %bitcast.20, f32[1,1024]{1,0:T(1,128)S(1)} %get-tuple-element.16.enc_bias, f32[1,1024]{1,0:T(1,128)S(1)} %get-tuple-element.17.threshold, bf16[1024,2304]{1,0:T(8,128)(2,1)S(1)} %bitcast.15), custom_call_target="tpu_custom_call" | custom-call | tf_op jit(solution)/shard_map/pallas_call | solution.py:26
  28.8 13.5 %all_to_all.21.terms = bf16[8,8,2304]{2,1,0:T(8,128)(2,1)S(1)} all-to-all(bf16[8,8,2304]{2,1,0:T(8,128)(2,1)S(1)} %bitcast.22), channel_id=1, replica_groups=mesh['layer'=4,'feat'=8] {'feat'}, dimensions={0} | all-to-all | bytes 589824 | tf_op jit(solution)/shard_map/all_to_all | solution.py:140
  42.3 0.0 copy-done.1
  42.3 0.0 copy-done.2
  42.3 0.0 copy-done.3
  42.3 0.2 shard_map.97
  42.5 13.1 %all_to_all.22.rows = bf16[8,8,2304]{2,1,0:T(8,128)(2,1)S(1)} all-to-all(bf16[8,8,2304]{2,1,0:T(8,128)(2,1)S(1)} %get-tuple-element.19), channel_id=1, replica_groups=mesh['layer'=4,'feat'=8] {'feat'}, dimensions={0} | all-to-all | bytes 589824 | tf_op jit(solution)/shard_map/all_to_all | solution.py:149
  55.6 1.5 %shard_map.98 = bf16[64,1024]{1,0:T(8,128)(2,1)S(1)} custom-call(bf16[8,8,2304]{2,1,0:T(8,128)(2,1)S(1)} %all_to_all.22.rows, bf16[1024,2304]{1,0:T(8,128)(2,1)S(1)} %bitcast.16), custom_call_target="tpu_custom_call" | custom-call | tf_op jit(solution)/shard_map/pallas_call | solution.py:26
  57.1 6.6 %all-gather.1 = bf16[256,1024]{1,0:T(8,128)(2,1)S(1)} all-gather(bf16[64,1024]{1,0:T(8,128)(2,1)S(1)} %shard_map.98), channel_id=3, replica_groups=mesh['layer'=4,'feat'=8] {'layer'}, dimensions={0}, use_global_device_ids=true | all-gather | bytes 655360 | tf_op jit(solution)/shard_map/all_gather | solution.py:151
  63.7 2.1 %shard_map.99 = (bf16[64,2304]{1,0:T(8,128)(2,1)S(1)}, f32[64,1024]{1,0:T(8,128)}) custom-call(bf16[4,64,1024]{2,1,0:T(8,128)(2,1)S(1)} %bitcast.21, f32[64,1024]{1,0:T(8,128)S(1)} %get-tuple-element.20.slope, bf16[2304,1024]{1,0:T(8,128)(2,1)S(1)} %bitcast.19), custom_call_target="tpu_custom_call" | custom-call | tf_op jit(solution)/shard_map/pallas_call | solution.py:26
  65.8 13.5 %all_to_all.23.terms = bf16[8,8,2304]{2,1,0:T(8,128)(2,1)S(1)} all-to-all(bf16[8,8,2304]{2,1,0:T(8,128)(2,1)S(1)} %bitcast.23), channel_id=1, replica_groups=mesh['layer'=4,'feat'=8] {'feat'}, dimensions={0} | all-to-all | bytes 589824 | tf_op jit(solution)/shard_map/all_to_all | solution.py:161
  79.3 0.7 shard_map.100
  (1 shorter events, 0.0 us)
Async XLA Ops:
  0.6 27.1 %slice-start = ((s8[4718592]{0:T(1024)(128)(4,1)}), s8[4194304]{0:T(1024)(128)(4,1)S(1)}, s32[]{:S(2)}) async-start(s8[4718592]{0:T(1024)(128)(4,1)} %bitcast.13), calls=%async_computation.4 | async-start | bytes 8388608
  0.6 19.0 %copy-start = (bf16[1,2304,1024]{2,1,0:T(8,128)(2,1)S(1)}, bf16[1,2304,1024]{2,1,0:T(8,128)(2,1)}, u32[]{:S(2)}) copy-start(bf16[1,2304,1024]{2,1,0:T(8,128)(2,1)} %param.8) | copy-start | bytes 14155780
  0.7 27.1 %slice-start.1 = ((s8[4718592]{0:T(1024)(128)(4,1)}), s8[524288]{0:T(1024)(128)(4,1)S(1)}, s32[]{:S(2)}) async-start(s8[4718592]{0:T(1024)(128)(4,1)} %bitcast.13), calls=%async_computation.5 | async-start | bytes 1048576
  19.6 22.6 %copy-start.1 = (bf16[8,1,2304]{2,0,1:T(8,128)(2,1)S(1)}, bf16[8,1,2304]{2,0,1:T(8,128)(2,1)}, u32[]{:S(2)}) copy-start(bf16[8,1,2304]{2,0,1:T(8,128)(2,1)} %param.7) | copy-start | bytes 110596
  19.6 22.6 %copy-start.2 = (f32[1,2304]{1,0:T(1,128)S(1)}, f32[1,2304]{1,0:T(1,128)}, u32[]{:S(2)}) copy-start(f32[1,2304]{1,0:T(1,128)} %dec_bias.1) | copy-start | bytes 27652
  19.6 22.6 %copy-start.3 = (s32[64]{0:T(128)S(1)}, s32[64]{0:T(128)}, u32[]{:S(2)}) copy-start(s32[64]{0:T(128)} %param.13) | copy-start | bytes 772

commit v3 on v2

--- a/solution.py
+++ b/solution.py
@@ -33,6 +33,20 @@
     )(*map(pltpu.with_memory_space_constraint, args, spaces))
 
 
+def add(one, other, out):
+    out[...] = (one[...].astype(wide) + other[...].astype(wide)).astype(half)
+
+
+def swap_sums(terms, axis):
+    n, span = lax.axis_size(axis), 1
+    while True:
+        other = lax.ppermute(terms, axis, [(i, i ^ span) for i in range(n)])
+        span *= 2
+        if span == n:
+            return terms, other
+        [terms] = call(add, [near(terms.shape, half)], terms, other)
+
+
 def rows_of(ref):
     return ref[...].reshape(-1, ref.shape[-1])
 
@@ -63,8 +77,8 @@
         ).astype(half)
 
 
-def decode(terms, enc_bias, threshold, weight, out, slope):
-    preact = jnp.sum(terms[...].astype(wide), axis=0) + enc_bias[...]
+def decode(terms, others, enc_bias, threshold, weight, out, slope):
+    preact = terms[...].astype(wide) + others[...].astype(wide) + enc_bias[...]
     gating = jax.nn.sigmoid((preact - threshold[...]) / jump_scale)
     slope[...] = gating + preact * gating * (1.0 - gating) / jump_scale
     latent = (preact * gating).astype(half)
@@ -74,8 +88,8 @@
         ).astype(half)
 
 
-def decode_turned(terms, slope, weight, out, result, total, done):
-    latent_grad = jnp.sum(terms[...].astype(wide), axis=0)
+def decode_turned(terms, others, slope, weight, out, result, total, done):
+    latent_grad = terms[...].astype(wide) + others[...].astype(wide)
     total[...] = latent_grad
     move = pltpu.make_async_copy(total, result, done)
     move.start()
@@ -128,11 +142,12 @@
     )
     whole_acts = exchange(copies)
     [terms] = call(encode, [near((tokens, width), half)], whole_acts, enc)
-    terms = lax.all_gather(terms, "layer")
+    terms, others = swap_sums(terms, "layer")
     decoded, slope = call(
         decode,
         [near((tokens, depth), half), near((tokens, width), wide)],
         terms,
+        others,
         enc_bias,
         threshold,
         dec,
@@ -148,11 +163,12 @@
     )
     error_all = exchange(copies)
     [terms] = call(encode_turned, [near((tokens, width), half)], error_all, dec)
-    terms = lax.all_gather(terms, "layer")
+    terms, others = swap_sums(terms, "layer")
     grads, latent_grad = call(
         decode_turned,
         [near((tokens, depth), half), free((tokens, width), wide)],
         terms,
+        others,
         slope,
         enc,
         scratch=[pltpu.VMEM((tokens, width), wide), pltpu.SemaphoreType.DMA],

time: 80.3 us -> 78 us (0.971)
  blocking collectives: 71.6 us -> 55.2 us
  waiting for transfers between devices: 0 us -> 10.8 us
  starting transfers between devices: 0 us -> 3.26 us
    all_gather x2 -> x0, blocking collectives: 13.8 us -> none  [shards(): terms = lax.all_gather(terms, 'layer')]
    ppermute x0 -> x4, waiting for transfers between devices: none -> 10.8 us  [swap_sums(): other = lax.ppermute(terms, axis, [(i, i ^ span) for i in range(n)])]
    ppermute x0 -> x4, starting transfers between devices: none -> 3.26 us  [swap_sums(): other = lax.ppermute(terms, axis, [(i, i ^ span) for i in range(n)])]
    all_to_all x1, blocking collectives: 13.5 us -> 12.5 us  [shards(): pieces = exchange(grads.reshape(by_owner))]
    all_to_all x1, blocking collectives: 13.5 us -> 12.5 us  [shards(): pieces = exchange(decoded.reshape(by_owner))]
    pallas_call x7 -> x9, Pallas kernels: 7.68 us -> 7.71 us  [call(): pl.pallas_call(body, out_shape=outs, in_specs=[away] * fetched + [here] *...]
  transfers between devices with their start and end apart: 0 -> 4, of which waited for: 0 -> 4; matrix products, arithmetic and copies ran while one was open for 0% -> 0% of each run, Pallas kernels for 0% -> 0%
where the time goes in v3:
time: 78 us; the launch traced here: 77.7 us
  blocking collectives  55.2 us (71%)
  waiting for transfers between devices  10.8 us (14%)
  Pallas kernels  7.71 us (10%)
  starting transfers between devices  3.26 us (4%)
    all_to_all x1, blocking collectives, shards(): whole_acts = exchange(copies)  17.7 us
    all_to_all x1, blocking collectives, shards(): pieces = exchange(decoded.reshape(by_owner))  12.5 us
    all_to_all x1, blocking collectives, shards(): pieces = exchange(grads.reshape(by_owner))  12.5 us
    all_to_all x1, blocking collectives, shards(): error_all = exchange(copies)  12.5 us
    ppermute x4, waiting for transfers between devices, swap_sums(): other = lax.ppermute(terms, axis, [(i, i ^ span) for i in range(n)])  10.8 us
    pallas_call x9, Pallas kernels, call(): pl.pallas_call(body, out_shape=outs, in_specs=[away] * fetched + [here] *...  7.71 us
    ppermute x4, starting transfers between devices, swap_sums(): other = lax.ppermute(terms, axis, [(i, i ^ span) for i in range(n)])  3.26 us
  transfers between devices with their start and end apart: 4, of which 4 were waited for; matrix products, arithmetic and copies ran while one was open for 0% of the time, Pallas kernels for 0%

profile of v3, /device:TPU:0, one launch (start us, length us, event | category | flops | bytes accessed | tf_op | source)
XLA Modules:
  0.0 77.7 jit_solution(4871472331866348119)
XLA Ops:
  0.6 0.0 slice-start
  0.6 0.0 copy-start
  0.7 0.0 slice-start.1
  0.7 1.3 %shard_map.94 = (bf16[8,8,2304]{2,1,0:T(8,128)(2,1)S(1)}, f32[1,1024]{1,0:T(1,128)S(1)}, f32[1,1024]{1,0:T(1,128)S(1)}) custom-call(bf16[8,2304]{1,0:T(8,128)(2,1)} %bitcast.20, f32[1,1024]{1,0:T(1,128)} %bitcast.23, f32[1,1024]{1,0:T(1,128)} %bitcast.24, bf16[2304,1024]{1,0:T(8,128)(2,1)} %bitcast.15, bf16[1024,2304]{1,0:T(8,128)(2,1)} %bitcast.10), custom_call_target="tpu_custom_call" | custom-call | tf_op jit(solution)/shard_map/pallas_call | solution.py:26
  2.0 17.7 %all_to_all.20.acts = bf16[8,8,2304]{2,1,0:T(8,128)(2,1)S(1)} all-to-all(bf16[8,8,2304]{2,1,0:T(8,128)(2,1)S(1)} %get-tuple-element.15), channel_id=1, replica_groups=mesh['layer'=4,'feat'=8] {'feat'}, dimensions={0} | all-to-all | bytes 589824 | tf_op jit(solution)/shard_map/all_to_all | solution.py:143
  19.6 0.0 copy-done
  19.6 0.0 copy-start.1
  19.6 0.0 copy-start.2
  19.6 0.0 copy-start.3
  19.6 0.9 %shard_map.95.one = bf16[64,1024]{1,0:T(8,128)(2,1)S(1)} custom-call(bf16[8,8,2304]{2,1,0:T(8,128)(2,1)S(1)} %all_to_all.20.acts, bf16[2304,1024]{1,0:T(8,128)(2,1)S(1)} %bitcast.16), custom_call_target="tpu_custom_call" | custom-call | tf_op jit(solution)/shard_map/pallas_call | solution.py:26
  20.6 0.1 collective-permute-start
  20.7 1.3 %collective-permute-done.other = bf16[64,1024]{1,0:T(8,128)(2,1)S(1)} collective-permute-done((bf16[64,1024]{1,0:T(8,128)(2,1)S(1)}, bf16[64,1024]{1,0:T(8,128)(2,1)S(1)}, u32[]{:S(2)}, u32[]{:S(2)}) %collective-permute-start) | collective-permute-done | bytes 131104 | tf_op jit(solution)/shard_map/ppermute | solution.py:43
  22.0 1.6 %collective-permute-start.1 = (bf16[64,1024]{1,0:T(8,128)(2,1)S(1)}, bf16[64,1024]{1,0:T(8,128)(2,1)S(1)}, u32[]{:S(2)}, u32[]{:S(2)}) collective-permute-start(bf16[64,1024]{1,0:T(8,128)(2,1)S(1)} %shard_map.96.terms), channel_id=1, source_target_pairs={{0,16},{8,24},{16,0},{24,8},{1,17},{9,25},{17,1},{25,9},{2,18},{10... | collective-permute-start | bytes 393224 | tf_op jit(solution)/shard_map/ppermute | solution.py:43
  23.6 4.1 %collective-permute-done.1.others = bf16[64,1024]{1,0:T(8,128)(2,1)S(1)} collective-permute-done((bf16[64,1024]{1,0:T(8,128)(2,1)S(1)}, bf16[64,1024]{1,0:T(8,128)(2,1)S(1)}, u32[]{:S(2)}, u32[]{:S(2)}) %collective-permute-start.1) | collective-permute-done | bytes 131104 | tf_op jit(solution)/shard_map/ppermute | solution.py:43
  27.7 0.0 slice-done
  27.7 0.0 slice-done.1
  27.7 1.0 %shard_map.97 = (bf16[64,2304]{1,0:T(8,128)(2,1)S(1)}, f32[64,1024]{1,0:T(8,128)S(1)}) custom-call(bf16[64,1024]{1,0:T(8,128)(2,1)S(1)} %shard_map.96.terms, bf16[64,1024]{1,0:T(8,128)(2,1)S(1)} %collective-permute-done.1.others, f32[1,1024]{1,0:T(1,128)S(1)} %get-tuple-element.16.enc_bias, f32[1,1024]{1,0:T(1,128)S(1)} %get-tuple-element.17.threshold, ...), custom_call_target="tpu_custom_call" | custom-call | tf_op jit(solution)/shard_map/pallas_call | solution.py:26
  28.6 12.5 %all_to_all.21.terms = bf16[8,8,2304]{2,1,0:T(8,128)(2,1)S(1)} all-to-all(bf16[8,8,2304]{2,1,0:T(8,128)(2,1)S(1)} %bitcast.18), channel_id=1, replica_groups=mesh['layer'=4,'feat'=8] {'feat'}, dimensions={0} | all-to-all | bytes 589824 | tf_op jit(solution)/shard_map/all_to_all | solution.py:155
  41.2 0.0 copy-done.1
  41.2 0.0 copy-done.2
  41.2 0.0 copy-done.3
  41.2 0.2 shard_map.98
  41.4 12.5 %all_to_all.22.rows = bf16[8,8,2304]{2,1,0:T(8,128)(2,1)S(1)} all-to-all(bf16[8,8,2304]{2,1,0:T(8,128)(2,1)S(1)} %get-tuple-element.19), channel_id=1, replica_groups=mesh['layer'=4,'feat'=8] {'feat'}, dimensions={0} | all-to-all | bytes 589824 | tf_op jit(solution)/shard_map/all_to_all | solution.py:164
  53.8 1.5 %shard_map.99.one = bf16[64,1024]{1,0:T(8,128)(2,1)S(1)} custom-call(bf16[8,8,2304]{2,1,0:T(8,128)(2,1)S(1)} %all_to_all.22.rows, bf16[1024,2304]{1,0:T(8,128)(2,1)S(1)} %bitcast.14), custom_call_target="tpu_custom_call" | custom-call | tf_op jit(solution)/shard_map/pallas_call | solution.py:26
  55.4 0.1 collective-permute-start.2
  55.4 1.3 %collective-permute-done.2.other = bf16[64,1024]{1,0:T(8,128)(2,1)S(1)} collective-permute-done((bf16[64,1024]{1,0:T(8,128)(2,1)S(1)}, bf16[64,1024]{1,0:T(8,128)(2,1)S(1)}, u32[]{:S(2)}, u32[]{:S(2)}) %collective-permute-start.2) | collective-permute-done | bytes 131104 | tf_op jit(solution)/shard_map/ppermute | solution.py:43
  56.8 1.6 %collective-permute-start.3 = (bf16[64,1024]{1,0:T(8,128)(2,1)S(1)}, bf16[64,1024]{1,0:T(8,128)(2,1)S(1)}, u32[]{:S(2)}, u32[]{:S(2)}) collective-permute-start(bf16[64,1024]{1,0:T(8,128)(2,1)S(1)} %shard_map.100.terms), channel_id=1, source_target_pairs={{0,16},{8,24},{16,0},{24,8},{1,17},{9,25},{17,1},{25,9},{2,18},{10... | collective-permute-start | bytes 393224 | tf_op jit(solution)/shard_map/ppermute | solution.py:43
  58.4 4.1 %collective-permute-done.3.others = bf16[64,1024]{1,0:T(8,128)(2,1)S(1)} collective-permute-done((bf16[64,1024]{1,0:T(8,128)(2,1)S(1)}, bf16[64,1024]{1,0:T(8,128)(2,1)S(1)}, u32[]{:S(2)}, u32[]{:S(2)}) %collective-permute-start.3) | collective-permute-done | bytes 131104 | tf_op jit(solution)/shard_map/ppermute | solution.py:43
  62.4 2.1 %shard_map.101 = (bf16[64,2304]{1,0:T(8,128)(2,1)S(1)}, f32[64,1024]{1,0:T(8,128)}) custom-call(bf16[64,1024]{1,0:T(8,128)(2,1)S(1)} %shard_map.100.terms, bf16[64,1024]{1,0:T(8,128)(2,1)S(1)} %collective-permute-done.3.others, f32[64,1024]{1,0:T(8,128)S(1)} %get-tuple-element.20.slope, bf16[2304,1024]{1,0:T(8,128)(2,1)S(1)} %bitcast.17), custom_call_target="tpu_custom_call" | custom-call | tf_op jit(solution)/shard_map/pallas_call | solution.py:26
  64.5 12.5 %all_to_all.23.terms = bf16[8,8,2304]{2,1,0:T(8,128)(2,1)S(1)} all-to-all(bf16[8,8,2304]{2,1,0:T(8,128)(2,1)S(1)} %bitcast.19), channel_id=1, replica_groups=mesh['layer'=4,'feat'=8] {'feat'}, dimensions={0} | all-to-all | bytes 589824 | tf_op jit(solution)/shard_map/all_to_all | solution.py:177
  77.0 0.7 shard_map.102
  (3 shorter events, 0.1 us)
Async XLA Ops:
  0.6 27.0 %slice-start = ((s8[4718592]{0:T(1024)(128)(4,1)}), s8[4194304]{0:T(1024)(128)(4,1)S(1)}, s32[]{:S(2)}) async-start(s8[4718592]{0:T(1024)(128)(4,1)} %bitcast.11), calls=%async_computation.4 | async-start | bytes 8388608
  0.6 19.0 %copy-start = (bf16[1,2304,1024]{2,1,0:T(8,128)(2,1)S(1)}, bf16[1,2304,1024]{2,1,0:T(8,128)(2,1)}, u32[]{:S(2)}) copy-start(bf16[1,2304,1024]{2,1,0:T(8,128)(2,1)} %param.8) | copy-start | bytes 14155780
  0.7 27.0 %slice-start.1 = ((s8[4718592]{0:T(1024)(128)(4,1)}), s8[524288]{0:T(1024)(128)(4,1)S(1)}, s32[]{:S(2)}) async-start(s8[4718592]{0:T(1024)(128)(4,1)} %bitcast.11), calls=%async_computation.5 | async-start | bytes 1048576
  19.6 21.5 %copy-start.1 = (bf16[8,1,2304]{2,0,1:T(8,128)(2,1)S(1)}, bf16[8,1,2304]{2,0,1:T(8,128)(2,1)}, u32[]{:S(2)}) copy-start(bf16[8,1,2304]{2,0,1:T(8,128)(2,1)} %param.7) | copy-start | bytes 110596
  19.6 21.5 %copy-start.2 = (f32[1,2304]{1,0:T(1,128)S(1)}, f32[1,2304]{1,0:T(1,128)}, u32[]{:S(2)}) copy-start(f32[1,2304]{1,0:T(1,128)} %dec_bias.1) | copy-start | bytes 27652
  19.6 21.5 %copy-start.3 = (s32[64]{0:T(128)S(1)}, s32[64]{0:T(128)}, u32[]{:S(2)}) copy-start(s32[64]{0:T(128)} %param.13) | copy-start | bytes 772
  20.6 1.4 %collective-permute-start = (bf16[64,1024]{1,0:T(8,128)(2,1)S(1)}, bf16[64,1024]{1,0:T(8,128)(2,1)S(1)}, u32[]{:S(2)}, u32[]{:S(2)}) collective-permute-start(bf16[64,1024]{1,0:T(8,128)(2,1)S(1)} %shard_map.95.one), channel_id=1, source_target_pairs={{0,8},{8,0},{16,24},{24,16},{1,9},{9,1},{17,25},{25,17},{2,10},{10... | collective-permute-start | bytes 393224 | tf_op jit(solution)/shard_map/ppermute | solution.py:43
  22.0 5.6 %collective-permute-start.1 = (bf16[64,1024]{1,0:T(8,128)(2,1)S(1)}, bf16[64,1024]{1,0:T(8,128)(2,1)S(1)}, u32[]{:S(2)}, u32[]{:S(2)}) collective-permute-start(bf16[64,1024]{1,0:T(8,128)(2,1)S(1)} %shard_map.96.terms), channel_id=1, source_target_pairs={{0,16},{8,24},{16,0},{24,8},{1,17},{9,25},{17,1},{25,9},{2,18},{10... | collective-permute-start | bytes 393224 | tf_op jit(solution)/shard_map/ppermute | solution.py:43
  55.4 1.4 %collective-permute-start.2 = (bf16[64,1024]{1,0:T(8,128)(2,1)S(1)}, bf16[64,1024]{1,0:T(8,128)(2,1)S(1)}, u32[]{:S(2)}, u32[]{:S(2)}) collective-permute-start(bf16[64,1024]{1,0:T(8,128)(2,1)S(1)} %shard_map.99.one), channel_id=1, source_target_pairs={{0,8},{8,0},{16,24},{24,16},{1,9},{9,1},{17,25},{25,17},{2,10},{10... | collective-permute-start | bytes 393224 | tf_op jit(solution)/shard_map/ppermute | solution.py:43
  56.8 5.6 %collective-permute-start.3 = (bf16[64,1024]{1,0:T(8,128)(2,1)S(1)}, bf16[64,1024]{1,0:T(8,128)(2,1)S(1)}, u32[]{:S(2)}, u32[]{:S(2)}) collective-permute-start(bf16[64,1024]{1,0:T(8,128)(2,1)S(1)} %shard_map.100.terms), channel_id=1, source_target_pairs={{0,16},{8,24},{16,0},{24,8},{1,17},{9,25},{17,1},{25,9},{2,18},{10... | collective-permute-start | bytes 393224 | tf_op jit(solution)/shard_map/ppermute | solution.py:43

commit v4 on v3

v4 whole, which is shorter than its diff:
```python
import functools

import jax
import jax.numpy as jnp
from jax import lax
from jax.experimental import pallas as pl
from jax.experimental.pallas import tpu as pltpu
from jax.sharding import PartitionSpec as P

jump_scale = 0.25
columns = 256
half, wide = jnp.bfloat16, jnp.float32


def near(shape, dtype):
    return pltpu.VMEM(shape, dtype)


def free(shape, dtype):
    return jax.ShapeDtypeStruct(shape, dtype)


def call(body, outs, *args, scratch=(), fetched=0, sent=0, work=False, same={}):
    here, away = pl.BlockSpec(memory_space=pltpu.VMEM), pl.BlockSpec(memory_space=pl.ANY)
    size = sum(a.size * a.dtype.itemsize for a in args)
    cost = pl.CostEstimate(flops=0, transcendentals=0, bytes_accessed=2 * size) if work else None
    spaces = [pltpu.HBM] * fetched + [pltpu.VMEM] * (len(args) - fetched)
    return pl.pallas_call(
        body,
        out_shape=outs,
        in_specs=[away] * fetched + [here] * (len(args) - fetched),
        out_specs=[here] * (len(outs) - sent) + [away] * sent,
        scratch_shapes=scratch,
        compiler_params=pltpu.CompilerParams(vmem_limit_bytes=16 << 20),
        cost_estimate=cost,
        input_output_aliases=same,
    )(*map(pltpu.with_memory_space_constraint, args, spaces))


def add(one, other, out):
    out[...] = (one[...].astype(wide) + other[...].astype(wide)).astype(half)


def swap_sums(terms, axis, weight):
    n, span = lax.axis_size(axis), 1
    while True:
        other = lax.ppermute(terms, axis, [(i, i ^ span) for i in range(n)])
        span *= 2
        if span == n:
            [turned] = call(turn, [near(weight.shape[::-1], half)], weight, terms, work=True)
            return terms, other, turned
        [terms] = call(add, [near(terms.shape, half)], terms, other)


def rows_of(ref):
    return ref[...].reshape(-1, ref.shape[-1])


def encode(acts, weight, out):
    x = rows_of(acts)
    for at in range(0, out.shape[1], columns):
        out[:, at : at + columns] = jnp.dot(
            x, weight[:, at : at + columns], preferred_element_type=wide
        ).astype(half)


def encode_first(enc_bias, threshold, acts, weight, out, bias_near, threshold_near, done):
    moves = [
        pltpu.make_async_copy(enc_bias, bias_near, done.at[0]),
        pltpu.make_async_copy(threshold, threshold_near, done.at[1]),
    ]
    for move in moves:
        move.start()
    encode(acts, weight, out)
    for move in moves:
        move.wait()


def turn(weight, after, out):
    for at in range(0, weight.shape[0], columns):
        out[:, at : at + columns] = weight[at : at + columns, :].T


def decode(terms, others, enc_bias, threshold, weight, before, out, slope):
    preact = terms[...].astype(wide) + others[...].astype(wide) + enc_bias[...]
    gating = jax.nn.sigmoid((preact - threshold[...]) / jump_scale)
    slope[...] = gating + preact * gating * (1.0 - gating) / jump_scale
    latent = (preact * gating).astype(half)
    for at in range(0, out.shape[1], columns):
        out[:, at : at + columns] = jnp.dot(
            latent, weight[:, at : at + columns], preferred_element_type=wide
        ).astype(half)


def decode_grad(terms, others, slope, weight, out, total):
    latent_grad = terms[...].astype(wide) + others[...].astype(wide)
    total[...] = latent_grad
    x = (latent_grad * slope[...]).astype(half)
    for at in range(0, out.shape[1], columns):
        out[:, at : at + columns] = jnp.dot(
            x, weight[:, at : at + columns], preferred_element_type=wide
        ).astype(half)


def compare(terms, dec_bias, acts, token_mask, error, copies, squared):
    rows, tokens = error.shape[0], token_mask.shape[1]
    token = lax.axis_index("feat") * rows + lax.broadcasted_iota(jnp.int32, (rows, tokens), 0)
    own = token == lax.broadcasted_iota(jnp.int32, (rows, tokens), 1)
    mask = jnp.sum(jnp.where(own, token_mask[...].astype(wide), 0.0), axis=1, keepdims=True)
    rebuilt = jnp.sum(terms[...].astype(wide), axis=0)
    found = mask * (rebuilt + dec_bias[...] - acts[...].astype(wide))
    error[...] = found
    copies[...] = jnp.broadcast_to(found.astype(half)[None], copies.shape)
    means = jnp.mean(found * found, axis=1, keepdims=True)
    one = lax.broadcasted_iota(jnp.int32, (rows, rows), 0) == lax.broadcasted_iota(jnp.int32, (rows, rows), 1)
    squared[...] = jnp.sum(jnp.where(one, means, 0.0), axis=0, keepdims=True)


def finish(terms, error, squared, total, out, squared_out, total_out, held, done):
    moves = [(total, total_out), (squared, squared_out), (held, out)]
    moves = [pltpu.make_async_copy(here, there, done.at[i]) for i, (here, there) in enumerate(moves)]
    moves[0].start()
    moves[1].start()
    held[...] = (jnp.sum(terms[...].astype(wide), axis=0) - error[...]).astype(half)
    moves[2].start()
    for move in moves:
        move.wait()


def shards(activations, enc_weight, dec_weight, enc_bias, threshold, dec_bias, token_mask):
    n_feat = lax.axis_size("feat")
    tok_dev, _, depth = activations.shape
    tokens, width = n_feat * tok_dev, enc_bias.shape[0]
    enc, dec = enc_weight[0], dec_weight[0]
    acts = activations[:, 0]
    exchange = functools.partial(lax.all_to_all, axis_name="feat", split_axis=0, concat_axis=0)
    by_owner = (n_feat, tok_dev, depth)

    copies = jnp.broadcast_to(acts[None], by_owner)
    [copies] = call(lambda *refs: None, [near(by_owner, half)], enc, dec, copies, fetched=2, same={2: 0})
    whole_acts = exchange(copies)
    terms, enc_bias, threshold = call(
        encode_first,
        [near((tokens, width), half), near((1, width), wide), near((1, width), wide)],
        enc_bias[None],
        threshold[None],
        whole_acts,
        enc,
        scratch=[pltpu.SemaphoreType.DMA((2,))],
        fetched=2,
    )
    terms, others, dec_turned = swap_sums(terms, "layer", dec)
    decoded, slope = call(
        decode,
        [near((tokens, depth), half), near((tokens, width), wide)],
        terms,
        others,
        enc_bias,
        threshold,
        dec,
        dec_turned,
    )
    pieces = exchange(decoded.reshape(by_owner))
    error, copies, squared = call(
        compare,
        [near((tok_dev, depth), wide), near(by_owner, half), near((1, tok_dev), wide)],
        pieces,
        dec_bias,
        acts,
        token_mask[None],
    )
    error_all = exchange(copies)
    [terms] = call(encode, [near((tokens, width), half)], error_all, dec_turned)
    terms, others, enc_turned = swap_sums(terms, "layer", enc)
    grads, latent_grad = call(
        decode_grad,
        [near((tokens, depth), half), near((tokens, width), wide)],
        terms,
        others,
        slope,
        enc_turned,
    )
    pieces = exchange(grads.reshape(by_owner))
    input_grad, squared, latent_grad = call(
        finish,
        [free((tok_dev, depth), half), free((1, tok_dev), wide), free((tokens, width), wide)],
        pieces,
        error,
        squared,
        latent_grad,
        scratch=[pltpu.VMEM((tok_dev, depth), half), pltpu.SemaphoreType.DMA((3,))],
        sent=3,
    )
    return (squared.T, latent_grad, input_grad[:, None])


def solution(mesh):
    return jax.shard_map(
        shards,
        mesh=mesh,
        in_specs=(
            P("feat", "layer", None),
            P("layer", None, "feat"),
            P("layer", "feat", None),
            P("feat"),
            P("feat"),
            P("layer", None),
            P(),
        ),
        out_specs=(P("feat", "layer"), P(None, "feat"), P("feat", "layer", None)),
        check_vma=False,
    )
```

time: 78 us -> 76 us (0.974)
  waiting for transfers between devices: 10.8 us -> 8.09 us
  local copies, waits for them, and re-layouts: 0.02 us -> 0.97 us
    ppermute x4, waiting for transfers between devices: 10.8 us -> 8.09 us  [swap_sums(): other = lax.ppermute(terms, axis, [(i, i ^ span) for i in range(n)])]
    broadcast_in_dim x0 -> x1, local copies, waits for them, and re-layouts: none -> 0.94 us  [shards(): copies = jnp.broadcast_to(acts[None], by_owner)]
    pallas_call x9 -> x11, Pallas kernels: 7.71 us -> 7.47 us  [call(): pl.pallas_call(body, out_shape=outs, in_specs=[away] * fetched + [here] *...]
  transfers between devices with their start and end apart: 4 -> 4, of which waited for: 4 -> 4; matrix products, arithmetic and copies ran while one was open for 0% -> 0% of each run, Pallas kernels for 0% -> 4%
where the time goes in v4:
time: 76 us; the launch traced here: 75.7 us
  blocking collectives  55.2 us (73%)
  waiting for transfers between devices  8.09 us (11%)
  Pallas kernels  7.47 us (10%)
  starting transfers between devices  3.25 us (4%)
  local copies, waits for them, and re-layouts  0.97 us (1%)
    all_to_all x1, blocking collectives, shards(): whole_acts = exchange(copies)  17.7 us
    all_to_all x1, blocking collectives, shards(): pieces = exchange(decoded.reshape(by_owner))  12.5 us
    all_to_all x1, blocking collectives, shards(): pieces = exchange(grads.reshape(by_owner))  12.5 us
    all_to_all x1, blocking collectives, shards(): error_all = exchange(copies)  12.5 us
    ppermute x4, waiting for transfers between devices, swap_sums(): other = lax.ppermute(terms, axis, [(i, i ^ span) for i in range(n)])  8.09 us
    pallas_call x11, Pallas kernels, call(): pl.pallas_call(body, out_shape=outs, in_specs=[away] * fetched + [here] *...  7.47 us
    ppermute x4, starting transfers between devices, swap_sums(): other = lax.ppermute(terms, axis, [(i, i ^ span) for i in range(n)])  3.25 us
  transfers between devices with their start and end apart: 4, of which 4 were waited for; matrix products, arithmetic and copies ran while one was open for 0% of the time, Pallas kernels for 4%

profile of v4, /device:TPU:0, one launch (start us, length us, event | category | flops | bytes accessed | tf_op | source)
XLA Modules:
  0.0 75.7 jit_solution(13640303699228136294)
XLA Ops:
  0.6 0.0 slice-start
  0.6 0.9 %broadcast_in_dim.22.refs_2_ = bf16[8,8,2304]{2,1,0:T(8,128)(2,1)S(1)} broadcast(bf16[8,2304]{1,0:T(8,128)(2,1)} %bitcast.20), dimensions={1,2} | broadcast | bytes 331776 | tf_op jit(solution)/shard_map/broadcast_in_dim | solution.py:139
  1.6 0.0 slice-start.1
  1.6 0.0 copy-start
  1.6 17.7 %all_to_all.20.acts = bf16[8,8,2304]{2,1,0:T(8,128)(2,1)S(1)} all-to-all(bf16[8,8,2304]{2,1,0:T(8,128)(2,1)S(1)} %shard_map.94), channel_id=1, replica_groups=mesh['layer'=4,'feat'=8] {'feat'}, dimensions={0} | all-to-all | bytes 589824 | tf_op jit(solution)/shard_map/all_to_all | solution.py:141
  19.3 0.0 slice-done
  19.3 0.0 slice-done.1
  19.3 1.0 %shard_map.95 = (bf16[64,1024]{1,0:T(8,128)(2,1)S(1)}, f32[1,1024]{1,0:T(1,128)S(1)}, f32[1,1024]{1,0:T(1,128)S(1)}) custom-call(f32[1,1024]{1,0:T(1,128)} %bitcast.23, f32[1,1024]{1,0:T(1,128)} %bitcast.24, bf16[8,8,2304]{2,1,0:T(8,128)(2,1)S(1)} %all_to_all.20.acts, bf16[2304,1024]{1,0:T(8,128)(2,1)S(1)} %bitcast.13), custom_call_target="tpu_custom_call" | custom-call | tf_op jit(solution)/shard_map/pallas_call | solution.py:28
  20.3 0.1 collective-permute-start
  20.4 1.3 %collective-permute-done.other = bf16[64,1024]{1,0:T(8,128)(2,1)S(1)} collective-permute-done((bf16[64,1024]{1,0:T(8,128)(2,1)S(1)}, bf16[64,1024]{1,0:T(8,128)(2,1)S(1)}, u32[]{:S(2)}, u32[]{:S(2)}) %collective-permute-start) | collective-permute-done | bytes 131104 | tf_op jit(solution)/shard_map/ppermute | solution.py:47
  21.7 1.6 %collective-permute-start.1 = (bf16[64,1024]{1,0:T(8,128)(2,1)S(1)}, bf16[64,1024]{1,0:T(8,128)(2,1)S(1)}, u32[]{:S(2)}, u32[]{:S(2)}) collective-permute-start(bf16[64,1024]{1,0:T(8,128)(2,1)S(1)} %shard_map.96.after.terms), channel_id=1, source_target_pairs={{0,16},{8,24},{16,0},{24,8},{1,17},{9,25},{17,1},{25,9},{2,18},{10... | collective-permute-start | bytes 393224 | tf_op jit(solution)/shard_map/ppermute | solution.py:47
  23.3 0.0 copy-done
  23.3 1.4 %shard_map.97.before.weight = bf16[2304,1024]{1,0:T(8,128)(2,1)S(1)} custom-call(bf16[1024,2304]{1,0:T(8,128)(2,1)S(1)} %bitcast.16, bf16[64,1024]{1,0:T(8,128)(2,1)S(1)} %shard_map.96.after.terms), custom_call_target="tpu_custom_call" | custom-call | bytes 9699328 | tf_op jit(solution)/shard_map/pallas_call | solution.py:28
  24.7 2.6 %collective-permute-done.1.others = bf16[64,1024]{1,0:T(8,128)(2,1)S(1)} collective-permute-done((bf16[64,1024]{1,0:T(8,128)(2,1)S(1)}, bf16[64,1024]{1,0:T(8,128)(2,1)S(1)}, u32[]{:S(2)}, u32[]{:S(2)}) %collective-permute-start.1) | collective-permute-done | bytes 131104 | tf_op jit(solution)/shard_map/ppermute | solution.py:47
  27.4 0.0 copy-start.1
  27.4 0.0 copy-start.2
  27.4 0.0 copy-start.3
  27.4 1.0 %shard_map.98 = (bf16[64,2304]{1,0:T(8,128)(2,1)S(1)}, f32[64,1024]{1,0:T(8,128)S(1)}) custom-call(bf16[64,1024]{1,0:T(8,128)(2,1)S(1)} %shard_map.96.after.terms, bf16[64,1024]{1,0:T(8,128)(2,1)S(1)} %collective-permute-done.1.others, f32[1,1024]{1,0:T(1,128)S(1)} %get-tuple-element.17.enc_bias, f32[1,1024]{1,0:T(1,128)S(1)} %get-tuple-element.18.threshold, ...), custom_call_target="tpu_custom_call" | custom-call | tf_op jit(solution)/shard_map/pallas_call | solution.py:28
  28.3 12.5 %all_to_all.21.terms = bf16[8,8,2304]{2,1,0:T(8,128)(2,1)S(1)} all-to-all(bf16[8,8,2304]{2,1,0:T(8,128)(2,1)S(1)} %bitcast.18), channel_id=1, replica_groups=mesh['layer'=4,'feat'=8] {'feat'}, dimensions={0} | all-to-all | bytes 589824 | tf_op jit(solution)/shard_map/all_to_all | solution.py:163
  40.8 0.0 copy-done.1
  40.9 0.0 copy-done.2
  40.9 0.0 copy-done.3
  40.9 0.2 shard_map.99
  41.1 12.5 %all_to_all.22.acts = bf16[8,8,2304]{2,1,0:T(8,128)(2,1)S(1)} all-to-all(bf16[8,8,2304]{2,1,0:T(8,128)(2,1)S(1)} %get-tuple-element.20), channel_id=1, replica_groups=mesh['layer'=4,'feat'=8] {'feat'}, dimensions={0} | all-to-all | bytes 589824 | tf_op jit(solution)/shard_map/all_to_all | solution.py:172
  53.5 0.9 %shard_map.100.one = bf16[64,1024]{1,0:T(8,128)(2,1)S(1)} custom-call(bf16[8,8,2304]{2,1,0:T(8,128)(2,1)S(1)} %all_to_all.22.acts, bf16[2304,1024]{1,0:T(8,128)(2,1)S(1)} %shard_map.97.before.weight), custom_call_target="tpu_custom_call" | custom-call | tf_op jit(solution)/shard_map/pallas_call | solution.py:28
  54.5 0.1 collective-permute-start.2
  54.5 1.3 %collective-permute-done.2.other = bf16[64,1024]{1,0:T(8,128)(2,1)S(1)} collective-permute-done((bf16[64,1024]{1,0:T(8,128)(2,1)S(1)}, bf16[64,1024]{1,0:T(8,128)(2,1)S(1)}, u32[]{:S(2)}, u32[]{:S(2)}) %collective-permute-start.2) | collective-permute-done | bytes 131104 | tf_op jit(solution)/shard_map/ppermute | solution.py:47
  55.9 1.6 %collective-permute-start.3 = (bf16[64,1024]{1,0:T(8,128)(2,1)S(1)}, bf16[64,1024]{1,0:T(8,128)(2,1)S(1)}, u32[]{:S(2)}, u32[]{:S(2)}) collective-permute-start(bf16[64,1024]{1,0:T(8,128)(2,1)S(1)} %shard_map.101.after.terms), channel_id=1, source_target_pairs={{0,16},{8,24},{16,0},{24,8},{1,17},{9,25},{17,1},{25,9},{2,18},{10... | collective-permute-start | bytes 393224 | tf_op jit(solution)/shard_map/ppermute | solution.py:47
  57.5 1.3 %shard_map.102.weight = bf16[1024,2304]{1,0:T(8,128)(2,1)S(1)} custom-call(bf16[2304,1024]{1,0:T(8,128)(2,1)S(1)} %bitcast.14, bf16[64,1024]{1,0:T(8,128)(2,1)S(1)} %shard_map.101.after.terms), custom_call_target="tpu_custom_call" | custom-call | bytes 9699328 | tf_op jit(solution)/shard_map/pallas_call | solution.py:28
  58.7 2.8 %collective-permute-done.3.others = bf16[64,1024]{1,0:T(8,128)(2,1)S(1)} collective-permute-done((bf16[64,1024]{1,0:T(8,128)(2,1)S(1)}, bf16[64,1024]{1,0:T(8,128)(2,1)S(1)}, u32[]{:S(2)}, u32[]{:S(2)}) %collective-permute-start.3) | collective-permute-done | bytes 131104 | tf_op jit(solution)/shard_map/ppermute | solution.py:47
  61.5 0.9 %shard_map.103 = (bf16[64,2304]{1,0:T(8,128)(2,1)S(1)}, f32[64,1024]{1,0:T(8,128)S(1)}) custom-call(bf16[64,1024]{1,0:T(8,128)(2,1)S(1)} %shard_map.101.after.terms, bf16[64,1024]{1,0:T(8,128)(2,1)S(1)} %collective-permute-done.3.others, f32[64,1024]{1,0:T(8,128)S(1)} %get-tuple-element.21.slope, bf16[1024,2304]{1,0:T(8,128)(2,1)S(1)} %shard_map.102.weight), custom_call_target="tpu_custom_call" | custom-call | tf_op jit(solution)/shard_map/pallas_call | solution.py:28
  62.5 12.5 %all_to_all.23.terms = bf16[8,8,2304]{2,1,0:T(8,128)(2,1)S(1)} all-to-all(bf16[8,8,2304]{2,1,0:T(8,128)(2,1)S(1)} %bitcast.19), channel_id=1, replica_groups=mesh['layer'=4,'feat'=8] {'feat'}, dimensions={0} | all-to-all | bytes 589824 | tf_op jit(solution)/shard_map/all_to_all | solution.py:183
  75.0 0.7 shard_map.104
  (4 shorter events, 0.1 us)
Async XLA Ops:
  0.6 18.7 %slice-start = ((s8[4718592]{0:T(1024)(128)(4,1)}), s8[4194304]{0:T(1024)(128)(4,1)S(1)}, s32[]{:S(2)}) async-start(s8[4718592]{0:T(1024)(128)(4,1)} %bitcast.11), calls=%async_computation.4 | async-start | bytes 8388608
  1.6 17.7 %slice-start.1 = ((s8[4718592]{0:T(1024)(128)(4,1)}), s8[524288]{0:T(1024)(128)(4,1)S(1)}, s32[]{:S(2)}) async-start(s8[4718592]{0:T(1024)(128)(4,1)} %bitcast.11), calls=%async_computation.5 | async-start | bytes 1048576
  1.6 21.7 %copy-start = (bf16[1,1024,2304]{2,1,0:T(8,128)(2,1)S(1)}, bf16[1,1024,2304]{2,1,0:T(8,128)(2,1)}, u32[]{:S(2)}) copy-start(bf16[1,1024,2304]{2,1,0:T(8,128)(2,1)} %param.9) | copy-start | bytes 14155780
  20.3 1.4 %collective-permute-start = (bf16[64,1024]{1,0:T(8,128)(2,1)S(1)}, bf16[64,1024]{1,0:T(8,128)(2,1)S(1)}, u32[]{:S(2)}, u32[]{:S(2)}) collective-permute-start(bf16[64,1024]{1,0:T(8,128)(2,1)S(1)} %get-tuple-element.16.one), channel_id=1, source_target_pairs={{0,8},{8,0},{16,24},{24,16},{1,9},{9,1},{17,25},{25,17},{2,10},{10... | collective-permute-start | bytes 393224 | tf_op jit(solution)/shard_map/ppermute | solution.py:47
  21.7 5.6 %collective-permute-start.1 = (bf16[64,1024]{1,0:T(8,128)(2,1)S(1)}, bf16[64,1024]{1,0:T(8,128)(2,1)S(1)}, u32[]{:S(2)}, u32[]{:S(2)}) collective-permute-start(bf16[64,1024]{1,0:T(8,128)(2,1)S(1)} %shard_map.96.after.terms), channel_id=1, source_target_pairs={{0,16},{8,24},{16,0},{24,8},{1,17},{9,25},{17,1},{25,9},{2,18},{10... | collective-permute-start | bytes 393224 | tf_op jit(solution)/shard_map/ppermute | solution.py:47
  27.4 13.5 %copy-start.1 = (bf16[8,1,2304]{2,0,1:T(8,128)(2,1)S(1)}, bf16[8,1,2304]{2,0,1:T(8,128)(2,1)}, u32[]{:S(2)}) copy-start(bf16[8,1,2304]{2,0,1:T(8,128)(2,1)} %param.7) | copy-start | bytes 110596
  27.4 13.5 %copy-start.2 = (f32[1,2304]{1,0:T(1,128)S(1)}, f32[1,2304]{1,0:T(1,128)}, u32[]{:S(2)}) copy-start(f32[1,2304]{1,0:T(1,128)} %dec_bias.1) | copy-start | bytes 27652
  27.4 13.5 %copy-start.3 = (s32[64]{0:T(128)S(1)}, s32[64]{0:T(128)}, u32[]{:S(2)}) copy-start(s32[64]{0:T(128)} %param.13) | copy-start | bytes 772
  54.5 1.4 %collective-permute-start.2 = (bf16[64,1024]{1,0:T(8,128)(2,1)S(1)}, bf16[64,1024]{1,0:T(8,128)(2,1)S(1)}, u32[]{:S(2)}, u32[]{:S(2)}) collective-permute-start(bf16[64,1024]{1,0:T(8,128)(2,1)S(1)} %shard_map.100.one), channel_id=1, source_target_pairs={{0,8},{8,0},{16,24},{24,16},{1,9},{9,1},{17,25},{25,17},{2,10},{10... | collective-permute-start | bytes 393224 | tf_op jit(solution)/shard_map/ppermute | solution.py:47
  55.9 5.6 %collective-permute-start.3 = (bf16[64,1024]{1,0:T(8,128)(2,1)S(1)}, bf16[64,1024]{1,0:T(8,128)(2,1)S(1)}, u32[]{:S(2)}, u32[]{:S(2)}) collective-permute-start(bf16[64,1024]{1,0:T(8,128)(2,1)S(1)} %shard_map.101.after.terms), channel_id=1, source_target_pairs={{0,16},{8,24},{16,0},{24,8},{1,17},{9,25},{17,1},{25,9},{2,18},{10... | collective-permute-start | bytes 393224 | tf_op jit(solution)/shard_map/ppermute | solution.py:47

commit v5 on v4

--- a/solution.py
+++ b/solution.py
@@ -76,16 +76,33 @@
         move.wait()
 
 
+def encode_paired(block, rows, weight, out):
+    x = rows_of(rows)
+    places = paired(out.shape[0] // block, block)
+    for at in range(0, out.shape[1], columns):
+        found = jnp.dot(x, weight[:, at : at + columns], preferred_element_type=wide)
+        found = jnp.concatenate([found[place] for place in places])
+        out[:, at : at + columns] = found.astype(half)
+
+
 def turn(weight, after, out):
     for at in range(0, weight.shape[0], columns):
         out[:, at : at + columns] = weight[at : at + columns, :].T
 
 
-def decode(terms, others, enc_bias, threshold, weight, before, out, slope):
+def paired(n, block):
+    at = [(2 * (i % (n // 2)) + i // (n // 2)) * block for i in range(n)]
+    return [slice(first, first + block) for first in at]
+
+
+def decode(block, terms, others, enc_bias, threshold, weight, before, out, slope):
     preact = terms[...].astype(wide) + others[...].astype(wide) + enc_bias[...]
     gating = jax.nn.sigmoid((preact - threshold[...]) / jump_scale)
     slope[...] = gating + preact * gating * (1.0 - gating) / jump_scale
-    latent = (preact * gating).astype(half)
+    n = out.shape[0] // block
+    latent = preact * gating
+    order = [i for first in range(n // 2) for i in (first, first + n // 2)]
+    latent = jnp.concatenate([latent[i * block : (i + 1) * block] for i in order]).astype(half)
     for at in range(0, out.shape[1], columns):
         out[:, at : at + columns] = jnp.dot(
             latent, weight[:, at : at + columns], preferred_element_type=wide
@@ -102,15 +119,26 @@
         ).astype(half)
 
 
-def compare(terms, dec_bias, acts, token_mask, error, copies, squared):
-    rows, tokens = error.shape[0], token_mask.shape[1]
-    token = lax.axis_index("feat") * rows + lax.broadcasted_iota(jnp.int32, (rows, tokens), 0)
-    own = token == lax.broadcasted_iota(jnp.int32, (rows, tokens), 1)
+def add_up(terms, out, sent):
+    found = jnp.sum(terms[...].astype(wide), axis=0)
+    out[...] = found
+    sent[...] = found.astype(half)
+
+
+def compare(one, other, dec_bias, acts, token_mask, error, copies, squared, held):
+    n, rows, _ = acts.shape
+    tokens = token_mask.shape[1]
+    me = lax.axis_index("feat")
+    place, upper = lax.rem(me, n // 2), me // (n // 2)
+    row = lax.broadcasted_iota(jnp.int32, (2 * rows, tokens), 0)
+    token = jnp.where(row < rows, place * rows + row, (place + n // 2) * rows + row - rows)
+    own = token == lax.broadcasted_iota(jnp.int32, (2 * rows, tokens), 1)
     mask = jnp.sum(jnp.where(own, token_mask[...].astype(wide), 0.0), axis=1, keepdims=True)
-    rebuilt = jnp.sum(terms[...].astype(wide), axis=0)
-    found = mask * (rebuilt + dec_bias[...] - acts[...].astype(wide))
+    here = jnp.concatenate([acts[place].astype(wide), acts[place + n // 2].astype(wide)])
+    held[...] = mask * (one[...] + other[...].astype(wide) + dec_bias[...] - here)
+    copies[...] = jnp.broadcast_to(held[...].astype(half)[None], copies.shape)
+    found = held[pl.ds(pl.multiple_of(upper * rows, rows), rows), :]
     error[...] = found
-    copies[...] = jnp.broadcast_to(found.astype(half)[None], copies.shape)
     means = jnp.mean(found * found, axis=1, keepdims=True)
     one = lax.broadcasted_iota(jnp.int32, (rows, rows), 0) == lax.broadcasted_iota(jnp.int32, (rows, rows), 1)
     squared[...] = jnp.sum(jnp.where(one, means, 0.0), axis=0, keepdims=True)
@@ -151,7 +179,7 @@
     )
     terms, others, dec_turned = swap_sums(terms, "layer", dec)
     decoded, slope = call(
-        decode,
+        functools.partial(decode, tok_dev),
         [near((tokens, depth), half), near((tokens, width), wide)],
         terms,
         others,
@@ -160,17 +188,25 @@
         dec,
         dec_turned,
     )
-    pieces = exchange(decoded.reshape(by_owner))
+    by_pair = (n_feat // 2, 2 * tok_dev, depth)
+    halves = [list(range(n_feat // 2)), list(range(n_feat // 2, n_feat))]
+    pieces = exchange(decoded.reshape(by_pair), axis_index_groups=halves)
+    one, other = call(add_up, [near(by_pair[1:], wide), near(by_pair[1:], half)], pieces)
+    other = lax.ppermute(other, "feat", [(i, (i + n_feat // 2) % n_feat) for i in range(n_feat)])
     error, copies, squared = call(
         compare,
-        [near((tok_dev, depth), wide), near(by_owner, half), near((1, tok_dev), wide)],
-        pieces,
+        [near((tok_dev, depth), wide), near(by_pair, half), near((1, tok_dev), wide)],
+        one,
+        other,
         dec_bias,
-        acts,
+        whole_acts,
         token_mask[None],
-    )
-    error_all = exchange(copies)
-    [terms] = call(encode, [near((tokens, width), half)], error_all, dec_turned)
+        scratch=[pltpu.VMEM(by_pair[1:], wide)],
+    )
+    error_all = exchange(copies, axis_index_groups=halves)
+    [terms] = call(
+        functools.partial(encode_paired, tok_dev), [near((tokens, width), half)], error_all, dec_turned
+    )
     terms, others, enc_turned = swap_sums(terms, "layer", enc)
     grads, latent_grad = call(
         decode_grad,

time: 76 us -> 74.1 us (0.975)
  blocking collectives: 55.2 us -> 47.2 us
  waiting for transfers between devices: 8.09 us -> 13.3 us
  starting transfers between devices: 3.25 us -> 4.18 us
    all_to_all x2, blocking collectives: 25 us -> 17 us  [the longest x1 8.53 us: shards(): pieces = exchange(decoded.reshape(by_pair), axis_index_groups=halves)]
    ppermute x0 -> x1, waiting for transfers between devices: none -> 5.18 us  [shards(): lax.ppermute(other, 'feat', [(i, (i + n_feat // 2) % n_feat) for i in ran...]
    ppermute x0 -> x1, starting transfers between devices: none -> 0.93 us  [shards(): lax.ppermute(other, 'feat', [(i, (i + n_feat // 2) % n_feat) for i in ran...]
    pallas_call x11 -> x12, Pallas kernels: 7.47 us -> 7.51 us  [call(): pl.pallas_call(body, out_shape=outs, in_specs=[away] * fetched + [here] *...]
  transfers between devices with their start and end apart: 4 -> 5, of which waited for: 4 -> 5; matrix products, arithmetic and copies ran while one was open for 0% -> 0% of each run, Pallas kernels for 4% -> 4%
where the time goes in v5:
time: 74.1 us; the launch traced here: 73.9 us
  blocking collectives  47.2 us (64%)
  waiting for transfers between devices  13.3 us (18%)
  Pallas kernels  7.51 us (10%)
  starting transfers between devices  4.18 us (6%)
  local copies, waits for them, and re-layouts  0.97 us (1%)
    all_to_all x1, blocking collectives, shards(): whole_acts = exchange(copies)  17.7 us
    all_to_all x1, blocking collectives, shards(): pieces = exchange(grads.reshape(by_owner))  12.5 us
    all_to_all x1, blocking collectives, shards(): pieces = exchange(decoded.reshape(by_pair), axis_index_groups=halves)  8.53 us
    all_to_all x1, blocking collectives, shards(): error_all = exchange(copies, axis_index_groups=halves)  8.51 us
    ppermute x4, waiting for transfers between devices, swap_sums(): other = lax.ppermute(terms, axis, [(i, i ^ span) for i in range(n)])  8.09 us
    pallas_call x12, Pallas kernels, call(): pl.pallas_call(body, out_shape=outs, in_specs=[away] * fetched + [here] *...  7.51 us
    ppermute x1, waiting for transfers between devices, shards(): lax.ppermute(other, 'feat', [(i, (i + n_feat // 2) % n_feat) for i in ran...  5.18 us
    ppermute x4, starting transfers between devices, swap_sums(): other = lax.ppermute(terms, axis, [(i, i ^ span) for i in range(n)])  3.25 us
  transfers between devices with their start and end apart: 5, of which 5 were waited for; matrix products, arithmetic and copies ran while one was open for 0% of the time, Pallas kernels for 4%

profile of v5, /device:TPU:0, one launch (start us, length us, event | category | flops | bytes accessed | tf_op | source)
XLA Modules:
  0.0 73.9 jit_solution(17904398129383933026)
XLA Ops:
  0.6 0.0 slice-start
  0.6 0.9 %broadcast_in_dim.22.refs_2_ = bf16[8,8,2304]{2,1,0:T(8,128)(2,1)S(1)} broadcast(bf16[8,2304]{1,0:T(8,128)(2,1)} %bitcast.21), dimensions={1,2} | broadcast | bytes 331776 | tf_op jit(solution)/shard_map/broadcast_in_dim | solution.py:167
  1.6 0.0 slice-start.1
  1.6 0.0 copy-start
  1.6 17.7 %all_to_all.20.acts = bf16[8,8,2304]{2,1,0:T(8,128)(2,1)S(1)} all-to-all(bf16[8,8,2304]{2,1,0:T(8,128)(2,1)S(1)} %shard_map.94), channel_id=1, replica_groups=mesh['layer'=4,'feat'=8] {'feat'}, dimensions={0} | all-to-all | bytes 589824 | tf_op jit(solution)/shard_map/all_to_all | solution.py:169
  19.3 0.0 slice-done
  19.3 0.0 slice-done.1
  19.3 1.0 %shard_map.95 = (bf16[64,1024]{1,0:T(8,128)(2,1)S(1)}, f32[1,1024]{1,0:T(1,128)S(1)}, f32[1,1024]{1,0:T(1,128)S(1)}) custom-call(f32[1,1024]{1,0:T(1,128)} %bitcast.22, f32[1,1024]{1,0:T(1,128)} %bitcast.23, bf16[8,8,2304]{2,1,0:T(8,128)(2,1)S(1)} %all_to_all.20.acts, bf16[2304,1024]{1,0:T(8,128)(2,1)S(1)} %bitcast.13), custom_call_target="tpu_custom_call" | custom-call | tf_op jit(solution)/shard_map/pallas_call | solution.py:28
  20.3 0.1 collective-permute-start
  20.4 1.3 %collective-permute-done.other = bf16[64,1024]{1,0:T(8,128)(2,1)S(1)} collective-permute-done((bf16[64,1024]{1,0:T(8,128)(2,1)S(1)}, bf16[64,1024]{1,0:T(8,128)(2,1)S(1)}, u32[]{:S(2)}, u32[]{:S(2)}) %collective-permute-start) | collective-permute-done | bytes 131104 | tf_op jit(solution)/shard_map/ppermute | solution.py:47
  21.7 1.6 %collective-permute-start.1 = (bf16[64,1024]{1,0:T(8,128)(2,1)S(1)}, bf16[64,1024]{1,0:T(8,128)(2,1)S(1)}, u32[]{:S(2)}, u32[]{:S(2)}) collective-permute-start(bf16[64,1024]{1,0:T(8,128)(2,1)S(1)} %shard_map.96.after.terms), channel_id=1, source_target_pairs={{0,16},{8,24},{16,0},{24,8},{1,17},{9,25},{17,1},{25,9},{2,18},{10... | collective-permute-start | bytes 393224 | tf_op jit(solution)/shard_map/ppermute | solution.py:47
  23.3 0.0 copy-done
  23.3 1.4 %shard_map.97.before.weight = bf16[2304,1024]{1,0:T(8,128)(2,1)S(1)} custom-call(bf16[1024,2304]{1,0:T(8,128)(2,1)S(1)} %bitcast.16, bf16[64,1024]{1,0:T(8,128)(2,1)S(1)} %shard_map.96.after.terms), custom_call_target="tpu_custom_call" | custom-call | bytes 9699328 | tf_op jit(solution)/shard_map/pallas_call | solution.py:28
  24.7 2.6 %collective-permute-done.1.others = bf16[64,1024]{1,0:T(8,128)(2,1)S(1)} collective-permute-done((bf16[64,1024]{1,0:T(8,128)(2,1)S(1)}, bf16[64,1024]{1,0:T(8,128)(2,1)S(1)}, u32[]{:S(2)}, u32[]{:S(2)}) %collective-permute-start.1) | collective-permute-done | bytes 131104 | tf_op jit(solution)/shard_map/ppermute | solution.py:47
  27.3 0.0 copy-start.1
  27.3 0.0 copy-start.2
  27.4 1.0 %shard_map.98 = (bf16[64,2304]{1,0:T(8,128)(2,1)S(1)}, f32[64,1024]{1,0:T(8,128)S(1)}) custom-call(bf16[64,1024]{1,0:T(8,128)(2,1)S(1)} %shard_map.96.after.terms, bf16[64,1024]{1,0:T(8,128)(2,1)S(1)} %collective-permute-done.1.others, f32[1,1024]{1,0:T(1,128)S(1)} %get-tuple-element.19.enc_bias, f32[1,1024]{1,0:T(1,128)S(1)} %get-tuple-element.20.threshold, ...), custom_call_target="tpu_custom_call" | custom-call | tf_op jit(solution)/shard_map/pallas_call | solution.py:28
  28.3 8.5 %all_to_all.21.terms = bf16[4,16,2304]{2,1,0:T(8,128)(2,1)S(1)} all-to-all(bf16[4,16,2304]{2,1,0:T(8,128)(2,1)S(1)} %bitcast.18), channel_id=1, replica_groups={{0,1,2,3},{4,5,6,7},{8,9,10,11},{12,13,14,15},{16,17,18,19},{20,21,22,2..., dimensions={0} | all-to-all | bytes 589824 | tf_op jit(solution)/shard_map/all_to_all | solution.py:193
  36.9 0.9 %collective-permute-start.2 = (bf16[16,2304]{1,0:T(8,128)(2,1)S(1)}, bf16[16,2304]{1,0:T(8,128)(2,1)S(1)}, u32[]{:S(2)}, u32[]{:S(2)}) collective-permute-start(bf16[16,2304]{1,0:T(8,128)(2,1)S(1)} %get-tuple-element.23), channel_id=1, source_target_pairs={{0,4},{1,5},{2,6},{3,7},{4,0},{5,1},{6,2},{7,3},{8,12},{9,13},{10,... | collective-permute-start | bytes 221192 | tf_op jit(solution)/shard_map/ppermute | solution.py:195
  37.8 5.2 %collective-permute-done.2.other = bf16[16,2304]{1,0:T(8,128)(2,1)S(1)} collective-permute-done((bf16[16,2304]{1,0:T(8,128)(2,1)S(1)}, bf16[16,2304]{1,0:T(8,128)(2,1)S(1)}, u32[]{:S(2)}, u32[]{:S(2)}) %collective-permute-start.2) | collective-permute-done | bytes 73760 | tf_op jit(solution)/shard_map/ppermute | solution.py:195
  43.0 0.0 copy-done.1
  43.0 0.0 copy-done.2
  43.0 0.2 shard_map.100
  43.2 8.5 %all_to_all.22.rows = bf16[4,16,2304]{2,1,0:T(8,128)(2,1)S(1)} all-to-all(bf16[4,16,2304]{2,1,0:T(8,128)(2,1)S(1)} %get-tuple-element.24), channel_id=1, replica_groups={{0,1,2,3},{4,5,6,7},{8,9,10,11},{12,13,14,15},{16,17,18,19},{20,21,22,2..., dimensions={0} | all-to-all | bytes 589824 | tf_op jit(solution)/shard_map/all_to_all | solution.py:206
  51.7 0.9 %shard_map.101.one = bf16[64,1024]{1,0:T(8,128)(2,1)S(1)} custom-call(bf16[4,16,2304]{2,1,0:T(8,128)(2,1)S(1)} %all_to_all.22.rows, bf16[2304,1024]{1,0:T(8,128)(2,1)S(1)} %shard_map.97.before.weight), custom_call_target="tpu_custom_call" | custom-call | tf_op jit(solution)/shard_map/pallas_call | solution.py:28
  52.6 0.1 collective-permute-start.3
  52.7 1.3 %collective-permute-done.3.other = bf16[64,1024]{1,0:T(8,128)(2,1)S(1)} collective-permute-done((bf16[64,1024]{1,0:T(8,128)(2,1)S(1)}, bf16[64,1024]{1,0:T(8,128)(2,1)S(1)}, u32[]{:S(2)}, u32[]{:S(2)}) %collective-permute-start.3) | collective-permute-done | bytes 131104 | tf_op jit(solution)/shard_map/ppermute | solution.py:47
  54.1 1.6 %collective-permute-start.4 = (bf16[64,1024]{1,0:T(8,128)(2,1)S(1)}, bf16[64,1024]{1,0:T(8,128)(2,1)S(1)}, u32[]{:S(2)}, u32[]{:S(2)}) collective-permute-start(bf16[64,1024]{1,0:T(8,128)(2,1)S(1)} %shard_map.102.after.terms), channel_id=1, source_target_pairs={{0,16},{8,24},{16,0},{24,8},{1,17},{9,25},{17,1},{25,9},{2,18},{10... | collective-permute-start | bytes 393224 | tf_op jit(solution)/shard_map/ppermute | solution.py:47
  55.7 1.3 %shard_map.103.weight = bf16[1024,2304]{1,0:T(8,128)(2,1)S(1)} custom-call(bf16[2304,1024]{1,0:T(8,128)(2,1)S(1)} %bitcast.14, bf16[64,1024]{1,0:T(8,128)(2,1)S(1)} %shard_map.102.after.terms), custom_call_target="tpu_custom_call" | custom-call | bytes 9699328 | tf_op jit(solution)/shard_map/pallas_call | solution.py:28
  56.9 2.8 %collective-permute-done.4.others = bf16[64,1024]{1,0:T(8,128)(2,1)S(1)} collective-permute-done((bf16[64,1024]{1,0:T(8,128)(2,1)S(1)}, bf16[64,1024]{1,0:T(8,128)(2,1)S(1)}, u32[]{:S(2)}, u32[]{:S(2)}) %collective-permute-start.4) | collective-permute-done | bytes 131104 | tf_op jit(solution)/shard_map/ppermute | solution.py:47
  59.7 0.9 %shard_map.104 = (bf16[64,2304]{1,0:T(8,128)(2,1)S(1)}, f32[64,1024]{1,0:T(8,128)S(1)}) custom-call(bf16[64,1024]{1,0:T(8,128)(2,1)S(1)} %shard_map.102.after.terms, bf16[64,1024]{1,0:T(8,128)(2,1)S(1)} %collective-permute-done.4.others, f32[64,1024]{1,0:T(8,128)S(1)} %get-tuple-element.25.slope, bf16[1024,2304]{1,0:T(8,128)(2,1)S(1)} %shard_map.103.weight), custom_call_target="tpu_custom_call" | custom-call | tf_op jit(solution)/shard_map/pallas_call | solution.py:28
  60.7 12.5 %all_to_all.23.terms = bf16[8,8,2304]{2,1,0:T(8,128)(2,1)S(1)} all-to-all(bf16[8,8,2304]{2,1,0:T(8,128)(2,1)S(1)} %bitcast.19), channel_id=1, replica_groups=mesh['layer'=4,'feat'=8] {'feat'}, dimensions={0} | all-to-all | bytes 589824 | tf_op jit(solution)/shard_map/all_to_all | solution.py:219
  73.2 0.7 shard_map.105
  (5 shorter events, 0.1 us)
Async XLA Ops:
  0.6 18.7 %slice-start = ((s8[4718592]{0:T(1024)(128)(4,1)}), s8[4194304]{0:T(1024)(128)(4,1)S(1)}, s32[]{:S(2)}) async-start(s8[4718592]{0:T(1024)(128)(4,1)} %bitcast.11), calls=%async_computation.4 | async-start | bytes 8388608
  1.6 17.7 %slice-start.1 = ((s8[4718592]{0:T(1024)(128)(4,1)}), s8[524288]{0:T(1024)(128)(4,1)S(1)}, s32[]{:S(2)}) async-start(s8[4718592]{0:T(1024)(128)(4,1)} %bitcast.11), calls=%async_computation.5 | async-start | bytes 1048576
  1.6 21.7 %copy-start = (bf16[1,1024,2304]{2,1,0:T(8,128)(2,1)S(1)}, bf16[1,1024,2304]{2,1,0:T(8,128)(2,1)}, u32[]{:S(2)}) copy-start(bf16[1,1024,2304]{2,1,0:T(8,128)(2,1)} %param.9) | copy-start | bytes 14155780
  20.3 1.4 %collective-permute-start = (bf16[64,1024]{1,0:T(8,128)(2,1)S(1)}, bf16[64,1024]{1,0:T(8,128)(2,1)S(1)}, u32[]{:S(2)}, u32[]{:S(2)}) collective-permute-start(bf16[64,1024]{1,0:T(8,128)(2,1)S(1)} %get-tuple-element.18.one), channel_id=1, source_target_pairs={{0,8},{8,0},{16,24},{24,16},{1,9},{9,1},{17,25},{25,17},{2,10},{10... | collective-permute-start | bytes 393224 | tf_op jit(solution)/shard_map/ppermute | solution.py:47
  21.7 5.6 %collective-permute-start.1 = (bf16[64,1024]{1,0:T(8,128)(2,1)S(1)}, bf16[64,1024]{1,0:T(8,128)(2,1)S(1)}, u32[]{:S(2)}, u32[]{:S(2)}) collective-permute-start(bf16[64,1024]{1,0:T(8,128)(2,1)S(1)} %shard_map.96.after.terms), channel_id=1, source_target_pairs={{0,16},{8,24},{16,0},{24,8},{1,17},{9,25},{17,1},{25,9},{2,18},{10... | collective-permute-start | bytes 393224 | tf_op jit(solution)/shard_map/ppermute | solution.py:47
  27.3 15.6 %copy-start.1 = (f32[1,2304]{1,0:T(1,128)S(1)}, f32[1,2304]{1,0:T(1,128)}, u32[]{:S(2)}) copy-start(f32[1,2304]{1,0:T(1,128)} %dec_bias.1) | copy-start | bytes 27652
  27.3 15.6 %copy-start.2 = (s32[64]{0:T(128)S(1)}, s32[64]{0:T(128)}, u32[]{:S(2)}) copy-start(s32[64]{0:T(128)} %param.13) | copy-start | bytes 772
  36.9 6.1 %collective-permute-start.2 = (bf16[16,2304]{1,0:T(8,128)(2,1)S(1)}, bf16[16,2304]{1,0:T(8,128)(2,1)S(1)}, u32[]{:S(2)}, u32[]{:S(2)}) collective-permute-start(bf16[16,2304]{1,0:T(8,128)(2,1)S(1)} %get-tuple-element.23), channel_id=1, source_target_pairs={{0,4},{1,5},{2,6},{3,7},{4,0},{5,1},{6,2},{7,3},{8,12},{9,13},{10,... | collective-permute-start | bytes 221192 | tf_op jit(solution)/shard_map/ppermute | solution.py:195
  52.6 1.4 %collective-permute-start.3 = (bf16[64,1024]{1,0:T(8,128)(2,1)S(1)}, bf16[64,1024]{1,0:T(8,128)(2,1)S(1)}, u32[]{:S(2)}, u32[]{:S(2)}) collective-permute-start(bf16[64,1024]{1,0:T(8,128)(2,1)S(1)} %shard_map.101.one), channel_id=1, source_target_pairs={{0,8},{8,0},{16,24},{24,16},{1,9},{9,1},{17,25},{25,17},{2,10},{10... | collective-permute-start | bytes 393224 | tf_op jit(solution)/shard_map/ppermute | solution.py:47
  54.1 5.6 %collective-permute-start.4 = (bf16[64,1024]{1,0:T(8,128)(2,1)S(1)}, bf16[64,1024]{1,0:T(8,128)(2,1)S(1)}, u32[]{:S(2)}, u32[]{:S(2)}) collective-permute-start(bf16[64,1024]{1,0:T(8,128)(2,1)S(1)} %shard_map.102.after.terms), channel_id=1, source_target_pairs={{0,16},{8,24},{16,0},{24,8},{1,17},{9,25},{17,1},{25,9},{2,18},{10... | collective-permute-start | bytes 393224 | tf_op jit(solution)/shard_map/ppermute | solution.py:47

commit v6 on v5

--- a/solution.py
+++ b/solution.py
@@ -56,22 +56,14 @@
     return ref[...].reshape(-1, ref.shape[-1])
 
 
-def encode(acts, weight, out):
-    x = rows_of(acts)
-    for at in range(0, out.shape[1], columns):
-        out[:, at : at + columns] = jnp.dot(
-            x, weight[:, at : at + columns], preferred_element_type=wide
-        ).astype(half)
-
-
-def encode_first(enc_bias, threshold, acts, weight, out, bias_near, threshold_near, done):
+def encode_first(block, enc_bias, threshold, acts, weight, out, bias_near, threshold_near, done):
     moves = [
         pltpu.make_async_copy(enc_bias, bias_near, done.at[0]),
         pltpu.make_async_copy(threshold, threshold_near, done.at[1]),
     ]
     for move in moves:
         move.start()
-    encode(acts, weight, out)
+    encode_paired(block, acts, weight, out)
     for move in moves:
         move.wait()
 
@@ -119,6 +111,19 @@
         ).astype(half)
 
 
+def bring(far, out, done):
+    move = pltpu.make_async_copy(far, out, done)
+    move.start()
+    move.wait()
+
+
+def join(acts, other, copies):
+    first = lax.axis_index("feat") < lax.axis_size("feat") // 2
+    mine, theirs = acts[...].astype(wide), other[...].astype(wide)
+    both = jnp.concatenate([jnp.where(first, mine, theirs), jnp.where(first, theirs, mine)]).astype(half)
+    copies[...] = jnp.broadcast_to(both[None], copies.shape)
+
+
 def add_up(terms, out, sent):
     found = jnp.sum(terms[...].astype(wide), axis=0)
     out[...] = found
@@ -126,7 +131,7 @@
 
 
 def compare(one, other, dec_bias, acts, token_mask, error, copies, squared, held):
-    n, rows, _ = acts.shape
+    n, rows = 2 * acts.shape[0], acts.shape[1] // 2
     tokens = token_mask.shape[1]
     me = lax.axis_index("feat")
     place, upper = lax.rem(me, n // 2), me // (n // 2)
@@ -134,8 +139,7 @@
     token = jnp.where(row < rows, place * rows + row, (place + n // 2) * rows + row - rows)
     own = token == lax.broadcasted_iota(jnp.int32, (2 * rows, tokens), 1)
     mask = jnp.sum(jnp.where(own, token_mask[...].astype(wide), 0.0), axis=1, keepdims=True)
-    here = jnp.concatenate([acts[place].astype(wide), acts[place + n // 2].astype(wide)])
-    held[...] = mask * (one[...] + other[...].astype(wide) + dec_bias[...] - here)
+    held[...] = mask * (one[...] + other[...].astype(wide) + dec_bias[...] - acts[place].astype(wide))
     copies[...] = jnp.broadcast_to(held[...].astype(half)[None], copies.shape)
     found = held[pl.ds(pl.multiple_of(upper * rows, rows), rows), :]
     error[...] = found
@@ -164,11 +168,18 @@
     exchange = functools.partial(lax.all_to_all, axis_name="feat", split_axis=0, concat_axis=0)
     by_owner = (n_feat, tok_dev, depth)
 
-    copies = jnp.broadcast_to(acts[None], by_owner)
-    [copies] = call(lambda *refs: None, [near(by_owner, half)], enc, dec, copies, fetched=2, same={2: 0})
-    whole_acts = exchange(copies)
+    mirror = [(i, (i + n_feat // 2) % n_feat) for i in range(n_feat)]
+    halves = [list(range(n_feat // 2)), list(range(n_feat // 2, n_feat))]
+    by_pair = (n_feat // 2, 2 * tok_dev, depth)
+    other = lax.ppermute(acts, "feat", mirror)
+    [acts] = call(
+        bring, [near(acts.shape, half)], acts, scratch=[pltpu.SemaphoreType.DMA], fetched=1, work=True
+    )
+    [copies] = call(join, [near(by_pair, half)], acts, other)
+    [copies] = call(lambda *refs: None, [near(by_pair, half)], enc, dec, copies, fetched=2, same={2: 0})
+    whole_acts = exchange(copies, axis_index_groups=halves)
     terms, enc_bias, threshold = call(
-        encode_first,
+        functools.partial(encode_first, tok_dev),
         [near((tokens, width), half), near((1, width), wide), near((1, width), wide)],
         enc_bias[None],
         threshold[None],
@@ -188,11 +199,9 @@
         dec,
         dec_turned,
     )
-    by_pair = (n_feat // 2, 2 * tok_dev, depth)
-    halves = [list(range(n_feat // 2)), list(range(n_feat // 2, n_feat))]
     pieces = exchange(decoded.reshape(by_pair), axis_index_groups=halves)
     one, other = call(add_up, [near(by_pair[1:], wide), near(by_pair[1:], half)], pieces)
-    other = lax.ppermute(other, "feat", [(i, (i + n_feat // 2) % n_feat) for i in range(n_feat)])
+    other = lax.ppermute(other, "feat", mirror)
     error, copies, squared = call(
         compare,
         [near((tok_dev, depth), wide), near(by_pair, half), near((1, tok_dev), wide)],

time: 74.1 us -> 72.8 us (0.982)
  blocking collectives: 47.2 us -> 40.1 us
  starting transfers between devices: 4.18 us -> 10.3 us
  local copies, waits for them, and re-layouts: 0.97 us -> 0.03 us
  Pallas kernels: 7.51 us -> 8.35 us
    all_to_all x1, blocking collectives: 17.7 us -> 9.96 us  [shards(): whole_acts = exchange(copies, axis_index_groups=halves)]
    ppermute x1 -> x2, starting transfers between devices: 0.93 us -> 7.04 us  [the longest x1 4.1 us: shards(): other = lax.ppermute(acts, 'feat', mirror)]
    broadcast_in_dim x1 -> x0, local copies, waits for them, and re-layouts: 0.94 us -> none  [shards(): copies = jnp.broadcast_to(acts[None], by_owner)]
    pallas_call x12 -> x14, Pallas kernels: 7.51 us -> 8.35 us  [call(): pl.pallas_call(body, out_shape=outs, in_specs=[away] * fetched + [here] *...]
    ppermute x1 -> x2, waiting for transfers between devices: 5.18 us -> 4.9 us  [the longest x1 3.17 us: shards(): other = lax.ppermute(other, 'feat', mirror)]
  transfers between devices with their start and end apart: 5 -> 6, of which waited for: 5 -> 6; matrix products, arithmetic and copies ran while one was open for 0% -> 0% of each run, Pallas kernels for 4% -> 5%
where the time goes in v6:
time: 72.8 us; the launch traced here: 72.5 us
  blocking collectives  40.1 us (55%)
  waiting for transfers between devices  13 us (18%)
  starting transfers between devices  10.3 us (14%)
  Pallas kernels  8.35 us (11%)
  between operations  0.75 us (1%)
    all_to_all x1, blocking collectives, shards(): pieces = exchange(grads.reshape(by_owner))  13.1 us
    all_to_all x1, blocking collectives, shards(): whole_acts = exchange(copies, axis_index_groups=halves)  9.96 us
    all_to_all x1, blocking collectives, shards(): pieces = exchange(decoded.reshape(by_pair), axis_index_groups=halves)  8.53 us
    all_to_all x1, blocking collectives, shards(): error_all = exchange(copies, axis_index_groups=halves)  8.51 us
    pallas_call x14, Pallas kernels, call(): pl.pallas_call(body, out_shape=outs, in_specs=[away] * fetched + [here] *...  8.35 us
    ppermute x4, waiting for transfers between devices, swap_sums(): other = lax.ppermute(terms, axis, [(i, i ^ span) for i in range(n)])  8.08 us
    ppermute x1, starting transfers between devices, shards(): other = lax.ppermute(acts, 'feat', mirror)  4.1 us
    ppermute x4, starting transfers between devices, swap_sums(): other = lax.ppermute(terms, axis, [(i, i ^ span) for i in range(n)])  3.26 us
  transfers between devices with their start and end apart: 6, of which 6 were waited for; matrix products, arithmetic and copies ran while one was open for 0% of the time, Pallas kernels for 5%

profile of v6, /device:TPU:0, one launch (start us, length us, event | category | flops | bytes accessed | tf_op | source)
XLA Modules:
  0.0 72.5 jit_solution(14438130523614465790)
XLA Ops:
  0.6 4.1 %collective-permute-start = (bf16[8,2304]{1,0:T(8,128)(2,1)}, bf16[8,2304]{1,0:T(8,128)(2,1)S(1)}, u32[]{:S(2)}, u32[]{:S(2)}) collective-permute-start(bf16[8,2304]{1,0:T(8,128)(2,1)} %bitcast.21), channel_id=1, source_target_pairs={{0,4},{1,5},{2,6},{3,7},{4,0},{5,1},{6,2},{7,3},{8,12},{9,13},{10,... | collective-permute-start | bytes 110600 | tf_op jit(solution)/shard_map/ppermute | solution.py:174
  4.7 0.8 %shard_map.94.acts = bf16[8,2304]{1,0:T(8,128)(2,1)S(1)} custom-call(bf16[8,2304]{1,0:T(8,128)(2,1)} %bitcast.22), custom_call_target="tpu_custom_call" | custom-call | bytes 73728 | tf_op jit(solution)/shard_map/pallas_call | solution.py:28
  5.5 1.7 %collective-permute-done.other = bf16[8,2304]{1,0:T(8,128)(2,1)S(1)} collective-permute-done((bf16[8,2304]{1,0:T(8,128)(2,1)}, bf16[8,2304]{1,0:T(8,128)(2,1)S(1)}, u32[]{:S(2)}, u32[]{:S(2)}) %collective-permute-start) | collective-permute-done | bytes 36896 | tf_op jit(solution)/shard_map/ppermute | solution.py:174
  7.3 0.0 slice-start
  7.3 0.0 slice-start.1
  7.3 0.0 copy-start
  7.3 10.0 %all_to_all.20.acts = bf16[4,16,2304]{2,1,0:T(8,128)(2,1)S(1)} all-to-all(bf16[4,16,2304]{2,1,0:T(8,128)(2,1)S(1)} %shard_map.96), channel_id=1, replica_groups={{0,1,2,3},{4,5,6,7},{8,9,10,11},{12,13,14,15},{16,17,18,19},{20,21,22,2..., dimensions={0} | all-to-all | bytes 589824 | tf_op jit(solution)/shard_map/all_to_all | solution.py:180
  17.3 0.0 slice-done
  17.3 0.0 slice-done.1
  17.3 1.0 %shard_map.97 = (bf16[64,1024]{1,0:T(8,128)(2,1)S(1)}, f32[1,1024]{1,0:T(1,128)S(1)}, f32[1,1024]{1,0:T(1,128)S(1)}) custom-call(f32[1,1024]{1,0:T(1,128)} %bitcast.23, f32[1,1024]{1,0:T(1,128)} %bitcast.24, bf16[4,16,2304]{2,1,0:T(8,128)(2,1)S(1)} %all_to_all.20.acts, bf16[2304,1024]{1,0:T(8,128)(2,1)S(1)} %bitcast.13), custom_call_target="tpu_custom_call" | custom-call | tf_op jit(solution)/shard_map/pallas_call | solution.py:28
  18.3 0.1 collective-permute-start.1
  18.4 1.3 %collective-permute-done.1.other = bf16[64,1024]{1,0:T(8,128)(2,1)S(1)} collective-permute-done((bf16[64,1024]{1,0:T(8,128)(2,1)S(1)}, bf16[64,1024]{1,0:T(8,128)(2,1)S(1)}, u32[]{:S(2)}, u32[]{:S(2)}) %collective-permute-start.1) | collective-permute-done | bytes 131104 | tf_op jit(solution)/shard_map/ppermute | solution.py:47
  19.7 1.6 %collective-permute-start.2 = (bf16[64,1024]{1,0:T(8,128)(2,1)S(1)}, bf16[64,1024]{1,0:T(8,128)(2,1)S(1)}, u32[]{:S(2)}, u32[]{:S(2)}) collective-permute-start(bf16[64,1024]{1,0:T(8,128)(2,1)S(1)} %shard_map.98.after.terms), channel_id=1, source_target_pairs={{0,16},{8,24},{16,0},{24,8},{1,17},{9,25},{17,1},{25,9},{2,18},{10... | collective-permute-start | bytes 393224 | tf_op jit(solution)/shard_map/ppermute | solution.py:47
  21.3 0.0 copy-done
  21.3 1.4 %shard_map.99.before.weight = bf16[2304,1024]{1,0:T(8,128)(2,1)S(1)} custom-call(bf16[1024,2304]{1,0:T(8,128)(2,1)S(1)} %bitcast.16, bf16[64,1024]{1,0:T(8,128)(2,1)S(1)} %shard_map.98.after.terms), custom_call_target="tpu_custom_call" | custom-call | bytes 9699328 | tf_op jit(solution)/shard_map/pallas_call | solution.py:28
  22.7 2.6 %collective-permute-done.2.others = bf16[64,1024]{1,0:T(8,128)(2,1)S(1)} collective-permute-done((bf16[64,1024]{1,0:T(8,128)(2,1)S(1)}, bf16[64,1024]{1,0:T(8,128)(2,1)S(1)}, u32[]{:S(2)}, u32[]{:S(2)}) %collective-permute-start.2) | collective-permute-done | bytes 131104 | tf_op jit(solution)/shard_map/ppermute | solution.py:47
  25.4 0.0 copy-start.1
  25.4 0.0 copy-start.2
  25.4 1.0 %shard_map.100 = (bf16[64,2304]{1,0:T(8,128)(2,1)S(1)}, f32[64,1024]{1,0:T(8,128)S(1)}) custom-call(bf16[64,1024]{1,0:T(8,128)(2,1)S(1)} %shard_map.98.after.terms, bf16[64,1024]{1,0:T(8,128)(2,1)S(1)} %collective-permute-done.2.others, f32[1,1024]{1,0:T(1,128)S(1)} %get-tuple-element.19.enc_bias, f32[1,1024]{1,0:T(1,128)S(1)} %get-tuple-element.20.threshold, ...), custom_call_target="tpu_custom_call" | custom-call | tf_op jit(solution)/shard_map/pallas_call | solution.py:28
  26.3 8.5 %all_to_all.21.terms = bf16[4,16,2304]{2,1,0:T(8,128)(2,1)S(1)} all-to-all(bf16[4,16,2304]{2,1,0:T(8,128)(2,1)S(1)} %bitcast.18), channel_id=1, replica_groups={{0,1,2,3},{4,5,6,7},{8,9,10,11},{12,13,14,15},{16,17,18,19},{20,21,22,2..., dimensions={0} | all-to-all | bytes 589824 | tf_op jit(solution)/shard_map/all_to_all | solution.py:202
  34.9 2.9 %collective-permute-start.3 = (bf16[16,2304]{1,0:T(8,128)(2,1)S(1)}, bf16[16,2304]{1,0:T(8,128)(2,1)S(1)}, u32[]{:S(2)}, u32[]{:S(2)}) collective-permute-start(bf16[16,2304]{1,0:T(8,128)(2,1)S(1)} %get-tuple-element.23), channel_id=1, source_target_pairs={{0,4},{1,5},{2,6},{3,7},{4,0},{5,1},{6,2},{7,3},{8,12},{9,13},{10,... | collective-permute-start | bytes 221192 | tf_op jit(solution)/shard_map/ppermute | solution.py:204
  37.8 3.2 %collective-permute-done.3.other = bf16[16,2304]{1,0:T(8,128)(2,1)S(1)} collective-permute-done((bf16[16,2304]{1,0:T(8,128)(2,1)S(1)}, bf16[16,2304]{1,0:T(8,128)(2,1)S(1)}, u32[]{:S(2)}, u32[]{:S(2)}) %collective-permute-start.3) | collective-permute-done | bytes 73760 | tf_op jit(solution)/shard_map/ppermute | solution.py:204
  41.0 0.0 copy-done.1
  41.0 0.0 copy-done.2
  41.0 0.2 shard_map.102
  41.2 8.5 %all_to_all.22.rows = bf16[4,16,2304]{2,1,0:T(8,128)(2,1)S(1)} all-to-all(bf16[4,16,2304]{2,1,0:T(8,128)(2,1)S(1)} %get-tuple-element.24), channel_id=1, replica_groups={{0,1,2,3},{4,5,6,7},{8,9,10,11},{12,13,14,15},{16,17,18,19},{20,21,22,2..., dimensions={0} | all-to-all | bytes 589824 | tf_op jit(solution)/shard_map/all_to_all | solution.py:215
  49.7 0.9 %shard_map.103.one = bf16[64,1024]{1,0:T(8,128)(2,1)S(1)} custom-call(bf16[4,16,2304]{2,1,0:T(8,128)(2,1)S(1)} %all_to_all.22.rows, bf16[2304,1024]{1,0:T(8,128)(2,1)S(1)} %shard_map.99.before.weight), custom_call_target="tpu_custom_call" | custom-call | tf_op jit(solution)/shard_map/pallas_call | solution.py:28
  50.7 0.1 collective-permute-start.4
  50.7 1.3 %collective-permute-done.4.other = bf16[64,1024]{1,0:T(8,128)(2,1)S(1)} collective-permute-done((bf16[64,1024]{1,0:T(8,128)(2,1)S(1)}, bf16[64,1024]{1,0:T(8,128)(2,1)S(1)}, u32[]{:S(2)}, u32[]{:S(2)}) %collective-permute-start.4) | collective-permute-done | bytes 131104 | tf_op jit(solution)/shard_map/ppermute | solution.py:47
  52.1 1.6 %collective-permute-start.5 = (bf16[64,1024]{1,0:T(8,128)(2,1)S(1)}, bf16[64,1024]{1,0:T(8,128)(2,1)S(1)}, u32[]{:S(2)}, u32[]{:S(2)}) collective-permute-start(bf16[64,1024]{1,0:T(8,128)(2,1)S(1)} %shard_map.104.after.terms), channel_id=1, source_target_pairs={{0,16},{8,24},{16,0},{24,8},{1,17},{9,25},{17,1},{25,9},{2,18},{10... | collective-permute-start | bytes 393224 | tf_op jit(solution)/shard_map/ppermute | solution.py:47
  53.7 1.3 %shard_map.105.weight = bf16[1024,2304]{1,0:T(8,128)(2,1)S(1)} custom-call(bf16[2304,1024]{1,0:T(8,128)(2,1)S(1)} %bitcast.14, bf16[64,1024]{1,0:T(8,128)(2,1)S(1)} %shard_map.104.after.terms), custom_call_target="tpu_custom_call" | custom-call | bytes 9699328 | tf_op jit(solution)/shard_map/pallas_call | solution.py:28
  54.9 2.8 %collective-permute-done.5.others = bf16[64,1024]{1,0:T(8,128)(2,1)S(1)} collective-permute-done((bf16[64,1024]{1,0:T(8,128)(2,1)S(1)}, bf16[64,1024]{1,0:T(8,128)(2,1)S(1)}, u32[]{:S(2)}, u32[]{:S(2)}) %collective-permute-start.5) | collective-permute-done | bytes 131104 | tf_op jit(solution)/shard_map/ppermute | solution.py:47
  57.7 0.9 %shard_map.106 = (bf16[64,2304]{1,0:T(8,128)(2,1)S(1)}, f32[64,1024]{1,0:T(8,128)S(1)}) custom-call(bf16[64,1024]{1,0:T(8,128)(2,1)S(1)} %shard_map.104.after.terms, bf16[64,1024]{1,0:T(8,128)(2,1)S(1)} %collective-permute-done.5.others, f32[64,1024]{1,0:T(8,128)S(1)} %get-tuple-element.25.slope, bf16[1024,2304]{1,0:T(8,128)(2,1)S(1)} %shard_map.105.weight), custom_call_target="tpu_custom_call" | custom-call | tf_op jit(solution)/shard_map/pallas_call | solution.py:28
  58.7 13.1 %all_to_all.23.terms = bf16[8,8,2304]{2,1,0:T(8,128)(2,1)S(1)} all-to-all(bf16[8,8,2304]{2,1,0:T(8,128)(2,1)S(1)} %bitcast.19), channel_id=1, replica_groups=mesh['layer'=4,'feat'=8] {'feat'}, dimensions={0} | all-to-all | bytes 589824 | tf_op jit(solution)/shard_map/all_to_all | solution.py:228
  71.8 0.7 %shard_map.107 = (bf16[8,2304]{1,0:T(8,128)(2,1)}, f32[1,8]{1,0:T(1,128)}, f32[64,1024]{1,0:T(8,128)}) custom-call(bf16[8,8,2304]{2,1,0:T(8,128)(2,1)S(1)} %all_to_all.23.terms, f32[8,2304]{1,0:T(8,128)S(1)} %get-tuple-element.27.error, f32[1,8]{1,0:T(1,128)S(1)} %get-tuple-element.28.squared, f32[64,1024]{1,0:T(8,128)S(1)} %get-tuple-element.29.total), custom_call_target="tpu_custom_call" | custom-call | tf_op jit(solution)/shard_map/pallas_call | solution.py:28
  (6 shorter events, 0.1 us)
Async XLA Ops:
  0.6 6.6 %collective-permute-start = (bf16[8,2304]{1,0:T(8,128)(2,1)}, bf16[8,2304]{1,0:T(8,128)(2,1)S(1)}, u32[]{:S(2)}, u32[]{:S(2)}) collective-permute-start(bf16[8,2304]{1,0:T(8,128)(2,1)} %bitcast.21), channel_id=1, source_target_pairs={{0,4},{1,5},{2,6},{3,7},{4,0},{5,1},{6,2},{7,3},{8,12},{9,13},{10,... | collective-permute-start | bytes 110600 | tf_op jit(solution)/shard_map/ppermute | solution.py:174
  7.3 10.0 %slice-start = ((s8[4718592]{0:T(1024)(128)(4,1)}), s8[4194304]{0:T(1024)(128)(4,1)S(1)}, s32[]{:S(2)}) async-start(s8[4718592]{0:T(1024)(128)(4,1)} %bitcast.11), calls=%async_computation.4 | async-start | bytes 8388608
  7.3 10.0 %slice-start.1 = ((s8[4718592]{0:T(1024)(128)(4,1)}), s8[524288]{0:T(1024)(128)(4,1)S(1)}, s32[]{:S(2)}) async-start(s8[4718592]{0:T(1024)(128)(4,1)} %bitcast.11), calls=%async_computation.5 | async-start | bytes 1048576
  7.3 14.0 %copy-start = (bf16[1,1024,2304]{2,1,0:T(8,128)(2,1)S(1)}, bf16[1,1024,2304]{2,1,0:T(8,128)(2,1)}, u32[]{:S(2)}) copy-start(bf16[1,1024,2304]{2,1,0:T(8,128)(2,1)} %param.9) | copy-start | bytes 14155780
  18.3 1.4 %collective-permute-start.1 = (bf16[64,1024]{1,0:T(8,128)(2,1)S(1)}, bf16[64,1024]{1,0:T(8,128)(2,1)S(1)}, u32[]{:S(2)}, u32[]{:S(2)}) collective-permute-start(bf16[64,1024]{1,0:T(8,128)(2,1)S(1)} %get-tuple-element.18.one), channel_id=1, source_target_pairs={{0,8},{8,0},{16,24},{24,16},{1,9},{9,1},{17,25},{25,17},{2,10},{10... | collective-permute-start | bytes 393224 | tf_op jit(solution)/shard_map/ppermute | solution.py:47
  19.7 5.6 %collective-permute-start.2 = (bf16[64,1024]{1,0:T(8,128)(2,1)S(1)}, bf16[64,1024]{1,0:T(8,128)(2,1)S(1)}, u32[]{:S(2)}, u32[]{:S(2)}) collective-permute-start(bf16[64,1024]{1,0:T(8,128)(2,1)S(1)} %shard_map.98.after.terms), channel_id=1, source_target_pairs={{0,16},{8,24},{16,0},{24,8},{1,17},{9,25},{17,1},{25,9},{2,18},{10... | collective-permute-start | bytes 393224 | tf_op jit(solution)/shard_map/ppermute | solution.py:47
  25.4 15.6 %copy-start.1 = (f32[1,2304]{1,0:T(1,128)S(1)}, f32[1,2304]{1,0:T(1,128)}, u32[]{:S(2)}) copy-start(f32[1,2304]{1,0:T(1,128)} %dec_bias.1) | copy-start | bytes 27652
  25.4 15.6 %copy-start.2 = (s32[64]{0:T(128)S(1)}, s32[64]{0:T(128)}, u32[]{:S(2)}) copy-start(s32[64]{0:T(128)} %param.13) | copy-start | bytes 772
  34.9 6.1 %collective-permute-start.3 = (bf16[16,2304]{1,0:T(8,128)(2,1)S(1)}, bf16[16,2304]{1,0:T(8,128)(2,1)S(1)}, u32[]{:S(2)}, u32[]{:S(2)}) collective-permute-start(bf16[16,2304]{1,0:T(8,128)(2,1)S(1)} %get-tuple-element.23), channel_id=1, source_target_pairs={{0,4},{1,5},{2,6},{3,7},{4,0},{5,1},{6,2},{7,3},{8,12},{9,13},{10,... | collective-permute-start | bytes 221192 | tf_op jit(solution)/shard_map/ppermute | solution.py:204
  50.7 1.4 %collective-permute-start.4 = (bf16[64,1024]{1,0:T(8,128)(2,1)S(1)}, bf16[64,1024]{1,0:T(8,128)(2,1)S(1)}, u32[]{:S(2)}, u32[]{:S(2)}) collective-permute-start(bf16[64,1024]{1,0:T(8,128)(2,1)S(1)} %shard_map.103.one), channel_id=1, source_target_pairs={{0,8},{8,0},{16,24},{24,16},{1,9},{9,1},{17,25},{25,17},{2,10},{10... | collective-permute-start | bytes 393224 | tf_op jit(solution)/shard_map/ppermute | solution.py:47
  52.1 5.6 %collective-permute-start.5 = (bf16[64,1024]{1,0:T(8,128)(2,1)S(1)}, bf16[64,1024]{1,0:T(8,128)(2,1)S(1)}, u32[]{:S(2)}, u32[]{:S(2)}) collective-permute-start(bf16[64,1024]{1,0:T(8,128)(2,1)S(1)} %shard_map.104.after.terms), channel_id=1, source_target_pairs={{0,16},{8,24},{16,0},{24,8},{1,17},{9,25},{17,1},{25,9},{2,18},{10... | collective-permute-start | bytes 393224 | tf_op jit(solution)/shard_map/ppermute | solution.py:47

commit v7 on v4

v7 whole, which is shorter than its diff:
```python
import functools

import jax
import jax.numpy as jnp
from jax import lax
from jax.experimental import pallas as pl
from jax.experimental.pallas import tpu as pltpu
from jax.sharding import PartitionSpec as P


jump_scale = 0.25
columns = 256
half, wide = jnp.bfloat16, jnp.float32


def near(shape, dtype):
    return pltpu.VMEM(shape, dtype)


def free(shape, dtype):
    return jax.ShapeDtypeStruct(shape, dtype)


def call(body, outs, *args, scratch=(), fetched=0, sent=0, work=False, same={}):
    here, away = pl.BlockSpec(memory_space=pltpu.VMEM), pl.BlockSpec(memory_space=pl.ANY)
    size = sum(a.size * a.dtype.itemsize for a in args)
    cost = pl.CostEstimate(flops=0, transcendentals=0, bytes_accessed=2 * size) if work else None
    spaces = [pltpu.HBM] * fetched + [pltpu.VMEM] * (len(args) - fetched)
    return pl.pallas_call(
        body,
        out_shape=outs,
        in_specs=[away] * fetched + [here] * (len(args) - fetched),
        out_specs=[here] * (len(outs) - sent) + [away] * sent,
        scratch_shapes=scratch,
        compiler_params=pltpu.CompilerParams(vmem_limit_bytes=16 << 20),
        cost_estimate=cost,
        input_output_aliases=same,
    )(*map(pltpu.with_memory_space_constraint, args, spaces))


def swap_sums(terms, axis, weight):
    n, span = lax.axis_size(axis), 1
    while True:
        other = lax.ppermute(terms, axis, [(i, i ^ span) for i in range(n)])
        span *= 2
        if span == n:
            [turned] = call(turn, [near(weight.shape[::-1], half)], weight, terms, work=True)
            return terms, other, turned
        [terms] = call(add, [near(terms.shape, half)], terms, other)


def trade(pieces):
    n, came = lax.axis_size("feat"), list(pieces)
    for k in reversed(range(1, n // 2)):
        came[k] = lax.ppermute(pieces[k], "feat", [(i, i ^ k) for i in range(n)])
    return came


def mirror(block):
    n = lax.axis_size("feat")
    return lax.ppermute(block, "feat", [(i, (i + n // 2) % n) for i in range(n)])


def in_first_half():
    return lax.axis_index("feat") < lax.axis_size("feat") // 2


def place():
    return lax.rem(lax.axis_index("feat"), lax.axis_size("feat") // 2)


def stack(refs):
    return jnp.concatenate([ref[...] for ref in refs])


def sum_of(refs):
    return functools.reduce(lambda so_far, ref: so_far + ref[...].astype(wide), refs[1:], refs[0][...].astype(wide))


def own_and_mirror(pair):
    rows = pair.shape[0] // 2
    first, low, high = in_first_half(), pair[:rows], pair[rows:]
    return jnp.where(first, low, high), jnp.where(first, high, low)


def add(one, other, out):
    out[...] = (one[...].astype(wide) + other[...].astype(wide)).astype(half)


def bring(far, out, done):
    move = pltpu.make_async_copy(far, out, done)
    move.start()
    move.wait()


def join(acts, other, pair):
    first = in_first_half()
    mine, theirs = acts[...].astype(wide), other[...].astype(wide)
    both = [jnp.where(first, mine, theirs), jnp.where(first, theirs, mine)]
    pair[...] = jnp.concatenate(both).astype(half)


def encode(weight, *rest):
    *groups, out = rest
    x = stack(groups)
    for at in range(0, out.shape[1], columns):
        out[:, at : at + columns] = jnp.dot(
            x, weight[:, at : at + columns], preferred_element_type=wide
        ).astype(half)


def encode_first(enc_bias, threshold, weight, *rest):
    *rest, bias_near, threshold_near, done = rest
    moves = [
        pltpu.make_async_copy(enc_bias, bias_near, done.at[0]),
        pltpu.make_async_copy(threshold, threshold_near, done.at[1]),
    ]
    for move in moves:
        move.start()
    encode(weight, *rest)
    for move in moves:
        move.wait()


def turn(weight, after, out):
    for at in range(0, weight.shape[0], columns):
        out[:, at : at + columns] = weight[at : at + columns, :].T


def spread_rows(x, weight, outs):
    for at in range(0, weight.shape[1], columns):
        found = jnp.dot(x, weight[:, at : at + columns], preferred_element_type=wide).astype(half)
        for k, out in enumerate(outs):
            rows = out.shape[0]
            out[:, at : at + columns] = found[k * rows : (k + 1) * rows]


def decode(terms, others, enc_bias, threshold, weight, before, slope, *outs):
    preact = terms[...].astype(wide) + others[...].astype(wide) + enc_bias[...]
    gating = jax.nn.sigmoid((preact - threshold[...]) / jump_scale)
    slope[...] = gating + preact * gating * (1.0 - gating) / jump_scale
    spread_rows((preact * gating).astype(half), weight, outs)


def decode_grad(terms, others, slope, weight, total, *outs):
    latent_grad = terms[...].astype(wide) + others[...].astype(wide)
    n, me = 2 * len(outs), place()
    rows = total.shape[0] // n
    for i in range(n):
        block = lax.bitwise_xor(me, i // 2) + i % 2 * (n // 2)
        total[pl.ds(pl.multiple_of(block * rows, rows), rows), :] = latent_grad[i * rows : (i + 1) * rows]
    spread_rows((latent_grad * slope[...]).astype(half), weight, outs)


def add_pair(*refs):
    *terms, out, sent = refs
    found = sum_of(terms)
    out[...] = found
    sent[...] = found.astype(half)


def add_last(*refs):
    *terms, out, sent = refs
    mine, theirs = own_and_mirror(sum_of(terms))
    out[...] = mine
    sent[...] = theirs.astype(half)


def compare(one, other, dec_bias, acts, token_mask, error, pair, squared):
    rows, tokens = error.shape[0], token_mask.shape[1]
    row = lax.broadcasted_iota(jnp.int32, (2 * rows, tokens), 0)
    token = place() * rows + jnp.where(row < rows, row, tokens // 2 + row - rows)
    own = token == lax.broadcasted_iota(jnp.int32, (2 * rows, tokens), 1)
    mask = jnp.sum(jnp.where(own, token_mask[...].astype(wide), 0.0), axis=1, keepdims=True)
    both = mask * (one[...] + other[...].astype(wide) + dec_bias[...] - acts[...].astype(wide))
    pair[...] = both.astype(half)
    found, _ = own_and_mirror(both)
    error[...] = found
    means = jnp.mean(found * found, axis=1, keepdims=True)
    same = lax.broadcasted_iota(jnp.int32, (rows, rows), 0) == lax.broadcasted_iota(jnp.int32, (rows, rows), 1)
    squared[...] = jnp.sum(jnp.where(same, means, 0.0), axis=0, keepdims=True)


def finish(one, other, error, squared, grad, out, squared_out, grad_out, held, done):
    moves = [(grad, grad_out), (squared, squared_out), (held, out)]
    moves = [pltpu.make_async_copy(here, there, done.at[i]) for i, (here, there) in enumerate(moves)]
    moves[0].start()
    moves[1].start()
    held[...] = (one[...] + other[...].astype(wide) - error[...]).astype(half)
    moves[2].start()
    for move in moves:
        move.wait()


def shards(activations, enc_weight, dec_weight, enc_bias, threshold, dec_bias, token_mask):
    n_feat = lax.axis_size("feat")
    tok_dev, _, depth = activations.shape
    tokens, width, groups = n_feat * tok_dev, enc_bias.shape[0], n_feat // 2
    enc, dec = enc_weight[0], dec_weight[0]
    acts = activations[:, 0]
    own, pair = (tok_dev, depth), (2 * tok_dev, depth)

    other = mirror(acts)
    [acts] = call(bring, [near(own, half)], acts, scratch=[pltpu.SemaphoreType.DMA], fetched=1, work=True)
    [acts_pair] = call(join, [near(pair, half)], acts, other)
    [acts_pair] = call(lambda *refs: None, [near(pair, half)], enc, dec, acts_pair, fetched=2, same={2: 0})
    terms, enc_bias, threshold = call(
        encode_first,
        [near((tokens, width), half), near((1, width), wide), near((1, width), wide)],
        enc_bias[None],
        threshold[None],
        enc,
        *trade([acts_pair] * groups),
        scratch=[pltpu.SemaphoreType.DMA((2,))],
        fetched=2,
    )
    terms, others, dec_turned = swap_sums(terms, "layer", dec)
    slope, *decoded = call(
        decode,
        [near((tokens, width), wide)] + [near(pair, half)] * groups,
        terms,
        others,
        enc_bias,
        threshold,
        dec,
        dec_turned,
    )
    one, other = call(add_pair, [near(pair, wide), near(pair, half)], *trade(decoded))
    error, error_pair, squared = call(
        compare,
        [near(own, wide), near(pair, half), near((1, tok_dev), wide)],
        one,
        mirror(other),
        dec_bias,
        acts_pair,
        token_mask[None],
    )
    [terms] = call(encode, [near((tokens, width), half)], dec_turned, *trade([error_pair] * groups))
    terms, others, enc_turned = swap_sums(terms, "layer", enc)
    latent_grad, *grads = call(
        decode_grad,
        [near((tokens, width), wide)] + [near(pair, half)] * groups,
        terms,
        others,
        slope,
        enc_turned,
    )
    one, other = call(add_last, [near(own, wide), near(own, half)], *trade(grads))
    input_grad, squared, latent_grad = call(
        finish,
        [free(own, half), free((1, tok_dev), wide), free((tokens, width), wide)],
        one,
        mirror(other),
        error,
        squared,
        latent_grad,
        scratch=[pltpu.VMEM(own, half), pltpu.SemaphoreType.DMA((3,))],
        sent=3,
    )
    return (squared.T, latent_grad, input_grad[:, None])


def solution(mesh):
    return jax.shard_map(
        shards,
        mesh=mesh,
        in_specs=(
            P("feat", "layer", None),
            P("layer", None, "feat"),
            P("layer", "feat", None),
            P("feat"),
            P("feat"),
            P("layer", None),
            P(),
        ),
        out_specs=(P("feat", "layer"), P(None, "feat"), P("feat", "layer", None)),
        check_vma=False,
    )
```

time: 76 us -> 66.5 us (0.88)
  blocking collectives: 55.2 us -> 0 us
  starting transfers between devices: 3.25 us -> 27.1 us
  waiting for transfers between devices: 8.09 us -> 30.1 us
  local copies, waits for them, and re-layouts: 0.97 us -> 0.03 us
  Pallas kernels: 7.47 us -> 8.4 us
    all_to_all x4 -> x0, blocking collectives: 55.2 us -> none  [the longest x1 17.7 us: shards(): whole_acts = exchange(copies)]
    ppermute x0 -> x15, starting transfers between devices: none -> 23.8 us  [the longest x12 14.1 us: trade(): came[k] = lax.ppermute(pieces[k], 'feat', [(i, i ^ k) for i in range(n)])]
    ppermute x0 -> x15, waiting for transfers between devices: none -> 22 us  [the longest x12 14.8 us: trade(): came[k] = lax.ppermute(pieces[k], 'feat', [(i, i ^ k) for i in range(n)])]
    broadcast_in_dim x1 -> x0, local copies, waits for them, and re-layouts: 0.94 us -> none  [shards(): copies = jnp.broadcast_to(acts[None], by_owner)]
    pallas_call x11 -> x15, Pallas kernels: 7.47 us -> 8.4 us  [call(): pl.pallas_call(body, out_shape=outs, in_specs=[away] * fetched + [here] *...]
  transfers between devices with their start and end apart: 4 -> 19, of which waited for: 4 -> 17; matrix products, arithmetic and copies ran while one was open for 0% -> 0% of each run, Pallas kernels for 4% -> 5%
where the time goes in v7:
time: 66.5 us; the launch traced here: 66.3 us
  waiting for transfers between devices  30.1 us (45%)
  starting transfers between devices  27.1 us (41%)
  Pallas kernels  8.4 us (13%)
  between operations  0.75 us (1%)
    ppermute x12, waiting for transfers between devices, trade(): came[k] = lax.ppermute(pieces[k], 'feat', [(i, i ^ k) for i in range(n)])  14.8 us
    ppermute x12, starting transfers between devices, trade(): came[k] = lax.ppermute(pieces[k], 'feat', [(i, i ^ k) for i in range(n)])  14.1 us
    ppermute x3, starting transfers between devices, mirror(): lax.ppermute(block, 'feat', [(i, (i + n // 2) % n) for i in range(n)])  9.64 us
    pallas_call x15, Pallas kernels, call(): pl.pallas_call(body, out_shape=outs, in_specs=[away] * fetched + [here] *...  8.4 us
    ppermute x4, waiting for transfers between devices, swap_sums(): other = lax.ppermute(terms, axis, [(i, i ^ span) for i in range(n)])  8.08 us
    ppermute x3, waiting for transfers between devices, mirror(): lax.ppermute(block, 'feat', [(i, (i + n // 2) % n) for i in range(n)])  7.21 us
    ppermute x4, starting transfers between devices, swap_sums(): other = lax.ppermute(terms, axis, [(i, i ^ span) for i in range(n)])  3.26 us
  transfers between devices with their start and end apart: 19, of which 17 were waited for; matrix products, arithmetic and copies ran while one was open for 0% of the time, Pallas kernels for 5%

profile of v7, /device:TPU:0, one launch (start us, length us, event | category | flops | bytes accessed | tf_op | source)
XLA Modules:
  0.0 66.3 jit_solution(17493071218594511292)
XLA Ops:
  0.6 4.1 %collective-permute-start = (bf16[8,2304]{1,0:T(8,128)(2,1)}, bf16[8,2304]{1,0:T(8,128)(2,1)S(1)}, u32[]{:S(2)}, u32[]{:S(2)}) collective-permute-start(bf16[8,2304]{1,0:T(8,128)(2,1)} %bitcast.17), channel_id=1, source_target_pairs={{0,4},{1,5},{2,6},{3,7},{4,0},{5,1},{6,2},{7,3},{8,12},{9,13},{10,... | collective-permute-start | bytes 110600 | tf_op jit(solution)/shard_map/ppermute | solution.py:61
  4.7 0.8 %shard_map.94.acts = bf16[8,2304]{1,0:T(8,128)(2,1)S(1)} custom-call(bf16[8,2304]{1,0:T(8,128)(2,1)} %bitcast.18), custom_call_target="tpu_custom_call" | custom-call | bytes 73728 | tf_op jit(solution)/shard_map/pallas_call | solution.py:29
  5.5 1.7 %collective-permute-done.other = bf16[8,2304]{1,0:T(8,128)(2,1)S(1)} collective-permute-done((bf16[8,2304]{1,0:T(8,128)(2,1)}, bf16[8,2304]{1,0:T(8,128)(2,1)S(1)}, u32[]{:S(2)}, u32[]{:S(2)}) %collective-permute-start) | collective-permute-done | bytes 36896 | tf_op jit(solution)/shard_map/ppermute | solution.py:61
  7.3 0.0 slice-start.1
  7.3 0.0 copy-start
  7.3 2.5 %collective-permute-start.3 = (bf16[16,2304]{1,0:T(8,128)(2,1)S(1)}, bf16[16,2304]{1,0:T(8,128)(2,1)S(1)}, u32[]{:S(2)}, u32[]{:S(2)}) collective-permute-start(bf16[16,2304]{1,0:T(8,128)(2,1)S(1)} %shard_map.96.rest_0_.acts), channel_id=1, source_target_pairs={{0,3},{1,2},{2,1},{3,0},{4,7},{5,6},{6,5},{7,4},{8,11},{9,10},{10,... | collective-permute-start | bytes 221192 | tf_op jit(solution)/shard_map/ppermute | solution.py:55
  9.9 0.7 %collective-permute-start.2 = (bf16[16,2304]{1,0:T(8,128)(2,1)S(1)}, bf16[16,2304]{1,0:T(8,128)(2,1)S(1)}, u32[]{:S(2)}, u32[]{:S(2)}) collective-permute-start(bf16[16,2304]{1,0:T(8,128)(2,1)S(1)} %shard_map.96.rest_0_.acts), channel_id=1, source_target_pairs={{0,2},{1,3},{2,0},{3,1},{4,6},{5,7},{6,4},{7,5},{8,10},{9,11},{10,... | collective-permute-start | bytes 221192 | tf_op jit(solution)/shard_map/ppermute | solution.py:55
  10.6 0.3 collective-permute-start.1
  10.9 1.8 %collective-permute-done.3.rest_3_ = bf16[16,2304]{1,0:T(8,128)(2,1)S(1)} collective-permute-done((bf16[16,2304]{1,0:T(8,128)(2,1)S(1)}, bf16[16,2304]{1,0:T(8,128)(2,1)S(1)}, u32[]{:S(2)}, u32[]{:S(2)}) %collective-permute-start.3) | collective-permute-done | bytes 73760 | tf_op jit(solution)/shard_map/ppermute | solution.py:55
  12.7 1.6 %collective-permute-done.2.rest_2_ = bf16[16,2304]{1,0:T(8,128)(2,1)S(1)} collective-permute-done((bf16[16,2304]{1,0:T(8,128)(2,1)S(1)}, bf16[16,2304]{1,0:T(8,128)(2,1)S(1)}, u32[]{:S(2)}, u32[]{:S(2)}) %collective-permute-start.2) | collective-permute-done | bytes 73760 | tf_op jit(solution)/shard_map/ppermute | solution.py:55
  14.2 0.7 %collective-permute-done.1.rest_1_ = bf16[16,2304]{1,0:T(8,128)(2,1)S(1)} collective-permute-done((bf16[16,2304]{1,0:T(8,128)(2,1)S(1)}, bf16[16,2304]{1,0:T(8,128)(2,1)S(1)}, u32[]{:S(2)}, u32[]{:S(2)}) %collective-permute-start.1) | collective-permute-done | bytes 73760 | tf_op jit(solution)/shard_map/ppermute | solution.py:55
  14.9 1.0 %shard_map.97 = (bf16[64,1024]{1,0:T(8,128)(2,1)S(1)}, f32[1,1024]{1,0:T(1,128)S(1)}, f32[1,1024]{1,0:T(1,128)S(1)}) custom-call(f32[1,1024]{1,0:T(1,128)} %bitcast.19, f32[1,1024]{1,0:T(1,128)} %bitcast.20, bf16[2304,1024]{1,0:T(8,128)(2,1)S(1)} %bitcast.11, bf16[16,2304]{1,0:T(8,128)(2,1)S(1)} %shard_map.96.rest_0_.acts, ...), custom_call_target="tpu_custom_call" | custom-call | tf_op jit(solution)/shard_map/pallas_call | solution.py:29
  15.9 0.1 collective-permute-start.4
  16.0 1.3 %collective-permute-done.4.other = bf16[64,1024]{1,0:T(8,128)(2,1)S(1)} collective-permute-done((bf16[64,1024]{1,0:T(8,128)(2,1)S(1)}, bf16[64,1024]{1,0:T(8,128)(2,1)S(1)}, u32[]{:S(2)}, u32[]{:S(2)}) %collective-permute-start.4) | collective-permute-done | bytes 131104 | tf_op jit(solution)/shard_map/ppermute | solution.py:44
  17.4 1.6 %collective-permute-start.5 = (bf16[64,1024]{1,0:T(8,128)(2,1)S(1)}, bf16[64,1024]{1,0:T(8,128)(2,1)S(1)}, u32[]{:S(2)}, u32[]{:S(2)}) collective-permute-start(bf16[64,1024]{1,0:T(8,128)(2,1)S(1)} %shard_map.98.after.terms), channel_id=1, source_target_pairs={{0,16},{8,24},{16,0},{24,8},{1,17},{9,25},{17,1},{25,9},{2,18},{10... | collective-permute-start | bytes 393224 | tf_op jit(solution)/shard_map/ppermute | solution.py:44
  18.9 1.4 %shard_map.99.before.weight = bf16[2304,1024]{1,0:T(8,128)(2,1)S(1)} custom-call(bf16[1024,2304]{1,0:T(8,128)(2,1)S(1)} %bitcast.14, bf16[64,1024]{1,0:T(8,128)(2,1)S(1)} %shard_map.98.after.terms), custom_call_target="tpu_custom_call" | custom-call | bytes 9699328 | tf_op jit(solution)/shard_map/pallas_call | solution.py:29
  20.4 2.6 %collective-permute-done.5.others = bf16[64,1024]{1,0:T(8,128)(2,1)S(1)} collective-permute-done((bf16[64,1024]{1,0:T(8,128)(2,1)S(1)}, bf16[64,1024]{1,0:T(8,128)(2,1)S(1)}, u32[]{:S(2)}, u32[]{:S(2)}) %collective-permute-start.5) | collective-permute-done | bytes 131104 | tf_op jit(solution)/shard_map/ppermute | solution.py:44
  23.0 1.0 %shard_map.100 = (f32[64,1024]{1,0:T(8,128)S(1)}, bf16[16,2304]{1,0:T(8,128)(2,1)S(1)}, bf16[16,2304]{1,0:T(8,128)(2,1)S(1)}, bf16[16,2304]{1,0:T(8,128)(2,1)S(1)}, bf16[16,2304]{1,0:T(8,128)(2,1)S(1)}) custom-call(bf16[64,1024]{1,0:T(8,128)(2,1)S(1)} %shard_map.98.after.terms, bf16[64,1024]{1,0:T(8,128)(2,1)S(1)} %collective-permute-done.5.others, ...), custom_call_target="tpu_custom_call" | custom-call | tf_op jit(solution)/shard_map/pallas_call | solution.py:29
  23.9 0.4 collective-permute-start.6
  24.3 1.5 %collective-permute-start.7 = (bf16[16,2304]{1,0:T(8,128)(2,1)S(1)}, bf16[16,2304]{1,0:T(8,128)(2,1)S(1)}, u32[]{:S(2)}, u32[]{:S(2)}) collective-permute-start(bf16[16,2304]{1,0:T(8,128)(2,1)S(1)} %get-tuple-element.31), channel_id=1, source_target_pairs={{0,2},{1,3},{2,0},{3,1},{4,6},{5,7},{6,4},{7,5},{8,10},{9,11},{10,... | collective-permute-start | bytes 221192 | tf_op jit(solution)/shard_map/ppermute | solution.py:55
  25.8 1.7 %collective-permute-start.8 = (bf16[16,2304]{1,0:T(8,128)(2,1)S(1)}, bf16[16,2304]{1,0:T(8,128)(2,1)S(1)}, u32[]{:S(2)}, u32[]{:S(2)}) collective-permute-start(bf16[16,2304]{1,0:T(8,128)(2,1)S(1)} %get-tuple-element.32), channel_id=1, source_target_pairs={{0,3},{1,2},{2,1},{3,0},{4,7},{5,6},{6,5},{7,4},{8,11},{9,10},{10,... | collective-permute-start | bytes 221192 | tf_op jit(solution)/shard_map/ppermute | solution.py:55
  27.5 1.7 %collective-permute-done.6.refs_1_ = bf16[16,2304]{1,0:T(8,128)(2,1)S(1)} collective-permute-done((bf16[16,2304]{1,0:T(8,128)(2,1)S(1)}, bf16[16,2304]{1,0:T(8,128)(2,1)S(1)}, u32[]{:S(2)}, u32[]{:S(2)}) %collective-permute-start.6) | collective-permute-done | bytes 73760 | tf_op jit(solution)/shard_map/ppermute | solution.py:55
  29.2 0.0 collective-permute-done.7.refs_2_
  29.2 1.9 %collective-permute-done.8.refs_3_ = bf16[16,2304]{1,0:T(8,128)(2,1)S(1)} collective-permute-done((bf16[16,2304]{1,0:T(8,128)(2,1)S(1)}, bf16[16,2304]{1,0:T(8,128)(2,1)S(1)}, u32[]{:S(2)}, u32[]{:S(2)}) %collective-permute-start.8) | collective-permute-done | bytes 73760 | tf_op jit(solution)/shard_map/ppermute | solution.py:55
  31.1 2.9 %collective-permute-start.9 = (bf16[16,2304]{1,0:T(8,128)(2,1)S(1)}, bf16[16,2304]{1,0:T(8,128)(2,1)S(1)}, u32[]{:S(2)}, u32[]{:S(2)}) collective-permute-start(bf16[16,2304]{1,0:T(8,128)(2,1)S(1)} %get-tuple-element.34), channel_id=1, source_target_pairs={{0,4},{1,5},{2,6},{3,7},{4,0},{5,1},{6,2},{7,3},{8,12},{9,13},{10,... | collective-permute-start | bytes 221192 | tf_op jit(solution)/shard_map/ppermute | solution.py:61
  34.1 3.2 %collective-permute-done.9.other = bf16[16,2304]{1,0:T(8,128)(2,1)S(1)} collective-permute-done((bf16[16,2304]{1,0:T(8,128)(2,1)S(1)}, bf16[16,2304]{1,0:T(8,128)(2,1)S(1)}, u32[]{:S(2)}, u32[]{:S(2)}) %collective-permute-start.9) | collective-permute-done | bytes 73760 | tf_op jit(solution)/shard_map/ppermute | solution.py:61
  37.2 0.2 shard_map.102
  37.4 1.0 %collective-permute-start.12 = (bf16[16,2304]{1,0:T(8,128)(2,1)S(1)}, bf16[16,2304]{1,0:T(8,128)(2,1)S(1)}, u32[]{:S(2)}, u32[]{:S(2)}) collective-permute-start(bf16[16,2304]{1,0:T(8,128)(2,1)S(1)} %get-tuple-element.35.rest_0_), channel_id=1, source_target_pairs={{0,3},{1,2},{2,1},{3,0},{4,7},{5,6},{6,5},{7,4},{8,11},{9,10},{10,... | collective-permute-start | bytes 221192 | tf_op jit(solution)/shard_map/ppermute | solution.py:55
  38.4 2.2 %collective-permute-start.11 = (bf16[16,2304]{1,0:T(8,128)(2,1)S(1)}, bf16[16,2304]{1,0:T(8,128)(2,1)S(1)}, u32[]{:S(2)}, u32[]{:S(2)}) collective-permute-start(bf16[16,2304]{1,0:T(8,128)(2,1)S(1)} %get-tuple-element.35.rest_0_), channel_id=1, source_target_pairs={{0,2},{1,3},{2,0},{3,1},{4,6},{5,7},{6,4},{7,5},{8,10},{9,11},{10,... | collective-permute-start | bytes 221192 | tf_op jit(solution)/shard_map/ppermute | solution.py:55
  40.6 0.3 collective-permute-start.10
  40.9 1.8 %collective-permute-done.12.rest_3_ = bf16[16,2304]{1,0:T(8,128)(2,1)S(1)} collective-permute-done((bf16[16,2304]{1,0:T(8,128)(2,1)S(1)}, bf16[16,2304]{1,0:T(8,128)(2,1)S(1)}, u32[]{:S(2)}, u32[]{:S(2)}) %collective-permute-start.12) | collective-permute-done | bytes 73760 | tf_op jit(solution)/shard_map/ppermute | solution.py:55
  42.7 1.0 %collective-permute-done.11.rest_2_ = bf16[16,2304]{1,0:T(8,128)(2,1)S(1)} collective-permute-done((bf16[16,2304]{1,0:T(8,128)(2,1)S(1)}, bf16[16,2304]{1,0:T(8,128)(2,1)S(1)}, u32[]{:S(2)}, u32[]{:S(2)}) %collective-permute-start.11) | collective-permute-done | bytes 73760 | tf_op jit(solution)/shard_map/ppermute | solution.py:55
  43.7 1.2 %collective-permute-done.10.rest_1_ = bf16[16,2304]{1,0:T(8,128)(2,1)S(1)} collective-permute-done((bf16[16,2304]{1,0:T(8,128)(2,1)S(1)}, bf16[16,2304]{1,0:T(8,128)(2,1)S(1)}, u32[]{:S(2)}, u32[]{:S(2)}) %collective-permute-start.10) | collective-permute-done | bytes 73760 | tf_op jit(solution)/shard_map/ppermute | solution.py:55
  45.0 0.9 %shard_map.103.one = bf16[64,1024]{1,0:T(8,128)(2,1)S(1)} custom-call(bf16[2304,1024]{1,0:T(8,128)(2,1)S(1)} %shard_map.99.before.weight, bf16[16,2304]{1,0:T(8,128)(2,1)S(1)} %get-tuple-element.35.rest_0_, bf16[16,2304]{1,0:T(8,128)(2,1)S(1)} %collective-permute-done.10.rest_1_, bf16[16,2304]{1,0:T(8,128)(2,1)S(1)} %collective-permute-done.11.rest_2_, ...), custom_call_target="tpu_custom_call" | custom-call | tf_op jit(solution)/shard_map/pallas_call | solution.py:29
  45.9 0.1 collective-permute-start.13
  46.0 1.3 %collective-permute-done.13.other = bf16[64,1024]{1,0:T(8,128)(2,1)S(1)} collective-permute-done((bf16[64,1024]{1,0:T(8,128)(2,1)S(1)}, bf16[64,1024]{1,0:T(8,128)(2,1)S(1)}, u32[]{:S(2)}, u32[]{:S(2)}) %collective-permute-start.13) | collective-permute-done | bytes 131104 | tf_op jit(solution)/shard_map/ppermute | solution.py:44
  47.4 1.6 %collective-permute-start.14 = (bf16[64,1024]{1,0:T(8,128)(2,1)S(1)}, bf16[64,1024]{1,0:T(8,128)(2,1)S(1)}, u32[]{:S(2)}, u32[]{:S(2)}) collective-permute-start(bf16[64,1024]{1,0:T(8,128)(2,1)S(1)} %shard_map.104.after.terms), channel_id=1, source_target_pairs={{0,16},{8,24},{16,0},{24,8},{1,17},{9,25},{17,1},{25,9},{2,18},{10... | collective-permute-start | bytes 393224 | tf_op jit(solution)/shard_map/ppermute | solution.py:44
  48.9 1.3 %shard_map.105.weight = bf16[1024,2304]{1,0:T(8,128)(2,1)S(1)} custom-call(bf16[2304,1024]{1,0:T(8,128)(2,1)S(1)} %bitcast.12, bf16[64,1024]{1,0:T(8,128)(2,1)S(1)} %shard_map.104.after.terms), custom_call_target="tpu_custom_call" | custom-call | bytes 9699328 | tf_op jit(solution)/shard_map/pallas_call | solution.py:29
  50.2 2.8 %collective-permute-done.14.others = bf16[64,1024]{1,0:T(8,128)(2,1)S(1)} collective-permute-done((bf16[64,1024]{1,0:T(8,128)(2,1)S(1)}, bf16[64,1024]{1,0:T(8,128)(2,1)S(1)}, u32[]{:S(2)}, u32[]{:S(2)}) %collective-permute-start.14) | collective-permute-done | bytes 131104 | tf_op jit(solution)/shard_map/ppermute | solution.py:44
  53.0 0.9 %shard_map.106 = (f32[64,1024]{1,0:T(8,128)S(1)}, bf16[16,2304]{1,0:T(8,128)(2,1)S(1)}, bf16[16,2304]{1,0:T(8,128)(2,1)S(1)}, bf16[16,2304]{1,0:T(8,128)(2,1)S(1)}, bf16[16,2304]{1,0:T(8,128)(2,1)S(1)}) custom-call(bf16[64,1024]{1,0:T(8,128)(2,1)S(1)} %shard_map.104.after.terms, bf16[64,1024]{1,0:T(8,128)(2,1)S(1)} %collective-permute-done.14.others, ...), custom_call_target="tpu_custom_call" | custom-call | tf_op jit(solution)/shard_map/pallas_call | solution.py:29
  53.9 0.4 collective-permute-start.15
  54.3 0.3 collective-permute-start.16
  54.6 2.9 %collective-permute-start.17 = (bf16[16,2304]{1,0:T(8,128)(2,1)S(1)}, bf16[16,2304]{1,0:T(8,128)(2,1)S(1)}, u32[]{:S(2)}, u32[]{:S(2)}) collective-permute-start(bf16[16,2304]{1,0:T(8,128)(2,1)S(1)} %get-tuple-element.40), channel_id=1, source_target_pairs={{0,3},{1,2},{2,1},{3,0},{4,7},{5,6},{6,5},{7,4},{8,11},{9,10},{10,... | collective-permute-start | bytes 221192 | tf_op jit(solution)/shard_map/ppermute | solution.py:55
  57.5 1.7 %collective-permute-done.15.refs_1_ = bf16[16,2304]{1,0:T(8,128)(2,1)S(1)} collective-permute-done((bf16[16,2304]{1,0:T(8,128)(2,1)S(1)}, bf16[16,2304]{1,0:T(8,128)(2,1)S(1)}, u32[]{:S(2)}, u32[]{:S(2)}) %collective-permute-start.15) | collective-permute-done | bytes 73760 | tf_op jit(solution)/shard_map/ppermute | solution.py:55
  59.1 1.5 %collective-permute-done.17.refs_3_ = bf16[16,2304]{1,0:T(8,128)(2,1)S(1)} collective-permute-done((bf16[16,2304]{1,0:T(8,128)(2,1)S(1)}, bf16[16,2304]{1,0:T(8,128)(2,1)S(1)}, u32[]{:S(2)}, u32[]{:S(2)}) %collective-permute-start.17) | collective-permute-done | bytes 73760 | tf_op jit(solution)/shard_map/ppermute | solution.py:55
  60.6 2.6 %collective-permute-start.18 = (bf16[8,2304]{1,0:T(8,128)(2,1)S(1)}, bf16[8,2304]{1,0:T(8,128)(2,1)S(1)}, u32[]{:S(2)}, u32[]{:S(2)}) collective-permute-start(bf16[8,2304]{1,0:T(8,128)(2,1)S(1)} %get-tuple-element.42), channel_id=1, source_target_pairs={{0,4},{1,5},{2,6},{3,7},{4,0},{5,1},{6,2},{7,3},{8,12},{9,13},{10,... | collective-permute-start | bytes 110600 | tf_op jit(solution)/shard_map/ppermute | solution.py:61
  63.2 2.3 %collective-permute-done.18.other = bf16[8,2304]{1,0:T(8,128)(2,1)S(1)} collective-permute-done((bf16[8,2304]{1,0:T(8,128)(2,1)S(1)}, bf16[8,2304]{1,0:T(8,128)(2,1)S(1)}, u32[]{:S(2)}, u32[]{:S(2)}) %collective-permute-start.18) | collective-permute-done | bytes 36896 | tf_op jit(solution)/shard_map/ppermute | solution.py:61
  65.6 0.7 %shard_map.108 = (bf16[8,2304]{1,0:T(8,128)(2,1)}, f32[1,8]{1,0:T(1,128)}, f32[64,1024]{1,0:T(8,128)}) custom-call(f32[8,2304]{1,0:T(8,128)S(1)} %get-tuple-element.41.one, bf16[8,2304]{1,0:T(8,128)(2,1)S(1)} %collective-permute-done.18.other, f32[8,2304]{1,0:T(8,128)S(1)} %get-tuple-element.43.error, f32[1,8]{1,0:T(1,128)S(1)} %get-tuple-element.44.squared, ...), custom_call_target="tpu_custom_call" | custom-call | tf_op jit(solution)/shard_map/pallas_call | solution.py:29
  (16 shorter events, 0.2 us)
Async XLA Ops:
  0.6 6.6 %collective-permute-start = (bf16[8,2304]{1,0:T(8,128)(2,1)}, bf16[8,2304]{1,0:T(8,128)(2,1)S(1)}, u32[]{:S(2)}, u32[]{:S(2)}) collective-permute-start(bf16[8,2304]{1,0:T(8,128)(2,1)} %bitcast.17), channel_id=1, source_target_pairs={{0,4},{1,5},{2,6},{3,7},{4,0},{5,1},{6,2},{7,3},{8,12},{9,13},{10,... | collective-permute-start | bytes 110600 | tf_op jit(solution)/shard_map/ppermute | solution.py:61
  7.3 7.7 %slice-start = ((s8[4718592]{0:T(1024)(128)(4,1)}), s8[4194304]{0:T(1024)(128)(4,1)S(1)}, s32[]{:S(2)}) async-start(s8[4718592]{0:T(1024)(128)(4,1)} %bitcast.9), calls=%async_computation | async-start | bytes 8388608
  7.3 7.7 %slice-start.1 = ((s8[4718592]{0:T(1024)(128)(4,1)}), s8[524288]{0:T(1024)(128)(4,1)S(1)}, s32[]{:S(2)}) async-start(s8[4718592]{0:T(1024)(128)(4,1)} %bitcast.9), calls=%async_computation.1 | async-start | bytes 1048576
  7.3 11.6 %copy-start = (bf16[1,1024,2304]{2,1,0:T(8,128)(2,1)S(1)}, bf16[1,1024,2304]{2,1,0:T(8,128)(2,1)}, u32[]{:S(2)}) copy-start(bf16[1,1024,2304]{2,1,0:T(8,128)(2,1)} %param.9) | copy-start | bytes 14155780
  7.3 5.3 %collective-permute-start.3 = (bf16[16,2304]{1,0:T(8,128)(2,1)S(1)}, bf16[16,2304]{1,0:T(8,128)(2,1)S(1)}, u32[]{:S(2)}, u32[]{:S(2)}) collective-permute-start(bf16[16,2304]{1,0:T(8,128)(2,1)S(1)} %shard_map.96.rest_0_.acts), channel_id=1, source_target_pairs={{0,3},{1,2},{2,1},{3,0},{4,7},{5,6},{6,5},{7,4},{8,11},{9,10},{10,... | collective-permute-start | bytes 221192 | tf_op jit(solution)/shard_map/ppermute | solution.py:55
  9.9 4.4 %collective-permute-start.2 = (bf16[16,2304]{1,0:T(8,128)(2,1)S(1)}, bf16[16,2304]{1,0:T(8,128)(2,1)S(1)}, u32[]{:S(2)}, u32[]{:S(2)}) collective-permute-start(bf16[16,2304]{1,0:T(8,128)(2,1)S(1)} %shard_map.96.rest_0_.acts), channel_id=1, source_target_pairs={{0,2},{1,3},{2,0},{3,1},{4,6},{5,7},{6,4},{7,5},{8,10},{9,11},{10,... | collective-permute-start | bytes 221192 | tf_op jit(solution)/shard_map/ppermute | solution.py:55
  10.6 4.4 %collective-permute-start.1 = (bf16[16,2304]{1,0:T(8,128)(2,1)S(1)}, bf16[16,2304]{1,0:T(8,128)(2,1)S(1)}, u32[]{:S(2)}, u32[]{:S(2)}) collective-permute-start(bf16[16,2304]{1,0:T(8,128)(2,1)S(1)} %shard_map.96.rest_0_.acts), channel_id=1, source_target_pairs={{0,1},{1,0},{2,3},{3,2},{4,5},{5,4},{6,7},{7,6},{8,9},{9,8},{10,11... | collective-permute-start | bytes 221192 | tf_op jit(solution)/shard_map/ppermute | solution.py:55
  15.9 1.4 %collective-permute-start.4 = (bf16[64,1024]{1,0:T(8,128)(2,1)S(1)}, bf16[64,1024]{1,0:T(8,128)(2,1)S(1)}, u32[]{:S(2)}, u32[]{:S(2)}) collective-permute-start(bf16[64,1024]{1,0:T(8,128)(2,1)S(1)} %get-tuple-element.26.one), channel_id=1, source_target_pairs={{0,8},{8,0},{16,24},{24,16},{1,9},{9,1},{17,25},{25,17},{2,10},{10... | collective-permute-start | bytes 393224 | tf_op jit(solution)/shard_map/ppermute | solution.py:44
  17.4 5.6 %collective-permute-start.5 = (bf16[64,1024]{1,0:T(8,128)(2,1)S(1)}, bf16[64,1024]{1,0:T(8,128)(2,1)S(1)}, u32[]{:S(2)}, u32[]{:S(2)}) collective-permute-start(bf16[64,1024]{1,0:T(8,128)(2,1)S(1)} %shard_map.98.after.terms), channel_id=1, source_target_pairs={{0,16},{8,24},{16,0},{24,8},{1,17},{9,25},{17,1},{25,9},{2,18},{10... | collective-permute-start | bytes 393224 | tf_op jit(solution)/shard_map/ppermute | solution.py:44
  23.0 14.3 %copy-start.1 = (f32[1,2304]{1,0:T(1,128)S(1)}, f32[1,2304]{1,0:T(1,128)}, u32[]{:S(2)}) copy-start(f32[1,2304]{1,0:T(1,128)} %dec_bias.1) | copy-start | bytes 27652
  23.0 14.3 %copy-start.2 = (s32[64]{0:T(128)S(1)}, s32[64]{0:T(128)}, u32[]{:S(2)}) copy-start(s32[64]{0:T(128)} %param.13) | copy-start | bytes 772
  23.9 5.2 %collective-permute-start.6 = (bf16[16,2304]{1,0:T(8,128)(2,1)S(1)}, bf16[16,2304]{1,0:T(8,128)(2,1)S(1)}, u32[]{:S(2)}, u32[]{:S(2)}) collective-permute-start(bf16[16,2304]{1,0:T(8,128)(2,1)S(1)} %get-tuple-element.30), channel_id=1, source_target_pairs={{0,1},{1,0},{2,3},{3,2},{4,5},{5,4},{6,7},{7,6},{8,9},{9,8},{10,11... | collective-permute-start | bytes 221192 | tf_op jit(solution)/shard_map/ppermute | solution.py:55
  24.3 4.9 %collective-permute-start.7 = (bf16[16,2304]{1,0:T(8,128)(2,1)S(1)}, bf16[16,2304]{1,0:T(8,128)(2,1)S(1)}, u32[]{:S(2)}, u32[]{:S(2)}) collective-permute-start(bf16[16,2304]{1,0:T(8,128)(2,1)S(1)} %get-tuple-element.31), channel_id=1, source_target_pairs={{0,2},{1,3},{2,0},{3,1},{4,6},{5,7},{6,4},{7,5},{8,10},{9,11},{10,... | collective-permute-start | bytes 221192 | tf_op jit(solution)/shard_map/ppermute | solution.py:55
  25.8 5.3 %collective-permute-start.8 = (bf16[16,2304]{1,0:T(8,128)(2,1)S(1)}, bf16[16,2304]{1,0:T(8,128)(2,1)S(1)}, u32[]{:S(2)}, u32[]{:S(2)}) collective-permute-start(bf16[16,2304]{1,0:T(8,128)(2,1)S(1)} %get-tuple-element.32), channel_id=1, source_target_pairs={{0,3},{1,2},{2,1},{3,0},{4,7},{5,6},{6,5},{7,4},{8,11},{9,10},{10,... | collective-permute-start | bytes 221192 | tf_op jit(solution)/shard_map/ppermute | solution.py:55
  31.1 6.1 %collective-permute-start.9 = (bf16[16,2304]{1,0:T(8,128)(2,1)S(1)}, bf16[16,2304]{1,0:T(8,128)(2,1)S(1)}, u32[]{:S(2)}, u32[]{:S(2)}) collective-permute-start(bf16[16,2304]{1,0:T(8,128)(2,1)S(1)} %get-tuple-element.34), channel_id=1, source_target_pairs={{0,4},{1,5},{2,6},{3,7},{4,0},{5,1},{6,2},{7,3},{8,12},{9,13},{10,... | collective-permute-start | bytes 221192 | tf_op jit(solution)/shard_map/ppermute | solution.py:61
  37.4 5.3 %collective-permute-start.12 = (bf16[16,2304]{1,0:T(8,128)(2,1)S(1)}, bf16[16,2304]{1,0:T(8,128)(2,1)S(1)}, u32[]{:S(2)}, u32[]{:S(2)}) collective-permute-start(bf16[16,2304]{1,0:T(8,128)(2,1)S(1)} %get-tuple-element.35.rest_0_), channel_id=1, source_target_pairs={{0,3},{1,2},{2,1},{3,0},{4,7},{5,6},{6,5},{7,4},{8,11},{9,10},{10,... | collective-permute-start | bytes 221192 | tf_op jit(solution)/shard_map/ppermute | solution.py:55
  38.4 5.3 %collective-permute-start.11 = (bf16[16,2304]{1,0:T(8,128)(2,1)S(1)}, bf16[16,2304]{1,0:T(8,128)(2,1)S(1)}, u32[]{:S(2)}, u32[]{:S(2)}) collective-permute-start(bf16[16,2304]{1,0:T(8,128)(2,1)S(1)} %get-tuple-element.35.rest_0_), channel_id=1, source_target_pairs={{0,2},{1,3},{2,0},{3,1},{4,6},{5,7},{6,4},{7,5},{8,10},{9,11},{10,... | collective-permute-start | bytes 221192 | tf_op jit(solution)/shard_map/ppermute | solution.py:55
  40.6 4.4 %collective-permute-start.10 = (bf16[16,2304]{1,0:T(8,128)(2,1)S(1)}, bf16[16,2304]{1,0:T(8,128)(2,1)S(1)}, u32[]{:S(2)}, u32[]{:S(2)}) collective-permute-start(bf16[16,2304]{1,0:T(8,128)(2,1)S(1)} %get-tuple-element.35.rest_0_), channel_id=1, source_target_pairs={{0,1},{1,0},{2,3},{3,2},{4,5},{5,4},{6,7},{7,6},{8,9},{9,8},{10,11... | collective-permute-start | bytes 221192 | tf_op jit(solution)/shard_map/ppermute | solution.py:55
  45.9 1.4 %collective-permute-start.13 = (bf16[64,1024]{1,0:T(8,128)(2,1)S(1)}, bf16[64,1024]{1,0:T(8,128)(2,1)S(1)}, u32[]{:S(2)}, u32[]{:S(2)}) collective-permute-start(bf16[64,1024]{1,0:T(8,128)(2,1)S(1)} %shard_map.103.one), channel_id=1, source_target_pairs={{0,8},{8,0},{16,24},{24,16},{1,9},{9,1},{17,25},{25,17},{2,10},{10... | collective-permute-start | bytes 393224 | tf_op jit(solution)/shard_map/ppermute | solution.py:44
  47.4 5.6 %collective-permute-start.14 = (bf16[64,1024]{1,0:T(8,128)(2,1)S(1)}, bf16[64,1024]{1,0:T(8,128)(2,1)S(1)}, u32[]{:S(2)}, u32[]{:S(2)}) collective-permute-start(bf16[64,1024]{1,0:T(8,128)(2,1)S(1)} %shard_map.104.after.terms), channel_id=1, source_target_pairs={{0,16},{8,24},{16,0},{24,8},{1,17},{9,25},{17,1},{25,9},{2,18},{10... | collective-permute-start | bytes 393224 | tf_op jit(solution)/shard_map/ppermute | solution.py:44
  53.9 5.2 %collective-permute-start.15 = (bf16[16,2304]{1,0:T(8,128)(2,1)S(1)}, bf16[16,2304]{1,0:T(8,128)(2,1)S(1)}, u32[]{:S(2)}, u32[]{:S(2)}) collective-permute-start(bf16[16,2304]{1,0:T(8,128)(2,1)S(1)} %get-tuple-element.38), channel_id=1, source_target_pairs={{0,1},{1,0},{2,3},{3,2},{4,5},{5,4},{6,7},{7,6},{8,9},{9,8},{10,11... | collective-permute-start | bytes 221192 | tf_op jit(solution)/shard_map/ppermute | solution.py:55
  54.3 4.8 %collective-permute-start.16 = (bf16[16,2304]{1,0:T(8,128)(2,1)S(1)}, bf16[16,2304]{1,0:T(8,128)(2,1)S(1)}, u32[]{:S(2)}, u32[]{:S(2)}) collective-permute-start(bf16[16,2304]{1,0:T(8,128)(2,1)S(1)} %get-tuple-element.39), channel_id=1, source_target_pairs={{0,2},{1,3},{2,0},{3,1},{4,6},{5,7},{6,4},{7,5},{8,10},{9,11},{10,... | collective-permute-start | bytes 221192 | tf_op jit(solution)/shard_map/ppermute | solution.py:55
  54.6 6.0 %collective-permute-start.17 = (bf16[16,2304]{1,0:T(8,128)(2,1)S(1)}, bf16[16,2304]{1,0:T(8,128)(2,1)S(1)}, u32[]{:S(2)}, u32[]{:S(2)}) collective-permute-start(bf16[16,2304]{1,0:T(8,128)(2,1)S(1)} %get-tuple-element.40), channel_id=1, source_target_pairs={{0,3},{1,2},{2,1},{3,0},{4,7},{5,6},{6,5},{7,4},{8,11},{9,10},{10,... | collective-permute-start | bytes 221192 | tf_op jit(solution)/shard_map/ppermute | solution.py:55
  60.6 4.9 %collective-permute-start.18 = (bf16[8,2304]{1,0:T(8,128)(2,1)S(1)}, bf16[8,2304]{1,0:T(8,128)(2,1)S(1)}, u32[]{:S(2)}, u32[]{:S(2)}) collective-permute-start(bf16[8,2304]{1,0:T(8,128)(2,1)S(1)} %get-tuple-element.42), channel_id=1, source_target_pairs={{0,4},{1,5},{2,6},{3,7},{4,0},{5,1},{6,2},{7,3},{8,12},{9,13},{10,... | collective-permute-start | bytes 110600 | tf_op jit(solution)/shard_map/ppermute | solution.py:61

commit v8 on v7

--- a/solution.py
+++ b/solution.py
@@ -225,7 +225,7 @@
         dec,
         dec_turned,
     )
-    one, other = call(add_pair, [near(pair, wide), near(pair, half)], *trade(decoded))
+    one, other = call(add_pair, [near(pair, wide), near(pair, half)], *reversed(trade(decoded)))
     error, error_pair, squared = call(
         compare,
         [near(own, wide), near(pair, half), near((1, tok_dev), wide)],
@@ -245,7 +245,7 @@
         slope,
         enc_turned,
     )
-    one, other = call(add_last, [near(own, wide), near(own, half)], *trade(grads))
+    one, other = call(add_last, [near(own, wide), near(own, half)], *reversed(trade(grads)))
     input_grad, squared, latent_grad = call(
         finish,
         [free(own, half), free((1, tok_dev), wide), free((tokens, width), wide)],

time: 66.5 us -> 64.5 us (0.970)
  waiting for transfers between devices: 30.1 us -> 27.8 us
    ppermute x12, waiting for transfers between devices: 14.8 us -> 13.5 us  [trade(): came[k] = lax.ppermute(pieces[k], 'feat', [(i, i ^ k) for i in range(n)])]
    ppermute x3, waiting for transfers between devices: 7.21 us -> 6.2 us  [mirror(): lax.ppermute(block, 'feat', [(i, (i + n // 2) % n) for i in range(n)])]
  transfers between devices with their start and end apart: 19 -> 19, of which waited for: 17 -> 19; matrix products, arithmetic and copies ran while one was open for 0% -> 0% of each run, Pallas kernels for 5% -> 5%
where the time goes in v8:
time: 64.5 us; the launch traced here: 64.3 us
  waiting for transfers between devices  27.8 us (43%)
  starting transfers between devices  27.3 us (42%)
  Pallas kernels  8.4 us (13%)
  between operations  0.75 us (1%)
    ppermute x12, starting transfers between devices, trade(): came[k] = lax.ppermute(pieces[k], 'feat', [(i, i ^ k) for i in range(n)])  14.2 us
    ppermute x12, waiting for transfers between devices, trade(): came[k] = lax.ppermute(pieces[k], 'feat', [(i, i ^ k) for i in range(n)])  13.5 us
    ppermute x3, starting transfers between devices, mirror(): lax.ppermute(block, 'feat', [(i, (i + n // 2) % n) for i in range(n)])  9.93 us
    pallas_call x15, Pallas kernels, call(): pl.pallas_call(body, out_shape=outs, in_specs=[away] * fetched + [here] *...  8.4 us
    ppermute x4, waiting for transfers between devices, swap_sums(): other = lax.ppermute(terms, axis, [(i, i ^ span) for i in range(n)])  8.08 us
    ppermute x3, waiting for transfers between devices, mirror(): lax.ppermute(block, 'feat', [(i, (i + n // 2) % n) for i in range(n)])  6.2 us
    ppermute x4, starting transfers between devices, swap_sums(): other = lax.ppermute(terms, axis, [(i, i ^ span) for i in range(n)])  3.26 us
  transfers between devices with their start and end apart: 19, of which 19 were waited for; matrix products, arithmetic and copies ran while one was open for 0% of the time, Pallas kernels for 5%

profile of v8, /device:TPU:0, one launch (start us, length us, event | category | flops | bytes accessed | tf_op | source)
XLA Modules:
  0.0 64.3 jit_solution(4069864263338214982)
XLA Ops:
  0.6 4.1 %collective-permute-start = (bf16[8,2304]{1,0:T(8,128)(2,1)}, bf16[8,2304]{1,0:T(8,128)(2,1)S(1)}, u32[]{:S(2)}, u32[]{:S(2)}) collective-permute-start(bf16[8,2304]{1,0:T(8,128)(2,1)} %bitcast.17), channel_id=1, source_target_pairs={{0,4},{1,5},{2,6},{3,7},{4,0},{5,1},{6,2},{7,3},{8,12},{9,13},{10,... | collective-permute-start | bytes 110600 | tf_op jit(solution)/shard_map/ppermute | solution.py:61
  4.7 0.8 %shard_map.94.acts = bf16[8,2304]{1,0:T(8,128)(2,1)S(1)} custom-call(bf16[8,2304]{1,0:T(8,128)(2,1)} %bitcast.18), custom_call_target="tpu_custom_call" | custom-call | bytes 73728 | tf_op jit(solution)/shard_map/pallas_call | solution.py:29
  5.5 1.7 %collective-permute-done.other = bf16[8,2304]{1,0:T(8,128)(2,1)S(1)} collective-permute-done((bf16[8,2304]{1,0:T(8,128)(2,1)}, bf16[8,2304]{1,0:T(8,128)(2,1)S(1)}, u32[]{:S(2)}, u32[]{:S(2)}) %collective-permute-start) | collective-permute-done | bytes 36896 | tf_op jit(solution)/shard_map/ppermute | solution.py:61
  7.3 0.0 slice-start.1
  7.3 2.5 %collective-permute-start.3 = (bf16[16,2304]{1,0:T(8,128)(2,1)S(1)}, bf16[16,2304]{1,0:T(8,128)(2,1)S(1)}, u32[]{:S(2)}, u32[]{:S(2)}) collective-permute-start(bf16[16,2304]{1,0:T(8,128)(2,1)S(1)} %shard_map.96.rest_0_.acts), channel_id=1, source_target_pairs={{0,3},{1,2},{2,1},{3,0},{4,7},{5,6},{6,5},{7,4},{8,11},{9,10},{10,... | collective-permute-start | bytes 221192 | tf_op jit(solution)/shard_map/ppermute | solution.py:55
  9.9 0.7 %collective-permute-start.2 = (bf16[16,2304]{1,0:T(8,128)(2,1)S(1)}, bf16[16,2304]{1,0:T(8,128)(2,1)S(1)}, u32[]{:S(2)}, u32[]{:S(2)}) collective-permute-start(bf16[16,2304]{1,0:T(8,128)(2,1)S(1)} %shard_map.96.rest_0_.acts), channel_id=1, source_target_pairs={{0,2},{1,3},{2,0},{3,1},{4,6},{5,7},{6,4},{7,5},{8,10},{9,11},{10,... | collective-permute-start | bytes 221192 | tf_op jit(solution)/shard_map/ppermute | solution.py:55
  10.6 0.3 collective-permute-start.1
  10.9 1.8 %collective-permute-done.3.rest_3_ = bf16[16,2304]{1,0:T(8,128)(2,1)S(1)} collective-permute-done((bf16[16,2304]{1,0:T(8,128)(2,1)S(1)}, bf16[16,2304]{1,0:T(8,128)(2,1)S(1)}, u32[]{:S(2)}, u32[]{:S(2)}) %collective-permute-start.3) | collective-permute-done | bytes 73760 | tf_op jit(solution)/shard_map/ppermute | solution.py:55
  12.7 1.6 %collective-permute-done.2.rest_2_ = bf16[16,2304]{1,0:T(8,128)(2,1)S(1)} collective-permute-done((bf16[16,2304]{1,0:T(8,128)(2,1)S(1)}, bf16[16,2304]{1,0:T(8,128)(2,1)S(1)}, u32[]{:S(2)}, u32[]{:S(2)}) %collective-permute-start.2) | collective-permute-done | bytes 73760 | tf_op jit(solution)/shard_map/ppermute | solution.py:55
  14.2 0.7 %collective-permute-done.1.rest_1_ = bf16[16,2304]{1,0:T(8,128)(2,1)S(1)} collective-permute-done((bf16[16,2304]{1,0:T(8,128)(2,1)S(1)}, bf16[16,2304]{1,0:T(8,128)(2,1)S(1)}, u32[]{:S(2)}, u32[]{:S(2)}) %collective-permute-start.1) | collective-permute-done | bytes 73760 | tf_op jit(solution)/shard_map/ppermute | solution.py:55
  14.9 1.0 %shard_map.97 = (bf16[64,1024]{1,0:T(8,128)(2,1)S(1)}, f32[1,1024]{1,0:T(1,128)S(1)}, f32[1,1024]{1,0:T(1,128)S(1)}) custom-call(f32[1,1024]{1,0:T(1,128)} %bitcast.19, f32[1,1024]{1,0:T(1,128)} %bitcast.20, bf16[2304,1024]{1,0:T(8,128)(2,1)S(1)} %bitcast.11, bf16[16,2304]{1,0:T(8,128)(2,1)S(1)} %shard_map.96.rest_0_.acts, ...), custom_call_target="tpu_custom_call" | custom-call | tf_op jit(solution)/shard_map/pallas_call | solution.py:29
  15.9 0.1 collective-permute-start.4
  16.0 1.3 %collective-permute-done.4.other = bf16[64,1024]{1,0:T(8,128)(2,1)S(1)} collective-permute-done((bf16[64,1024]{1,0:T(8,128)(2,1)S(1)}, bf16[64,1024]{1,0:T(8,128)(2,1)S(1)}, u32[]{:S(2)}, u32[]{:S(2)}) %collective-permute-start.4) | collective-permute-done | bytes 131104 | tf_op jit(solution)/shard_map/ppermute | solution.py:44
  17.4 1.6 %collective-permute-start.5 = (bf16[64,1024]{1,0:T(8,128)(2,1)S(1)}, bf16[64,1024]{1,0:T(8,128)(2,1)S(1)}, u32[]{:S(2)}, u32[]{:S(2)}) collective-permute-start(bf16[64,1024]{1,0:T(8,128)(2,1)S(1)} %shard_map.98.after.terms), channel_id=1, source_target_pairs={{0,16},{8,24},{16,0},{24,8},{1,17},{9,25},{17,1},{25,9},{2,18},{10... | collective-permute-start | bytes 393224 | tf_op jit(solution)/shard_map/ppermute | solution.py:44
  18.9 1.4 %shard_map.99.before.weight = bf16[2304,1024]{1,0:T(8,128)(2,1)S(1)} custom-call(bf16[1024,2304]{1,0:T(8,128)(2,1)S(1)} %bitcast.14, bf16[64,1024]{1,0:T(8,128)(2,1)S(1)} %shard_map.98.after.terms), custom_call_target="tpu_custom_call" | custom-call | bytes 9699328 | tf_op jit(solution)/shard_map/pallas_call | solution.py:29
  20.4 2.6 %collective-permute-done.5.others = bf16[64,1024]{1,0:T(8,128)(2,1)S(1)} collective-permute-done((bf16[64,1024]{1,0:T(8,128)(2,1)S(1)}, bf16[64,1024]{1,0:T(8,128)(2,1)S(1)}, u32[]{:S(2)}, u32[]{:S(2)}) %collective-permute-start.5) | collective-permute-done | bytes 131104 | tf_op jit(solution)/shard_map/ppermute | solution.py:44
  23.0 1.0 %shard_map.100 = (f32[64,1024]{1,0:T(8,128)S(1)}, bf16[16,2304]{1,0:T(8,128)(2,1)S(1)}, bf16[16,2304]{1,0:T(8,128)(2,1)S(1)}, bf16[16,2304]{1,0:T(8,128)(2,1)S(1)}, bf16[16,2304]{1,0:T(8,128)(2,1)S(1)}) custom-call(bf16[64,1024]{1,0:T(8,128)(2,1)S(1)} %shard_map.98.after.terms, bf16[64,1024]{1,0:T(8,128)(2,1)S(1)} %collective-permute-done.5.others, ...), custom_call_target="tpu_custom_call" | custom-call | tf_op jit(solution)/shard_map/pallas_call | solution.py:29
  23.9 1.3 %collective-permute-start.6 = (bf16[16,2304]{1,0:T(8,128)(2,1)S(1)}, bf16[16,2304]{1,0:T(8,128)(2,1)S(1)}, u32[]{:S(2)}, u32[]{:S(2)}) collective-permute-start(bf16[16,2304]{1,0:T(8,128)(2,1)S(1)} %get-tuple-element.29), channel_id=1, source_target_pairs={{0,3},{1,2},{2,1},{3,0},{4,7},{5,6},{6,5},{7,4},{8,11},{9,10},{10,... | collective-permute-start | bytes 221192 | tf_op jit(solution)/shard_map/ppermute | solution.py:55
  25.3 0.5 collective-permute-start.7
  25.8 1.7 %collective-permute-start.8 = (bf16[16,2304]{1,0:T(8,128)(2,1)S(1)}, bf16[16,2304]{1,0:T(8,128)(2,1)S(1)}, u32[]{:S(2)}, u32[]{:S(2)}) collective-permute-start(bf16[16,2304]{1,0:T(8,128)(2,1)S(1)} %get-tuple-element.31), channel_id=1, source_target_pairs={{0,1},{1,0},{2,3},{3,2},{4,5},{5,4},{6,7},{7,6},{8,9},{9,8},{10,11... | collective-permute-start | bytes 221192 | tf_op jit(solution)/shard_map/ppermute | solution.py:55
  27.5 1.9 %collective-permute-done.6.refs_0_ = bf16[16,2304]{1,0:T(8,128)(2,1)S(1)} collective-permute-done((bf16[16,2304]{1,0:T(8,128)(2,1)S(1)}, bf16[16,2304]{1,0:T(8,128)(2,1)S(1)}, u32[]{:S(2)}, u32[]{:S(2)}) %collective-permute-start.6) | collective-permute-done | bytes 73760 | tf_op jit(solution)/shard_map/ppermute | solution.py:55
  29.4 0.2 collective-permute-done.7.refs_1_
  29.6 0.6 collective-permute-done.8.refs_2_
  30.3 2.8 %collective-permute-start.9 = (bf16[16,2304]{1,0:T(8,128)(2,1)S(1)}, bf16[16,2304]{1,0:T(8,128)(2,1)S(1)}, u32[]{:S(2)}, u32[]{:S(2)}) collective-permute-start(bf16[16,2304]{1,0:T(8,128)(2,1)S(1)} %get-tuple-element.34), channel_id=1, source_target_pairs={{0,4},{1,5},{2,6},{3,7},{4,0},{5,1},{6,2},{7,3},{8,12},{9,13},{10,... | collective-permute-start | bytes 221192 | tf_op jit(solution)/shard_map/ppermute | solution.py:61
  33.1 2.5 %collective-permute-done.9.other = bf16[16,2304]{1,0:T(8,128)(2,1)S(1)} collective-permute-done((bf16[16,2304]{1,0:T(8,128)(2,1)S(1)}, bf16[16,2304]{1,0:T(8,128)(2,1)S(1)}, u32[]{:S(2)}, u32[]{:S(2)}) %collective-permute-start.9) | collective-permute-done | bytes 73760 | tf_op jit(solution)/shard_map/ppermute | solution.py:61
  35.6 0.2 shard_map.102
  35.8 2.4 %collective-permute-start.12 = (bf16[16,2304]{1,0:T(8,128)(2,1)S(1)}, bf16[16,2304]{1,0:T(8,128)(2,1)S(1)}, u32[]{:S(2)}, u32[]{:S(2)}) collective-permute-start(bf16[16,2304]{1,0:T(8,128)(2,1)S(1)} %get-tuple-element.35.rest_0_), channel_id=1, source_target_pairs={{0,3},{1,2},{2,1},{3,0},{4,7},{5,6},{6,5},{7,4},{8,11},{9,10},{10,... | collective-permute-start | bytes 221192 | tf_op jit(solution)/shard_map/ppermute | solution.py:55
  38.2 0.7 %collective-permute-start.11 = (bf16[16,2304]{1,0:T(8,128)(2,1)S(1)}, bf16[16,2304]{1,0:T(8,128)(2,1)S(1)}, u32[]{:S(2)}, u32[]{:S(2)}) collective-permute-start(bf16[16,2304]{1,0:T(8,128)(2,1)S(1)} %get-tuple-element.35.rest_0_), channel_id=1, source_target_pairs={{0,2},{1,3},{2,0},{3,1},{4,6},{5,7},{6,4},{7,5},{8,10},{9,11},{10,... | collective-permute-start | bytes 221192 | tf_op jit(solution)/shard_map/ppermute | solution.py:55
  38.9 0.4 collective-permute-start.10
  39.3 1.8 %collective-permute-done.12.rest_3_ = bf16[16,2304]{1,0:T(8,128)(2,1)S(1)} collective-permute-done((bf16[16,2304]{1,0:T(8,128)(2,1)S(1)}, bf16[16,2304]{1,0:T(8,128)(2,1)S(1)}, u32[]{:S(2)}, u32[]{:S(2)}) %collective-permute-start.12) | collective-permute-done | bytes 73760 | tf_op jit(solution)/shard_map/ppermute | solution.py:55
  41.0 1.5 %collective-permute-done.11.rest_2_ = bf16[16,2304]{1,0:T(8,128)(2,1)S(1)} collective-permute-done((bf16[16,2304]{1,0:T(8,128)(2,1)S(1)}, bf16[16,2304]{1,0:T(8,128)(2,1)S(1)}, u32[]{:S(2)}, u32[]{:S(2)}) %collective-permute-start.11) | collective-permute-done | bytes 73760 | tf_op jit(solution)/shard_map/ppermute | solution.py:55
  42.6 0.7 %collective-permute-done.10.rest_1_ = bf16[16,2304]{1,0:T(8,128)(2,1)S(1)} collective-permute-done((bf16[16,2304]{1,0:T(8,128)(2,1)S(1)}, bf16[16,2304]{1,0:T(8,128)(2,1)S(1)}, u32[]{:S(2)}, u32[]{:S(2)}) %collective-permute-start.10) | collective-permute-done | bytes 73760 | tf_op jit(solution)/shard_map/ppermute | solution.py:55
  43.3 0.9 %shard_map.103.one = bf16[64,1024]{1,0:T(8,128)(2,1)S(1)} custom-call(bf16[2304,1024]{1,0:T(8,128)(2,1)S(1)} %shard_map.99.before.weight, bf16[16,2304]{1,0:T(8,128)(2,1)S(1)} %get-tuple-element.35.rest_0_, bf16[16,2304]{1,0:T(8,128)(2,1)S(1)} %collective-permute-done.10.rest_1_, bf16[16,2304]{1,0:T(8,128)(2,1)S(1)} %collective-permute-done.11.rest_2_, ...), custom_call_target="tpu_custom_call" | custom-call | tf_op jit(solution)/shard_map/pallas_call | solution.py:29
  44.2 0.1 collective-permute-start.13
  44.3 1.3 %collective-permute-done.13.other = bf16[64,1024]{1,0:T(8,128)(2,1)S(1)} collective-permute-done((bf16[64,1024]{1,0:T(8,128)(2,1)S(1)}, bf16[64,1024]{1,0:T(8,128)(2,1)S(1)}, u32[]{:S(2)}, u32[]{:S(2)}) %collective-permute-start.13) | collective-permute-done | bytes 131104 | tf_op jit(solution)/shard_map/ppermute | solution.py:44
  45.7 1.6 %collective-permute-start.14 = (bf16[64,1024]{1,0:T(8,128)(2,1)S(1)}, bf16[64,1024]{1,0:T(8,128)(2,1)S(1)}, u32[]{:S(2)}, u32[]{:S(2)}) collective-permute-start(bf16[64,1024]{1,0:T(8,128)(2,1)S(1)} %shard_map.104.after.terms), channel_id=1, source_target_pairs={{0,16},{8,24},{16,0},{24,8},{1,17},{9,25},{17,1},{25,9},{2,18},{10... | collective-permute-start | bytes 393224 | tf_op jit(solution)/shard_map/ppermute | solution.py:44
  47.2 1.3 %shard_map.105.weight = bf16[1024,2304]{1,0:T(8,128)(2,1)S(1)} custom-call(bf16[2304,1024]{1,0:T(8,128)(2,1)S(1)} %bitcast.12, bf16[64,1024]{1,0:T(8,128)(2,1)S(1)} %shard_map.104.after.terms), custom_call_target="tpu_custom_call" | custom-call | bytes 9699328 | tf_op jit(solution)/shard_map/pallas_call | solution.py:29
  48.5 2.8 %collective-permute-done.14.others = bf16[64,1024]{1,0:T(8,128)(2,1)S(1)} collective-permute-done((bf16[64,1024]{1,0:T(8,128)(2,1)S(1)}, bf16[64,1024]{1,0:T(8,128)(2,1)S(1)}, u32[]{:S(2)}, u32[]{:S(2)}) %collective-permute-start.14) | collective-permute-done | bytes 131104 | tf_op jit(solution)/shard_map/ppermute | solution.py:44
  51.3 0.9 %shard_map.106 = (f32[64,1024]{1,0:T(8,128)S(1)}, bf16[16,2304]{1,0:T(8,128)(2,1)S(1)}, bf16[16,2304]{1,0:T(8,128)(2,1)S(1)}, bf16[16,2304]{1,0:T(8,128)(2,1)S(1)}, bf16[16,2304]{1,0:T(8,128)(2,1)S(1)}) custom-call(bf16[64,1024]{1,0:T(8,128)(2,1)S(1)} %shard_map.104.after.terms, bf16[64,1024]{1,0:T(8,128)(2,1)S(1)} %collective-permute-done.14.others, ...), custom_call_target="tpu_custom_call" | custom-call | tf_op jit(solution)/shard_map/pallas_call | solution.py:29
  52.2 1.5 %collective-permute-start.15 = (bf16[16,2304]{1,0:T(8,128)(2,1)S(1)}, bf16[16,2304]{1,0:T(8,128)(2,1)S(1)}, u32[]{:S(2)}, u32[]{:S(2)}) collective-permute-start(bf16[16,2304]{1,0:T(8,128)(2,1)S(1)} %get-tuple-element.37), channel_id=1, source_target_pairs={{0,3},{1,2},{2,1},{3,0},{4,7},{5,6},{6,5},{7,4},{8,11},{9,10},{10,... | collective-permute-start | bytes 221192 | tf_op jit(solution)/shard_map/ppermute | solution.py:55
  53.7 0.4 collective-permute-start.16
  54.1 1.6 %collective-permute-start.17 = (bf16[16,2304]{1,0:T(8,128)(2,1)S(1)}, bf16[16,2304]{1,0:T(8,128)(2,1)S(1)}, u32[]{:S(2)}, u32[]{:S(2)}) collective-permute-start(bf16[16,2304]{1,0:T(8,128)(2,1)S(1)} %get-tuple-element.39), channel_id=1, source_target_pairs={{0,1},{1,0},{2,3},{3,2},{4,5},{5,4},{6,7},{7,6},{8,9},{9,8},{10,11... | collective-permute-start | bytes 221192 | tf_op jit(solution)/shard_map/ppermute | solution.py:55
  55.8 2.0 %collective-permute-done.15.refs_0_ = bf16[16,2304]{1,0:T(8,128)(2,1)S(1)} collective-permute-done((bf16[16,2304]{1,0:T(8,128)(2,1)S(1)}, bf16[16,2304]{1,0:T(8,128)(2,1)S(1)}, u32[]{:S(2)}, u32[]{:S(2)}) %collective-permute-start.15) | collective-permute-done | bytes 73760 | tf_op jit(solution)/shard_map/ppermute | solution.py:55
  57.7 0.3 collective-permute-done.16.refs_1_
  58.0 0.5 collective-permute-done.17.refs_2_
  58.6 3.0 %collective-permute-start.18 = (bf16[8,2304]{1,0:T(8,128)(2,1)S(1)}, bf16[8,2304]{1,0:T(8,128)(2,1)S(1)}, u32[]{:S(2)}, u32[]{:S(2)}) collective-permute-start(bf16[8,2304]{1,0:T(8,128)(2,1)S(1)} %get-tuple-element.42), channel_id=1, source_target_pairs={{0,4},{1,5},{2,6},{3,7},{4,0},{5,1},{6,2},{7,3},{8,12},{9,13},{10,... | collective-permute-start | bytes 110600 | tf_op jit(solution)/shard_map/ppermute | solution.py:61
  61.6 1.9 %collective-permute-done.18.other = bf16[8,2304]{1,0:T(8,128)(2,1)S(1)} collective-permute-done((bf16[8,2304]{1,0:T(8,128)(2,1)S(1)}, bf16[8,2304]{1,0:T(8,128)(2,1)S(1)}, u32[]{:S(2)}, u32[]{:S(2)}) %collective-permute-start.18) | collective-permute-done | bytes 36896 | tf_op jit(solution)/shard_map/ppermute | solution.py:61
  63.6 0.7 %shard_map.108 = (bf16[8,2304]{1,0:T(8,128)(2,1)}, f32[1,8]{1,0:T(1,128)}, f32[64,1024]{1,0:T(8,128)}) custom-call(f32[8,2304]{1,0:T(8,128)S(1)} %get-tuple-element.41.one, bf16[8,2304]{1,0:T(8,128)(2,1)S(1)} %collective-permute-done.18.other, f32[8,2304]{1,0:T(8,128)S(1)} %get-tuple-element.43.error, f32[1,8]{1,0:T(1,128)S(1)} %get-tuple-element.44.squared, ...), custom_call_target="tpu_custom_call" | custom-call | tf_op jit(solution)/shard_map/pallas_call | solution.py:29
  (16 shorter events, 0.2 us)
Async XLA Ops:
  0.6 6.6 %collective-permute-start = (bf16[8,2304]{1,0:T(8,128)(2,1)}, bf16[8,2304]{1,0:T(8,128)(2,1)S(1)}, u32[]{:S(2)}, u32[]{:S(2)}) collective-permute-start(bf16[8,2304]{1,0:T(8,128)(2,1)} %bitcast.17), channel_id=1, source_target_pairs={{0,4},{1,5},{2,6},{3,7},{4,0},{5,1},{6,2},{7,3},{8,12},{9,13},{10,... | collective-permute-start | bytes 110600 | tf_op jit(solution)/shard_map/ppermute | solution.py:61
  7.3 7.7 %slice-start = ((s8[4718592]{0:T(1024)(128)(4,1)}), s8[4194304]{0:T(1024)(128)(4,1)S(1)}, s32[]{:S(2)}) async-start(s8[4718592]{0:T(1024)(128)(4,1)} %bitcast.9), calls=%async_computation | async-start | bytes 8388608
  7.3 7.7 %slice-start.1 = ((s8[4718592]{0:T(1024)(128)(4,1)}), s8[524288]{0:T(1024)(128)(4,1)S(1)}, s32[]{:S(2)}) async-start(s8[4718592]{0:T(1024)(128)(4,1)} %bitcast.9), calls=%async_computation.1 | async-start | bytes 1048576
  7.3 11.6 %copy-start = (bf16[1,1024,2304]{2,1,0:T(8,128)(2,1)S(1)}, bf16[1,1024,2304]{2,1,0:T(8,128)(2,1)}, u32[]{:S(2)}) copy-start(bf16[1,1024,2304]{2,1,0:T(8,128)(2,1)} %param.9) | copy-start | bytes 14155780
  7.3 5.3 %collective-permute-start.3 = (bf16[16,2304]{1,0:T(8,128)(2,1)S(1)}, bf16[16,2304]{1,0:T(8,128)(2,1)S(1)}, u32[]{:S(2)}, u32[]{:S(2)}) collective-permute-start(bf16[16,2304]{1,0:T(8,128)(2,1)S(1)} %shard_map.96.rest_0_.acts), channel_id=1, source_target_pairs={{0,3},{1,2},{2,1},{3,0},{4,7},{5,6},{6,5},{7,4},{8,11},{9,10},{10,... | collective-permute-start | bytes 221192 | tf_op jit(solution)/shard_map/ppermute | solution.py:55
  9.9 4.4 %collective-permute-start.2 = (bf16[16,2304]{1,0:T(8,128)(2,1)S(1)}, bf16[16,2304]{1,0:T(8,128)(2,1)S(1)}, u32[]{:S(2)}, u32[]{:S(2)}) collective-permute-start(bf16[16,2304]{1,0:T(8,128)(2,1)S(1)} %shard_map.96.rest_0_.acts), channel_id=1, source_target_pairs={{0,2},{1,3},{2,0},{3,1},{4,6},{5,7},{6,4},{7,5},{8,10},{9,11},{10,... | collective-permute-start | bytes 221192 | tf_op jit(solution)/shard_map/ppermute | solution.py:55
  10.6 4.4 %collective-permute-start.1 = (bf16[16,2304]{1,0:T(8,128)(2,1)S(1)}, bf16[16,2304]{1,0:T(8,128)(2,1)S(1)}, u32[]{:S(2)}, u32[]{:S(2)}) collective-permute-start(bf16[16,2304]{1,0:T(8,128)(2,1)S(1)} %shard_map.96.rest_0_.acts), channel_id=1, source_target_pairs={{0,1},{1,0},{2,3},{3,2},{4,5},{5,4},{6,7},{7,6},{8,9},{9,8},{10,11... | collective-permute-start | bytes 221192 | tf_op jit(solution)/shard_map/ppermute | solution.py:55
  15.9 1.4 %collective-permute-start.4 = (bf16[64,1024]{1,0:T(8,128)(2,1)S(1)}, bf16[64,1024]{1,0:T(8,128)(2,1)S(1)}, u32[]{:S(2)}, u32[]{:S(2)}) collective-permute-start(bf16[64,1024]{1,0:T(8,128)(2,1)S(1)} %get-tuple-element.26.one), channel_id=1, source_target_pairs={{0,8},{8,0},{16,24},{24,16},{1,9},{9,1},{17,25},{25,17},{2,10},{10... | collective-permute-start | bytes 393224 | tf_op jit(solution)/shard_map/ppermute | solution.py:44
  17.4 5.6 %collective-permute-start.5 = (bf16[64,1024]{1,0:T(8,128)(2,1)S(1)}, bf16[64,1024]{1,0:T(8,128)(2,1)S(1)}, u32[]{:S(2)}, u32[]{:S(2)}) collective-permute-start(bf16[64,1024]{1,0:T(8,128)(2,1)S(1)} %shard_map.98.after.terms), channel_id=1, source_target_pairs={{0,16},{8,24},{16,0},{24,8},{1,17},{9,25},{17,1},{25,9},{2,18},{10... | collective-permute-start | bytes 393224 | tf_op jit(solution)/shard_map/ppermute | solution.py:44
  23.0 12.6 %copy-start.1 = (f32[1,2304]{1,0:T(1,128)S(1)}, f32[1,2304]{1,0:T(1,128)}, u32[]{:S(2)}) copy-start(f32[1,2304]{1,0:T(1,128)} %dec_bias.1) | copy-start | bytes 27652
  23.0 12.6 %copy-start.2 = (s32[64]{0:T(128)S(1)}, s32[64]{0:T(128)}, u32[]{:S(2)}) copy-start(s32[64]{0:T(128)} %param.13) | copy-start | bytes 772
  23.9 5.5 %collective-permute-start.6 = (bf16[16,2304]{1,0:T(8,128)(2,1)S(1)}, bf16[16,2304]{1,0:T(8,128)(2,1)S(1)}, u32[]{:S(2)}, u32[]{:S(2)}) collective-permute-start(bf16[16,2304]{1,0:T(8,128)(2,1)S(1)} %get-tuple-element.29), channel_id=1, source_target_pairs={{0,3},{1,2},{2,1},{3,0},{4,7},{5,6},{6,5},{7,4},{8,11},{9,10},{10,... | collective-permute-start | bytes 221192 | tf_op jit(solution)/shard_map/ppermute | solution.py:55
  25.3 4.4 %collective-permute-start.7 = (bf16[16,2304]{1,0:T(8,128)(2,1)S(1)}, bf16[16,2304]{1,0:T(8,128)(2,1)S(1)}, u32[]{:S(2)}, u32[]{:S(2)}) collective-permute-start(bf16[16,2304]{1,0:T(8,128)(2,1)S(1)} %get-tuple-element.30), channel_id=1, source_target_pairs={{0,2},{1,3},{2,0},{3,1},{4,6},{5,7},{6,4},{7,5},{8,10},{9,11},{10,... | collective-permute-start | bytes 221192 | tf_op jit(solution)/shard_map/ppermute | solution.py:55
  25.8 4.4 %collective-permute-start.8 = (bf16[16,2304]{1,0:T(8,128)(2,1)S(1)}, bf16[16,2304]{1,0:T(8,128)(2,1)S(1)}, u32[]{:S(2)}, u32[]{:S(2)}) collective-permute-start(bf16[16,2304]{1,0:T(8,128)(2,1)S(1)} %get-tuple-element.31), channel_id=1, source_target_pairs={{0,1},{1,0},{2,3},{3,2},{4,5},{5,4},{6,7},{7,6},{8,9},{9,8},{10,11... | collective-permute-start | bytes 221192 | tf_op jit(solution)/shard_map/ppermute | solution.py:55
  30.3 5.3 %collective-permute-start.9 = (bf16[16,2304]{1,0:T(8,128)(2,1)S(1)}, bf16[16,2304]{1,0:T(8,128)(2,1)S(1)}, u32[]{:S(2)}, u32[]{:S(2)}) collective-permute-start(bf16[16,2304]{1,0:T(8,128)(2,1)S(1)} %get-tuple-element.34), channel_id=1, source_target_pairs={{0,4},{1,5},{2,6},{3,7},{4,0},{5,1},{6,2},{7,3},{8,12},{9,13},{10,... | collective-permute-start | bytes 221192 | tf_op jit(solution)/shard_map/ppermute | solution.py:61
  35.8 5.3 %collective-permute-start.12 = (bf16[16,2304]{1,0:T(8,128)(2,1)S(1)}, bf16[16,2304]{1,0:T(8,128)(2,1)S(1)}, u32[]{:S(2)}, u32[]{:S(2)}) collective-permute-start(bf16[16,2304]{1,0:T(8,128)(2,1)S(1)} %get-tuple-element.35.rest_0_), channel_id=1, source_target_pairs={{0,3},{1,2},{2,1},{3,0},{4,7},{5,6},{6,5},{7,4},{8,11},{9,10},{10,... | collective-permute-start | bytes 221192 | tf_op jit(solution)/shard_map/ppermute | solution.py:55
  38.2 4.4 %collective-permute-start.11 = (bf16[16,2304]{1,0:T(8,128)(2,1)S(1)}, bf16[16,2304]{1,0:T(8,128)(2,1)S(1)}, u32[]{:S(2)}, u32[]{:S(2)}) collective-permute-start(bf16[16,2304]{1,0:T(8,128)(2,1)S(1)} %get-tuple-element.35.rest_0_), channel_id=1, source_target_pairs={{0,2},{1,3},{2,0},{3,1},{4,6},{5,7},{6,4},{7,5},{8,10},{9,11},{10,... | collective-permute-start | bytes 221192 | tf_op jit(solution)/shard_map/ppermute | solution.py:55
  38.9 4.4 %collective-permute-start.10 = (bf16[16,2304]{1,0:T(8,128)(2,1)S(1)}, bf16[16,2304]{1,0:T(8,128)(2,1)S(1)}, u32[]{:S(2)}, u32[]{:S(2)}) collective-permute-start(bf16[16,2304]{1,0:T(8,128)(2,1)S(1)} %get-tuple-element.35.rest_0_), channel_id=1, source_target_pairs={{0,1},{1,0},{2,3},{3,2},{4,5},{5,4},{6,7},{7,6},{8,9},{9,8},{10,11... | collective-permute-start | bytes 221192 | tf_op jit(solution)/shard_map/ppermute | solution.py:55
  44.2 1.4 %collective-permute-start.13 = (bf16[64,1024]{1,0:T(8,128)(2,1)S(1)}, bf16[64,1024]{1,0:T(8,128)(2,1)S(1)}, u32[]{:S(2)}, u32[]{:S(2)}) collective-permute-start(bf16[64,1024]{1,0:T(8,128)(2,1)S(1)} %shard_map.103.one), channel_id=1, source_target_pairs={{0,8},{8,0},{16,24},{24,16},{1,9},{9,1},{17,25},{25,17},{2,10},{10... | collective-permute-start | bytes 393224 | tf_op jit(solution)/shard_map/ppermute | solution.py:44
  45.7 5.6 %collective-permute-start.14 = (bf16[64,1024]{1,0:T(8,128)(2,1)S(1)}, bf16[64,1024]{1,0:T(8,128)(2,1)S(1)}, u32[]{:S(2)}, u32[]{:S(2)}) collective-permute-start(bf16[64,1024]{1,0:T(8,128)(2,1)S(1)} %shard_map.104.after.terms), channel_id=1, source_target_pairs={{0,16},{8,24},{16,0},{24,8},{1,17},{9,25},{17,1},{25,9},{2,18},{10... | collective-permute-start | bytes 393224 | tf_op jit(solution)/shard_map/ppermute | solution.py:44
  52.2 5.5 %collective-permute-start.15 = (bf16[16,2304]{1,0:T(8,128)(2,1)S(1)}, bf16[16,2304]{1,0:T(8,128)(2,1)S(1)}, u32[]{:S(2)}, u32[]{:S(2)}) collective-permute-start(bf16[16,2304]{1,0:T(8,128)(2,1)S(1)} %get-tuple-element.37), channel_id=1, source_target_pairs={{0,3},{1,2},{2,1},{3,0},{4,7},{5,6},{6,5},{7,4},{8,11},{9,10},{10,... | collective-permute-start | bytes 221192 | tf_op jit(solution)/shard_map/ppermute | solution.py:55
  53.7 4.4 %collective-permute-start.16 = (bf16[16,2304]{1,0:T(8,128)(2,1)S(1)}, bf16[16,2304]{1,0:T(8,128)(2,1)S(1)}, u32[]{:S(2)}, u32[]{:S(2)}) collective-permute-start(bf16[16,2304]{1,0:T(8,128)(2,1)S(1)} %get-tuple-element.38), channel_id=1, source_target_pairs={{0,2},{1,3},{2,0},{3,1},{4,6},{5,7},{6,4},{7,5},{8,10},{9,11},{10,... | collective-permute-start | bytes 221192 | tf_op jit(solution)/shard_map/ppermute | solution.py:55
  54.1 4.4 %collective-permute-start.17 = (bf16[16,2304]{1,0:T(8,128)(2,1)S(1)}, bf16[16,2304]{1,0:T(8,128)(2,1)S(1)}, u32[]{:S(2)}, u32[]{:S(2)}) collective-permute-start(bf16[16,2304]{1,0:T(8,128)(2,1)S(1)} %get-tuple-element.39), channel_id=1, source_target_pairs={{0,1},{1,0},{2,3},{3,2},{4,5},{5,4},{6,7},{7,6},{8,9},{9,8},{10,11... | collective-permute-start | bytes 221192 | tf_op jit(solution)/shard_map/ppermute | solution.py:55
  58.6 5.0 %collective-permute-start.18 = (bf16[8,2304]{1,0:T(8,128)(2,1)S(1)}, bf16[8,2304]{1,0:T(8,128)(2,1)S(1)}, u32[]{:S(2)}, u32[]{:S(2)}) collective-permute-start(bf16[8,2304]{1,0:T(8,128)(2,1)S(1)} %get-tuple-element.42), channel_id=1, source_target_pairs={{0,4},{1,5},{2,6},{3,7},{4,0},{5,1},{6,2},{7,3},{8,12},{9,13},{10,... | collective-permute-start | bytes 110600 | tf_op jit(solution)/shard_map/ppermute | solution.py:61

commit v9 on v8

--- a/solution.py
+++ b/solution.py
@@ -38,15 +38,22 @@
     )(*map(pltpu.with_memory_space_constraint, args, spaces))
 
 
-def swap_sums(terms, axis, weight):
-    n, span = lax.axis_size(axis), 1
-    while True:
-        other = lax.ppermute(terms, axis, [(i, i ^ span) for i in range(n)])
-        span *= 2
-        if span == n:
-            [turned] = call(turn, [near(weight.shape[::-1], half)], weight, terms, work=True)
-            return terms, other, turned
-        [terms] = call(add, [near(terms.shape, half)], terms, other)
+def layer_sum(make, weight):
+    n = lax.axis_size("layer")
+    near_by, far_off = [[(i, i ^ span) for i in range(n)] for span in (1, n // 2)]
+    theirs = lax.ppermute(make(True), "layer", near_by)
+    mine = make(False)
+    [pair] = call(add, [near(mine.shape, half)], mine, theirs)
+    [turned] = call(turn, [near(weight.shape[::-1], half)], weight, pair, work=True)
+    far = lax.ppermute(pair, "layer", far_off)
+    [far] = call(lambda *refs: None, [near(far.shape, half)], turned, far, same={1: 0})
+    other = [lax.ppermute(x, "layer", near_by) for x in (pair, far)]
+    return (pair, far), other, turned
+
+
+def features(other, width):
+    which = lax.rem(lax.axis_index("layer") + int(other), 2)
+    return pl.ds(pl.multiple_of(which * width, width), width)
 
 
 def trade(pieces):
@@ -87,10 +94,14 @@
     out[...] = (one[...].astype(wide) + other[...].astype(wide)).astype(half)
 
 
-def bring(far, out, done):
-    move = pltpu.make_async_copy(far, out, done)
-    move.start()
-    move.wait()
+def bring(*refs):
+    *refs, done = refs
+    n = len(refs) // 2
+    moves = [pltpu.make_async_copy(refs[i], refs[n + i], done.at[i]) for i in range(n)]
+    for move in moves:
+        move.start()
+    for move in moves:
+        move.wait()
 
 
 def join(acts, other, pair):
@@ -100,26 +111,13 @@
     pair[...] = jnp.concatenate(both).astype(half)
 
 
-def encode(weight, *rest):
+def encode(other, weight, *rest):
     *groups, out = rest
     x = stack(groups)
+    first = features(other, out.shape[1]).start
     for at in range(0, out.shape[1], columns):
-        out[:, at : at + columns] = jnp.dot(
-            x, weight[:, at : at + columns], preferred_element_type=wide
-        ).astype(half)
-
-
-def encode_first(enc_bias, threshold, weight, *rest):
-    *rest, bias_near, threshold_near, done = rest
-    moves = [
-        pltpu.make_async_copy(enc_bias, bias_near, done.at[0]),
-        pltpu.make_async_copy(threshold, threshold_near, done.at[1]),
-    ]
-    for move in moves:
-        move.start()
-    encode(weight, *rest)
-    for move in moves:
-        move.wait()
+        there = pl.ds(pl.multiple_of(first + at, columns), columns)
+        out[:, at : at + columns] = jnp.dot(x, weight[:, there], preferred_element_type=wide).astype(out.dtype)
 
 
 def turn(weight, after, out):
@@ -127,29 +125,36 @@
         out[:, at : at + columns] = weight[at : at + columns, :].T
 
 
-def spread_rows(x, weight, outs):
+def spread_rows(x, weight, rows_in, so_far, outs):
     for at in range(0, weight.shape[1], columns):
-        found = jnp.dot(x, weight[:, at : at + columns], preferred_element_type=wide).astype(half)
+        there = slice(at, at + columns)
+        found = jnp.dot(x, weight[rows_in, there], preferred_element_type=wide)
+        if so_far is None:
+            outs[0][:, there] = found
+            continue
+        found = (found + so_far[:, there]).astype(half)
         for k, out in enumerate(outs):
             rows = out.shape[0]
-            out[:, at : at + columns] = found[k * rows : (k + 1) * rows]
-
-
-def decode(terms, others, enc_bias, threshold, weight, before, slope, *outs):
-    preact = terms[...].astype(wide) + others[...].astype(wide) + enc_bias[...]
-    gating = jax.nn.sigmoid((preact - threshold[...]) / jump_scale)
+            out[:, there] = found[k * rows : (k + 1) * rows]
+
+
+def decode(other, terms, others, enc_bias, threshold, weight, before, slope, *outs):
+    which = features(other, terms.shape[1])
+    preact = terms[...].astype(wide) + others[...].astype(wide) + enc_bias[:, which]
+    gating = jax.nn.sigmoid((preact - threshold[:, which]) / jump_scale)
     slope[...] = gating + preact * gating * (1.0 - gating) / jump_scale
-    spread_rows((preact * gating).astype(half), weight, outs)
-
-
-def decode_grad(terms, others, slope, weight, total, *outs):
+    spread_rows((preact * gating).astype(half), weight, which, before if other else None, outs)
+
+
+def decode_grad(other, terms, others, slope, weight, before, total, *outs):
     latent_grad = terms[...].astype(wide) + others[...].astype(wide)
-    n, me = 2 * len(outs), place()
+    n, me = lax.axis_size("feat"), place()
     rows = total.shape[0] // n
     for i in range(n):
         block = lax.bitwise_xor(me, i // 2) + i % 2 * (n // 2)
         total[pl.ds(pl.multiple_of(block * rows, rows), rows), :] = latent_grad[i * rows : (i + 1) * rows]
-    spread_rows((latent_grad * slope[...]).astype(half), weight, outs)
+    x = (latent_grad * slope[...]).astype(half)
+    spread_rows(x, weight, features(other, terms.shape[1]), before if other else None, outs)
 
 
 def add_pair(*refs):
@@ -181,13 +186,14 @@
     squared[...] = jnp.sum(jnp.where(same, means, 0.0), axis=0, keepdims=True)
 
 
-def finish(one, other, error, squared, grad, out, squared_out, grad_out, held, done):
-    moves = [(grad, grad_out), (squared, squared_out), (held, out)]
+def finish(one, other, error, squared, grad, grad_other, out, squared_out, grad_out, held, done):
+    mine, theirs = [grad_out.at[:, features(which, grad.shape[1])] for which in (False, True)]
+    moves = [(grad, mine), (grad_other, theirs), (squared, squared_out), (held, out)]
     moves = [pltpu.make_async_copy(here, there, done.at[i]) for i, (here, there) in enumerate(moves)]
-    moves[0].start()
-    moves[1].start()
+    for move in moves[:-1]:
+        move.start()
     held[...] = (one[...] + other[...].astype(wide) - error[...]).astype(half)
-    moves[2].start()
+    moves[-1].start()
     for move in moves:
         move.wait()
 
@@ -201,30 +207,28 @@
     own, pair = (tok_dev, depth), (2 * tok_dev, depth)
 
     other = mirror(acts)
-    [acts] = call(bring, [near(own, half)], acts, scratch=[pltpu.SemaphoreType.DMA], fetched=1, work=True)
+    far = (acts, enc_bias[None], threshold[None])
+    acts, enc_bias, threshold = call(
+        bring,
+        [near(x.shape, x.dtype) for x in far],
+        *far,
+        scratch=[pltpu.SemaphoreType.DMA((len(far),))],
+        fetched=len(far),
+        work=True,
+    )
     [acts_pair] = call(join, [near(pair, half)], acts, other)
     [acts_pair] = call(lambda *refs: None, [near(pair, half)], enc, dec, acts_pair, fetched=2, same={2: 0})
-    terms, enc_bias, threshold = call(
-        encode_first,
-        [near((tokens, width), half), near((1, width), wide), near((1, width), wide)],
-        enc_bias[None],
-        threshold[None],
-        enc,
-        *trade([acts_pair] * groups),
-        scratch=[pltpu.SemaphoreType.DMA((2,))],
-        fetched=2,
-    )
-    terms, others, dec_turned = swap_sums(terms, "layer", dec)
-    slope, *decoded = call(
-        decode,
-        [near((tokens, width), wide)] + [near(pair, half)] * groups,
-        terms,
-        others,
-        enc_bias,
-        threshold,
-        dec,
-        dec_turned,
-    )
+    groups_of = trade([acts_pair] * groups)
+    [sent] = call(functools.partial(encode, True), [near((tokens, width // 2), half)], enc, *groups_of)
+    kept = lambda weight, given: call(
+        functools.partial(encode, False), [near((tokens, width // 2), wide)], weight, *given
+    )[0]
+    mine, theirs, dec_turned = layer_sum(lambda other: sent if other else kept(enc, groups_of), dec)
+    by_feature, whole = near((tokens, width // 2), wide), near((tokens, depth), wide)
+    by_group = [near(pair, half)] * groups
+    given = (enc_bias, threshold, dec)
+    slope, part = call(functools.partial(decode, False), [by_feature, whole], *mine, *given, dec_turned)
+    slope_other, *decoded = call(functools.partial(decode, True), [by_feature, *by_group], *theirs, *given, part)
     one, other = call(add_pair, [near(pair, wide), near(pair, half)], *reversed(trade(decoded)))
     error, error_pair, squared = call(
         compare,
@@ -235,15 +239,12 @@
         acts_pair,
         token_mask[None],
     )
-    [terms] = call(encode, [near((tokens, width), half)], dec_turned, *trade([error_pair] * groups))
-    terms, others, enc_turned = swap_sums(terms, "layer", enc)
-    latent_grad, *grads = call(
-        decode_grad,
-        [near((tokens, width), wide)] + [near(pair, half)] * groups,
-        terms,
-        others,
-        slope,
-        enc_turned,
+    errors = trade([error_pair] * groups)
+    [sent] = call(functools.partial(encode, True), [near((tokens, width // 2), half)], dec_turned, *errors)
+    mine, theirs, enc_turned = layer_sum(lambda other: sent if other else kept(dec_turned, errors), enc)
+    grad, part = call(functools.partial(decode_grad, False), [by_feature, whole], *mine, slope, enc_turned, sent)
+    grad_other, *grads = call(
+        functools.partial(decode_grad, True), [by_feature, *by_group], *theirs, slope_other, enc_turned, part
     )
     one, other = call(add_last, [near(own, wide), near(own, half)], *reversed(trade(grads)))
     input_grad, squared, latent_grad = call(
@@ -253,8 +254,9 @@
         mirror(other),
         error,
         squared,
-        latent_grad,
-        scratch=[pltpu.VMEM(own, half), pltpu.SemaphoreType.DMA((3,))],
+        grad,
+        grad_other,
+        scratch=[pltpu.VMEM(own, half), pltpu.SemaphoreType.DMA((4,))],
         sent=3,
     )
     return (squared.T, latent_grad, input_grad[:, None])

time: 64.5 us -> 64.2 us (level)
  starting transfers between devices: 27.3 us -> 25.8 us
    ppermute x3, waiting for transfers between devices: 6.2 us -> 8.71 us  [mirror(): lax.ppermute(block, 'feat', [(i, (i + n // 2) % n) for i in range(n)])]
    ppermute x4 -> x8, waiting for transfers between devices: 8.08 us -> 5.58 us  [the longest x2 2.84 us: layer_sum(): far = lax.ppermute(pair, 'layer', far_off)]
    ppermute x3, starting transfers between devices: 9.93 us -> 8.45 us  [mirror(): lax.ppermute(block, 'feat', [(i, (i + n // 2) % n) for i in range(n)])]
    pallas_call x15 -> x21, Pallas kernels: 8.4 us -> 8.99 us  [call(): pl.pallas_call(body, out_shape=outs, in_specs=[away] * fetched + [here] *...]
    ppermute x4 -> x8, starting transfers between devices: 3.26 us -> 3.25 us  [the longest x2 3.1 us: layer_sum(): far = lax.ppermute(pair, 'layer', far_off)]
  transfers between devices with their start and end apart: 19 -> 23, of which waited for: 19 -> 19; matrix products, arithmetic and copies ran while one was open for 0% -> 0% of each run, Pallas kernels for 5% -> 9%
where the time goes in v9:
time: 64.2 us; the launch traced here: 64 us
  waiting for transfers between devices  28.3 us (44%)
  starting transfers between devices  25.8 us (40%)
  Pallas kernels  8.99 us (14%)
  between operations  0.81 us (1%)
    ppermute x12, starting transfers between devices, trade(): came[k] = lax.ppermute(pieces[k], 'feat', [(i, i ^ k) for i in range(n)])  14.1 us
    ppermute x12, waiting for transfers between devices, trade(): came[k] = lax.ppermute(pieces[k], 'feat', [(i, i ^ k) for i in range(n)])  14 us
    pallas_call x21, Pallas kernels, call(): pl.pallas_call(body, out_shape=outs, in_specs=[away] * fetched + [here] *...  8.99 us
    ppermute x3, waiting for transfers between devices, mirror(): lax.ppermute(block, 'feat', [(i, (i + n // 2) % n) for i in range(n)])  8.71 us
    ppermute x3, starting transfers between devices, mirror(): lax.ppermute(block, 'feat', [(i, (i + n // 2) % n) for i in range(n)])  8.45 us
    ppermute x2, starting transfers between devices, layer_sum(): far = lax.ppermute(pair, 'layer', far_off)  3.1 us
    ppermute x2, waiting for transfers between devices, layer_sum(): far = lax.ppermute(pair, 'layer', far_off)  2.84 us
    ppermute x4, waiting for transfers between devices, layer_sum(): other = [lax.ppermute(x, 'layer', near_by) for x in (pair, far)]  1.38 us
  transfers between devices with their start and end apart: 23, of which 19 were waited for; matrix products, arithmetic and copies ran while one was open for 0% of the time, Pallas kernels for 9%

profile of v9, /device:TPU:0, one launch (start us, length us, event | category | flops | bytes accessed | tf_op | source)
XLA Modules:
  0.0 64.0 jit_solution(11055809128681432494)
XLA Ops:
  0.6 4.1 %collective-permute-start = (bf16[8,2304]{1,0:T(8,128)(2,1)}, bf16[8,2304]{1,0:T(8,128)(2,1)S(1)}, u32[]{:S(2)}, u32[]{:S(2)}) collective-permute-start(bf16[8,2304]{1,0:T(8,128)(2,1)} %bitcast.21), channel_id=1, source_target_pairs={{0,4},{1,5},{2,6},{3,7},{4,0},{5,1},{6,2},{7,3},{8,12},{9,13},{10,... | collective-permute-start | bytes 110600 | tf_op jit(solution)/shard_map/ppermute | solution.py:68
  4.7 0.8 %shard_map.94 = (bf16[8,2304]{1,0:T(8,128)(2,1)S(1)}, f32[1,1024]{1,0:T(1,128)S(1)}, f32[1,1024]{1,0:T(1,128)S(1)}) custom-call(bf16[8,2304]{1,0:T(8,128)(2,1)} %bitcast.22, f32[1,1024]{1,0:T(1,128)} %bitcast.23, f32[1,1024]{1,0:T(1,128)} %bitcast.24), custom_call_target="tpu_custom_call" | custom-call | bytes 90112 | tf_op jit(solution)/shard_map/pallas_call | solution.py:29
  5.6 1.7 %collective-permute-done.other = bf16[8,2304]{1,0:T(8,128)(2,1)S(1)} collective-permute-done((bf16[8,2304]{1,0:T(8,128)(2,1)}, bf16[8,2304]{1,0:T(8,128)(2,1)S(1)}, u32[]{:S(2)}, u32[]{:S(2)}) %collective-permute-start) | collective-permute-done | bytes 36896 | tf_op jit(solution)/shard_map/ppermute | solution.py:68
  7.3 2.5 %collective-permute-start.3 = (bf16[16,2304]{1,0:T(8,128)(2,1)S(1)}, bf16[16,2304]{1,0:T(8,128)(2,1)S(1)}, u32[]{:S(2)}, u32[]{:S(2)}) collective-permute-start(bf16[16,2304]{1,0:T(8,128)(2,1)S(1)} %shard_map.96.rest_0_.acts), channel_id=1, source_target_pairs={{0,3},{1,2},{2,1},{3,0},{4,7},{5,6},{6,5},{7,4},{8,11},{9,10},{10,... | collective-permute-start | bytes 221192 | tf_op jit(solution)/shard_map/ppermute | solution.py:62
  9.9 0.7 %collective-permute-start.2 = (bf16[16,2304]{1,0:T(8,128)(2,1)S(1)}, bf16[16,2304]{1,0:T(8,128)(2,1)S(1)}, u32[]{:S(2)}, u32[]{:S(2)}) collective-permute-start(bf16[16,2304]{1,0:T(8,128)(2,1)S(1)} %shard_map.96.rest_0_.acts), channel_id=1, source_target_pairs={{0,2},{1,3},{2,0},{3,1},{4,6},{5,7},{6,4},{7,5},{8,10},{9,11},{10,... | collective-permute-start | bytes 221192 | tf_op jit(solution)/shard_map/ppermute | solution.py:62
  10.6 0.3 collective-permute-start.1
  10.9 1.8 %collective-permute-done.3.rest_3_ = bf16[16,2304]{1,0:T(8,128)(2,1)S(1)} collective-permute-done((bf16[16,2304]{1,0:T(8,128)(2,1)S(1)}, bf16[16,2304]{1,0:T(8,128)(2,1)S(1)}, u32[]{:S(2)}, u32[]{:S(2)}) %collective-permute-start.3) | collective-permute-done | bytes 73760 | tf_op jit(solution)/shard_map/ppermute | solution.py:62
  12.7 1.6 %collective-permute-done.2.rest_2_ = bf16[16,2304]{1,0:T(8,128)(2,1)S(1)} collective-permute-done((bf16[16,2304]{1,0:T(8,128)(2,1)S(1)}, bf16[16,2304]{1,0:T(8,128)(2,1)S(1)}, u32[]{:S(2)}, u32[]{:S(2)}) %collective-permute-start.2) | collective-permute-done | bytes 73760 | tf_op jit(solution)/shard_map/ppermute | solution.py:62
  14.2 0.7 %collective-permute-done.1.rest_1_ = bf16[16,2304]{1,0:T(8,128)(2,1)S(1)} collective-permute-done((bf16[16,2304]{1,0:T(8,128)(2,1)S(1)}, bf16[16,2304]{1,0:T(8,128)(2,1)S(1)}, u32[]{:S(2)}, u32[]{:S(2)}) %collective-permute-start.1) | collective-permute-done | bytes 73760 | tf_op jit(solution)/shard_map/ppermute | solution.py:62
  15.0 0.5 shard_map.98
  15.6 0.6 shard_map.97.one
  16.2 0.7 %collective-permute-done.4.other = bf16[64,512]{1,0:T(8,128)(2,1)S(1)} collective-permute-done((bf16[64,512]{1,0:T(8,128)(2,1)S(1)}, bf16[64,512]{1,0:T(8,128)(2,1)S(1)}, u32[]{:S(2)}, u32[]{:S(2)}) %collective-permute-start.4) | collective-permute-done | bytes 65568 | tf_op jit(solution)/shard_map/ppermute | solution.py:44
  16.9 1.6 %collective-permute-start.6 = (bf16[64,512]{1,0:T(8,128)(2,1)S(1)}, bf16[64,512]{1,0:T(8,128)(2,1)S(1)}, u32[]{:S(2)}, u32[]{:S(2)}) collective-permute-start(bf16[64,512]{1,0:T(8,128)(2,1)S(1)} %shard_map.99.after.terms), channel_id=1, source_target_pairs={{0,16},{8,24},{16,0},{24,8},{1,17},{9,25},{17,1},{25,9},{2,18},{10... | collective-permute-start | bytes 196616 | tf_op jit(solution)/shard_map/ppermute | solution.py:48
  18.4 1.4 %shard_map.100.refs_0_.before.weight = bf16[2304,1024]{1,0:T(8,128)(2,1)S(1)} custom-call(bf16[1024,2304]{1,0:T(8,128)(2,1)S(1)} %bitcast.17, bf16[64,512]{1,0:T(8,128)(2,1)S(1)} %shard_map.99.after.terms), custom_call_target="tpu_custom_call" | custom-call | bytes 9568256 | tf_op jit(solution)/shard_map/pallas_call | solution.py:29
  19.9 1.3 %collective-permute-done.6.refs_1_ = bf16[64,512]{1,0:T(8,128)(2,1)S(1)} collective-permute-done((bf16[64,512]{1,0:T(8,128)(2,1)S(1)}, bf16[64,512]{1,0:T(8,128)(2,1)S(1)}, u32[]{:S(2)}, u32[]{:S(2)}) %collective-permute-start.6) | collective-permute-done | bytes 65568 | tf_op jit(solution)/shard_map/ppermute | solution.py:48
  21.2 0.5 shard_map.102
  21.8 0.7 %collective-permute-done.7.others = bf16[64,512]{1,0:T(8,128)(2,1)S(1)} collective-permute-done((bf16[64,512]{1,0:T(8,128)(2,1)S(1)}, bf16[64,512]{1,0:T(8,128)(2,1)S(1)}, u32[]{:S(2)}, u32[]{:S(2)}) %collective-permute-start.7) | collective-permute-done | bytes 65568 | tf_op jit(solution)/shard_map/ppermute | solution.py:50
  22.5 0.5 shard_map.103
  23.0 1.3 %collective-permute-start.8 = (bf16[16,2304]{1,0:T(8,128)(2,1)S(1)}, bf16[16,2304]{1,0:T(8,128)(2,1)S(1)}, u32[]{:S(2)}, u32[]{:S(2)}) collective-permute-start(bf16[16,2304]{1,0:T(8,128)(2,1)S(1)} %get-tuple-element.34), channel_id=1, source_target_pairs={{0,3},{1,2},{2,1},{3,0},{4,7},{5,6},{6,5},{7,4},{8,11},{9,10},{10,... | collective-permute-start | bytes 221192 | tf_op jit(solution)/shard_map/ppermute | solution.py:62
  24.3 0.5 collective-permute-start.9
  24.8 1.7 %collective-permute-start.10 = (bf16[16,2304]{1,0:T(8,128)(2,1)S(1)}, bf16[16,2304]{1,0:T(8,128)(2,1)S(1)}, u32[]{:S(2)}, u32[]{:S(2)}) collective-permute-start(bf16[16,2304]{1,0:T(8,128)(2,1)S(1)} %get-tuple-element.36), channel_id=1, source_target_pairs={{0,1},{1,0},{2,3},{3,2},{4,5},{5,4},{6,7},{7,6},{8,9},{9,8},{10,11... | collective-permute-start | bytes 221192 | tf_op jit(solution)/shard_map/ppermute | solution.py:62
  26.5 2.3 %collective-permute-done.8.refs_0_ = bf16[16,2304]{1,0:T(8,128)(2,1)S(1)} collective-permute-done((bf16[16,2304]{1,0:T(8,128)(2,1)S(1)}, bf16[16,2304]{1,0:T(8,128)(2,1)S(1)}, u32[]{:S(2)}, u32[]{:S(2)}) %collective-permute-start.8) | collective-permute-done | bytes 73760 | tf_op jit(solution)/shard_map/ppermute | solution.py:62
  28.9 1.0 %collective-permute-done.10.refs_2_ = bf16[16,2304]{1,0:T(8,128)(2,1)S(1)} collective-permute-done((bf16[16,2304]{1,0:T(8,128)(2,1)S(1)}, bf16[16,2304]{1,0:T(8,128)(2,1)S(1)}, u32[]{:S(2)}, u32[]{:S(2)}) %collective-permute-start.10) | collective-permute-done | bytes 73760 | tf_op jit(solution)/shard_map/ppermute | solution.py:62
  29.9 2.4 %collective-permute-start.11 = (bf16[16,2304]{1,0:T(8,128)(2,1)S(1)}, bf16[16,2304]{1,0:T(8,128)(2,1)S(1)}, u32[]{:S(2)}, u32[]{:S(2)}) collective-permute-start(bf16[16,2304]{1,0:T(8,128)(2,1)S(1)} %get-tuple-element.39), channel_id=1, source_target_pairs={{0,4},{1,5},{2,6},{3,7},{4,0},{5,1},{6,2},{7,3},{8,12},{9,13},{10,... | collective-permute-start | bytes 221192 | tf_op jit(solution)/shard_map/ppermute | solution.py:68
  32.3 4.0 %collective-permute-done.11.other = bf16[16,2304]{1,0:T(8,128)(2,1)S(1)} collective-permute-done((bf16[16,2304]{1,0:T(8,128)(2,1)S(1)}, bf16[16,2304]{1,0:T(8,128)(2,1)S(1)}, u32[]{:S(2)}, u32[]{:S(2)}) %collective-permute-start.11) | collective-permute-done | bytes 73760 | tf_op jit(solution)/shard_map/ppermute | solution.py:68
  36.5 0.7 %collective-permute-start.14 = (bf16[16,2304]{1,0:T(8,128)(2,1)S(1)}, bf16[16,2304]{1,0:T(8,128)(2,1)S(1)}, u32[]{:S(2)}, u32[]{:S(2)}) collective-permute-start(bf16[16,2304]{1,0:T(8,128)(2,1)S(1)} %get-tuple-element.40.rest_0_), channel_id=1, source_target_pairs={{0,3},{1,2},{2,1},{3,0},{4,7},{5,6},{6,5},{7,4},{8,11},{9,10},{10,... | collective-permute-start | bytes 221192 | tf_op jit(solution)/shard_map/ppermute | solution.py:62
  37.3 0.7 %collective-permute-start.13 = (bf16[16,2304]{1,0:T(8,128)(2,1)S(1)}, bf16[16,2304]{1,0:T(8,128)(2,1)S(1)}, u32[]{:S(2)}, u32[]{:S(2)}) collective-permute-start(bf16[16,2304]{1,0:T(8,128)(2,1)S(1)} %get-tuple-element.40.rest_0_), channel_id=1, source_target_pairs={{0,2},{1,3},{2,0},{3,1},{4,6},{5,7},{6,4},{7,5},{8,10},{9,11},{10,... | collective-permute-start | bytes 221192 | tf_op jit(solution)/shard_map/ppermute | solution.py:62
  37.9 2.1 %collective-permute-start.12 = (bf16[16,2304]{1,0:T(8,128)(2,1)S(1)}, bf16[16,2304]{1,0:T(8,128)(2,1)S(1)}, u32[]{:S(2)}, u32[]{:S(2)}) collective-permute-start(bf16[16,2304]{1,0:T(8,128)(2,1)S(1)} %get-tuple-element.40.rest_0_), channel_id=1, source_target_pairs={{0,1},{1,0},{2,3},{3,2},{4,5},{5,4},{6,7},{7,6},{8,9},{9,8},{10,11... | collective-permute-start | bytes 221192 | tf_op jit(solution)/shard_map/ppermute | solution.py:62
  40.0 1.8 %collective-permute-done.14.rest_3_ = bf16[16,2304]{1,0:T(8,128)(2,1)S(1)} collective-permute-done((bf16[16,2304]{1,0:T(8,128)(2,1)S(1)}, bf16[16,2304]{1,0:T(8,128)(2,1)S(1)}, u32[]{:S(2)}, u32[]{:S(2)}) %collective-permute-start.14) | collective-permute-done | bytes 73760 | tf_op jit(solution)/shard_map/ppermute | solution.py:62
  41.8 0.8 %collective-permute-done.12.rest_1_ = bf16[16,2304]{1,0:T(8,128)(2,1)S(1)} collective-permute-done((bf16[16,2304]{1,0:T(8,128)(2,1)S(1)}, bf16[16,2304]{1,0:T(8,128)(2,1)S(1)}, u32[]{:S(2)}, u32[]{:S(2)}) %collective-permute-start.12) | collective-permute-done | bytes 73760 | tf_op jit(solution)/shard_map/ppermute | solution.py:62
  42.6 0.5 shard_map.107.before
  43.2 0.6 shard_map.106.one
  43.8 0.7 %collective-permute-done.15.other = bf16[64,512]{1,0:T(8,128)(2,1)S(1)} collective-permute-done((bf16[64,512]{1,0:T(8,128)(2,1)S(1)}, bf16[64,512]{1,0:T(8,128)(2,1)S(1)}, u32[]{:S(2)}, u32[]{:S(2)}) %collective-permute-start.15) | collective-permute-done | bytes 65568 | tf_op jit(solution)/shard_map/ppermute | solution.py:44
  44.5 1.5 %collective-permute-start.17 = (bf16[64,512]{1,0:T(8,128)(2,1)S(1)}, bf16[64,512]{1,0:T(8,128)(2,1)S(1)}, u32[]{:S(2)}, u32[]{:S(2)}) collective-permute-start(bf16[64,512]{1,0:T(8,128)(2,1)S(1)} %shard_map.108.after.terms), channel_id=1, source_target_pairs={{0,16},{8,24},{16,0},{24,8},{1,17},{9,25},{17,1},{25,9},{2,18},{10... | collective-permute-start | bytes 196616 | tf_op jit(solution)/shard_map/ppermute | solution.py:48
  46.0 1.3 %shard_map.109.refs_0_.weight = bf16[1024,2304]{1,0:T(8,128)(2,1)S(1)} custom-call(bf16[2304,1024]{1,0:T(8,128)(2,1)S(1)} %bitcast.13, bf16[64,512]{1,0:T(8,128)(2,1)S(1)} %shard_map.108.after.terms), custom_call_target="tpu_custom_call" | custom-call | bytes 9568256 | tf_op jit(solution)/shard_map/pallas_call | solution.py:29
  47.3 1.5 %collective-permute-done.17.refs_1_ = bf16[64,512]{1,0:T(8,128)(2,1)S(1)} collective-permute-done((bf16[64,512]{1,0:T(8,128)(2,1)S(1)}, bf16[64,512]{1,0:T(8,128)(2,1)S(1)}, u32[]{:S(2)}, u32[]{:S(2)}) %collective-permute-start.17) | collective-permute-done | bytes 65568 | tf_op jit(solution)/shard_map/ppermute | solution.py:48
  48.8 0.6 shard_map.111
  49.4 0.7 %collective-permute-done.18.others = bf16[64,512]{1,0:T(8,128)(2,1)S(1)} collective-permute-done((bf16[64,512]{1,0:T(8,128)(2,1)S(1)}, bf16[64,512]{1,0:T(8,128)(2,1)S(1)}, u32[]{:S(2)}, u32[]{:S(2)}) %collective-permute-start.18) | collective-permute-done | bytes 65568 | tf_op jit(solution)/shard_map/ppermute | solution.py:50
  50.1 0.5 shard_map.112
  50.6 1.8 %collective-permute-start.19 = (bf16[16,2304]{1,0:T(8,128)(2,1)S(1)}, bf16[16,2304]{1,0:T(8,128)(2,1)S(1)}, u32[]{:S(2)}, u32[]{:S(2)}) collective-permute-start(bf16[16,2304]{1,0:T(8,128)(2,1)S(1)} %get-tuple-element.44), channel_id=1, source_target_pairs={{0,3},{1,2},{2,1},{3,0},{4,7},{5,6},{6,5},{7,4},{8,11},{9,10},{10,... | collective-permute-start | bytes 221192 | tf_op jit(solution)/shard_map/ppermute | solution.py:62
  52.4 1.5 %collective-permute-start.20 = (bf16[16,2304]{1,0:T(8,128)(2,1)S(1)}, bf16[16,2304]{1,0:T(8,128)(2,1)S(1)}, u32[]{:S(2)}, u32[]{:S(2)}) collective-permute-start(bf16[16,2304]{1,0:T(8,128)(2,1)S(1)} %get-tuple-element.45), channel_id=1, source_target_pairs={{0,2},{1,3},{2,0},{3,1},{4,6},{5,7},{6,4},{7,5},{8,10},{9,11},{10,... | collective-permute-start | bytes 221192 | tf_op jit(solution)/shard_map/ppermute | solution.py:62
  53.9 0.2 collective-permute-start.21
  54.2 2.5 %collective-permute-done.19.refs_0_ = bf16[16,2304]{1,0:T(8,128)(2,1)S(1)} collective-permute-done((bf16[16,2304]{1,0:T(8,128)(2,1)S(1)}, bf16[16,2304]{1,0:T(8,128)(2,1)S(1)}, u32[]{:S(2)}, u32[]{:S(2)}) %collective-permute-start.19) | collective-permute-done | bytes 73760 | tf_op jit(solution)/shard_map/ppermute | solution.py:62
  56.7 1.1 %collective-permute-done.20.refs_1_ = bf16[16,2304]{1,0:T(8,128)(2,1)S(1)} collective-permute-done((bf16[16,2304]{1,0:T(8,128)(2,1)S(1)}, bf16[16,2304]{1,0:T(8,128)(2,1)S(1)}, u32[]{:S(2)}, u32[]{:S(2)}) %collective-permute-start.20) | collective-permute-done | bytes 73760 | tf_op jit(solution)/shard_map/ppermute | solution.py:62
  57.8 0.5 collective-permute-done.21.refs_2_
  58.3 1.9 %collective-permute-start.22 = (bf16[8,2304]{1,0:T(8,128)(2,1)S(1)}, bf16[8,2304]{1,0:T(8,128)(2,1)S(1)}, u32[]{:S(2)}, u32[]{:S(2)}) collective-permute-start(bf16[8,2304]{1,0:T(8,128)(2,1)S(1)} %get-tuple-element.49), channel_id=1, source_target_pairs={{0,4},{1,5},{2,6},{3,7},{4,0},{5,1},{6,2},{7,3},{8,12},{9,13},{10,... | collective-permute-start | bytes 110600 | tf_op jit(solution)/shard_map/ppermute | solution.py:68
  60.3 3.0 %collective-permute-done.22.other = bf16[8,2304]{1,0:T(8,128)(2,1)S(1)} collective-permute-done((bf16[8,2304]{1,0:T(8,128)(2,1)S(1)}, bf16[8,2304]{1,0:T(8,128)(2,1)S(1)}, u32[]{:S(2)}, u32[]{:S(2)}) %collective-permute-start.22) | collective-permute-done | bytes 36896 | tf_op jit(solution)/shard_map/ppermute | solution.py:68
  63.3 0.8 %shard_map.114 = (bf16[8,2304]{1,0:T(8,128)(2,1)}, f32[1,8]{1,0:T(1,128)}, f32[64,1024]{1,0:T(8,128)}) custom-call(f32[8,2304]{1,0:T(8,128)S(1)} %get-tuple-element.48.one, bf16[8,2304]{1,0:T(8,128)(2,1)S(1)} %collective-permute-done.22.other, f32[8,2304]{1,0:T(8,128)S(1)} %get-tuple-element.50.error, f32[1,8]{1,0:T(1,128)S(1)} %get-tuple-element.51.squared, ...), custom_call_target="tpu_custom_call" | custom-call | tf_op jit(solution)/shard_map/pallas_call | solution.py:29
  (33 shorter events, 0.5 us)
Async XLA Ops:
  0.6 6.6 %collective-permute-start = (bf16[8,2304]{1,0:T(8,128)(2,1)}, bf16[8,2304]{1,0:T(8,128)(2,1)S(1)}, u32[]{:S(2)}, u32[]{:S(2)}) collective-permute-start(bf16[8,2304]{1,0:T(8,128)(2,1)} %bitcast.21), channel_id=1, source_target_pairs={{0,4},{1,5},{2,6},{3,7},{4,0},{5,1},{6,2},{7,3},{8,12},{9,13},{10,... | collective-permute-start | bytes 110600 | tf_op jit(solution)/shard_map/ppermute | solution.py:68
  7.3 7.7 %slice-start = ((s8[4718592]{0:T(1024)(128)(4,1)}), s8[4194304]{0:T(1024)(128)(4,1)S(1)}, s32[]{:S(2)}) async-start(s8[4718592]{0:T(1024)(128)(4,1)} %bitcast.9), calls=%async_computation | async-start | bytes 8388608
  7.3 7.7 %slice-start.1 = ((s8[4718592]{0:T(1024)(128)(4,1)}), s8[524288]{0:T(1024)(128)(4,1)S(1)}, s32[]{:S(2)}) async-start(s8[4718592]{0:T(1024)(128)(4,1)} %bitcast.9), calls=%async_computation.1 | async-start | bytes 1048576
  7.3 11.1 %slice-start.2 = ((s8[4718592]{0:T(1024)(128)(4,1)}), s8[4194304]{0:T(1024)(128)(4,1)S(1)}, s32[]{:S(2)}) async-start(s8[4718592]{0:T(1024)(128)(4,1)} %bitcast.15), calls=%async_computation.2 | async-start | bytes 8388608
  7.3 11.1 %slice-start.3 = ((s8[4718592]{0:T(1024)(128)(4,1)}), s8[524288]{0:T(1024)(128)(4,1)S(1)}, s32[]{:S(2)}) async-start(s8[4718592]{0:T(1024)(128)(4,1)} %bitcast.15), calls=%async_computation.3 | async-start | bytes 1048576
  7.3 5.3 %collective-permute-start.3 = (bf16[16,2304]{1,0:T(8,128)(2,1)S(1)}, bf16[16,2304]{1,0:T(8,128)(2,1)S(1)}, u32[]{:S(2)}, u32[]{:S(2)}) collective-permute-start(bf16[16,2304]{1,0:T(8,128)(2,1)S(1)} %shard_map.96.rest_0_.acts), channel_id=1, source_target_pairs={{0,3},{1,2},{2,1},{3,0},{4,7},{5,6},{6,5},{7,4},{8,11},{9,10},{10,... | collective-permute-start | bytes 221192 | tf_op jit(solution)/shard_map/ppermute | solution.py:62
  9.9 4.4 %collective-permute-start.2 = (bf16[16,2304]{1,0:T(8,128)(2,1)S(1)}, bf16[16,2304]{1,0:T(8,128)(2,1)S(1)}, u32[]{:S(2)}, u32[]{:S(2)}) collective-permute-start(bf16[16,2304]{1,0:T(8,128)(2,1)S(1)} %shard_map.96.rest_0_.acts), channel_id=1, source_target_pairs={{0,2},{1,3},{2,0},{3,1},{4,6},{5,7},{6,4},{7,5},{8,10},{9,11},{10,... | collective-permute-start | bytes 221192 | tf_op jit(solution)/shard_map/ppermute | solution.py:62
  10.6 4.4 %collective-permute-start.1 = (bf16[16,2304]{1,0:T(8,128)(2,1)S(1)}, bf16[16,2304]{1,0:T(8,128)(2,1)S(1)}, u32[]{:S(2)}, u32[]{:S(2)}) collective-permute-start(bf16[16,2304]{1,0:T(8,128)(2,1)S(1)} %shard_map.96.rest_0_.acts), channel_id=1, source_target_pairs={{0,1},{1,0},{2,3},{3,2},{4,5},{5,4},{6,7},{7,6},{8,9},{9,8},{10,11... | collective-permute-start | bytes 221192 | tf_op jit(solution)/shard_map/ppermute | solution.py:62
  15.5 1.3 %collective-permute-start.4 = (bf16[64,512]{1,0:T(8,128)(2,1)S(1)}, bf16[64,512]{1,0:T(8,128)(2,1)S(1)}, u32[]{:S(2)}, u32[]{:S(2)}) collective-permute-start(bf16[64,512]{1,0:T(8,128)(2,1)S(1)} %shard_map.98), channel_id=1, source_target_pairs={{0,8},{8,0},{16,24},{24,16},{1,9},{9,1},{17,25},{25,17},{2,10},{10... | collective-permute-start | bytes 196616 | tf_op jit(solution)/shard_map/ppermute | solution.py:44
  16.9 4.3 %collective-permute-start.6 = (bf16[64,512]{1,0:T(8,128)(2,1)S(1)}, bf16[64,512]{1,0:T(8,128)(2,1)S(1)}, u32[]{:S(2)}, u32[]{:S(2)}) collective-permute-start(bf16[64,512]{1,0:T(8,128)(2,1)S(1)} %shard_map.99.after.terms), channel_id=1, source_target_pairs={{0,16},{8,24},{16,0},{24,8},{1,17},{9,25},{17,1},{25,9},{2,18},{10... | collective-permute-start | bytes 196616 | tf_op jit(solution)/shard_map/ppermute | solution.py:48
  18.4 3.3 %collective-permute-start.5 = (bf16[64,512]{1,0:T(8,128)(2,1)S(1)}, bf16[64,512]{1,0:T(8,128)(2,1)S(1)}, u32[]{:S(2)}, u32[]{:S(2)}) collective-permute-start(bf16[64,512]{1,0:T(8,128)(2,1)S(1)} %shard_map.99.after.terms), channel_id=1, source_target_pairs={{0,8},{8,0},{16,24},{24,16},{1,9},{9,1},{17,25},{25,17},{2,10},{10... | collective-permute-start | bytes 196616 | tf_op jit(solution)/shard_map/ppermute | solution.py:50
  21.2 1.3 %collective-permute-start.7 = (bf16[64,512]{1,0:T(8,128)(2,1)S(1)}, bf16[64,512]{1,0:T(8,128)(2,1)S(1)}, u32[]{:S(2)}, u32[]{:S(2)}) collective-permute-start(bf16[64,512]{1,0:T(8,128)(2,1)S(1)} %shard_map.101.others), channel_id=1, source_target_pairs={{0,8},{8,0},{16,24},{24,16},{1,9},{9,1},{17,25},{25,17},{2,10},{10... | collective-permute-start | bytes 196616 | tf_op jit(solution)/shard_map/ppermute | solution.py:50
  21.7 14.6 %copy-start = (f32[1,2304]{1,0:T(1,128)S(1)}, f32[1,2304]{1,0:T(1,128)}, u32[]{:S(2)}) copy-start(f32[1,2304]{1,0:T(1,128)} %dec_bias.1) | copy-start | bytes 27652
  21.7 14.6 %copy-start.1 = (s32[64]{0:T(128)S(1)}, s32[64]{0:T(128)}, u32[]{:S(2)}) copy-start(s32[64]{0:T(128)} %param.13) | copy-start | bytes 772
  23.0 5.9 %collective-permute-start.8 = (bf16[16,2304]{1,0:T(8,128)(2,1)S(1)}, bf16[16,2304]{1,0:T(8,128)(2,1)S(1)}, u32[]{:S(2)}, u32[]{:S(2)}) collective-permute-start(bf16[16,2304]{1,0:T(8,128)(2,1)S(1)} %get-tuple-element.34), channel_id=1, source_target_pairs={{0,3},{1,2},{2,1},{3,0},{4,7},{5,6},{6,5},{7,4},{8,11},{9,10},{10,... | collective-permute-start | bytes 221192 | tf_op jit(solution)/shard_map/ppermute | solution.py:62
  24.3 4.6 %collective-permute-start.9 = (bf16[16,2304]{1,0:T(8,128)(2,1)S(1)}, bf16[16,2304]{1,0:T(8,128)(2,1)S(1)}, u32[]{:S(2)}, u32[]{:S(2)}) collective-permute-start(bf16[16,2304]{1,0:T(8,128)(2,1)S(1)} %get-tuple-element.35), channel_id=1, source_target_pairs={{0,2},{1,3},{2,0},{3,1},{4,6},{5,7},{6,4},{7,5},{8,10},{9,11},{10,... | collective-permute-start | bytes 221192 | tf_op jit(solution)/shard_map/ppermute | solution.py:62
  24.8 5.0 %collective-permute-start.10 = (bf16[16,2304]{1,0:T(8,128)(2,1)S(1)}, bf16[16,2304]{1,0:T(8,128)(2,1)S(1)}, u32[]{:S(2)}, u32[]{:S(2)}) collective-permute-start(bf16[16,2304]{1,0:T(8,128)(2,1)S(1)} %get-tuple-element.36), channel_id=1, source_target_pairs={{0,1},{1,0},{2,3},{3,2},{4,5},{5,4},{6,7},{7,6},{8,9},{9,8},{10,11... | collective-permute-start | bytes 221192 | tf_op jit(solution)/shard_map/ppermute | solution.py:62
  29.9 6.4 %collective-permute-start.11 = (bf16[16,2304]{1,0:T(8,128)(2,1)S(1)}, bf16[16,2304]{1,0:T(8,128)(2,1)S(1)}, u32[]{:S(2)}, u32[]{:S(2)}) collective-permute-start(bf16[16,2304]{1,0:T(8,128)(2,1)S(1)} %get-tuple-element.39), channel_id=1, source_target_pairs={{0,4},{1,5},{2,6},{3,7},{4,0},{5,1},{6,2},{7,3},{8,12},{9,13},{10,... | collective-permute-start | bytes 221192 | tf_op jit(solution)/shard_map/ppermute | solution.py:68
  36.5 5.3 %collective-permute-start.14 = (bf16[16,2304]{1,0:T(8,128)(2,1)S(1)}, bf16[16,2304]{1,0:T(8,128)(2,1)S(1)}, u32[]{:S(2)}, u32[]{:S(2)}) collective-permute-start(bf16[16,2304]{1,0:T(8,128)(2,1)S(1)} %get-tuple-element.40.rest_0_), channel_id=1, source_target_pairs={{0,3},{1,2},{2,1},{3,0},{4,7},{5,6},{6,5},{7,4},{8,11},{9,10},{10,... | collective-permute-start | bytes 221192 | tf_op jit(solution)/shard_map/ppermute | solution.py:62
  37.3 4.6 %collective-permute-start.13 = (bf16[16,2304]{1,0:T(8,128)(2,1)S(1)}, bf16[16,2304]{1,0:T(8,128)(2,1)S(1)}, u32[]{:S(2)}, u32[]{:S(2)}) collective-permute-start(bf16[16,2304]{1,0:T(8,128)(2,1)S(1)} %get-tuple-element.40.rest_0_), channel_id=1, source_target_pairs={{0,2},{1,3},{2,0},{3,1},{4,6},{5,7},{6,4},{7,5},{8,10},{9,11},{10,... | collective-permute-start | bytes 221192 | tf_op jit(solution)/shard_map/ppermute | solution.py:62
  37.9 4.6 %collective-permute-start.12 = (bf16[16,2304]{1,0:T(8,128)(2,1)S(1)}, bf16[16,2304]{1,0:T(8,128)(2,1)S(1)}, u32[]{:S(2)}, u32[]{:S(2)}) collective-permute-start(bf16[16,2304]{1,0:T(8,128)(2,1)S(1)} %get-tuple-element.40.rest_0_), channel_id=1, source_target_pairs={{0,1},{1,0},{2,3},{3,2},{4,5},{5,4},{6,7},{7,6},{8,9},{9,8},{10,11... | collective-permute-start | bytes 221192 | tf_op jit(solution)/shard_map/ppermute | solution.py:62
  43.1 1.3 %collective-permute-start.15 = (bf16[64,512]{1,0:T(8,128)(2,1)S(1)}, bf16[64,512]{1,0:T(8,128)(2,1)S(1)}, u32[]{:S(2)}, u32[]{:S(2)}) collective-permute-start(bf16[64,512]{1,0:T(8,128)(2,1)S(1)} %shard_map.107.before), channel_id=1, source_target_pairs={{0,8},{8,0},{16,24},{24,16},{1,9},{9,1},{17,25},{25,17},{2,10},{10... | collective-permute-start | bytes 196616 | tf_op jit(solution)/shard_map/ppermute | solution.py:44
  44.5 4.3 %collective-permute-start.17 = (bf16[64,512]{1,0:T(8,128)(2,1)S(1)}, bf16[64,512]{1,0:T(8,128)(2,1)S(1)}, u32[]{:S(2)}, u32[]{:S(2)}) collective-permute-start(bf16[64,512]{1,0:T(8,128)(2,1)S(1)} %shard_map.108.after.terms), channel_id=1, source_target_pairs={{0,16},{8,24},{16,0},{24,8},{1,17},{9,25},{17,1},{25,9},{2,18},{10... | collective-permute-start | bytes 196616 | tf_op jit(solution)/shard_map/ppermute | solution.py:48
  46.0 3.4 %collective-permute-start.16 = (bf16[64,512]{1,0:T(8,128)(2,1)S(1)}, bf16[64,512]{1,0:T(8,128)(2,1)S(1)}, u32[]{:S(2)}, u32[]{:S(2)}) collective-permute-start(bf16[64,512]{1,0:T(8,128)(2,1)S(1)} %shard_map.108.after.terms), channel_id=1, source_target_pairs={{0,8},{8,0},{16,24},{24,16},{1,9},{9,1},{17,25},{25,17},{2,10},{10... | collective-permute-start | bytes 196616 | tf_op jit(solution)/shard_map/ppermute | solution.py:50
  48.8 1.3 %collective-permute-start.18 = (bf16[64,512]{1,0:T(8,128)(2,1)S(1)}, bf16[64,512]{1,0:T(8,128)(2,1)S(1)}, u32[]{:S(2)}, u32[]{:S(2)}) collective-permute-start(bf16[64,512]{1,0:T(8,128)(2,1)S(1)} %shard_map.110.others), channel_id=1, source_target_pairs={{0,8},{8,0},{16,24},{24,16},{1,9},{9,1},{17,25},{25,17},{2,10},{10... | collective-permute-start | bytes 196616 | tf_op jit(solution)/shard_map/ppermute | solution.py:50
  50.6 6.1 %collective-permute-start.19 = (bf16[16,2304]{1,0:T(8,128)(2,1)S(1)}, bf16[16,2304]{1,0:T(8,128)(2,1)S(1)}, u32[]{:S(2)}, u32[]{:S(2)}) collective-permute-start(bf16[16,2304]{1,0:T(8,128)(2,1)S(1)} %get-tuple-element.44), channel_id=1, source_target_pairs={{0,3},{1,2},{2,1},{3,0},{4,7},{5,6},{6,5},{7,4},{8,11},{9,10},{10,... | collective-permute-start | bytes 221192 | tf_op jit(solution)/shard_map/ppermute | solution.py:62
  52.4 5.4 %collective-permute-start.20 = (bf16[16,2304]{1,0:T(8,128)(2,1)S(1)}, bf16[16,2304]{1,0:T(8,128)(2,1)S(1)}, u32[]{:S(2)}, u32[]{:S(2)}) collective-permute-start(bf16[16,2304]{1,0:T(8,128)(2,1)S(1)} %get-tuple-element.45), channel_id=1, source_target_pairs={{0,2},{1,3},{2,0},{3,1},{4,6},{5,7},{6,4},{7,5},{8,10},{9,11},{10,... | collective-permute-start | bytes 221192 | tf_op jit(solution)/shard_map/ppermute | solution.py:62
  53.9 4.4 %collective-permute-start.21 = (bf16[16,2304]{1,0:T(8,128)(2,1)S(1)}, bf16[16,2304]{1,0:T(8,128)(2,1)S(1)}, u32[]{:S(2)}, u32[]{:S(2)}) collective-permute-start(bf16[16,2304]{1,0:T(8,128)(2,1)S(1)} %get-tuple-element.46), channel_id=1, source_target_pairs={{0,1},{1,0},{2,3},{3,2},{4,5},{5,4},{6,7},{7,6},{8,9},{9,8},{10,11... | collective-permute-start | bytes 221192 | tf_op jit(solution)/shard_map/ppermute | solution.py:62
  58.3 4.9 %collective-permute-start.22 = (bf16[8,2304]{1,0:T(8,128)(2,1)S(1)}, bf16[8,2304]{1,0:T(8,128)(2,1)S(1)}, u32[]{:S(2)}, u32[]{:S(2)}) collective-permute-start(bf16[8,2304]{1,0:T(8,128)(2,1)S(1)} %get-tuple-element.49), channel_id=1, source_target_pairs={{0,4},{1,5},{2,6},{3,7},{4,0},{5,1},{6,2},{7,3},{8,12},{9,13},{10,... | collective-permute-start | bytes 110600 | tf_op jit(solution)/shard_map/ppermute | solution.py:68

commit v10 on v9

--- a/solution.py
+++ b/solution.py
@@ -76,6 +76,10 @@
     return lax.rem(lax.axis_index("feat"), lax.axis_size("feat") // 2)
 
 
+def last(came):
+    return [*came[:2:-1], *came[1:3], came[0]]
+
+
 def stack(refs):
     return jnp.concatenate([ref[...] for ref in refs])
 
@@ -186,16 +190,18 @@
     squared[...] = jnp.sum(jnp.where(same, means, 0.0), axis=0, keepdims=True)
 
 
-def finish(one, other, error, squared, grad, grad_other, out, squared_out, grad_out, held, done):
+def leave(grad, grad_other, squared, grad_out, squared_out, done):
     mine, theirs = [grad_out.at[:, features(which, grad.shape[1])] for which in (False, True)]
-    moves = [(grad, mine), (grad_other, theirs), (squared, squared_out), (held, out)]
+    moves = [(grad, mine), (grad_other, theirs), (squared, squared_out)]
     moves = [pltpu.make_async_copy(here, there, done.at[i]) for i, (here, there) in enumerate(moves)]
-    for move in moves[:-1]:
+    for move in moves:
         move.start()
-    held[...] = (one[...] + other[...].astype(wide) - error[...]).astype(half)
-    moves[-1].start()
     for move in moves:
         move.wait()
+
+
+def finish(one, other, error, out):
+    out[...] = (one[...] + other[...].astype(wide) - error[...]).astype(half)
 
 
 def shards(activations, enc_weight, dec_weight, enc_bias, threshold, dec_bias, token_mask):
@@ -246,19 +252,18 @@
     grad_other, *grads = call(
         functools.partial(decode_grad, True), [by_feature, *by_group], *theirs, slope_other, enc_turned, part
     )
-    one, other = call(add_last, [near(own, wide), near(own, half)], *reversed(trade(grads)))
-    input_grad, squared, latent_grad = call(
-        finish,
-        [free(own, half), free((1, tok_dev), wide), free((tokens, width), wide)],
-        one,
-        mirror(other),
-        error,
-        squared,
+    one, other = call(add_last, [near(own, wide), near(own, half)], *last(trade(grads)))
+    latent_grad, squared = call(
+        leave,
+        [free((tokens, width), wide), free((1, tok_dev), wide)],
         grad,
         grad_other,
-        scratch=[pltpu.VMEM(own, half), pltpu.SemaphoreType.DMA((4,))],
-        sent=3,
-    )
+        squared,
+        scratch=[pltpu.SemaphoreType.DMA((3,))],
+        sent=2,
+        work=True,
+    )
+    [input_grad] = call(finish, [free(own, half)], one, mirror(other), error)
     return (squared.T, latent_grad, input_grad[:, None])
 
 

time: 64.2 us -> 63.7 us (level)
  waiting for transfers between devices: 28.3 us -> 26.1 us
  starting transfers between devices: 25.8 us -> 26.9 us
    ppermute x3, waiting for transfers between devices: 8.71 us -> 6.94 us  [mirror(): lax.ppermute(block, 'feat', [(i, (i + n // 2) % n) for i in range(n)])]
    ppermute x3, starting transfers between devices: 8.45 us -> 9.53 us  [mirror(): lax.ppermute(block, 'feat', [(i, (i + n // 2) % n) for i in range(n)])]
    pallas_call x21 -> x22, Pallas kernels: 8.99 us -> 9.59 us  [call(): pl.pallas_call(body, out_shape=outs, in_specs=[away] * fetched + [here] *...]
  transfers between devices with their start and end apart: 23 -> 23, of which waited for: 19 -> 19; matrix products, arithmetic and copies ran while one was open for 0% -> 0% of each run, Pallas kernels for 9% -> 10%
where the time goes in v10:
time: 63.7 us; the launch traced here: 63.5 us
  starting transfers between devices  26.9 us (42%)
  waiting for transfers between devices  26.1 us (41%)
  Pallas kernels  9.59 us (15%)
  between operations  0.82 us (1%)
    ppermute x12, starting transfers between devices, trade(): came[k] = lax.ppermute(pieces[k], 'feat', [(i, i ^ k) for i in range(n)])  14.1 us
    ppermute x12, waiting for transfers between devices, trade(): came[k] = lax.ppermute(pieces[k], 'feat', [(i, i ^ k) for i in range(n)])  13.6 us
    pallas_call x22, Pallas kernels, call(): pl.pallas_call(body, out_shape=outs, in_specs=[away] * fetched + [here] *...  9.59 us
    ppermute x3, starting transfers between devices, mirror(): lax.ppermute(block, 'feat', [(i, (i + n // 2) % n) for i in range(n)])  9.53 us
    ppermute x3, waiting for transfers between devices, mirror(): lax.ppermute(block, 'feat', [(i, (i + n // 2) % n) for i in range(n)])  6.94 us
    ppermute x2, starting transfers between devices, layer_sum(): far = lax.ppermute(pair, 'layer', far_off)  3.1 us
    ppermute x2, waiting for transfers between devices, layer_sum(): far = lax.ppermute(pair, 'layer', far_off)  2.84 us
    ppermute x4, waiting for transfers between devices, layer_sum(): other = [lax.ppermute(x, 'layer', near_by) for x in (pair, far)]  1.38 us
  transfers between devices with their start and end apart: 23, of which 19 were waited for; matrix products, arithmetic and copies ran while one was open for 0% of the time, Pallas kernels for 10%

profile of v10, /device:TPU:0, one launch (start us, length us, event | category | flops | bytes accessed | tf_op | source)
XLA Modules:
  0.0 63.5 jit_solution(2263909230984248373)
XLA Ops:
  0.6 4.1 %collective-permute-start = (bf16[8,2304]{1,0:T(8,128)(2,1)}, bf16[8,2304]{1,0:T(8,128)(2,1)S(1)}, u32[]{:S(2)}, u32[]{:S(2)}) collective-permute-start(bf16[8,2304]{1,0:T(8,128)(2,1)} %bitcast.22), channel_id=1, source_target_pairs={{0,4},{1,5},{2,6},{3,7},{4,0},{5,1},{6,2},{7,3},{8,12},{9,13},{10,... | collective-permute-start | bytes 110600 | tf_op jit(solution)/shard_map/ppermute | solution.py:68
  4.7 0.8 %shard_map.94 = (bf16[8,2304]{1,0:T(8,128)(2,1)S(1)}, f32[1,1024]{1,0:T(1,128)S(1)}, f32[1,1024]{1,0:T(1,128)S(1)}) custom-call(bf16[8,2304]{1,0:T(8,128)(2,1)} %bitcast.23, f32[1,1024]{1,0:T(1,128)} %bitcast.24, f32[1,1024]{1,0:T(1,128)} %bitcast.25), custom_call_target="tpu_custom_call" | custom-call | bytes 90112 | tf_op jit(solution)/shard_map/pallas_call | solution.py:29
  5.6 1.7 %collective-permute-done.other = bf16[8,2304]{1,0:T(8,128)(2,1)S(1)} collective-permute-done((bf16[8,2304]{1,0:T(8,128)(2,1)}, bf16[8,2304]{1,0:T(8,128)(2,1)S(1)}, u32[]{:S(2)}, u32[]{:S(2)}) %collective-permute-start) | collective-permute-done | bytes 36896 | tf_op jit(solution)/shard_map/ppermute | solution.py:68
  7.3 2.5 %collective-permute-start.3 = (bf16[16,2304]{1,0:T(8,128)(2,1)S(1)}, bf16[16,2304]{1,0:T(8,128)(2,1)S(1)}, u32[]{:S(2)}, u32[]{:S(2)}) collective-permute-start(bf16[16,2304]{1,0:T(8,128)(2,1)S(1)} %shard_map.96.rest_0_.acts), channel_id=1, source_target_pairs={{0,3},{1,2},{2,1},{3,0},{4,7},{5,6},{6,5},{7,4},{8,11},{9,10},{10,... | collective-permute-start | bytes 221192 | tf_op jit(solution)/shard_map/ppermute | solution.py:62
  9.9 0.7 %collective-permute-start.2 = (bf16[16,2304]{1,0:T(8,128)(2,1)S(1)}, bf16[16,2304]{1,0:T(8,128)(2,1)S(1)}, u32[]{:S(2)}, u32[]{:S(2)}) collective-permute-start(bf16[16,2304]{1,0:T(8,128)(2,1)S(1)} %shard_map.96.rest_0_.acts), channel_id=1, source_target_pairs={{0,2},{1,3},{2,0},{3,1},{4,6},{5,7},{6,4},{7,5},{8,10},{9,11},{10,... | collective-permute-start | bytes 221192 | tf_op jit(solution)/shard_map/ppermute | solution.py:62
  10.9 1.8 %collective-permute-done.3.rest_3_ = bf16[16,2304]{1,0:T(8,128)(2,1)S(1)} collective-permute-done((bf16[16,2304]{1,0:T(8,128)(2,1)S(1)}, bf16[16,2304]{1,0:T(8,128)(2,1)S(1)}, u32[]{:S(2)}, u32[]{:S(2)}) %collective-permute-start.3) | collective-permute-done | bytes 73760 | tf_op jit(solution)/shard_map/ppermute | solution.py:62
  12.7 1.6 %collective-permute-done.2.rest_2_ = bf16[16,2304]{1,0:T(8,128)(2,1)S(1)} collective-permute-done((bf16[16,2304]{1,0:T(8,128)(2,1)S(1)}, bf16[16,2304]{1,0:T(8,128)(2,1)S(1)}, u32[]{:S(2)}, u32[]{:S(2)}) %collective-permute-start.2) | collective-permute-done | bytes 73760 | tf_op jit(solution)/shard_map/ppermute | solution.py:62
  14.2 0.7 %collective-permute-done.1.rest_1_ = bf16[16,2304]{1,0:T(8,128)(2,1)S(1)} collective-permute-done((bf16[16,2304]{1,0:T(8,128)(2,1)S(1)}, bf16[16,2304]{1,0:T(8,128)(2,1)S(1)}, u32[]{:S(2)}, u32[]{:S(2)}) %collective-permute-start.1) | collective-permute-done | bytes 73760 | tf_op jit(solution)/shard_map/ppermute | solution.py:62
  15.0 0.5 shard_map.98
  15.6 0.6 shard_map.97.one
  16.2 0.7 %collective-permute-done.4.other = bf16[64,512]{1,0:T(8,128)(2,1)S(1)} collective-permute-done((bf16[64,512]{1,0:T(8,128)(2,1)S(1)}, bf16[64,512]{1,0:T(8,128)(2,1)S(1)}, u32[]{:S(2)}, u32[]{:S(2)}) %collective-permute-start.4) | collective-permute-done | bytes 65568 | tf_op jit(solution)/shard_map/ppermute | solution.py:44
  16.9 1.6 %collective-permute-start.6 = (bf16[64,512]{1,0:T(8,128)(2,1)S(1)}, bf16[64,512]{1,0:T(8,128)(2,1)S(1)}, u32[]{:S(2)}, u32[]{:S(2)}) collective-permute-start(bf16[64,512]{1,0:T(8,128)(2,1)S(1)} %shard_map.99.after.terms), channel_id=1, source_target_pairs={{0,16},{8,24},{16,0},{24,8},{1,17},{9,25},{17,1},{25,9},{2,18},{10... | collective-permute-start | bytes 196616 | tf_op jit(solution)/shard_map/ppermute | solution.py:48
  18.4 1.4 %shard_map.100.refs_0_.before.weight = bf16[2304,1024]{1,0:T(8,128)(2,1)S(1)} custom-call(bf16[1024,2304]{1,0:T(8,128)(2,1)S(1)} %bitcast.17, bf16[64,512]{1,0:T(8,128)(2,1)S(1)} %shard_map.99.after.terms), custom_call_target="tpu_custom_call" | custom-call | bytes 9568256 | tf_op jit(solution)/shard_map/pallas_call | solution.py:29
  19.9 1.3 %collective-permute-done.6.refs_1_ = bf16[64,512]{1,0:T(8,128)(2,1)S(1)} collective-permute-done((bf16[64,512]{1,0:T(8,128)(2,1)S(1)}, bf16[64,512]{1,0:T(8,128)(2,1)S(1)}, u32[]{:S(2)}, u32[]{:S(2)}) %collective-permute-start.6) | collective-permute-done | bytes 65568 | tf_op jit(solution)/shard_map/ppermute | solution.py:48
  21.2 0.5 shard_map.102
  21.8 0.7 %collective-permute-done.7.others = bf16[64,512]{1,0:T(8,128)(2,1)S(1)} collective-permute-done((bf16[64,512]{1,0:T(8,128)(2,1)S(1)}, bf16[64,512]{1,0:T(8,128)(2,1)S(1)}, u32[]{:S(2)}, u32[]{:S(2)}) %collective-permute-start.7) | collective-permute-done | bytes 65568 | tf_op jit(solution)/shard_map/ppermute | solution.py:50
  22.5 0.5 shard_map.103
  23.0 1.3 %collective-permute-start.8 = (bf16[16,2304]{1,0:T(8,128)(2,1)S(1)}, bf16[16,2304]{1,0:T(8,128)(2,1)S(1)}, u32[]{:S(2)}, u32[]{:S(2)}) collective-permute-start(bf16[16,2304]{1,0:T(8,128)(2,1)S(1)} %get-tuple-element.33), channel_id=1, source_target_pairs={{0,3},{1,2},{2,1},{3,0},{4,7},{5,6},{6,5},{7,4},{8,11},{9,10},{10,... | collective-permute-start | bytes 221192 | tf_op jit(solution)/shard_map/ppermute | solution.py:62
  24.3 0.5 collective-permute-start.9
  24.8 1.7 %collective-permute-start.10 = (bf16[16,2304]{1,0:T(8,128)(2,1)S(1)}, bf16[16,2304]{1,0:T(8,128)(2,1)S(1)}, u32[]{:S(2)}, u32[]{:S(2)}) collective-permute-start(bf16[16,2304]{1,0:T(8,128)(2,1)S(1)} %get-tuple-element.35), channel_id=1, source_target_pairs={{0,1},{1,0},{2,3},{3,2},{4,5},{5,4},{6,7},{7,6},{8,9},{9,8},{10,11... | collective-permute-start | bytes 221192 | tf_op jit(solution)/shard_map/ppermute | solution.py:62
  26.5 2.3 %collective-permute-done.8.refs_0_ = bf16[16,2304]{1,0:T(8,128)(2,1)S(1)} collective-permute-done((bf16[16,2304]{1,0:T(8,128)(2,1)S(1)}, bf16[16,2304]{1,0:T(8,128)(2,1)S(1)}, u32[]{:S(2)}, u32[]{:S(2)}) %collective-permute-start.8) | collective-permute-done | bytes 73760 | tf_op jit(solution)/shard_map/ppermute | solution.py:62
  28.9 1.0 %collective-permute-done.10.refs_2_ = bf16[16,2304]{1,0:T(8,128)(2,1)S(1)} collective-permute-done((bf16[16,2304]{1,0:T(8,128)(2,1)S(1)}, bf16[16,2304]{1,0:T(8,128)(2,1)S(1)}, u32[]{:S(2)}, u32[]{:S(2)}) %collective-permute-start.10) | collective-permute-done | bytes 73760 | tf_op jit(solution)/shard_map/ppermute | solution.py:62
  29.9 2.4 %collective-permute-start.11 = (bf16[16,2304]{1,0:T(8,128)(2,1)S(1)}, bf16[16,2304]{1,0:T(8,128)(2,1)S(1)}, u32[]{:S(2)}, u32[]{:S(2)}) collective-permute-start(bf16[16,2304]{1,0:T(8,128)(2,1)S(1)} %get-tuple-element.38), channel_id=1, source_target_pairs={{0,4},{1,5},{2,6},{3,7},{4,0},{5,1},{6,2},{7,3},{8,12},{9,13},{10,... | collective-permute-start | bytes 221192 | tf_op jit(solution)/shard_map/ppermute | solution.py:68
  32.3 4.0 %collective-permute-done.11.other = bf16[16,2304]{1,0:T(8,128)(2,1)S(1)} collective-permute-done((bf16[16,2304]{1,0:T(8,128)(2,1)S(1)}, bf16[16,2304]{1,0:T(8,128)(2,1)S(1)}, u32[]{:S(2)}, u32[]{:S(2)}) %collective-permute-start.11) | collective-permute-done | bytes 73760 | tf_op jit(solution)/shard_map/ppermute | solution.py:68
  36.5 0.7 %collective-permute-start.14 = (bf16[16,2304]{1,0:T(8,128)(2,1)S(1)}, bf16[16,2304]{1,0:T(8,128)(2,1)S(1)}, u32[]{:S(2)}, u32[]{:S(2)}) collective-permute-start(bf16[16,2304]{1,0:T(8,128)(2,1)S(1)} %get-tuple-element.39.rest_0_), channel_id=1, source_target_pairs={{0,3},{1,2},{2,1},{3,0},{4,7},{5,6},{6,5},{7,4},{8,11},{9,10},{10,... | collective-permute-start | bytes 221192 | tf_op jit(solution)/shard_map/ppermute | solution.py:62
  37.3 0.7 %collective-permute-start.13 = (bf16[16,2304]{1,0:T(8,128)(2,1)S(1)}, bf16[16,2304]{1,0:T(8,128)(2,1)S(1)}, u32[]{:S(2)}, u32[]{:S(2)}) collective-permute-start(bf16[16,2304]{1,0:T(8,128)(2,1)S(1)} %get-tuple-element.39.rest_0_), channel_id=1, source_target_pairs={{0,2},{1,3},{2,0},{3,1},{4,6},{5,7},{6,4},{7,5},{8,10},{9,11},{10,... | collective-permute-start | bytes 221192 | tf_op jit(solution)/shard_map/ppermute | solution.py:62
  37.9 2.1 %collective-permute-start.12 = (bf16[16,2304]{1,0:T(8,128)(2,1)S(1)}, bf16[16,2304]{1,0:T(8,128)(2,1)S(1)}, u32[]{:S(2)}, u32[]{:S(2)}) collective-permute-start(bf16[16,2304]{1,0:T(8,128)(2,1)S(1)} %get-tuple-element.39.rest_0_), channel_id=1, source_target_pairs={{0,1},{1,0},{2,3},{3,2},{4,5},{5,4},{6,7},{7,6},{8,9},{9,8},{10,11... | collective-permute-start | bytes 221192 | tf_op jit(solution)/shard_map/ppermute | solution.py:62
  40.0 1.8 %collective-permute-done.14.rest_3_ = bf16[16,2304]{1,0:T(8,128)(2,1)S(1)} collective-permute-done((bf16[16,2304]{1,0:T(8,128)(2,1)S(1)}, bf16[16,2304]{1,0:T(8,128)(2,1)S(1)}, u32[]{:S(2)}, u32[]{:S(2)}) %collective-permute-start.14) | collective-permute-done | bytes 73760 | tf_op jit(solution)/shard_map/ppermute | solution.py:62
  41.8 0.8 %collective-permute-done.12.rest_1_ = bf16[16,2304]{1,0:T(8,128)(2,1)S(1)} collective-permute-done((bf16[16,2304]{1,0:T(8,128)(2,1)S(1)}, bf16[16,2304]{1,0:T(8,128)(2,1)S(1)}, u32[]{:S(2)}, u32[]{:S(2)}) %collective-permute-start.12) | collective-permute-done | bytes 73760 | tf_op jit(solution)/shard_map/ppermute | solution.py:62
  42.6 0.5 shard_map.107.before
  43.2 0.6 shard_map.106.one
  43.8 0.7 %collective-permute-done.15.other = bf16[64,512]{1,0:T(8,128)(2,1)S(1)} collective-permute-done((bf16[64,512]{1,0:T(8,128)(2,1)S(1)}, bf16[64,512]{1,0:T(8,128)(2,1)S(1)}, u32[]{:S(2)}, u32[]{:S(2)}) %collective-permute-start.15) | collective-permute-done | bytes 65568 | tf_op jit(solution)/shard_map/ppermute | solution.py:44
  44.5 1.5 %collective-permute-start.16 = (bf16[64,512]{1,0:T(8,128)(2,1)S(1)}, bf16[64,512]{1,0:T(8,128)(2,1)S(1)}, u32[]{:S(2)}, u32[]{:S(2)}) collective-permute-start(bf16[64,512]{1,0:T(8,128)(2,1)S(1)} %shard_map.108.after.terms), channel_id=1, source_target_pairs={{0,16},{8,24},{16,0},{24,8},{1,17},{9,25},{17,1},{25,9},{2,18},{10... | collective-permute-start | bytes 196616 | tf_op jit(solution)/shard_map/ppermute | solution.py:48
  46.0 1.3 %shard_map.109.refs_0_.weight = bf16[1024,2304]{1,0:T(8,128)(2,1)S(1)} custom-call(bf16[2304,1024]{1,0:T(8,128)(2,1)S(1)} %bitcast.13, bf16[64,512]{1,0:T(8,128)(2,1)S(1)} %shard_map.108.after.terms), custom_call_target="tpu_custom_call" | custom-call | bytes 9568256 | tf_op jit(solution)/shard_map/pallas_call | solution.py:29
  47.3 1.5 %collective-permute-done.16.refs_1_ = bf16[64,512]{1,0:T(8,128)(2,1)S(1)} collective-permute-done((bf16[64,512]{1,0:T(8,128)(2,1)S(1)}, bf16[64,512]{1,0:T(8,128)(2,1)S(1)}, u32[]{:S(2)}, u32[]{:S(2)}) %collective-permute-start.16) | collective-permute-done | bytes 65568 | tf_op jit(solution)/shard_map/ppermute | solution.py:48
  48.8 0.6 shard_map.111
  49.4 0.7 %collective-permute-done.18.others = bf16[64,512]{1,0:T(8,128)(2,1)S(1)} collective-permute-done((bf16[64,512]{1,0:T(8,128)(2,1)S(1)}, bf16[64,512]{1,0:T(8,128)(2,1)S(1)}, u32[]{:S(2)}, u32[]{:S(2)}) %collective-permute-start.18) | collective-permute-done | bytes 65568 | tf_op jit(solution)/shard_map/ppermute | solution.py:50
  50.1 0.5 shard_map.112
  50.6 1.8 %collective-permute-start.19 = (bf16[16,2304]{1,0:T(8,128)(2,1)S(1)}, bf16[16,2304]{1,0:T(8,128)(2,1)S(1)}, u32[]{:S(2)}, u32[]{:S(2)}) collective-permute-start(bf16[16,2304]{1,0:T(8,128)(2,1)S(1)} %get-tuple-element.48), channel_id=1, source_target_pairs={{0,3},{1,2},{2,1},{3,0},{4,7},{5,6},{6,5},{7,4},{8,11},{9,10},{10,... | collective-permute-start | bytes 221192 | tf_op jit(solution)/shard_map/ppermute | solution.py:62
  52.4 0.8 %collective-permute-start.20 = (bf16[16,2304]{1,0:T(8,128)(2,1)S(1)}, bf16[16,2304]{1,0:T(8,128)(2,1)S(1)}, u32[]{:S(2)}, u32[]{:S(2)}) collective-permute-start(bf16[16,2304]{1,0:T(8,128)(2,1)S(1)} %get-tuple-element.49), channel_id=1, source_target_pairs={{0,1},{1,0},{2,3},{3,2},{4,5},{5,4},{6,7},{7,6},{8,9},{9,8},{10,11... | collective-permute-start | bytes 221192 | tf_op jit(solution)/shard_map/ppermute | solution.py:62
  53.2 1.0 %collective-permute-start.21 = (bf16[16,2304]{1,0:T(8,128)(2,1)S(1)}, bf16[16,2304]{1,0:T(8,128)(2,1)S(1)}, u32[]{:S(2)}, u32[]{:S(2)}) collective-permute-start(bf16[16,2304]{1,0:T(8,128)(2,1)S(1)} %get-tuple-element.50), channel_id=1, source_target_pairs={{0,2},{1,3},{2,0},{3,1},{4,6},{5,7},{6,4},{7,5},{8,10},{9,11},{10,... | collective-permute-start | bytes 221192 | tf_op jit(solution)/shard_map/ppermute | solution.py:62
  54.2 1.8 %collective-permute-done.19.refs_0_ = bf16[16,2304]{1,0:T(8,128)(2,1)S(1)} collective-permute-done((bf16[16,2304]{1,0:T(8,128)(2,1)S(1)}, bf16[16,2304]{1,0:T(8,128)(2,1)S(1)}, u32[]{:S(2)}, u32[]{:S(2)}) %collective-permute-start.19) | collective-permute-done | bytes 73760 | tf_op jit(solution)/shard_map/ppermute | solution.py:62
  56.0 1.5 %collective-permute-done.20.refs_1_ = bf16[16,2304]{1,0:T(8,128)(2,1)S(1)} collective-permute-done((bf16[16,2304]{1,0:T(8,128)(2,1)S(1)}, bf16[16,2304]{1,0:T(8,128)(2,1)S(1)}, u32[]{:S(2)}, u32[]{:S(2)}) %collective-permute-start.20) | collective-permute-done | bytes 73760 | tf_op jit(solution)/shard_map/ppermute | solution.py:62
  57.5 0.3 collective-permute-done.21.refs_2_
  57.9 3.0 %collective-permute-start.22 = (bf16[8,2304]{1,0:T(8,128)(2,1)S(1)}, bf16[8,2304]{1,0:T(8,128)(2,1)S(1)}, u32[]{:S(2)}, u32[]{:S(2)}) collective-permute-start(bf16[8,2304]{1,0:T(8,128)(2,1)S(1)} %get-tuple-element.53), channel_id=1, source_target_pairs={{0,4},{1,5},{2,6},{3,7},{4,0},{5,1},{6,2},{7,3},{8,12},{9,13},{10,... | collective-permute-start | bytes 110600 | tf_op jit(solution)/shard_map/ppermute | solution.py:68
  60.9 0.7 %shard_map.113 = (f32[64,1024]{1,0:T(8,128)}, f32[1,8]{1,0:T(1,128)}) custom-call(f32[64,512]{1,0:T(8,128)S(1)} %get-tuple-element.41.grad, f32[64,512]{1,0:T(8,128)S(1)} %get-tuple-element.44.grad_other, f32[1,8]{1,0:T(1,128)S(1)} %get-tuple-element.45.squared), custom_call_target="tpu_custom_call" | custom-call | bytes 524352 | tf_op jit(solution)/shard_map/pallas_call | solution.py:29
  61.6 1.2 %collective-permute-done.22.other = bf16[8,2304]{1,0:T(8,128)(2,1)S(1)} collective-permute-done((bf16[8,2304]{1,0:T(8,128)(2,1)S(1)}, bf16[8,2304]{1,0:T(8,128)(2,1)S(1)}, u32[]{:S(2)}, u32[]{:S(2)}) %collective-permute-start.22) | collective-permute-done | bytes 36896 | tf_op jit(solution)/shard_map/ppermute | solution.py:68
  62.8 0.6 shard_map.115
  (34 shorter events, 0.8 us)
Async XLA Ops:
  0.6 6.6 %collective-permute-start = (bf16[8,2304]{1,0:T(8,128)(2,1)}, bf16[8,2304]{1,0:T(8,128)(2,1)S(1)}, u32[]{:S(2)}, u32[]{:S(2)}) collective-permute-start(bf16[8,2304]{1,0:T(8,128)(2,1)} %bitcast.22), channel_id=1, source_target_pairs={{0,4},{1,5},{2,6},{3,7},{4,0},{5,1},{6,2},{7,3},{8,12},{9,13},{10,... | collective-permute-start | bytes 110600 | tf_op jit(solution)/shard_map/ppermute | solution.py:68
  7.3 7.7 %slice-start = ((s8[4718592]{0:T(1024)(128)(4,1)}), s8[4194304]{0:T(1024)(128)(4,1)S(1)}, s32[]{:S(2)}) async-start(s8[4718592]{0:T(1024)(128)(4,1)} %bitcast.9), calls=%async_computation | async-start | bytes 8388608
  7.3 7.7 %slice-start.1 = ((s8[4718592]{0:T(1024)(128)(4,1)}), s8[524288]{0:T(1024)(128)(4,1)S(1)}, s32[]{:S(2)}) async-start(s8[4718592]{0:T(1024)(128)(4,1)} %bitcast.9), calls=%async_computation.1 | async-start | bytes 1048576
  7.3 11.1 %slice-start.2 = ((s8[4718592]{0:T(1024)(128)(4,1)}), s8[4194304]{0:T(1024)(128)(4,1)S(1)}, s32[]{:S(2)}) async-start(s8[4718592]{0:T(1024)(128)(4,1)} %bitcast.15), calls=%async_computation.2 | async-start | bytes 8388608
  7.3 11.1 %slice-start.3 = ((s8[4718592]{0:T(1024)(128)(4,1)}), s8[524288]{0:T(1024)(128)(4,1)S(1)}, s32[]{:S(2)}) async-start(s8[4718592]{0:T(1024)(128)(4,1)} %bitcast.15), calls=%async_computation.3 | async-start | bytes 1048576
  7.3 5.3 %collective-permute-start.3 = (bf16[16,2304]{1,0:T(8,128)(2,1)S(1)}, bf16[16,2304]{1,0:T(8,128)(2,1)S(1)}, u32[]{:S(2)}, u32[]{:S(2)}) collective-permute-start(bf16[16,2304]{1,0:T(8,128)(2,1)S(1)} %shard_map.96.rest_0_.acts), channel_id=1, source_target_pairs={{0,3},{1,2},{2,1},{3,0},{4,7},{5,6},{6,5},{7,4},{8,11},{9,10},{10,... | collective-permute-start | bytes 221192 | tf_op jit(solution)/shard_map/ppermute | solution.py:62
  9.9 4.4 %collective-permute-start.2 = (bf16[16,2304]{1,0:T(8,128)(2,1)S(1)}, bf16[16,2304]{1,0:T(8,128)(2,1)S(1)}, u32[]{:S(2)}, u32[]{:S(2)}) collective-permute-start(bf16[16,2304]{1,0:T(8,128)(2,1)S(1)} %shard_map.96.rest_0_.acts), channel_id=1, source_target_pairs={{0,2},{1,3},{2,0},{3,1},{4,6},{5,7},{6,4},{7,5},{8,10},{9,11},{10,... | collective-permute-start | bytes 221192 | tf_op jit(solution)/shard_map/ppermute | solution.py:62
  10.6 4.4 %collective-permute-start.1 = (bf16[16,2304]{1,0:T(8,128)(2,1)S(1)}, bf16[16,2304]{1,0:T(8,128)(2,1)S(1)}, u32[]{:S(2)}, u32[]{:S(2)}) collective-permute-start(bf16[16,2304]{1,0:T(8,128)(2,1)S(1)} %shard_map.96.rest_0_.acts), channel_id=1, source_target_pairs={{0,1},{1,0},{2,3},{3,2},{4,5},{5,4},{6,7},{7,6},{8,9},{9,8},{10,11... | collective-permute-start | bytes 221192 | tf_op jit(solution)/shard_map/ppermute | solution.py:62
  15.5 1.3 %collective-permute-start.4 = (bf16[64,512]{1,0:T(8,128)(2,1)S(1)}, bf16[64,512]{1,0:T(8,128)(2,1)S(1)}, u32[]{:S(2)}, u32[]{:S(2)}) collective-permute-start(bf16[64,512]{1,0:T(8,128)(2,1)S(1)} %shard_map.98), channel_id=1, source_target_pairs={{0,8},{8,0},{16,24},{24,16},{1,9},{9,1},{17,25},{25,17},{2,10},{10... | collective-permute-start | bytes 196616 | tf_op jit(solution)/shard_map/ppermute | solution.py:44
  16.9 4.3 %collective-permute-start.6 = (bf16[64,512]{1,0:T(8,128)(2,1)S(1)}, bf16[64,512]{1,0:T(8,128)(2,1)S(1)}, u32[]{:S(2)}, u32[]{:S(2)}) collective-permute-start(bf16[64,512]{1,0:T(8,128)(2,1)S(1)} %shard_map.99.after.terms), channel_id=1, source_target_pairs={{0,16},{8,24},{16,0},{24,8},{1,17},{9,25},{17,1},{25,9},{2,18},{10... | collective-permute-start | bytes 196616 | tf_op jit(solution)/shard_map/ppermute | solution.py:48
  18.4 3.3 %collective-permute-start.5 = (bf16[64,512]{1,0:T(8,128)(2,1)S(1)}, bf16[64,512]{1,0:T(8,128)(2,1)S(1)}, u32[]{:S(2)}, u32[]{:S(2)}) collective-permute-start(bf16[64,512]{1,0:T(8,128)(2,1)S(1)} %shard_map.99.after.terms), channel_id=1, source_target_pairs={{0,8},{8,0},{16,24},{24,16},{1,9},{9,1},{17,25},{25,17},{2,10},{10... | collective-permute-start | bytes 196616 | tf_op jit(solution)/shard_map/ppermute | solution.py:50
  21.2 1.3 %collective-permute-start.7 = (bf16[64,512]{1,0:T(8,128)(2,1)S(1)}, bf16[64,512]{1,0:T(8,128)(2,1)S(1)}, u32[]{:S(2)}, u32[]{:S(2)}) collective-permute-start(bf16[64,512]{1,0:T(8,128)(2,1)S(1)} %shard_map.101.others), channel_id=1, source_target_pairs={{0,8},{8,0},{16,24},{24,16},{1,9},{9,1},{17,25},{25,17},{2,10},{10... | collective-permute-start | bytes 196616 | tf_op jit(solution)/shard_map/ppermute | solution.py:50
  21.7 14.6 %copy-start = (f32[1,2304]{1,0:T(1,128)S(1)}, f32[1,2304]{1,0:T(1,128)}, u32[]{:S(2)}) copy-start(f32[1,2304]{1,0:T(1,128)} %dec_bias.1) | copy-start | bytes 27652
  21.7 14.6 %copy-start.1 = (s32[64]{0:T(128)S(1)}, s32[64]{0:T(128)}, u32[]{:S(2)}) copy-start(s32[64]{0:T(128)} %param.13) | copy-start | bytes 772
  23.0 5.9 %collective-permute-start.8 = (bf16[16,2304]{1,0:T(8,128)(2,1)S(1)}, bf16[16,2304]{1,0:T(8,128)(2,1)S(1)}, u32[]{:S(2)}, u32[]{:S(2)}) collective-permute-start(bf16[16,2304]{1,0:T(8,128)(2,1)S(1)} %get-tuple-element.33), channel_id=1, source_target_pairs={{0,3},{1,2},{2,1},{3,0},{4,7},{5,6},{6,5},{7,4},{8,11},{9,10},{10,... | collective-permute-start | bytes 221192 | tf_op jit(solution)/shard_map/ppermute | solution.py:62
  24.3 4.6 %collective-permute-start.9 = (bf16[16,2304]{1,0:T(8,128)(2,1)S(1)}, bf16[16,2304]{1,0:T(8,128)(2,1)S(1)}, u32[]{:S(2)}, u32[]{:S(2)}) collective-permute-start(bf16[16,2304]{1,0:T(8,128)(2,1)S(1)} %get-tuple-element.34), channel_id=1, source_target_pairs={{0,2},{1,3},{2,0},{3,1},{4,6},{5,7},{6,4},{7,5},{8,10},{9,11},{10,... | collective-permute-start | bytes 221192 | tf_op jit(solution)/shard_map/ppermute | solution.py:62
  24.8 5.0 %collective-permute-start.10 = (bf16[16,2304]{1,0:T(8,128)(2,1)S(1)}, bf16[16,2304]{1,0:T(8,128)(2,1)S(1)}, u32[]{:S(2)}, u32[]{:S(2)}) collective-permute-start(bf16[16,2304]{1,0:T(8,128)(2,1)S(1)} %get-tuple-element.35), channel_id=1, source_target_pairs={{0,1},{1,0},{2,3},{3,2},{4,5},{5,4},{6,7},{7,6},{8,9},{9,8},{10,11... | collective-permute-start | bytes 221192 | tf_op jit(solution)/shard_map/ppermute | solution.py:62
  29.9 6.4 %collective-permute-start.11 = (bf16[16,2304]{1,0:T(8,128)(2,1)S(1)}, bf16[16,2304]{1,0:T(8,128)(2,1)S(1)}, u32[]{:S(2)}, u32[]{:S(2)}) collective-permute-start(bf16[16,2304]{1,0:T(8,128)(2,1)S(1)} %get-tuple-element.38), channel_id=1, source_target_pairs={{0,4},{1,5},{2,6},{3,7},{4,0},{5,1},{6,2},{7,3},{8,12},{9,13},{10,... | collective-permute-start | bytes 221192 | tf_op jit(solution)/shard_map/ppermute | solution.py:68
  36.5 5.3 %collective-permute-start.14 = (bf16[16,2304]{1,0:T(8,128)(2,1)S(1)}, bf16[16,2304]{1,0:T(8,128)(2,1)S(1)}, u32[]{:S(2)}, u32[]{:S(2)}) collective-permute-start(bf16[16,2304]{1,0:T(8,128)(2,1)S(1)} %get-tuple-element.39.rest_0_), channel_id=1, source_target_pairs={{0,3},{1,2},{2,1},{3,0},{4,7},{5,6},{6,5},{7,4},{8,11},{9,10},{10,... | collective-permute-start | bytes 221192 | tf_op jit(solution)/shard_map/ppermute | solution.py:62
  37.3 4.6 %collective-permute-start.13 = (bf16[16,2304]{1,0:T(8,128)(2,1)S(1)}, bf16[16,2304]{1,0:T(8,128)(2,1)S(1)}, u32[]{:S(2)}, u32[]{:S(2)}) collective-permute-start(bf16[16,2304]{1,0:T(8,128)(2,1)S(1)} %get-tuple-element.39.rest_0_), channel_id=1, source_target_pairs={{0,2},{1,3},{2,0},{3,1},{4,6},{5,7},{6,4},{7,5},{8,10},{9,11},{10,... | collective-permute-start | bytes 221192 | tf_op jit(solution)/shard_map/ppermute | solution.py:62
  37.9 4.6 %collective-permute-start.12 = (bf16[16,2304]{1,0:T(8,128)(2,1)S(1)}, bf16[16,2304]{1,0:T(8,128)(2,1)S(1)}, u32[]{:S(2)}, u32[]{:S(2)}) collective-permute-start(bf16[16,2304]{1,0:T(8,128)(2,1)S(1)} %get-tuple-element.39.rest_0_), channel_id=1, source_target_pairs={{0,1},{1,0},{2,3},{3,2},{4,5},{5,4},{6,7},{7,6},{8,9},{9,8},{10,11... | collective-permute-start | bytes 221192 | tf_op jit(solution)/shard_map/ppermute | solution.py:62
  43.1 1.3 %collective-permute-start.15 = (bf16[64,512]{1,0:T(8,128)(2,1)S(1)}, bf16[64,512]{1,0:T(8,128)(2,1)S(1)}, u32[]{:S(2)}, u32[]{:S(2)}) collective-permute-start(bf16[64,512]{1,0:T(8,128)(2,1)S(1)} %shard_map.107.before), channel_id=1, source_target_pairs={{0,8},{8,0},{16,24},{24,16},{1,9},{9,1},{17,25},{25,17},{2,10},{10... | collective-permute-start | bytes 196616 | tf_op jit(solution)/shard_map/ppermute | solution.py:44
  44.5 4.3 %collective-permute-start.16 = (bf16[64,512]{1,0:T(8,128)(2,1)S(1)}, bf16[64,512]{1,0:T(8,128)(2,1)S(1)}, u32[]{:S(2)}, u32[]{:S(2)}) collective-permute-start(bf16[64,512]{1,0:T(8,128)(2,1)S(1)} %shard_map.108.after.terms), channel_id=1, source_target_pairs={{0,16},{8,24},{16,0},{24,8},{1,17},{9,25},{17,1},{25,9},{2,18},{10... | collective-permute-start | bytes 196616 | tf_op jit(solution)/shard_map/ppermute | solution.py:48
  46.0 3.4 %collective-permute-start.17 = (bf16[64,512]{1,0:T(8,128)(2,1)S(1)}, bf16[64,512]{1,0:T(8,128)(2,1)S(1)}, u32[]{:S(2)}, u32[]{:S(2)}) collective-permute-start(bf16[64,512]{1,0:T(8,128)(2,1)S(1)} %shard_map.108.after.terms), channel_id=1, source_target_pairs={{0,8},{8,0},{16,24},{24,16},{1,9},{9,1},{17,25},{25,17},{2,10},{10... | collective-permute-start | bytes 196616 | tf_op jit(solution)/shard_map/ppermute | solution.py:50
  48.8 1.3 %collective-permute-start.18 = (bf16[64,512]{1,0:T(8,128)(2,1)S(1)}, bf16[64,512]{1,0:T(8,128)(2,1)S(1)}, u32[]{:S(2)}, u32[]{:S(2)}) collective-permute-start(bf16[64,512]{1,0:T(8,128)(2,1)S(1)} %shard_map.110.others), channel_id=1, source_target_pairs={{0,8},{8,0},{16,24},{24,16},{1,9},{9,1},{17,25},{25,17},{2,10},{10... | collective-permute-start | bytes 196616 | tf_op jit(solution)/shard_map/ppermute | solution.py:50
  50.6 5.4 %collective-permute-start.19 = (bf16[16,2304]{1,0:T(8,128)(2,1)S(1)}, bf16[16,2304]{1,0:T(8,128)(2,1)S(1)}, u32[]{:S(2)}, u32[]{:S(2)}) collective-permute-start(bf16[16,2304]{1,0:T(8,128)(2,1)S(1)} %get-tuple-element.48), channel_id=1, source_target_pairs={{0,3},{1,2},{2,1},{3,0},{4,7},{5,6},{6,5},{7,4},{8,11},{9,10},{10,... | collective-permute-start | bytes 221192 | tf_op jit(solution)/shard_map/ppermute | solution.py:62
  52.4 5.1 %collective-permute-start.20 = (bf16[16,2304]{1,0:T(8,128)(2,1)S(1)}, bf16[16,2304]{1,0:T(8,128)(2,1)S(1)}, u32[]{:S(2)}, u32[]{:S(2)}) collective-permute-start(bf16[16,2304]{1,0:T(8,128)(2,1)S(1)} %get-tuple-element.49), channel_id=1, source_target_pairs={{0,1},{1,0},{2,3},{3,2},{4,5},{5,4},{6,7},{7,6},{8,9},{9,8},{10,11... | collective-permute-start | bytes 221192 | tf_op jit(solution)/shard_map/ppermute | solution.py:62
  53.2 4.6 %collective-permute-start.21 = (bf16[16,2304]{1,0:T(8,128)(2,1)S(1)}, bf16[16,2304]{1,0:T(8,128)(2,1)S(1)}, u32[]{:S(2)}, u32[]{:S(2)}) collective-permute-start(bf16[16,2304]{1,0:T(8,128)(2,1)S(1)} %get-tuple-element.50), channel_id=1, source_target_pairs={{0,2},{1,3},{2,0},{3,1},{4,6},{5,7},{6,4},{7,5},{8,10},{9,11},{10,... | collective-permute-start | bytes 221192 | tf_op jit(solution)/shard_map/ppermute | solution.py:62
  57.9 5.0 %collective-permute-start.22 = (bf16[8,2304]{1,0:T(8,128)(2,1)S(1)}, bf16[8,2304]{1,0:T(8,128)(2,1)S(1)}, u32[]{:S(2)}, u32[]{:S(2)}) collective-permute-start(bf16[8,2304]{1,0:T(8,128)(2,1)S(1)} %get-tuple-element.53), channel_id=1, source_target_pairs={{0,4},{1,5},{2,6},{3,7},{4,0},{5,1},{6,2},{7,3},{8,12},{9,13},{10,... | collective-permute-start | bytes 110600 | tf_op jit(solution)/shard_map/ppermute | solution.py:68

commit v11 on v10

--- a/solution.py
+++ b/solution.py
@@ -40,15 +40,15 @@
 
 def layer_sum(make, weight):
     n = lax.axis_size("layer")
-    near_by, far_off = [[(i, i ^ span) for i in range(n)] for span in (1, n // 2)]
+    near_by, far_off = [[(i, i ^ span) for i in range(n)] for span in (1, n // 2 + 1)]
     theirs = lax.ppermute(make(True), "layer", near_by)
     mine = make(False)
     [pair] = call(add, [near(mine.shape, half)], mine, theirs)
     [turned] = call(turn, [near(weight.shape[::-1], half)], weight, pair, work=True)
     far = lax.ppermute(pair, "layer", far_off)
     [far] = call(lambda *refs: None, [near(far.shape, half)], turned, far, same={1: 0})
-    other = [lax.ppermute(x, "layer", near_by) for x in (pair, far)]
-    return (pair, far), other, turned
+    back = [lax.ppermute(x, "layer", near_by) for x in (pair, far)]
+    return (back[0], far), (pair, back[1]), turned
 
 
 def features(other, width):
@@ -142,15 +142,15 @@
             out[:, there] = found[k * rows : (k + 1) * rows]
 
 
-def decode(other, terms, others, enc_bias, threshold, weight, before, slope, *outs):
-    which = features(other, terms.shape[1])
+def decode(last, terms, others, enc_bias, threshold, weight, before, slope, *outs):
+    which = features(not last, terms.shape[1])
     preact = terms[...].astype(wide) + others[...].astype(wide) + enc_bias[:, which]
     gating = jax.nn.sigmoid((preact - threshold[:, which]) / jump_scale)
     slope[...] = gating + preact * gating * (1.0 - gating) / jump_scale
-    spread_rows((preact * gating).astype(half), weight, which, before if other else None, outs)
-
-
-def decode_grad(other, terms, others, slope, weight, before, total, *outs):
+    spread_rows((preact * gating).astype(half), weight, which, before if last else None, outs)
+
+
+def decode_grad(last, terms, others, slope, weight, before, total, *outs):
     latent_grad = terms[...].astype(wide) + others[...].astype(wide)
     n, me = lax.axis_size("feat"), place()
     rows = total.shape[0] // n
@@ -158,7 +158,7 @@
         block = lax.bitwise_xor(me, i // 2) + i % 2 * (n // 2)
         total[pl.ds(pl.multiple_of(block * rows, rows), rows), :] = latent_grad[i * rows : (i + 1) * rows]
     x = (latent_grad * slope[...]).astype(half)
-    spread_rows(x, weight, features(other, terms.shape[1]), before if other else None, outs)
+    spread_rows(x, weight, features(not last, terms.shape[1]), before if last else None, outs)
 
 
 def add_pair(*refs):
@@ -191,7 +191,7 @@
 
 
 def leave(grad, grad_other, squared, grad_out, squared_out, done):
-    mine, theirs = [grad_out.at[:, features(which, grad.shape[1])] for which in (False, True)]
+    mine, theirs = [grad_out.at[:, features(which, grad.shape[1])] for which in (True, False)]
     moves = [(grad, mine), (grad_other, theirs), (squared, squared_out)]
     moves = [pltpu.make_async_copy(here, there, done.at[i]) for i, (here, there) in enumerate(moves)]
     for move in moves:

time: 63.7 us -> 63.3 us (level)
  waiting for transfers between devices: 26.1 us -> 25.3 us
    ppermute x4, starting transfers between devices: 0.01 us -> 1.03 us  [layer_sum(): back = [lax.ppermute(x, 'layer', near_by) for x in (pair, far)]]
where the time goes in v11:
time: 63.3 us; the launch traced here: 63.1 us
  starting transfers between devices  27.4 us (43%)
  waiting for transfers between devices  25.3 us (40%)
  Pallas kernels  9.59 us (15%)
  between operations  0.8 us (1%)
    ppermute x12, starting transfers between devices, trade(): came[k] = lax.ppermute(pieces[k], 'feat', [(i, i ^ k) for i in range(n)])  14.1 us
    ppermute x12, waiting for transfers between devices, trade(): came[k] = lax.ppermute(pieces[k], 'feat', [(i, i ^ k) for i in range(n)])  13.6 us
    pallas_call x22, Pallas kernels, call(): pl.pallas_call(body, out_shape=outs, in_specs=[away] * fetched + [here] *...  9.59 us
    ppermute x3, starting transfers between devices, mirror(): lax.ppermute(block, 'feat', [(i, (i + n // 2) % n) for i in range(n)])  9.47 us
    ppermute x3, waiting for transfers between devices, mirror(): lax.ppermute(block, 'feat', [(i, (i + n // 2) % n) for i in range(n)])  7.02 us
    ppermute x2, starting transfers between devices, layer_sum(): far = lax.ppermute(pair, 'layer', far_off)  2.57 us
    ppermute x2, waiting for transfers between devices, layer_sum(): far = lax.ppermute(pair, 'layer', far_off)  2.25 us
    ppermute x2, waiting for transfers between devices, layer_sum(): theirs = lax.ppermute(make(True), 'layer', near_by)  1.36 us
  transfers between devices with their start and end apart: 23, of which 19 were waited for; matrix products, arithmetic and copies ran while one was open for 0% of the time, Pallas kernels for 10%

profile of v11, /device:TPU:0, one launch (start us, length us, event | category | flops | bytes accessed | tf_op | source)
XLA Modules:
  0.0 63.1 jit_solution(15104310927071108711)
XLA Ops:
  0.6 4.1 %collective-permute-start = (bf16[8,2304]{1,0:T(8,128)(2,1)}, bf16[8,2304]{1,0:T(8,128)(2,1)S(1)}, u32[]{:S(2)}, u32[]{:S(2)}) collective-permute-start(bf16[8,2304]{1,0:T(8,128)(2,1)} %bitcast.22), channel_id=1, source_target_pairs={{0,4},{1,5},{2,6},{3,7},{4,0},{5,1},{6,2},{7,3},{8,12},{9,13},{10,... | collective-permute-start | bytes 110600 | tf_op jit(solution)/shard_map/ppermute | solution.py:68
  4.7 0.8 %shard_map.94 = (bf16[8,2304]{1,0:T(8,128)(2,1)S(1)}, f32[1,1024]{1,0:T(1,128)S(1)}, f32[1,1024]{1,0:T(1,128)S(1)}) custom-call(bf16[8,2304]{1,0:T(8,128)(2,1)} %bitcast.23, f32[1,1024]{1,0:T(1,128)} %bitcast.24, f32[1,1024]{1,0:T(1,128)} %bitcast.25), custom_call_target="tpu_custom_call" | custom-call | bytes 90112 | tf_op jit(solution)/shard_map/pallas_call | solution.py:29
  5.6 1.7 %collective-permute-done.other = bf16[8,2304]{1,0:T(8,128)(2,1)S(1)} collective-permute-done((bf16[8,2304]{1,0:T(8,128)(2,1)}, bf16[8,2304]{1,0:T(8,128)(2,1)S(1)}, u32[]{:S(2)}, u32[]{:S(2)}) %collective-permute-start) | collective-permute-done | bytes 36896 | tf_op jit(solution)/shard_map/ppermute | solution.py:68
  7.3 2.5 %collective-permute-start.3 = (bf16[16,2304]{1,0:T(8,128)(2,1)S(1)}, bf16[16,2304]{1,0:T(8,128)(2,1)S(1)}, u32[]{:S(2)}, u32[]{:S(2)}) collective-permute-start(bf16[16,2304]{1,0:T(8,128)(2,1)S(1)} %shard_map.96.rest_0_.acts), channel_id=1, source_target_pairs={{0,3},{1,2},{2,1},{3,0},{4,7},{5,6},{6,5},{7,4},{8,11},{9,10},{10,... | collective-permute-start | bytes 221192 | tf_op jit(solution)/shard_map/ppermute | solution.py:62
  9.9 0.7 %collective-permute-start.2 = (bf16[16,2304]{1,0:T(8,128)(2,1)S(1)}, bf16[16,2304]{1,0:T(8,128)(2,1)S(1)}, u32[]{:S(2)}, u32[]{:S(2)}) collective-permute-start(bf16[16,2304]{1,0:T(8,128)(2,1)S(1)} %shard_map.96.rest_0_.acts), channel_id=1, source_target_pairs={{0,2},{1,3},{2,0},{3,1},{4,6},{5,7},{6,4},{7,5},{8,10},{9,11},{10,... | collective-permute-start | bytes 221192 | tf_op jit(solution)/shard_map/ppermute | solution.py:62
  10.9 1.8 %collective-permute-done.3.rest_3_ = bf16[16,2304]{1,0:T(8,128)(2,1)S(1)} collective-permute-done((bf16[16,2304]{1,0:T(8,128)(2,1)S(1)}, bf16[16,2304]{1,0:T(8,128)(2,1)S(1)}, u32[]{:S(2)}, u32[]{:S(2)}) %collective-permute-start.3) | collective-permute-done | bytes 73760 | tf_op jit(solution)/shard_map/ppermute | solution.py:62
  12.7 1.6 %collective-permute-done.2.rest_2_ = bf16[16,2304]{1,0:T(8,128)(2,1)S(1)} collective-permute-done((bf16[16,2304]{1,0:T(8,128)(2,1)S(1)}, bf16[16,2304]{1,0:T(8,128)(2,1)S(1)}, u32[]{:S(2)}, u32[]{:S(2)}) %collective-permute-start.2) | collective-permute-done | bytes 73760 | tf_op jit(solution)/shard_map/ppermute | solution.py:62
  14.2 0.7 %collective-permute-done.1.rest_1_ = bf16[16,2304]{1,0:T(8,128)(2,1)S(1)} collective-permute-done((bf16[16,2304]{1,0:T(8,128)(2,1)S(1)}, bf16[16,2304]{1,0:T(8,128)(2,1)S(1)}, u32[]{:S(2)}, u32[]{:S(2)}) %collective-permute-start.1) | collective-permute-done | bytes 73760 | tf_op jit(solution)/shard_map/ppermute | solution.py:62
  15.0 0.5 shard_map.98
  15.6 0.6 shard_map.97.one
  16.2 0.7 %collective-permute-done.4.other = bf16[64,512]{1,0:T(8,128)(2,1)S(1)} collective-permute-done((bf16[64,512]{1,0:T(8,128)(2,1)S(1)}, bf16[64,512]{1,0:T(8,128)(2,1)S(1)}, u32[]{:S(2)}, u32[]{:S(2)}) %collective-permute-start.4) | collective-permute-done | bytes 65568 | tf_op jit(solution)/shard_map/ppermute | solution.py:44
  16.9 1.3 %collective-permute-start.5 = (bf16[64,512]{1,0:T(8,128)(2,1)S(1)}, bf16[64,512]{1,0:T(8,128)(2,1)S(1)}, u32[]{:S(2)}, u32[]{:S(2)}) collective-permute-start(bf16[64,512]{1,0:T(8,128)(2,1)S(1)} %shard_map.99.after.terms), channel_id=1, source_target_pairs={{0,24},{8,16},{16,8},{24,0},{1,25},{9,17},{17,9},{25,1},{2,26},{10... | collective-permute-start | bytes 196616 | tf_op jit(solution)/shard_map/ppermute | solution.py:48
  18.2 0.4 collective-permute-start.7
  18.5 1.4 %shard_map.100.refs_0_.before.weight = bf16[2304,1024]{1,0:T(8,128)(2,1)S(1)} custom-call(bf16[1024,2304]{1,0:T(8,128)(2,1)S(1)} %bitcast.17, bf16[64,512]{1,0:T(8,128)(2,1)S(1)} %shard_map.99.after.terms), custom_call_target="tpu_custom_call" | custom-call | bytes 9568256 | tf_op jit(solution)/shard_map/pallas_call | solution.py:29
  20.0 1.0 %collective-permute-done.5.refs_1_ = bf16[64,512]{1,0:T(8,128)(2,1)S(1)} collective-permute-done((bf16[64,512]{1,0:T(8,128)(2,1)S(1)}, bf16[64,512]{1,0:T(8,128)(2,1)S(1)}, u32[]{:S(2)}, u32[]{:S(2)}) %collective-permute-start.5) | collective-permute-done | bytes 65568 | tf_op jit(solution)/shard_map/ppermute | solution.py:48
  21.1 0.5 shard_map.102
  21.7 0.5 collective-permute-done.6.others
  22.2 0.5 shard_map.103
  22.8 1.3 %collective-permute-start.8 = (bf16[16,2304]{1,0:T(8,128)(2,1)S(1)}, bf16[16,2304]{1,0:T(8,128)(2,1)S(1)}, u32[]{:S(2)}, u32[]{:S(2)}) collective-permute-start(bf16[16,2304]{1,0:T(8,128)(2,1)S(1)} %get-tuple-element.33), channel_id=1, source_target_pairs={{0,3},{1,2},{2,1},{3,0},{4,7},{5,6},{6,5},{7,4},{8,11},{9,10},{10,... | collective-permute-start | bytes 221192 | tf_op jit(solution)/shard_map/ppermute | solution.py:62
  24.1 0.5 collective-permute-start.9
  24.6 1.7 %collective-permute-start.10 = (bf16[16,2304]{1,0:T(8,128)(2,1)S(1)}, bf16[16,2304]{1,0:T(8,128)(2,1)S(1)}, u32[]{:S(2)}, u32[]{:S(2)}) collective-permute-start(bf16[16,2304]{1,0:T(8,128)(2,1)S(1)} %get-tuple-element.35), channel_id=1, source_target_pairs={{0,1},{1,0},{2,3},{3,2},{4,5},{5,4},{6,7},{7,6},{8,9},{9,8},{10,11... | collective-permute-start | bytes 221192 | tf_op jit(solution)/shard_map/ppermute | solution.py:62
  26.3 2.3 %collective-permute-done.8.refs_0_ = bf16[16,2304]{1,0:T(8,128)(2,1)S(1)} collective-permute-done((bf16[16,2304]{1,0:T(8,128)(2,1)S(1)}, bf16[16,2304]{1,0:T(8,128)(2,1)S(1)}, u32[]{:S(2)}, u32[]{:S(2)}) %collective-permute-start.8) | collective-permute-done | bytes 73760 | tf_op jit(solution)/shard_map/ppermute | solution.py:62
  28.7 1.0 %collective-permute-done.10.refs_2_ = bf16[16,2304]{1,0:T(8,128)(2,1)S(1)} collective-permute-done((bf16[16,2304]{1,0:T(8,128)(2,1)S(1)}, bf16[16,2304]{1,0:T(8,128)(2,1)S(1)}, u32[]{:S(2)}, u32[]{:S(2)}) %collective-permute-start.10) | collective-permute-done | bytes 73760 | tf_op jit(solution)/shard_map/ppermute | solution.py:62
  29.7 2.4 %collective-permute-start.11 = (bf16[16,2304]{1,0:T(8,128)(2,1)S(1)}, bf16[16,2304]{1,0:T(8,128)(2,1)S(1)}, u32[]{:S(2)}, u32[]{:S(2)}) collective-permute-start(bf16[16,2304]{1,0:T(8,128)(2,1)S(1)} %get-tuple-element.38), channel_id=1, source_target_pairs={{0,4},{1,5},{2,6},{3,7},{4,0},{5,1},{6,2},{7,3},{8,12},{9,13},{10,... | collective-permute-start | bytes 221192 | tf_op jit(solution)/shard_map/ppermute | solution.py:68
  32.1 4.1 %collective-permute-done.11.other = bf16[16,2304]{1,0:T(8,128)(2,1)S(1)} collective-permute-done((bf16[16,2304]{1,0:T(8,128)(2,1)S(1)}, bf16[16,2304]{1,0:T(8,128)(2,1)S(1)}, u32[]{:S(2)}, u32[]{:S(2)}) %collective-permute-start.11) | collective-permute-done | bytes 73760 | tf_op jit(solution)/shard_map/ppermute | solution.py:68
  36.4 0.7 %collective-permute-start.14 = (bf16[16,2304]{1,0:T(8,128)(2,1)S(1)}, bf16[16,2304]{1,0:T(8,128)(2,1)S(1)}, u32[]{:S(2)}, u32[]{:S(2)}) collective-permute-start(bf16[16,2304]{1,0:T(8,128)(2,1)S(1)} %get-tuple-element.39.rest_0_), channel_id=1, source_target_pairs={{0,3},{1,2},{2,1},{3,0},{4,7},{5,6},{6,5},{7,4},{8,11},{9,10},{10,... | collective-permute-start | bytes 221192 | tf_op jit(solution)/shard_map/ppermute | solution.py:62
  37.0 0.7 %collective-permute-start.13 = (bf16[16,2304]{1,0:T(8,128)(2,1)S(1)}, bf16[16,2304]{1,0:T(8,128)(2,1)S(1)}, u32[]{:S(2)}, u32[]{:S(2)}) collective-permute-start(bf16[16,2304]{1,0:T(8,128)(2,1)S(1)} %get-tuple-element.39.rest_0_), channel_id=1, source_target_pairs={{0,2},{1,3},{2,0},{3,1},{4,6},{5,7},{6,4},{7,5},{8,10},{9,11},{10,... | collective-permute-start | bytes 221192 | tf_op jit(solution)/shard_map/ppermute | solution.py:62
  37.7 2.2 %collective-permute-start.12 = (bf16[16,2304]{1,0:T(8,128)(2,1)S(1)}, bf16[16,2304]{1,0:T(8,128)(2,1)S(1)}, u32[]{:S(2)}, u32[]{:S(2)}) collective-permute-start(bf16[16,2304]{1,0:T(8,128)(2,1)S(1)} %get-tuple-element.39.rest_0_), channel_id=1, source_target_pairs={{0,1},{1,0},{2,3},{3,2},{4,5},{5,4},{6,7},{7,6},{8,9},{9,8},{10,11... | collective-permute-start | bytes 221192 | tf_op jit(solution)/shard_map/ppermute | solution.py:62
  39.9 1.8 %collective-permute-done.14.rest_3_ = bf16[16,2304]{1,0:T(8,128)(2,1)S(1)} collective-permute-done((bf16[16,2304]{1,0:T(8,128)(2,1)S(1)}, bf16[16,2304]{1,0:T(8,128)(2,1)S(1)}, u32[]{:S(2)}, u32[]{:S(2)}) %collective-permute-start.14) | collective-permute-done | bytes 73760 | tf_op jit(solution)/shard_map/ppermute | solution.py:62
  41.7 0.8 %collective-permute-done.12.rest_1_ = bf16[16,2304]{1,0:T(8,128)(2,1)S(1)} collective-permute-done((bf16[16,2304]{1,0:T(8,128)(2,1)S(1)}, bf16[16,2304]{1,0:T(8,128)(2,1)S(1)}, u32[]{:S(2)}, u32[]{:S(2)}) %collective-permute-start.12) | collective-permute-done | bytes 73760 | tf_op jit(solution)/shard_map/ppermute | solution.py:62
  42.4 0.5 shard_map.107.before
  43.1 0.6 shard_map.106.one
  43.6 0.7 %collective-permute-done.15.other = bf16[64,512]{1,0:T(8,128)(2,1)S(1)} collective-permute-done((bf16[64,512]{1,0:T(8,128)(2,1)S(1)}, bf16[64,512]{1,0:T(8,128)(2,1)S(1)}, u32[]{:S(2)}, u32[]{:S(2)}) %collective-permute-start.15) | collective-permute-done | bytes 65568 | tf_op jit(solution)/shard_map/ppermute | solution.py:44
  44.3 1.3 %collective-permute-start.17 = (bf16[64,512]{1,0:T(8,128)(2,1)S(1)}, bf16[64,512]{1,0:T(8,128)(2,1)S(1)}, u32[]{:S(2)}, u32[]{:S(2)}) collective-permute-start(bf16[64,512]{1,0:T(8,128)(2,1)S(1)} %shard_map.108.after.terms), channel_id=1, source_target_pairs={{0,24},{8,16},{16,8},{24,0},{1,25},{9,17},{17,9},{25,1},{2,26},{10... | collective-permute-start | bytes 196616 | tf_op jit(solution)/shard_map/ppermute | solution.py:48
  45.9 1.3 %shard_map.109.refs_0_.weight = bf16[1024,2304]{1,0:T(8,128)(2,1)S(1)} custom-call(bf16[2304,1024]{1,0:T(8,128)(2,1)S(1)} %bitcast.13, bf16[64,512]{1,0:T(8,128)(2,1)S(1)} %shard_map.108.after.terms), custom_call_target="tpu_custom_call" | custom-call | bytes 9568256 | tf_op jit(solution)/shard_map/pallas_call | solution.py:29
  47.2 1.2 %collective-permute-done.17.refs_1_ = bf16[64,512]{1,0:T(8,128)(2,1)S(1)} collective-permute-done((bf16[64,512]{1,0:T(8,128)(2,1)S(1)}, bf16[64,512]{1,0:T(8,128)(2,1)S(1)}, u32[]{:S(2)}, u32[]{:S(2)}) %collective-permute-start.17) | collective-permute-done | bytes 65568 | tf_op jit(solution)/shard_map/ppermute | solution.py:48
  48.6 0.6 shard_map.111
  49.2 0.5 collective-permute-done.18.others
  49.7 0.5 shard_map.112
  50.3 1.8 %collective-permute-start.19 = (bf16[16,2304]{1,0:T(8,128)(2,1)S(1)}, bf16[16,2304]{1,0:T(8,128)(2,1)S(1)}, u32[]{:S(2)}, u32[]{:S(2)}) collective-permute-start(bf16[16,2304]{1,0:T(8,128)(2,1)S(1)} %get-tuple-element.48), channel_id=1, source_target_pairs={{0,3},{1,2},{2,1},{3,0},{4,7},{5,6},{6,5},{7,4},{8,11},{9,10},{10,... | collective-permute-start | bytes 221192 | tf_op jit(solution)/shard_map/ppermute | solution.py:62
  52.0 0.7 %collective-permute-start.20 = (bf16[16,2304]{1,0:T(8,128)(2,1)S(1)}, bf16[16,2304]{1,0:T(8,128)(2,1)S(1)}, u32[]{:S(2)}, u32[]{:S(2)}) collective-permute-start(bf16[16,2304]{1,0:T(8,128)(2,1)S(1)} %get-tuple-element.49), channel_id=1, source_target_pairs={{0,1},{1,0},{2,3},{3,2},{4,5},{5,4},{6,7},{7,6},{8,9},{9,8},{10,11... | collective-permute-start | bytes 221192 | tf_op jit(solution)/shard_map/ppermute | solution.py:62
  52.8 1.0 %collective-permute-start.21 = (bf16[16,2304]{1,0:T(8,128)(2,1)S(1)}, bf16[16,2304]{1,0:T(8,128)(2,1)S(1)}, u32[]{:S(2)}, u32[]{:S(2)}) collective-permute-start(bf16[16,2304]{1,0:T(8,128)(2,1)S(1)} %get-tuple-element.50), channel_id=1, source_target_pairs={{0,2},{1,3},{2,0},{3,1},{4,6},{5,7},{6,4},{7,5},{8,10},{9,11},{10,... | collective-permute-start | bytes 221192 | tf_op jit(solution)/shard_map/ppermute | solution.py:62
  53.8 1.8 %collective-permute-done.19.refs_0_ = bf16[16,2304]{1,0:T(8,128)(2,1)S(1)} collective-permute-done((bf16[16,2304]{1,0:T(8,128)(2,1)S(1)}, bf16[16,2304]{1,0:T(8,128)(2,1)S(1)}, u32[]{:S(2)}, u32[]{:S(2)}) %collective-permute-start.19) | collective-permute-done | bytes 73760 | tf_op jit(solution)/shard_map/ppermute | solution.py:62
  55.7 1.5 %collective-permute-done.20.refs_1_ = bf16[16,2304]{1,0:T(8,128)(2,1)S(1)} collective-permute-done((bf16[16,2304]{1,0:T(8,128)(2,1)S(1)}, bf16[16,2304]{1,0:T(8,128)(2,1)S(1)}, u32[]{:S(2)}, u32[]{:S(2)}) %collective-permute-start.20) | collective-permute-done | bytes 73760 | tf_op jit(solution)/shard_map/ppermute | solution.py:62
  57.5 3.0 %collective-permute-start.22 = (bf16[8,2304]{1,0:T(8,128)(2,1)S(1)}, bf16[8,2304]{1,0:T(8,128)(2,1)S(1)}, u32[]{:S(2)}, u32[]{:S(2)}) collective-permute-start(bf16[8,2304]{1,0:T(8,128)(2,1)S(1)} %get-tuple-element.53), channel_id=1, source_target_pairs={{0,4},{1,5},{2,6},{3,7},{4,0},{5,1},{6,2},{7,3},{8,12},{9,13},{10,... | collective-permute-start | bytes 110600 | tf_op jit(solution)/shard_map/ppermute | solution.py:68
  60.5 0.7 %shard_map.113 = (f32[64,1024]{1,0:T(8,128)}, f32[1,8]{1,0:T(1,128)}) custom-call(f32[64,512]{1,0:T(8,128)S(1)} %get-tuple-element.41.grad, f32[64,512]{1,0:T(8,128)S(1)} %get-tuple-element.44.grad_other, f32[1,8]{1,0:T(1,128)S(1)} %get-tuple-element.45.squared), custom_call_target="tpu_custom_call" | custom-call | bytes 524352 | tf_op jit(solution)/shard_map/pallas_call | solution.py:29
  61.2 1.2 %collective-permute-done.22.other = bf16[8,2304]{1,0:T(8,128)(2,1)S(1)} collective-permute-done((bf16[8,2304]{1,0:T(8,128)(2,1)S(1)}, bf16[8,2304]{1,0:T(8,128)(2,1)S(1)}, u32[]{:S(2)}, u32[]{:S(2)}) %collective-permute-start.22) | collective-permute-done | bytes 36896 | tf_op jit(solution)/shard_map/ppermute | solution.py:68
  62.4 0.6 %shard_map.115 = bf16[8,2304]{1,0:T(8,128)(2,1)} custom-call(f32[8,2304]{1,0:T(8,128)S(1)} %get-tuple-element.52.one, bf16[8,2304]{1,0:T(8,128)(2,1)S(1)} %collective-permute-done.22.other, f32[8,2304]{1,0:T(8,128)S(1)} %get-tuple-element.54.error), custom_call_target="tpu_custom_call" | custom-call | tf_op jit(solution)/shard_map/pallas_call | solution.py:29
  (34 shorter events, 1.8 us)
Async XLA Ops:
  0.6 6.6 %collective-permute-start = (bf16[8,2304]{1,0:T(8,128)(2,1)}, bf16[8,2304]{1,0:T(8,128)(2,1)S(1)}, u32[]{:S(2)}, u32[]{:S(2)}) collective-permute-start(bf16[8,2304]{1,0:T(8,128)(2,1)} %bitcast.22), channel_id=1, source_target_pairs={{0,4},{1,5},{2,6},{3,7},{4,0},{5,1},{6,2},{7,3},{8,12},{9,13},{10,... | collective-permute-start | bytes 110600 | tf_op jit(solution)/shard_map/ppermute | solution.py:68
  7.3 7.7 %slice-start = ((s8[4718592]{0:T(1024)(128)(4,1)}), s8[4194304]{0:T(1024)(128)(4,1)S(1)}, s32[]{:S(2)}) async-start(s8[4718592]{0:T(1024)(128)(4,1)} %bitcast.9), calls=%async_computation | async-start | bytes 8388608
  7.3 7.7 %slice-start.1 = ((s8[4718592]{0:T(1024)(128)(4,1)}), s8[524288]{0:T(1024)(128)(4,1)S(1)}, s32[]{:S(2)}) async-start(s8[4718592]{0:T(1024)(128)(4,1)} %bitcast.9), calls=%async_computation.1 | async-start | bytes 1048576
  7.3 11.2 %slice-start.2 = ((s8[4718592]{0:T(1024)(128)(4,1)}), s8[4194304]{0:T(1024)(128)(4,1)S(1)}, s32[]{:S(2)}) async-start(s8[4718592]{0:T(1024)(128)(4,1)} %bitcast.15), calls=%async_computation.2 | async-start | bytes 8388608
  7.3 11.2 %slice-start.3 = ((s8[4718592]{0:T(1024)(128)(4,1)}), s8[524288]{0:T(1024)(128)(4,1)S(1)}, s32[]{:S(2)}) async-start(s8[4718592]{0:T(1024)(128)(4,1)} %bitcast.15), calls=%async_computation.3 | async-start | bytes 1048576
  7.3 5.3 %collective-permute-start.3 = (bf16[16,2304]{1,0:T(8,128)(2,1)S(1)}, bf16[16,2304]{1,0:T(8,128)(2,1)S(1)}, u32[]{:S(2)}, u32[]{:S(2)}) collective-permute-start(bf16[16,2304]{1,0:T(8,128)(2,1)S(1)} %shard_map.96.rest_0_.acts), channel_id=1, source_target_pairs={{0,3},{1,2},{2,1},{3,0},{4,7},{5,6},{6,5},{7,4},{8,11},{9,10},{10,... | collective-permute-start | bytes 221192 | tf_op jit(solution)/shard_map/ppermute | solution.py:62
  9.9 4.4 %collective-permute-start.2 = (bf16[16,2304]{1,0:T(8,128)(2,1)S(1)}, bf16[16,2304]{1,0:T(8,128)(2,1)S(1)}, u32[]{:S(2)}, u32[]{:S(2)}) collective-permute-start(bf16[16,2304]{1,0:T(8,128)(2,1)S(1)} %shard_map.96.rest_0_.acts), channel_id=1, source_target_pairs={{0,2},{1,3},{2,0},{3,1},{4,6},{5,7},{6,4},{7,5},{8,10},{9,11},{10,... | collective-permute-start | bytes 221192 | tf_op jit(solution)/shard_map/ppermute | solution.py:62
  10.6 4.4 %collective-permute-start.1 = (bf16[16,2304]{1,0:T(8,128)(2,1)S(1)}, bf16[16,2304]{1,0:T(8,128)(2,1)S(1)}, u32[]{:S(2)}, u32[]{:S(2)}) collective-permute-start(bf16[16,2304]{1,0:T(8,128)(2,1)S(1)} %shard_map.96.rest_0_.acts), channel_id=1, source_target_pairs={{0,1},{1,0},{2,3},{3,2},{4,5},{5,4},{6,7},{7,6},{8,9},{9,8},{10,11... | collective-permute-start | bytes 221192 | tf_op jit(solution)/shard_map/ppermute | solution.py:62
  15.5 1.3 %collective-permute-start.4 = (bf16[64,512]{1,0:T(8,128)(2,1)S(1)}, bf16[64,512]{1,0:T(8,128)(2,1)S(1)}, u32[]{:S(2)}, u32[]{:S(2)}) collective-permute-start(bf16[64,512]{1,0:T(8,128)(2,1)S(1)} %shard_map.98), channel_id=1, source_target_pairs={{0,8},{8,0},{16,24},{24,16},{1,9},{9,1},{17,25},{25,17},{2,10},{10... | collective-permute-start | bytes 196616 | tf_op jit(solution)/shard_map/ppermute | solution.py:44
  16.9 4.1 %collective-permute-start.5 = (bf16[64,512]{1,0:T(8,128)(2,1)S(1)}, bf16[64,512]{1,0:T(8,128)(2,1)S(1)}, u32[]{:S(2)}, u32[]{:S(2)}) collective-permute-start(bf16[64,512]{1,0:T(8,128)(2,1)S(1)} %shard_map.99.after.terms), channel_id=1, source_target_pairs={{0,24},{8,16},{16,8},{24,0},{1,25},{9,17},{17,9},{25,1},{2,26},{10... | collective-permute-start | bytes 196616 | tf_op jit(solution)/shard_map/ppermute | solution.py:48
  18.2 3.0 %collective-permute-start.7 = (bf16[64,512]{1,0:T(8,128)(2,1)S(1)}, bf16[64,512]{1,0:T(8,128)(2,1)S(1)}, u32[]{:S(2)}, u32[]{:S(2)}) collective-permute-start(bf16[64,512]{1,0:T(8,128)(2,1)S(1)} %shard_map.99.after.terms), channel_id=1, source_target_pairs={{0,8},{8,0},{16,24},{24,16},{1,9},{9,1},{17,25},{25,17},{2,10},{10... | collective-permute-start | bytes 196616 | tf_op jit(solution)/shard_map/ppermute | solution.py:50
  21.0 1.3 %collective-permute-start.6 = (bf16[64,512]{1,0:T(8,128)(2,1)S(1)}, bf16[64,512]{1,0:T(8,128)(2,1)S(1)}, u32[]{:S(2)}, u32[]{:S(2)}) collective-permute-start(bf16[64,512]{1,0:T(8,128)(2,1)S(1)} %shard_map.101.others), channel_id=1, source_target_pairs={{0,8},{8,0},{16,24},{24,16},{1,9},{9,1},{17,25},{25,17},{2,10},{10... | collective-permute-start | bytes 196616 | tf_op jit(solution)/shard_map/ppermute | solution.py:50
  21.7 14.5 %copy-start = (f32[1,2304]{1,0:T(1,128)S(1)}, f32[1,2304]{1,0:T(1,128)}, u32[]{:S(2)}) copy-start(f32[1,2304]{1,0:T(1,128)} %dec_bias.1) | copy-start | bytes 27652
  21.7 14.5 %copy-start.1 = (s32[64]{0:T(128)S(1)}, s32[64]{0:T(128)}, u32[]{:S(2)}) copy-start(s32[64]{0:T(128)} %param.13) | copy-start | bytes 772
  22.8 5.9 %collective-permute-start.8 = (bf16[16,2304]{1,0:T(8,128)(2,1)S(1)}, bf16[16,2304]{1,0:T(8,128)(2,1)S(1)}, u32[]{:S(2)}, u32[]{:S(2)}) collective-permute-start(bf16[16,2304]{1,0:T(8,128)(2,1)S(1)} %get-tuple-element.33), channel_id=1, source_target_pairs={{0,3},{1,2},{2,1},{3,0},{4,7},{5,6},{6,5},{7,4},{8,11},{9,10},{10,... | collective-permute-start | bytes 221192 | tf_op jit(solution)/shard_map/ppermute | solution.py:62
  24.1 4.6 %collective-permute-start.9 = (bf16[16,2304]{1,0:T(8,128)(2,1)S(1)}, bf16[16,2304]{1,0:T(8,128)(2,1)S(1)}, u32[]{:S(2)}, u32[]{:S(2)}) collective-permute-start(bf16[16,2304]{1,0:T(8,128)(2,1)S(1)} %get-tuple-element.34), channel_id=1, source_target_pairs={{0,2},{1,3},{2,0},{3,1},{4,6},{5,7},{6,4},{7,5},{8,10},{9,11},{10,... | collective-permute-start | bytes 221192 | tf_op jit(solution)/shard_map/ppermute | solution.py:62
  24.6 5.1 %collective-permute-start.10 = (bf16[16,2304]{1,0:T(8,128)(2,1)S(1)}, bf16[16,2304]{1,0:T(8,128)(2,1)S(1)}, u32[]{:S(2)}, u32[]{:S(2)}) collective-permute-start(bf16[16,2304]{1,0:T(8,128)(2,1)S(1)} %get-tuple-element.35), channel_id=1, source_target_pairs={{0,1},{1,0},{2,3},{3,2},{4,5},{5,4},{6,7},{7,6},{8,9},{9,8},{10,11... | collective-permute-start | bytes 221192 | tf_op jit(solution)/shard_map/ppermute | solution.py:62
  29.7 6.5 %collective-permute-start.11 = (bf16[16,2304]{1,0:T(8,128)(2,1)S(1)}, bf16[16,2304]{1,0:T(8,128)(2,1)S(1)}, u32[]{:S(2)}, u32[]{:S(2)}) collective-permute-start(bf16[16,2304]{1,0:T(8,128)(2,1)S(1)} %get-tuple-element.38), channel_id=1, source_target_pairs={{0,4},{1,5},{2,6},{3,7},{4,0},{5,1},{6,2},{7,3},{8,12},{9,13},{10,... | collective-permute-start | bytes 221192 | tf_op jit(solution)/shard_map/ppermute | solution.py:68
  36.4 5.3 %collective-permute-start.14 = (bf16[16,2304]{1,0:T(8,128)(2,1)S(1)}, bf16[16,2304]{1,0:T(8,128)(2,1)S(1)}, u32[]{:S(2)}, u32[]{:S(2)}) collective-permute-start(bf16[16,2304]{1,0:T(8,128)(2,1)S(1)} %get-tuple-element.39.rest_0_), channel_id=1, source_target_pairs={{0,3},{1,2},{2,1},{3,0},{4,7},{5,6},{6,5},{7,4},{8,11},{9,10},{10,... | collective-permute-start | bytes 221192 | tf_op jit(solution)/shard_map/ppermute | solution.py:62
  37.0 4.6 %collective-permute-start.13 = (bf16[16,2304]{1,0:T(8,128)(2,1)S(1)}, bf16[16,2304]{1,0:T(8,128)(2,1)S(1)}, u32[]{:S(2)}, u32[]{:S(2)}) collective-permute-start(bf16[16,2304]{1,0:T(8,128)(2,1)S(1)} %get-tuple-element.39.rest_0_), channel_id=1, source_target_pairs={{0,2},{1,3},{2,0},{3,1},{4,6},{5,7},{6,4},{7,5},{8,10},{9,11},{10,... | collective-permute-start | bytes 221192 | tf_op jit(solution)/shard_map/ppermute | solution.py:62
  37.7 4.7 %collective-permute-start.12 = (bf16[16,2304]{1,0:T(8,128)(2,1)S(1)}, bf16[16,2304]{1,0:T(8,128)(2,1)S(1)}, u32[]{:S(2)}, u32[]{:S(2)}) collective-permute-start(bf16[16,2304]{1,0:T(8,128)(2,1)S(1)} %get-tuple-element.39.rest_0_), channel_id=1, source_target_pairs={{0,1},{1,0},{2,3},{3,2},{4,5},{5,4},{6,7},{7,6},{8,9},{9,8},{10,11... | collective-permute-start | bytes 221192 | tf_op jit(solution)/shard_map/ppermute | solution.py:62
  43.0 1.3 %collective-permute-start.15 = (bf16[64,512]{1,0:T(8,128)(2,1)S(1)}, bf16[64,512]{1,0:T(8,128)(2,1)S(1)}, u32[]{:S(2)}, u32[]{:S(2)}) collective-permute-start(bf16[64,512]{1,0:T(8,128)(2,1)S(1)} %shard_map.107.before), channel_id=1, source_target_pairs={{0,8},{8,0},{16,24},{24,16},{1,9},{9,1},{17,25},{25,17},{2,10},{10... | collective-permute-start | bytes 196616 | tf_op jit(solution)/shard_map/ppermute | solution.py:44
  44.3 4.1 %collective-permute-start.17 = (bf16[64,512]{1,0:T(8,128)(2,1)S(1)}, bf16[64,512]{1,0:T(8,128)(2,1)S(1)}, u32[]{:S(2)}, u32[]{:S(2)}) collective-permute-start(bf16[64,512]{1,0:T(8,128)(2,1)S(1)} %shard_map.108.after.terms), channel_id=1, source_target_pairs={{0,24},{8,16},{16,8},{24,0},{1,25},{9,17},{17,9},{25,1},{2,26},{10... | collective-permute-start | bytes 196616 | tf_op jit(solution)/shard_map/ppermute | solution.py:48
  45.6 3.0 %collective-permute-start.16 = (bf16[64,512]{1,0:T(8,128)(2,1)S(1)}, bf16[64,512]{1,0:T(8,128)(2,1)S(1)}, u32[]{:S(2)}, u32[]{:S(2)}) collective-permute-start(bf16[64,512]{1,0:T(8,128)(2,1)S(1)} %shard_map.108.after.terms), channel_id=1, source_target_pairs={{0,8},{8,0},{16,24},{24,16},{1,9},{9,1},{17,25},{25,17},{2,10},{10... | collective-permute-start | bytes 196616 | tf_op jit(solution)/shard_map/ppermute | solution.py:50
  48.4 1.3 %collective-permute-start.18 = (bf16[64,512]{1,0:T(8,128)(2,1)S(1)}, bf16[64,512]{1,0:T(8,128)(2,1)S(1)}, u32[]{:S(2)}, u32[]{:S(2)}) collective-permute-start(bf16[64,512]{1,0:T(8,128)(2,1)S(1)} %shard_map.110.others), channel_id=1, source_target_pairs={{0,8},{8,0},{16,24},{24,16},{1,9},{9,1},{17,25},{25,17},{2,10},{10... | collective-permute-start | bytes 196616 | tf_op jit(solution)/shard_map/ppermute | solution.py:50
  50.3 5.4 %collective-permute-start.19 = (bf16[16,2304]{1,0:T(8,128)(2,1)S(1)}, bf16[16,2304]{1,0:T(8,128)(2,1)S(1)}, u32[]{:S(2)}, u32[]{:S(2)}) collective-permute-start(bf16[16,2304]{1,0:T(8,128)(2,1)S(1)} %get-tuple-element.48), channel_id=1, source_target_pairs={{0,3},{1,2},{2,1},{3,0},{4,7},{5,6},{6,5},{7,4},{8,11},{9,10},{10,... | collective-permute-start | bytes 221192 | tf_op jit(solution)/shard_map/ppermute | solution.py:62
  52.0 5.1 %collective-permute-start.20 = (bf16[16,2304]{1,0:T(8,128)(2,1)S(1)}, bf16[16,2304]{1,0:T(8,128)(2,1)S(1)}, u32[]{:S(2)}, u32[]{:S(2)}) collective-permute-start(bf16[16,2304]{1,0:T(8,128)(2,1)S(1)} %get-tuple-element.49), channel_id=1, source_target_pairs={{0,1},{1,0},{2,3},{3,2},{4,5},{5,4},{6,7},{7,6},{8,9},{9,8},{10,11... | collective-permute-start | bytes 221192 | tf_op jit(solution)/shard_map/ppermute | solution.py:62
  52.8 4.7 %collective-permute-start.21 = (bf16[16,2304]{1,0:T(8,128)(2,1)S(1)}, bf16[16,2304]{1,0:T(8,128)(2,1)S(1)}, u32[]{:S(2)}, u32[]{:S(2)}) collective-permute-start(bf16[16,2304]{1,0:T(8,128)(2,1)S(1)} %get-tuple-element.50), channel_id=1, source_target_pairs={{0,2},{1,3},{2,0},{3,1},{4,6},{5,7},{6,4},{7,5},{8,10},{9,11},{10,... | collective-permute-start | bytes 221192 | tf_op jit(solution)/shard_map/ppermute | solution.py:62
  57.5 4.9 %collective-permute-start.22 = (bf16[8,2304]{1,0:T(8,128)(2,1)S(1)}, bf16[8,2304]{1,0:T(8,128)(2,1)S(1)}, u32[]{:S(2)}, u32[]{:S(2)}) collective-permute-start(bf16[8,2304]{1,0:T(8,128)(2,1)S(1)} %get-tuple-element.53), channel_id=1, source_target_pairs={{0,4},{1,5},{2,6},{3,7},{4,0},{5,1},{6,2},{7,3},{8,12},{9,13},{10,... | collective-permute-start | bytes 110600 | tf_op jit(solution)/shard_map/ppermute | solution.py:68

commit v12 on v11

--- a/solution.py
+++ b/solution.py
@@ -76,6 +76,10 @@
     return lax.rem(lax.axis_index("feat"), lax.axis_size("feat") // 2)
 
 
+def nearest_last(came):
+    return [came[0], *came[:0:-1]]
+
+
 def last(came):
     return [*came[:2:-1], *came[1:3], came[0]]
 
@@ -235,7 +239,7 @@
     given = (enc_bias, threshold, dec)
     slope, part = call(functools.partial(decode, False), [by_feature, whole], *mine, *given, dec_turned)
     slope_other, *decoded = call(functools.partial(decode, True), [by_feature, *by_group], *theirs, *given, part)
-    one, other = call(add_pair, [near(pair, wide), near(pair, half)], *reversed(trade(decoded)))
+    one, other = call(add_pair, [near(pair, wide), near(pair, half)], *nearest_last(trade(decoded)))
     error, error_pair, squared = call(
         compare,
         [near(own, wide), near(pair, half), near((1, tok_dev), wide)],

time: 63.3 us -> 63.3 us (level)
  no operation moved by 1% of the time
where the time goes in v12:
time: 63.3 us; the launch traced here: 63.1 us
  starting transfers between devices  27.4 us (43%)
  waiting for transfers between devices  25.3 us (40%)
  Pallas kernels  9.59 us (15%)
  between operations  0.8 us (1%)
    ppermute x12, starting transfers between devices, trade(): came[k] = lax.ppermute(pieces[k], 'feat', [(i, i ^ k) for i in range(n)])  14.1 us
    ppermute x12, waiting for transfers between devices, trade(): came[k] = lax.ppermute(pieces[k], 'feat', [(i, i ^ k) for i in range(n)])  13.6 us
    pallas_call x22, Pallas kernels, call(): pl.pallas_call(body, out_shape=outs, in_specs=[away] * fetched + [here] *...  9.59 us
    ppermute x3, starting transfers between devices, mirror(): lax.ppermute(block, 'feat', [(i, (i + n // 2) % n) for i in range(n)])  9.47 us
    ppermute x3, waiting for transfers between devices, mirror(): lax.ppermute(block, 'feat', [(i, (i + n // 2) % n) for i in range(n)])  7.02 us
    ppermute x2, starting transfers between devices, layer_sum(): far = lax.ppermute(pair, 'layer', far_off)  2.57 us
    ppermute x2, waiting for transfers between devices, layer_sum(): far = lax.ppermute(pair, 'layer', far_off)  2.25 us
    ppermute x2, waiting for transfers between devices, layer_sum(): theirs = lax.ppermute(make(True), 'layer', near_by)  1.36 us
  transfers between devices with their start and end apart: 23, of which 19 were waited for; matrix products, arithmetic and copies ran while one was open for 0% of the time, Pallas kernels for 10%

profile of v12, /device:TPU:0, one launch (start us, length us, event | category | flops | bytes accessed | tf_op | source)
XLA Modules:
  0.0 63.1 jit_solution(7787142092608799914)
XLA Ops:
  0.6 4.1 %collective-permute-start = (bf16[8,2304]{1,0:T(8,128)(2,1)}, bf16[8,2304]{1,0:T(8,128)(2,1)S(1)}, u32[]{:S(2)}, u32[]{:S(2)}) collective-permute-start(bf16[8,2304]{1,0:T(8,128)(2,1)} %bitcast.22), channel_id=1, source_target_pairs={{0,4},{1,5},{2,6},{3,7},{4,0},{5,1},{6,2},{7,3},{8,12},{9,13},{10,... | collective-permute-start | bytes 110600 | tf_op jit(solution)/shard_map/ppermute | solution.py:68
  4.7 0.8 %shard_map.94 = (bf16[8,2304]{1,0:T(8,128)(2,1)S(1)}, f32[1,1024]{1,0:T(1,128)S(1)}, f32[1,1024]{1,0:T(1,128)S(1)}) custom-call(bf16[8,2304]{1,0:T(8,128)(2,1)} %bitcast.23, f32[1,1024]{1,0:T(1,128)} %bitcast.24, f32[1,1024]{1,0:T(1,128)} %bitcast.25), custom_call_target="tpu_custom_call" | custom-call | bytes 90112 | tf_op jit(solution)/shard_map/pallas_call | solution.py:29
  5.6 1.7 %collective-permute-done.other = bf16[8,2304]{1,0:T(8,128)(2,1)S(1)} collective-permute-done((bf16[8,2304]{1,0:T(8,128)(2,1)}, bf16[8,2304]{1,0:T(8,128)(2,1)S(1)}, u32[]{:S(2)}, u32[]{:S(2)}) %collective-permute-start) | collective-permute-done | bytes 36896 | tf_op jit(solution)/shard_map/ppermute | solution.py:68
  7.3 2.5 %collective-permute-start.3 = (bf16[16,2304]{1,0:T(8,128)(2,1)S(1)}, bf16[16,2304]{1,0:T(8,128)(2,1)S(1)}, u32[]{:S(2)}, u32[]{:S(2)}) collective-permute-start(bf16[16,2304]{1,0:T(8,128)(2,1)S(1)} %shard_map.96.rest_0_.acts), channel_id=1, source_target_pairs={{0,3},{1,2},{2,1},{3,0},{4,7},{5,6},{6,5},{7,4},{8,11},{9,10},{10,... | collective-permute-start | bytes 221192 | tf_op jit(solution)/shard_map/ppermute | solution.py:62
  9.9 0.7 %collective-permute-start.2 = (bf16[16,2304]{1,0:T(8,128)(2,1)S(1)}, bf16[16,2304]{1,0:T(8,128)(2,1)S(1)}, u32[]{:S(2)}, u32[]{:S(2)}) collective-permute-start(bf16[16,2304]{1,0:T(8,128)(2,1)S(1)} %shard_map.96.rest_0_.acts), channel_id=1, source_target_pairs={{0,2},{1,3},{2,0},{3,1},{4,6},{5,7},{6,4},{7,5},{8,10},{9,11},{10,... | collective-permute-start | bytes 221192 | tf_op jit(solution)/shard_map/ppermute | solution.py:62
  10.9 1.8 %collective-permute-done.3.rest_3_ = bf16[16,2304]{1,0:T(8,128)(2,1)S(1)} collective-permute-done((bf16[16,2304]{1,0:T(8,128)(2,1)S(1)}, bf16[16,2304]{1,0:T(8,128)(2,1)S(1)}, u32[]{:S(2)}, u32[]{:S(2)}) %collective-permute-start.3) | collective-permute-done | bytes 73760 | tf_op jit(solution)/shard_map/ppermute | solution.py:62
  12.7 1.6 %collective-permute-done.2.rest_2_ = bf16[16,2304]{1,0:T(8,128)(2,1)S(1)} collective-permute-done((bf16[16,2304]{1,0:T(8,128)(2,1)S(1)}, bf16[16,2304]{1,0:T(8,128)(2,1)S(1)}, u32[]{:S(2)}, u32[]{:S(2)}) %collective-permute-start.2) | collective-permute-done | bytes 73760 | tf_op jit(solution)/shard_map/ppermute | solution.py:62
  14.2 0.7 %collective-permute-done.1.rest_1_ = bf16[16,2304]{1,0:T(8,128)(2,1)S(1)} collective-permute-done((bf16[16,2304]{1,0:T(8,128)(2,1)S(1)}, bf16[16,2304]{1,0:T(8,128)(2,1)S(1)}, u32[]{:S(2)}, u32[]{:S(2)}) %collective-permute-start.1) | collective-permute-done | bytes 73760 | tf_op jit(solution)/shard_map/ppermute | solution.py:62
  15.0 0.5 shard_map.98
  15.6 0.6 shard_map.97.one
  16.2 0.7 %collective-permute-done.4.other = bf16[64,512]{1,0:T(8,128)(2,1)S(1)} collective-permute-done((bf16[64,512]{1,0:T(8,128)(2,1)S(1)}, bf16[64,512]{1,0:T(8,128)(2,1)S(1)}, u32[]{:S(2)}, u32[]{:S(2)}) %collective-permute-start.4) | collective-permute-done | bytes 65568 | tf_op jit(solution)/shard_map/ppermute | solution.py:44
  16.9 1.3 %collective-permute-start.5 = (bf16[64,512]{1,0:T(8,128)(2,1)S(1)}, bf16[64,512]{1,0:T(8,128)(2,1)S(1)}, u32[]{:S(2)}, u32[]{:S(2)}) collective-permute-start(bf16[64,512]{1,0:T(8,128)(2,1)S(1)} %shard_map.99.after.terms), channel_id=1, source_target_pairs={{0,24},{8,16},{16,8},{24,0},{1,25},{9,17},{17,9},{25,1},{2,26},{10... | collective-permute-start | bytes 196616 | tf_op jit(solution)/shard_map/ppermute | solution.py:48
  18.2 0.4 collective-permute-start.7
  18.5 1.4 %shard_map.100.refs_0_.before.weight = bf16[2304,1024]{1,0:T(8,128)(2,1)S(1)} custom-call(bf16[1024,2304]{1,0:T(8,128)(2,1)S(1)} %bitcast.17, bf16[64,512]{1,0:T(8,128)(2,1)S(1)} %shard_map.99.after.terms), custom_call_target="tpu_custom_call" | custom-call | bytes 9568256 | tf_op jit(solution)/shard_map/pallas_call | solution.py:29
  20.0 1.0 %collective-permute-done.5.refs_1_ = bf16[64,512]{1,0:T(8,128)(2,1)S(1)} collective-permute-done((bf16[64,512]{1,0:T(8,128)(2,1)S(1)}, bf16[64,512]{1,0:T(8,128)(2,1)S(1)}, u32[]{:S(2)}, u32[]{:S(2)}) %collective-permute-start.5) | collective-permute-done | bytes 65568 | tf_op jit(solution)/shard_map/ppermute | solution.py:48
  21.1 0.5 shard_map.102
  21.7 0.5 collective-permute-done.6.others
  22.2 0.5 shard_map.103
  22.8 1.3 %collective-permute-start.8 = (bf16[16,2304]{1,0:T(8,128)(2,1)S(1)}, bf16[16,2304]{1,0:T(8,128)(2,1)S(1)}, u32[]{:S(2)}, u32[]{:S(2)}) collective-permute-start(bf16[16,2304]{1,0:T(8,128)(2,1)S(1)} %get-tuple-element.34), channel_id=1, source_target_pairs={{0,3},{1,2},{2,1},{3,0},{4,7},{5,6},{6,5},{7,4},{8,11},{9,10},{10,... | collective-permute-start | bytes 221192 | tf_op jit(solution)/shard_map/ppermute | solution.py:62
  24.1 0.5 collective-permute-start.9
  24.6 1.7 %collective-permute-start.10 = (bf16[16,2304]{1,0:T(8,128)(2,1)S(1)}, bf16[16,2304]{1,0:T(8,128)(2,1)S(1)}, u32[]{:S(2)}, u32[]{:S(2)}) collective-permute-start(bf16[16,2304]{1,0:T(8,128)(2,1)S(1)} %get-tuple-element.36), channel_id=1, source_target_pairs={{0,1},{1,0},{2,3},{3,2},{4,5},{5,4},{6,7},{7,6},{8,9},{9,8},{10,11... | collective-permute-start | bytes 221192 | tf_op jit(solution)/shard_map/ppermute | solution.py:62
  26.3 2.3 %collective-permute-done.8.refs_1_ = bf16[16,2304]{1,0:T(8,128)(2,1)S(1)} collective-permute-done((bf16[16,2304]{1,0:T(8,128)(2,1)S(1)}, bf16[16,2304]{1,0:T(8,128)(2,1)S(1)}, u32[]{:S(2)}, u32[]{:S(2)}) %collective-permute-start.8) | collective-permute-done | bytes 73760 | tf_op jit(solution)/shard_map/ppermute | solution.py:62
  28.7 1.0 %collective-permute-done.10.refs_3_ = bf16[16,2304]{1,0:T(8,128)(2,1)S(1)} collective-permute-done((bf16[16,2304]{1,0:T(8,128)(2,1)S(1)}, bf16[16,2304]{1,0:T(8,128)(2,1)S(1)}, u32[]{:S(2)}, u32[]{:S(2)}) %collective-permute-start.10) | collective-permute-done | bytes 73760 | tf_op jit(solution)/shard_map/ppermute | solution.py:62
  29.7 2.4 %collective-permute-start.11 = (bf16[16,2304]{1,0:T(8,128)(2,1)S(1)}, bf16[16,2304]{1,0:T(8,128)(2,1)S(1)}, u32[]{:S(2)}, u32[]{:S(2)}) collective-permute-start(bf16[16,2304]{1,0:T(8,128)(2,1)S(1)} %get-tuple-element.38), channel_id=1, source_target_pairs={{0,4},{1,5},{2,6},{3,7},{4,0},{5,1},{6,2},{7,3},{8,12},{9,13},{10,... | collective-permute-start | bytes 221192 | tf_op jit(solution)/shard_map/ppermute | solution.py:68
  32.1 4.1 %collective-permute-done.11.other = bf16[16,2304]{1,0:T(8,128)(2,1)S(1)} collective-permute-done((bf16[16,2304]{1,0:T(8,128)(2,1)S(1)}, bf16[16,2304]{1,0:T(8,128)(2,1)S(1)}, u32[]{:S(2)}, u32[]{:S(2)}) %collective-permute-start.11) | collective-permute-done | bytes 73760 | tf_op jit(solution)/shard_map/ppermute | solution.py:68
  36.4 0.7 %collective-permute-start.14 = (bf16[16,2304]{1,0:T(8,128)(2,1)S(1)}, bf16[16,2304]{1,0:T(8,128)(2,1)S(1)}, u32[]{:S(2)}, u32[]{:S(2)}) collective-permute-start(bf16[16,2304]{1,0:T(8,128)(2,1)S(1)} %get-tuple-element.39.rest_0_), channel_id=1, source_target_pairs={{0,3},{1,2},{2,1},{3,0},{4,7},{5,6},{6,5},{7,4},{8,11},{9,10},{10,... | collective-permute-start | bytes 221192 | tf_op jit(solution)/shard_map/ppermute | solution.py:62
  37.0 0.7 %collective-permute-start.13 = (bf16[16,2304]{1,0:T(8,128)(2,1)S(1)}, bf16[16,2304]{1,0:T(8,128)(2,1)S(1)}, u32[]{:S(2)}, u32[]{:S(2)}) collective-permute-start(bf16[16,2304]{1,0:T(8,128)(2,1)S(1)} %get-tuple-element.39.rest_0_), channel_id=1, source_target_pairs={{0,2},{1,3},{2,0},{3,1},{4,6},{5,7},{6,4},{7,5},{8,10},{9,11},{10,... | collective-permute-start | bytes 221192 | tf_op jit(solution)/shard_map/ppermute | solution.py:62
  37.7 2.2 %collective-permute-start.12 = (bf16[16,2304]{1,0:T(8,128)(2,1)S(1)}, bf16[16,2304]{1,0:T(8,128)(2,1)S(1)}, u32[]{:S(2)}, u32[]{:S(2)}) collective-permute-start(bf16[16,2304]{1,0:T(8,128)(2,1)S(1)} %get-tuple-element.39.rest_0_), channel_id=1, source_target_pairs={{0,1},{1,0},{2,3},{3,2},{4,5},{5,4},{6,7},{7,6},{8,9},{9,8},{10,11... | collective-permute-start | bytes 221192 | tf_op jit(solution)/shard_map/ppermute | solution.py:62
  39.9 1.8 %collective-permute-done.14.rest_3_ = bf16[16,2304]{1,0:T(8,128)(2,1)S(1)} collective-permute-done((bf16[16,2304]{1,0:T(8,128)(2,1)S(1)}, bf16[16,2304]{1,0:T(8,128)(2,1)S(1)}, u32[]{:S(2)}, u32[]{:S(2)}) %collective-permute-start.14) | collective-permute-done | bytes 73760 | tf_op jit(solution)/shard_map/ppermute | solution.py:62
  41.7 0.8 %collective-permute-done.12.rest_1_ = bf16[16,2304]{1,0:T(8,128)(2,1)S(1)} collective-permute-done((bf16[16,2304]{1,0:T(8,128)(2,1)S(1)}, bf16[16,2304]{1,0:T(8,128)(2,1)S(1)}, u32[]{:S(2)}, u32[]{:S(2)}) %collective-permute-start.12) | collective-permute-done | bytes 73760 | tf_op jit(solution)/shard_map/ppermute | solution.py:62
  42.4 0.5 shard_map.107.before
  43.1 0.6 shard_map.106.one
  43.6 0.7 %collective-permute-done.15.other = bf16[64,512]{1,0:T(8,128)(2,1)S(1)} collective-permute-done((bf16[64,512]{1,0:T(8,128)(2,1)S(1)}, bf16[64,512]{1,0:T(8,128)(2,1)S(1)}, u32[]{:S(2)}, u32[]{:S(2)}) %collective-permute-start.15) | collective-permute-done | bytes 65568 | tf_op jit(solution)/shard_map/ppermute | solution.py:44
  44.3 1.3 %collective-permute-start.17 = (bf16[64,512]{1,0:T(8,128)(2,1)S(1)}, bf16[64,512]{1,0:T(8,128)(2,1)S(1)}, u32[]{:S(2)}, u32[]{:S(2)}) collective-permute-start(bf16[64,512]{1,0:T(8,128)(2,1)S(1)} %shard_map.108.after.terms), channel_id=1, source_target_pairs={{0,24},{8,16},{16,8},{24,0},{1,25},{9,17},{17,9},{25,1},{2,26},{10... | collective-permute-start | bytes 196616 | tf_op jit(solution)/shard_map/ppermute | solution.py:48
  45.9 1.3 %shard_map.109.refs_0_.weight = bf16[1024,2304]{1,0:T(8,128)(2,1)S(1)} custom-call(bf16[2304,1024]{1,0:T(8,128)(2,1)S(1)} %bitcast.13, bf16[64,512]{1,0:T(8,128)(2,1)S(1)} %shard_map.108.after.terms), custom_call_target="tpu_custom_call" | custom-call | bytes 9568256 | tf_op jit(solution)/shard_map/pallas_call | solution.py:29
  47.2 1.2 %collective-permute-done.17.refs_1_ = bf16[64,512]{1,0:T(8,128)(2,1)S(1)} collective-permute-done((bf16[64,512]{1,0:T(8,128)(2,1)S(1)}, bf16[64,512]{1,0:T(8,128)(2,1)S(1)}, u32[]{:S(2)}, u32[]{:S(2)}) %collective-permute-start.17) | collective-permute-done | bytes 65568 | tf_op jit(solution)/shard_map/ppermute | solution.py:48
  48.6 0.6 shard_map.111
  49.2 0.5 collective-permute-done.18.others
  49.7 0.5 shard_map.112
  50.3 1.8 %collective-permute-start.19 = (bf16[16,2304]{1,0:T(8,128)(2,1)S(1)}, bf16[16,2304]{1,0:T(8,128)(2,1)S(1)}, u32[]{:S(2)}, u32[]{:S(2)}) collective-permute-start(bf16[16,2304]{1,0:T(8,128)(2,1)S(1)} %get-tuple-element.48), channel_id=1, source_target_pairs={{0,3},{1,2},{2,1},{3,0},{4,7},{5,6},{6,5},{7,4},{8,11},{9,10},{10,... | collective-permute-start | bytes 221192 | tf_op jit(solution)/shard_map/ppermute | solution.py:62
  52.0 0.7 %collective-permute-start.20 = (bf16[16,2304]{1,0:T(8,128)(2,1)S(1)}, bf16[16,2304]{1,0:T(8,128)(2,1)S(1)}, u32[]{:S(2)}, u32[]{:S(2)}) collective-permute-start(bf16[16,2304]{1,0:T(8,128)(2,1)S(1)} %get-tuple-element.49), channel_id=1, source_target_pairs={{0,1},{1,0},{2,3},{3,2},{4,5},{5,4},{6,7},{7,6},{8,9},{9,8},{10,11... | collective-permute-start | bytes 221192 | tf_op jit(solution)/shard_map/ppermute | solution.py:62
  52.8 1.0 %collective-permute-start.21 = (bf16[16,2304]{1,0:T(8,128)(2,1)S(1)}, bf16[16,2304]{1,0:T(8,128)(2,1)S(1)}, u32[]{:S(2)}, u32[]{:S(2)}) collective-permute-start(bf16[16,2304]{1,0:T(8,128)(2,1)S(1)} %get-tuple-element.50), channel_id=1, source_target_pairs={{0,2},{1,3},{2,0},{3,1},{4,6},{5,7},{6,4},{7,5},{8,10},{9,11},{10,... | collective-permute-start | bytes 221192 | tf_op jit(solution)/shard_map/ppermute | solution.py:62
  53.8 1.8 %collective-permute-done.19.refs_0_ = bf16[16,2304]{1,0:T(8,128)(2,1)S(1)} collective-permute-done((bf16[16,2304]{1,0:T(8,128)(2,1)S(1)}, bf16[16,2304]{1,0:T(8,128)(2,1)S(1)}, u32[]{:S(2)}, u32[]{:S(2)}) %collective-permute-start.19) | collective-permute-done | bytes 73760 | tf_op jit(solution)/shard_map/ppermute | solution.py:62
  55.7 1.5 %collective-permute-done.20.refs_1_ = bf16[16,2304]{1,0:T(8,128)(2,1)S(1)} collective-permute-done((bf16[16,2304]{1,0:T(8,128)(2,1)S(1)}, bf16[16,2304]{1,0:T(8,128)(2,1)S(1)}, u32[]{:S(2)}, u32[]{:S(2)}) %collective-permute-start.20) | collective-permute-done | bytes 73760 | tf_op jit(solution)/shard_map/ppermute | solution.py:62
  57.5 3.0 %collective-permute-start.22 = (bf16[8,2304]{1,0:T(8,128)(2,1)S(1)}, bf16[8,2304]{1,0:T(8,128)(2,1)S(1)}, u32[]{:S(2)}, u32[]{:S(2)}) collective-permute-start(bf16[8,2304]{1,0:T(8,128)(2,1)S(1)} %get-tuple-element.53), channel_id=1, source_target_pairs={{0,4},{1,5},{2,6},{3,7},{4,0},{5,1},{6,2},{7,3},{8,12},{9,13},{10,... | collective-permute-start | bytes 110600 | tf_op jit(solution)/shard_map/ppermute | solution.py:68
  60.5 0.7 %shard_map.113 = (f32[64,1024]{1,0:T(8,128)}, f32[1,8]{1,0:T(1,128)}) custom-call(f32[64,512]{1,0:T(8,128)S(1)} %get-tuple-element.41.grad, f32[64,512]{1,0:T(8,128)S(1)} %get-tuple-element.44.grad_other, f32[1,8]{1,0:T(1,128)S(1)} %get-tuple-element.45.squared), custom_call_target="tpu_custom_call" | custom-call | bytes 524352 | tf_op jit(solution)/shard_map/pallas_call | solution.py:29
  61.2 1.2 %collective-permute-done.22.other = bf16[8,2304]{1,0:T(8,128)(2,1)S(1)} collective-permute-done((bf16[8,2304]{1,0:T(8,128)(2,1)S(1)}, bf16[8,2304]{1,0:T(8,128)(2,1)S(1)}, u32[]{:S(2)}, u32[]{:S(2)}) %collective-permute-start.22) | collective-permute-done | bytes 36896 | tf_op jit(solution)/shard_map/ppermute | solution.py:68
  62.4 0.6 %shard_map.115 = bf16[8,2304]{1,0:T(8,128)(2,1)} custom-call(f32[8,2304]{1,0:T(8,128)S(1)} %get-tuple-element.52.one, bf16[8,2304]{1,0:T(8,128)(2,1)S(1)} %collective-permute-done.22.other, f32[8,2304]{1,0:T(8,128)S(1)} %get-tuple-element.54.error), custom_call_target="tpu_custom_call" | custom-call | tf_op jit(solution)/shard_map/pallas_call | solution.py:29
  (34 shorter events, 1.8 us)
Async XLA Ops:
  0.6 6.6 %collective-permute-start = (bf16[8,2304]{1,0:T(8,128)(2,1)}, bf16[8,2304]{1,0:T(8,128)(2,1)S(1)}, u32[]{:S(2)}, u32[]{:S(2)}) collective-permute-start(bf16[8,2304]{1,0:T(8,128)(2,1)} %bitcast.22), channel_id=1, source_target_pairs={{0,4},{1,5},{2,6},{3,7},{4,0},{5,1},{6,2},{7,3},{8,12},{9,13},{10,... | collective-permute-start | bytes 110600 | tf_op jit(solution)/shard_map/ppermute | solution.py:68
  7.3 7.7 %slice-start = ((s8[4718592]{0:T(1024)(128)(4,1)}), s8[4194304]{0:T(1024)(128)(4,1)S(1)}, s32[]{:S(2)}) async-start(s8[4718592]{0:T(1024)(128)(4,1)} %bitcast.9), calls=%async_computation | async-start | bytes 8388608
  7.3 7.7 %slice-start.1 = ((s8[4718592]{0:T(1024)(128)(4,1)}), s8[524288]{0:T(1024)(128)(4,1)S(1)}, s32[]{:S(2)}) async-start(s8[4718592]{0:T(1024)(128)(4,1)} %bitcast.9), calls=%async_computation.1 | async-start | bytes 1048576
  7.3 11.2 %slice-start.2 = ((s8[4718592]{0:T(1024)(128)(4,1)}), s8[4194304]{0:T(1024)(128)(4,1)S(1)}, s32[]{:S(2)}) async-start(s8[4718592]{0:T(1024)(128)(4,1)} %bitcast.15), calls=%async_computation.2 | async-start | bytes 8388608
  7.3 11.2 %slice-start.3 = ((s8[4718592]{0:T(1024)(128)(4,1)}), s8[524288]{0:T(1024)(128)(4,1)S(1)}, s32[]{:S(2)}) async-start(s8[4718592]{0:T(1024)(128)(4,1)} %bitcast.15), calls=%async_computation.3 | async-start | bytes 1048576
  7.3 5.3 %collective-permute-start.3 = (bf16[16,2304]{1,0:T(8,128)(2,1)S(1)}, bf16[16,2304]{1,0:T(8,128)(2,1)S(1)}, u32[]{:S(2)}, u32[]{:S(2)}) collective-permute-start(bf16[16,2304]{1,0:T(8,128)(2,1)S(1)} %shard_map.96.rest_0_.acts), channel_id=1, source_target_pairs={{0,3},{1,2},{2,1},{3,0},{4,7},{5,6},{6,5},{7,4},{8,11},{9,10},{10,... | collective-permute-start | bytes 221192 | tf_op jit(solution)/shard_map/ppermute | solution.py:62
  9.9 4.4 %collective-permute-start.2 = (bf16[16,2304]{1,0:T(8,128)(2,1)S(1)}, bf16[16,2304]{1,0:T(8,128)(2,1)S(1)}, u32[]{:S(2)}, u32[]{:S(2)}) collective-permute-start(bf16[16,2304]{1,0:T(8,128)(2,1)S(1)} %shard_map.96.rest_0_.acts), channel_id=1, source_target_pairs={{0,2},{1,3},{2,0},{3,1},{4,6},{5,7},{6,4},{7,5},{8,10},{9,11},{10,... | collective-permute-start | bytes 221192 | tf_op jit(solution)/shard_map/ppermute | solution.py:62
  10.6 4.4 %collective-permute-start.1 = (bf16[16,2304]{1,0:T(8,128)(2,1)S(1)}, bf16[16,2304]{1,0:T(8,128)(2,1)S(1)}, u32[]{:S(2)}, u32[]{:S(2)}) collective-permute-start(bf16[16,2304]{1,0:T(8,128)(2,1)S(1)} %shard_map.96.rest_0_.acts), channel_id=1, source_target_pairs={{0,1},{1,0},{2,3},{3,2},{4,5},{5,4},{6,7},{7,6},{8,9},{9,8},{10,11... | collective-permute-start | bytes 221192 | tf_op jit(solution)/shard_map/ppermute | solution.py:62
  15.5 1.3 %collective-permute-start.4 = (bf16[64,512]{1,0:T(8,128)(2,1)S(1)}, bf16[64,512]{1,0:T(8,128)(2,1)S(1)}, u32[]{:S(2)}, u32[]{:S(2)}) collective-permute-start(bf16[64,512]{1,0:T(8,128)(2,1)S(1)} %shard_map.98), channel_id=1, source_target_pairs={{0,8},{8,0},{16,24},{24,16},{1,9},{9,1},{17,25},{25,17},{2,10},{10... | collective-permute-start | bytes 196616 | tf_op jit(solution)/shard_map/ppermute | solution.py:44
  16.9 4.1 %collective-permute-start.5 = (bf16[64,512]{1,0:T(8,128)(2,1)S(1)}, bf16[64,512]{1,0:T(8,128)(2,1)S(1)}, u32[]{:S(2)}, u32[]{:S(2)}) collective-permute-start(bf16[64,512]{1,0:T(8,128)(2,1)S(1)} %shard_map.99.after.terms), channel_id=1, source_target_pairs={{0,24},{8,16},{16,8},{24,0},{1,25},{9,17},{17,9},{25,1},{2,26},{10... | collective-permute-start | bytes 196616 | tf_op jit(solution)/shard_map/ppermute | solution.py:48
  18.2 3.0 %collective-permute-start.7 = (bf16[64,512]{1,0:T(8,128)(2,1)S(1)}, bf16[64,512]{1,0:T(8,128)(2,1)S(1)}, u32[]{:S(2)}, u32[]{:S(2)}) collective-permute-start(bf16[64,512]{1,0:T(8,128)(2,1)S(1)} %shard_map.99.after.terms), channel_id=1, source_target_pairs={{0,8},{8,0},{16,24},{24,16},{1,9},{9,1},{17,25},{25,17},{2,10},{10... | collective-permute-start | bytes 196616 | tf_op jit(solution)/shard_map/ppermute | solution.py:50
  21.0 1.3 %collective-permute-start.6 = (bf16[64,512]{1,0:T(8,128)(2,1)S(1)}, bf16[64,512]{1,0:T(8,128)(2,1)S(1)}, u32[]{:S(2)}, u32[]{:S(2)}) collective-permute-start(bf16[64,512]{1,0:T(8,128)(2,1)S(1)} %shard_map.101.others), channel_id=1, source_target_pairs={{0,8},{8,0},{16,24},{24,16},{1,9},{9,1},{17,25},{25,17},{2,10},{10... | collective-permute-start | bytes 196616 | tf_op jit(solution)/shard_map/ppermute | solution.py:50
  21.7 14.5 %copy-start = (f32[1,2304]{1,0:T(1,128)S(1)}, f32[1,2304]{1,0:T(1,128)}, u32[]{:S(2)}) copy-start(f32[1,2304]{1,0:T(1,128)} %dec_bias.1) | copy-start | bytes 27652
  21.7 14.5 %copy-start.1 = (s32[64]{0:T(128)S(1)}, s32[64]{0:T(128)}, u32[]{:S(2)}) copy-start(s32[64]{0:T(128)} %param.13) | copy-start | bytes 772
  22.8 5.9 %collective-permute-start.8 = (bf16[16,2304]{1,0:T(8,128)(2,1)S(1)}, bf16[16,2304]{1,0:T(8,128)(2,1)S(1)}, u32[]{:S(2)}, u32[]{:S(2)}) collective-permute-start(bf16[16,2304]{1,0:T(8,128)(2,1)S(1)} %get-tuple-element.34), channel_id=1, source_target_pairs={{0,3},{1,2},{2,1},{3,0},{4,7},{5,6},{6,5},{7,4},{8,11},{9,10},{10,... | collective-permute-start | bytes 221192 | tf_op jit(solution)/shard_map/ppermute | solution.py:62
  24.1 4.6 %collective-permute-start.9 = (bf16[16,2304]{1,0:T(8,128)(2,1)S(1)}, bf16[16,2304]{1,0:T(8,128)(2,1)S(1)}, u32[]{:S(2)}, u32[]{:S(2)}) collective-permute-start(bf16[16,2304]{1,0:T(8,128)(2,1)S(1)} %get-tuple-element.35), channel_id=1, source_target_pairs={{0,2},{1,3},{2,0},{3,1},{4,6},{5,7},{6,4},{7,5},{8,10},{9,11},{10,... | collective-permute-start | bytes 221192 | tf_op jit(solution)/shard_map/ppermute | solution.py:62
  24.6 5.1 %collective-permute-start.10 = (bf16[16,2304]{1,0:T(8,128)(2,1)S(1)}, bf16[16,2304]{1,0:T(8,128)(2,1)S(1)}, u32[]{:S(2)}, u32[]{:S(2)}) collective-permute-start(bf16[16,2304]{1,0:T(8,128)(2,1)S(1)} %get-tuple-element.36), channel_id=1, source_target_pairs={{0,1},{1,0},{2,3},{3,2},{4,5},{5,4},{6,7},{7,6},{8,9},{9,8},{10,11... | collective-permute-start | bytes 221192 | tf_op jit(solution)/shard_map/ppermute | solution.py:62
  29.7 6.5 %collective-permute-start.11 = (bf16[16,2304]{1,0:T(8,128)(2,1)S(1)}, bf16[16,2304]{1,0:T(8,128)(2,1)S(1)}, u32[]{:S(2)}, u32[]{:S(2)}) collective-permute-start(bf16[16,2304]{1,0:T(8,128)(2,1)S(1)} %get-tuple-element.38), channel_id=1, source_target_pairs={{0,4},{1,5},{2,6},{3,7},{4,0},{5,1},{6,2},{7,3},{8,12},{9,13},{10,... | collective-permute-start | bytes 221192 | tf_op jit(solution)/shard_map/ppermute | solution.py:68
  36.4 5.3 %collective-permute-start.14 = (bf16[16,2304]{1,0:T(8,128)(2,1)S(1)}, bf16[16,2304]{1,0:T(8,128)(2,1)S(1)}, u32[]{:S(2)}, u32[]{:S(2)}) collective-permute-start(bf16[16,2304]{1,0:T(8,128)(2,1)S(1)} %get-tuple-element.39.rest_0_), channel_id=1, source_target_pairs={{0,3},{1,2},{2,1},{3,0},{4,7},{5,6},{6,5},{7,4},{8,11},{9,10},{10,... | collective-permute-start | bytes 221192 | tf_op jit(solution)/shard_map/ppermute | solution.py:62
  37.0 4.6 %collective-permute-start.13 = (bf16[16,2304]{1,0:T(8,128)(2,1)S(1)}, bf16[16,2304]{1,0:T(8,128)(2,1)S(1)}, u32[]{:S(2)}, u32[]{:S(2)}) collective-permute-start(bf16[16,2304]{1,0:T(8,128)(2,1)S(1)} %get-tuple-element.39.rest_0_), channel_id=1, source_target_pairs={{0,2},{1,3},{2,0},{3,1},{4,6},{5,7},{6,4},{7,5},{8,10},{9,11},{10,... | collective-permute-start | bytes 221192 | tf_op jit(solution)/shard_map/ppermute | solution.py:62
  37.7 4.7 %collective-permute-start.12 = (bf16[16,2304]{1,0:T(8,128)(2,1)S(1)}, bf16[16,2304]{1,0:T(8,128)(2,1)S(1)}, u32[]{:S(2)}, u32[]{:S(2)}) collective-permute-start(bf16[16,2304]{1,0:T(8,128)(2,1)S(1)} %get-tuple-element.39.rest_0_), channel_id=1, source_target_pairs={{0,1},{1,0},{2,3},{3,2},{4,5},{5,4},{6,7},{7,6},{8,9},{9,8},{10,11... | collective-permute-start | bytes 221192 | tf_op jit(solution)/shard_map/ppermute | solution.py:62
  43.0 1.3 %collective-permute-start.15 = (bf16[64,512]{1,0:T(8,128)(2,1)S(1)}, bf16[64,512]{1,0:T(8,128)(2,1)S(1)}, u32[]{:S(2)}, u32[]{:S(2)}) collective-permute-start(bf16[64,512]{1,0:T(8,128)(2,1)S(1)} %shard_map.107.before), channel_id=1, source_target_pairs={{0,8},{8,0},{16,24},{24,16},{1,9},{9,1},{17,25},{25,17},{2,10},{10... | collective-permute-start | bytes 196616 | tf_op jit(solution)/shard_map/ppermute | solution.py:44
  44.3 4.1 %collective-permute-start.17 = (bf16[64,512]{1,0:T(8,128)(2,1)S(1)}, bf16[64,512]{1,0:T(8,128)(2,1)S(1)}, u32[]{:S(2)}, u32[]{:S(2)}) collective-permute-start(bf16[64,512]{1,0:T(8,128)(2,1)S(1)} %shard_map.108.after.terms), channel_id=1, source_target_pairs={{0,24},{8,16},{16,8},{24,0},{1,25},{9,17},{17,9},{25,1},{2,26},{10... | collective-permute-start | bytes 196616 | tf_op jit(solution)/shard_map/ppermute | solution.py:48
  45.6 3.0 %collective-permute-start.16 = (bf16[64,512]{1,0:T(8,128)(2,1)S(1)}, bf16[64,512]{1,0:T(8,128)(2,1)S(1)}, u32[]{:S(2)}, u32[]{:S(2)}) collective-permute-start(bf16[64,512]{1,0:T(8,128)(2,1)S(1)} %shard_map.108.after.terms), channel_id=1, source_target_pairs={{0,8},{8,0},{16,24},{24,16},{1,9},{9,1},{17,25},{25,17},{2,10},{10... | collective-permute-start | bytes 196616 | tf_op jit(solution)/shard_map/ppermute | solution.py:50
  48.4 1.3 %collective-permute-start.18 = (bf16[64,512]{1,0:T(8,128)(2,1)S(1)}, bf16[64,512]{1,0:T(8,128)(2,1)S(1)}, u32[]{:S(2)}, u32[]{:S(2)}) collective-permute-start(bf16[64,512]{1,0:T(8,128)(2,1)S(1)} %shard_map.110.others), channel_id=1, source_target_pairs={{0,8},{8,0},{16,24},{24,16},{1,9},{9,1},{17,25},{25,17},{2,10},{10... | collective-permute-start | bytes 196616 | tf_op jit(solution)/shard_map/ppermute | solution.py:50
  50.3 5.4 %collective-permute-start.19 = (bf16[16,2304]{1,0:T(8,128)(2,1)S(1)}, bf16[16,2304]{1,0:T(8,128)(2,1)S(1)}, u32[]{:S(2)}, u32[]{:S(2)}) collective-permute-start(bf16[16,2304]{1,0:T(8,128)(2,1)S(1)} %get-tuple-element.48), channel_id=1, source_target_pairs={{0,3},{1,2},{2,1},{3,0},{4,7},{5,6},{6,5},{7,4},{8,11},{9,10},{10,... | collective-permute-start | bytes 221192 | tf_op jit(solution)/shard_map/ppermute | solution.py:62
  52.0 5.1 %collective-permute-start.20 = (bf16[16,2304]{1,0:T(8,128)(2,1)S(1)}, bf16[16,2304]{1,0:T(8,128)(2,1)S(1)}, u32[]{:S(2)}, u32[]{:S(2)}) collective-permute-start(bf16[16,2304]{1,0:T(8,128)(2,1)S(1)} %get-tuple-element.49), channel_id=1, source_target_pairs={{0,1},{1,0},{2,3},{3,2},{4,5},{5,4},{6,7},{7,6},{8,9},{9,8},{10,11... | collective-permute-start | bytes 221192 | tf_op jit(solution)/shard_map/ppermute | solution.py:62
  52.8 4.7 %collective-permute-start.21 = (bf16[16,2304]{1,0:T(8,128)(2,1)S(1)}, bf16[16,2304]{1,0:T(8,128)(2,1)S(1)}, u32[]{:S(2)}, u32[]{:S(2)}) collective-permute-start(bf16[16,2304]{1,0:T(8,128)(2,1)S(1)} %get-tuple-element.50), channel_id=1, source_target_pairs={{0,2},{1,3},{2,0},{3,1},{4,6},{5,7},{6,4},{7,5},{8,10},{9,11},{10,... | collective-permute-start | bytes 221192 | tf_op jit(solution)/shard_map/ppermute | solution.py:62
  57.5 4.9 %collective-permute-start.22 = (bf16[8,2304]{1,0:T(8,128)(2,1)S(1)}, bf16[8,2304]{1,0:T(8,128)(2,1)S(1)}, u32[]{:S(2)}, u32[]{:S(2)}) collective-permute-start(bf16[8,2304]{1,0:T(8,128)(2,1)S(1)} %get-tuple-element.53), channel_id=1, source_target_pairs={{0,4},{1,5},{2,6},{3,7},{4,0},{5,1},{6,2},{7,3},{8,12},{9,13},{10,... | collective-permute-start | bytes 110600 | tf_op jit(solution)/shard_map/ppermute | solution.py:68

commit v13 on v12

--- a/solution.py
+++ b/solution.py
@@ -81,7 +81,7 @@
 
 
 def last(came):
-    return [*came[:2:-1], *came[1:3], came[0]]
+    return [came[0], *came[:2:-1], *came[1:3]]
 
 
 def stack(refs):

time: 63.3 us -> 63.3 us (level)
  no operation moved by 1% of the time
where the time goes in v13:
time: 63.3 us; the launch traced here: 63.1 us
  starting transfers between devices  27.4 us (43%)
  waiting for transfers between devices  25.3 us (40%)
  Pallas kernels  9.59 us (15%)
  between operations  0.8 us (1%)
    ppermute x12, starting transfers between devices, trade(): came[k] = lax.ppermute(pieces[k], 'feat', [(i, i ^ k) for i in range(n)])  14.1 us
    ppermute x12, waiting for transfers between devices, trade(): came[k] = lax.ppermute(pieces[k], 'feat', [(i, i ^ k) for i in range(n)])  13.6 us
    pallas_call x22, Pallas kernels, call(): pl.pallas_call(body, out_shape=outs, in_specs=[away] * fetched + [here] *...  9.59 us
    ppermute x3, starting transfers between devices, mirror(): lax.ppermute(block, 'feat', [(i, (i + n // 2) % n) for i in range(n)])  9.47 us
    ppermute x3, waiting for transfers between devices, mirror(): lax.ppermute(block, 'feat', [(i, (i + n // 2) % n) for i in range(n)])  7.02 us
    ppermute x2, starting transfers between devices, layer_sum(): far = lax.ppermute(pair, 'layer', far_off)  2.57 us
    ppermute x2, waiting for transfers between devices, layer_sum(): far = lax.ppermute(pair, 'layer', far_off)  2.25 us
    ppermute x2, waiting for transfers between devices, layer_sum(): theirs = lax.ppermute(make(True), 'layer', near_by)  1.36 us
  transfers between devices with their start and end apart: 23, of which 19 were waited for; matrix products, arithmetic and copies ran while one was open for 0% of the time, Pallas kernels for 10%

profile of v13, /device:TPU:0, one launch (start us, length us, event | category | flops | bytes accessed | tf_op | source)
XLA Modules:
  0.0 63.1 jit_solution(5308314359658587600)
XLA Ops:
  0.6 4.1 %collective-permute-start = (bf16[8,2304]{1,0:T(8,128)(2,1)}, bf16[8,2304]{1,0:T(8,128)(2,1)S(1)}, u32[]{:S(2)}, u32[]{:S(2)}) collective-permute-start(bf16[8,2304]{1,0:T(8,128)(2,1)} %bitcast.22), channel_id=1, source_target_pairs={{0,4},{1,5},{2,6},{3,7},{4,0},{5,1},{6,2},{7,3},{8,12},{9,13},{10,... | collective-permute-start | bytes 110600 | tf_op jit(solution)/shard_map/ppermute | solution.py:68
  4.7 0.8 %shard_map.94 = (bf16[8,2304]{1,0:T(8,128)(2,1)S(1)}, f32[1,1024]{1,0:T(1,128)S(1)}, f32[1,1024]{1,0:T(1,128)S(1)}) custom-call(bf16[8,2304]{1,0:T(8,128)(2,1)} %bitcast.23, f32[1,1024]{1,0:T(1,128)} %bitcast.24, f32[1,1024]{1,0:T(1,128)} %bitcast.25), custom_call_target="tpu_custom_call" | custom-call | bytes 90112 | tf_op jit(solution)/shard_map/pallas_call | solution.py:29
  5.6 1.7 %collective-permute-done.other = bf16[8,2304]{1,0:T(8,128)(2,1)S(1)} collective-permute-done((bf16[8,2304]{1,0:T(8,128)(2,1)}, bf16[8,2304]{1,0:T(8,128)(2,1)S(1)}, u32[]{:S(2)}, u32[]{:S(2)}) %collective-permute-start) | collective-permute-done | bytes 36896 | tf_op jit(solution)/shard_map/ppermute | solution.py:68
  7.3 2.5 %collective-permute-start.3 = (bf16[16,2304]{1,0:T(8,128)(2,1)S(1)}, bf16[16,2304]{1,0:T(8,128)(2,1)S(1)}, u32[]{:S(2)}, u32[]{:S(2)}) collective-permute-start(bf16[16,2304]{1,0:T(8,128)(2,1)S(1)} %shard_map.96.rest_0_.acts), channel_id=1, source_target_pairs={{0,3},{1,2},{2,1},{3,0},{4,7},{5,6},{6,5},{7,4},{8,11},{9,10},{10,... | collective-permute-start | bytes 221192 | tf_op jit(solution)/shard_map/ppermute | solution.py:62
  9.9 0.7 %collective-permute-start.2 = (bf16[16,2304]{1,0:T(8,128)(2,1)S(1)}, bf16[16,2304]{1,0:T(8,128)(2,1)S(1)}, u32[]{:S(2)}, u32[]{:S(2)}) collective-permute-start(bf16[16,2304]{1,0:T(8,128)(2,1)S(1)} %shard_map.96.rest_0_.acts), channel_id=1, source_target_pairs={{0,2},{1,3},{2,0},{3,1},{4,6},{5,7},{6,4},{7,5},{8,10},{9,11},{10,... | collective-permute-start | bytes 221192 | tf_op jit(solution)/shard_map/ppermute | solution.py:62
  10.9 1.8 %collective-permute-done.3.rest_3_ = bf16[16,2304]{1,0:T(8,128)(2,1)S(1)} collective-permute-done((bf16[16,2304]{1,0:T(8,128)(2,1)S(1)}, bf16[16,2304]{1,0:T(8,128)(2,1)S(1)}, u32[]{:S(2)}, u32[]{:S(2)}) %collective-permute-start.3) | collective-permute-done | bytes 73760 | tf_op jit(solution)/shard_map/ppermute | solution.py:62
  12.7 1.6 %collective-permute-done.2.rest_2_ = bf16[16,2304]{1,0:T(8,128)(2,1)S(1)} collective-permute-done((bf16[16,2304]{1,0:T(8,128)(2,1)S(1)}, bf16[16,2304]{1,0:T(8,128)(2,1)S(1)}, u32[]{:S(2)}, u32[]{:S(2)}) %collective-permute-start.2) | collective-permute-done | bytes 73760 | tf_op jit(solution)/shard_map/ppermute | solution.py:62
  14.2 0.7 %collective-permute-done.1.rest_1_ = bf16[16,2304]{1,0:T(8,128)(2,1)S(1)} collective-permute-done((bf16[16,2304]{1,0:T(8,128)(2,1)S(1)}, bf16[16,2304]{1,0:T(8,128)(2,1)S(1)}, u32[]{:S(2)}, u32[]{:S(2)}) %collective-permute-start.1) | collective-permute-done | bytes 73760 | tf_op jit(solution)/shard_map/ppermute | solution.py:62
  15.0 0.5 shard_map.98
  15.6 0.6 shard_map.97.one
  16.2 0.7 %collective-permute-done.4.other = bf16[64,512]{1,0:T(8,128)(2,1)S(1)} collective-permute-done((bf16[64,512]{1,0:T(8,128)(2,1)S(1)}, bf16[64,512]{1,0:T(8,128)(2,1)S(1)}, u32[]{:S(2)}, u32[]{:S(2)}) %collective-permute-start.4) | collective-permute-done | bytes 65568 | tf_op jit(solution)/shard_map/ppermute | solution.py:44
  16.9 1.3 %collective-permute-start.5 = (bf16[64,512]{1,0:T(8,128)(2,1)S(1)}, bf16[64,512]{1,0:T(8,128)(2,1)S(1)}, u32[]{:S(2)}, u32[]{:S(2)}) collective-permute-start(bf16[64,512]{1,0:T(8,128)(2,1)S(1)} %shard_map.99.after.terms), channel_id=1, source_target_pairs={{0,24},{8,16},{16,8},{24,0},{1,25},{9,17},{17,9},{25,1},{2,26},{10... | collective-permute-start | bytes 196616 | tf_op jit(solution)/shard_map/ppermute | solution.py:48
  18.2 0.4 collective-permute-start.7
  18.5 1.4 %shard_map.100.refs_0_.before.weight = bf16[2304,1024]{1,0:T(8,128)(2,1)S(1)} custom-call(bf16[1024,2304]{1,0:T(8,128)(2,1)S(1)} %bitcast.17, bf16[64,512]{1,0:T(8,128)(2,1)S(1)} %shard_map.99.after.terms), custom_call_target="tpu_custom_call" | custom-call | bytes 9568256 | tf_op jit(solution)/shard_map/pallas_call | solution.py:29
  20.0 1.0 %collective-permute-done.5.refs_1_ = bf16[64,512]{1,0:T(8,128)(2,1)S(1)} collective-permute-done((bf16[64,512]{1,0:T(8,128)(2,1)S(1)}, bf16[64,512]{1,0:T(8,128)(2,1)S(1)}, u32[]{:S(2)}, u32[]{:S(2)}) %collective-permute-start.5) | collective-permute-done | bytes 65568 | tf_op jit(solution)/shard_map/ppermute | solution.py:48
  21.1 0.5 shard_map.102
  21.7 0.5 collective-permute-done.6.others
  22.2 0.5 shard_map.103
  22.8 1.3 %collective-permute-start.8 = (bf16[16,2304]{1,0:T(8,128)(2,1)S(1)}, bf16[16,2304]{1,0:T(8,128)(2,1)S(1)}, u32[]{:S(2)}, u32[]{:S(2)}) collective-permute-start(bf16[16,2304]{1,0:T(8,128)(2,1)S(1)} %get-tuple-element.34), channel_id=1, source_target_pairs={{0,3},{1,2},{2,1},{3,0},{4,7},{5,6},{6,5},{7,4},{8,11},{9,10},{10,... | collective-permute-start | bytes 221192 | tf_op jit(solution)/shard_map/ppermute | solution.py:62
  24.1 0.5 collective-permute-start.9
  24.6 1.7 %collective-permute-start.10 = (bf16[16,2304]{1,0:T(8,128)(2,1)S(1)}, bf16[16,2304]{1,0:T(8,128)(2,1)S(1)}, u32[]{:S(2)}, u32[]{:S(2)}) collective-permute-start(bf16[16,2304]{1,0:T(8,128)(2,1)S(1)} %get-tuple-element.36), channel_id=1, source_target_pairs={{0,1},{1,0},{2,3},{3,2},{4,5},{5,4},{6,7},{7,6},{8,9},{9,8},{10,11... | collective-permute-start | bytes 221192 | tf_op jit(solution)/shard_map/ppermute | solution.py:62
  26.3 2.3 %collective-permute-done.8.refs_1_ = bf16[16,2304]{1,0:T(8,128)(2,1)S(1)} collective-permute-done((bf16[16,2304]{1,0:T(8,128)(2,1)S(1)}, bf16[16,2304]{1,0:T(8,128)(2,1)S(1)}, u32[]{:S(2)}, u32[]{:S(2)}) %collective-permute-start.8) | collective-permute-done | bytes 73760 | tf_op jit(solution)/shard_map/ppermute | solution.py:62
  28.7 1.0 %collective-permute-done.10.refs_3_ = bf16[16,2304]{1,0:T(8,128)(2,1)S(1)} collective-permute-done((bf16[16,2304]{1,0:T(8,128)(2,1)S(1)}, bf16[16,2304]{1,0:T(8,128)(2,1)S(1)}, u32[]{:S(2)}, u32[]{:S(2)}) %collective-permute-start.10) | collective-permute-done | bytes 73760 | tf_op jit(solution)/shard_map/ppermute | solution.py:62
  29.7 2.4 %collective-permute-start.11 = (bf16[16,2304]{1,0:T(8,128)(2,1)S(1)}, bf16[16,2304]{1,0:T(8,128)(2,1)S(1)}, u32[]{:S(2)}, u32[]{:S(2)}) collective-permute-start(bf16[16,2304]{1,0:T(8,128)(2,1)S(1)} %get-tuple-element.38), channel_id=1, source_target_pairs={{0,4},{1,5},{2,6},{3,7},{4,0},{5,1},{6,2},{7,3},{8,12},{9,13},{10,... | collective-permute-start | bytes 221192 | tf_op jit(solution)/shard_map/ppermute | solution.py:68
  32.1 4.1 %collective-permute-done.11.other = bf16[16,2304]{1,0:T(8,128)(2,1)S(1)} collective-permute-done((bf16[16,2304]{1,0:T(8,128)(2,1)S(1)}, bf16[16,2304]{1,0:T(8,128)(2,1)S(1)}, u32[]{:S(2)}, u32[]{:S(2)}) %collective-permute-start.11) | collective-permute-done | bytes 73760 | tf_op jit(solution)/shard_map/ppermute | solution.py:68
  36.4 0.7 %collective-permute-start.14 = (bf16[16,2304]{1,0:T(8,128)(2,1)S(1)}, bf16[16,2304]{1,0:T(8,128)(2,1)S(1)}, u32[]{:S(2)}, u32[]{:S(2)}) collective-permute-start(bf16[16,2304]{1,0:T(8,128)(2,1)S(1)} %get-tuple-element.39.rest_0_), channel_id=1, source_target_pairs={{0,3},{1,2},{2,1},{3,0},{4,7},{5,6},{6,5},{7,4},{8,11},{9,10},{10,... | collective-permute-start | bytes 221192 | tf_op jit(solution)/shard_map/ppermute | solution.py:62
  37.0 0.7 %collective-permute-start.13 = (bf16[16,2304]{1,0:T(8,128)(2,1)S(1)}, bf16[16,2304]{1,0:T(8,128)(2,1)S(1)}, u32[]{:S(2)}, u32[]{:S(2)}) collective-permute-start(bf16[16,2304]{1,0:T(8,128)(2,1)S(1)} %get-tuple-element.39.rest_0_), channel_id=1, source_target_pairs={{0,2},{1,3},{2,0},{3,1},{4,6},{5,7},{6,4},{7,5},{8,10},{9,11},{10,... | collective-permute-start | bytes 221192 | tf_op jit(solution)/shard_map/ppermute | solution.py:62
  37.7 2.2 %collective-permute-start.12 = (bf16[16,2304]{1,0:T(8,128)(2,1)S(1)}, bf16[16,2304]{1,0:T(8,128)(2,1)S(1)}, u32[]{:S(2)}, u32[]{:S(2)}) collective-permute-start(bf16[16,2304]{1,0:T(8,128)(2,1)S(1)} %get-tuple-element.39.rest_0_), channel_id=1, source_target_pairs={{0,1},{1,0},{2,3},{3,2},{4,5},{5,4},{6,7},{7,6},{8,9},{9,8},{10,11... | collective-permute-start | bytes 221192 | tf_op jit(solution)/shard_map/ppermute | solution.py:62
  39.9 1.8 %collective-permute-done.14.rest_3_ = bf16[16,2304]{1,0:T(8,128)(2,1)S(1)} collective-permute-done((bf16[16,2304]{1,0:T(8,128)(2,1)S(1)}, bf16[16,2304]{1,0:T(8,128)(2,1)S(1)}, u32[]{:S(2)}, u32[]{:S(2)}) %collective-permute-start.14) | collective-permute-done | bytes 73760 | tf_op jit(solution)/shard_map/ppermute | solution.py:62
  41.7 0.8 %collective-permute-done.12.rest_1_ = bf16[16,2304]{1,0:T(8,128)(2,1)S(1)} collective-permute-done((bf16[16,2304]{1,0:T(8,128)(2,1)S(1)}, bf16[16,2304]{1,0:T(8,128)(2,1)S(1)}, u32[]{:S(2)}, u32[]{:S(2)}) %collective-permute-start.12) | collective-permute-done | bytes 73760 | tf_op jit(solution)/shard_map/ppermute | solution.py:62
  42.4 0.5 shard_map.107.before
  43.1 0.6 shard_map.106.one
  43.6 0.7 %collective-permute-done.15.other = bf16[64,512]{1,0:T(8,128)(2,1)S(1)} collective-permute-done((bf16[64,512]{1,0:T(8,128)(2,1)S(1)}, bf16[64,512]{1,0:T(8,128)(2,1)S(1)}, u32[]{:S(2)}, u32[]{:S(2)}) %collective-permute-start.15) | collective-permute-done | bytes 65568 | tf_op jit(solution)/shard_map/ppermute | solution.py:44
  44.3 1.3 %collective-permute-start.17 = (bf16[64,512]{1,0:T(8,128)(2,1)S(1)}, bf16[64,512]{1,0:T(8,128)(2,1)S(1)}, u32[]{:S(2)}, u32[]{:S(2)}) collective-permute-start(bf16[64,512]{1,0:T(8,128)(2,1)S(1)} %shard_map.108.after.terms), channel_id=1, source_target_pairs={{0,24},{8,16},{16,8},{24,0},{1,25},{9,17},{17,9},{25,1},{2,26},{10... | collective-permute-start | bytes 196616 | tf_op jit(solution)/shard_map/ppermute | solution.py:48
  45.9 1.3 %shard_map.109.refs_0_.weight = bf16[1024,2304]{1,0:T(8,128)(2,1)S(1)} custom-call(bf16[2304,1024]{1,0:T(8,128)(2,1)S(1)} %bitcast.13, bf16[64,512]{1,0:T(8,128)(2,1)S(1)} %shard_map.108.after.terms), custom_call_target="tpu_custom_call" | custom-call | bytes 9568256 | tf_op jit(solution)/shard_map/pallas_call | solution.py:29
  47.2 1.2 %collective-permute-done.17.refs_1_ = bf16[64,512]{1,0:T(8,128)(2,1)S(1)} collective-permute-done((bf16[64,512]{1,0:T(8,128)(2,1)S(1)}, bf16[64,512]{1,0:T(8,128)(2,1)S(1)}, u32[]{:S(2)}, u32[]{:S(2)}) %collective-permute-start.17) | collective-permute-done | bytes 65568 | tf_op jit(solution)/shard_map/ppermute | solution.py:48
  48.6 0.6 shard_map.111
  49.2 0.5 collective-permute-done.18.others
  49.7 0.5 shard_map.112
  50.3 1.8 %collective-permute-start.19 = (bf16[16,2304]{1,0:T(8,128)(2,1)S(1)}, bf16[16,2304]{1,0:T(8,128)(2,1)S(1)}, u32[]{:S(2)}, u32[]{:S(2)}) collective-permute-start(bf16[16,2304]{1,0:T(8,128)(2,1)S(1)} %get-tuple-element.49), channel_id=1, source_target_pairs={{0,3},{1,2},{2,1},{3,0},{4,7},{5,6},{6,5},{7,4},{8,11},{9,10},{10,... | collective-permute-start | bytes 221192 | tf_op jit(solution)/shard_map/ppermute | solution.py:62
  52.0 0.7 %collective-permute-start.20 = (bf16[16,2304]{1,0:T(8,128)(2,1)S(1)}, bf16[16,2304]{1,0:T(8,128)(2,1)S(1)}, u32[]{:S(2)}, u32[]{:S(2)}) collective-permute-start(bf16[16,2304]{1,0:T(8,128)(2,1)S(1)} %get-tuple-element.50), channel_id=1, source_target_pairs={{0,1},{1,0},{2,3},{3,2},{4,5},{5,4},{6,7},{7,6},{8,9},{9,8},{10,11... | collective-permute-start | bytes 221192 | tf_op jit(solution)/shard_map/ppermute | solution.py:62
  52.8 1.0 %collective-permute-start.21 = (bf16[16,2304]{1,0:T(8,128)(2,1)S(1)}, bf16[16,2304]{1,0:T(8,128)(2,1)S(1)}, u32[]{:S(2)}, u32[]{:S(2)}) collective-permute-start(bf16[16,2304]{1,0:T(8,128)(2,1)S(1)} %get-tuple-element.51), channel_id=1, source_target_pairs={{0,2},{1,3},{2,0},{3,1},{4,6},{5,7},{6,4},{7,5},{8,10},{9,11},{10,... | collective-permute-start | bytes 221192 | tf_op jit(solution)/shard_map/ppermute | solution.py:62
  53.8 1.8 %collective-permute-done.19.refs_1_ = bf16[16,2304]{1,0:T(8,128)(2,1)S(1)} collective-permute-done((bf16[16,2304]{1,0:T(8,128)(2,1)S(1)}, bf16[16,2304]{1,0:T(8,128)(2,1)S(1)}, u32[]{:S(2)}, u32[]{:S(2)}) %collective-permute-start.19) | collective-permute-done | bytes 73760 | tf_op jit(solution)/shard_map/ppermute | solution.py:62
  55.7 1.5 %collective-permute-done.20.refs_2_ = bf16[16,2304]{1,0:T(8,128)(2,1)S(1)} collective-permute-done((bf16[16,2304]{1,0:T(8,128)(2,1)S(1)}, bf16[16,2304]{1,0:T(8,128)(2,1)S(1)}, u32[]{:S(2)}, u32[]{:S(2)}) %collective-permute-start.20) | collective-permute-done | bytes 73760 | tf_op jit(solution)/shard_map/ppermute | solution.py:62
  57.5 3.0 %collective-permute-start.22 = (bf16[8,2304]{1,0:T(8,128)(2,1)S(1)}, bf16[8,2304]{1,0:T(8,128)(2,1)S(1)}, u32[]{:S(2)}, u32[]{:S(2)}) collective-permute-start(bf16[8,2304]{1,0:T(8,128)(2,1)S(1)} %get-tuple-element.53), channel_id=1, source_target_pairs={{0,4},{1,5},{2,6},{3,7},{4,0},{5,1},{6,2},{7,3},{8,12},{9,13},{10,... | collective-permute-start | bytes 110600 | tf_op jit(solution)/shard_map/ppermute | solution.py:68
  60.5 0.7 %shard_map.113 = (f32[64,1024]{1,0:T(8,128)}, f32[1,8]{1,0:T(1,128)}) custom-call(f32[64,512]{1,0:T(8,128)S(1)} %get-tuple-element.41.grad, f32[64,512]{1,0:T(8,128)S(1)} %get-tuple-element.44.grad_other, f32[1,8]{1,0:T(1,128)S(1)} %get-tuple-element.45.squared), custom_call_target="tpu_custom_call" | custom-call | bytes 524352 | tf_op jit(solution)/shard_map/pallas_call | solution.py:29
  61.2 1.2 %collective-permute-done.22.other = bf16[8,2304]{1,0:T(8,128)(2,1)S(1)} collective-permute-done((bf16[8,2304]{1,0:T(8,128)(2,1)S(1)}, bf16[8,2304]{1,0:T(8,128)(2,1)S(1)}, u32[]{:S(2)}, u32[]{:S(2)}) %collective-permute-start.22) | collective-permute-done | bytes 36896 | tf_op jit(solution)/shard_map/ppermute | solution.py:68
  62.4 0.6 %shard_map.115 = bf16[8,2304]{1,0:T(8,128)(2,1)} custom-call(f32[8,2304]{1,0:T(8,128)S(1)} %get-tuple-element.52.one, bf16[8,2304]{1,0:T(8,128)(2,1)S(1)} %collective-permute-done.22.other, f32[8,2304]{1,0:T(8,128)S(1)} %get-tuple-element.54.error), custom_call_target="tpu_custom_call" | custom-call | tf_op jit(solution)/shard_map/pallas_call | solution.py:29
  (34 shorter events, 1.8 us)
Async XLA Ops:
  0.6 6.6 %collective-permute-start = (bf16[8,2304]{1,0:T(8,128)(2,1)}, bf16[8,2304]{1,0:T(8,128)(2,1)S(1)}, u32[]{:S(2)}, u32[]{:S(2)}) collective-permute-start(bf16[8,2304]{1,0:T(8,128)(2,1)} %bitcast.22), channel_id=1, source_target_pairs={{0,4},{1,5},{2,6},{3,7},{4,0},{5,1},{6,2},{7,3},{8,12},{9,13},{10,... | collective-permute-start | bytes 110600 | tf_op jit(solution)/shard_map/ppermute | solution.py:68
  7.3 7.7 %slice-start = ((s8[4718592]{0:T(1024)(128)(4,1)}), s8[4194304]{0:T(1024)(128)(4,1)S(1)}, s32[]{:S(2)}) async-start(s8[4718592]{0:T(1024)(128)(4,1)} %bitcast.9), calls=%async_computation | async-start | bytes 8388608
  7.3 7.7 %slice-start.1 = ((s8[4718592]{0:T(1024)(128)(4,1)}), s8[524288]{0:T(1024)(128)(4,1)S(1)}, s32[]{:S(2)}) async-start(s8[4718592]{0:T(1024)(128)(4,1)} %bitcast.9), calls=%async_computation.1 | async-start | bytes 1048576
  7.3 11.2 %slice-start.2 = ((s8[4718592]{0:T(1024)(128)(4,1)}), s8[4194304]{0:T(1024)(128)(4,1)S(1)}, s32[]{:S(2)}) async-start(s8[4718592]{0:T(1024)(128)(4,1)} %bitcast.15), calls=%async_computation.2 | async-start | bytes 8388608
  7.3 11.2 %slice-start.3 = ((s8[4718592]{0:T(1024)(128)(4,1)}), s8[524288]{0:T(1024)(128)(4,1)S(1)}, s32[]{:S(2)}) async-start(s8[4718592]{0:T(1024)(128)(4,1)} %bitcast.15), calls=%async_computation.3 | async-start | bytes 1048576
  7.3 5.3 %collective-permute-start.3 = (bf16[16,2304]{1,0:T(8,128)(2,1)S(1)}, bf16[16,2304]{1,0:T(8,128)(2,1)S(1)}, u32[]{:S(2)}, u32[]{:S(2)}) collective-permute-start(bf16[16,2304]{1,0:T(8,128)(2,1)S(1)} %shard_map.96.rest_0_.acts), channel_id=1, source_target_pairs={{0,3},{1,2},{2,1},{3,0},{4,7},{5,6},{6,5},{7,4},{8,11},{9,10},{10,... | collective-permute-start | bytes 221192 | tf_op jit(solution)/shard_map/ppermute | solution.py:62
  9.9 4.4 %collective-permute-start.2 = (bf16[16,2304]{1,0:T(8,128)(2,1)S(1)}, bf16[16,2304]{1,0:T(8,128)(2,1)S(1)}, u32[]{:S(2)}, u32[]{:S(2)}) collective-permute-start(bf16[16,2304]{1,0:T(8,128)(2,1)S(1)} %shard_map.96.rest_0_.acts), channel_id=1, source_target_pairs={{0,2},{1,3},{2,0},{3,1},{4,6},{5,7},{6,4},{7,5},{8,10},{9,11},{10,... | collective-permute-start | bytes 221192 | tf_op jit(solution)/shard_map/ppermute | solution.py:62
  10.6 4.4 %collective-permute-start.1 = (bf16[16,2304]{1,0:T(8,128)(2,1)S(1)}, bf16[16,2304]{1,0:T(8,128)(2,1)S(1)}, u32[]{:S(2)}, u32[]{:S(2)}) collective-permute-start(bf16[16,2304]{1,0:T(8,128)(2,1)S(1)} %shard_map.96.rest_0_.acts), channel_id=1, source_target_pairs={{0,1},{1,0},{2,3},{3,2},{4,5},{5,4},{6,7},{7,6},{8,9},{9,8},{10,11... | collective-permute-start | bytes 221192 | tf_op jit(solution)/shard_map/ppermute | solution.py:62
  15.5 1.3 %collective-permute-start.4 = (bf16[64,512]{1,0:T(8,128)(2,1)S(1)}, bf16[64,512]{1,0:T(8,128)(2,1)S(1)}, u32[]{:S(2)}, u32[]{:S(2)}) collective-permute-start(bf16[64,512]{1,0:T(8,128)(2,1)S(1)} %shard_map.98), channel_id=1, source_target_pairs={{0,8},{8,0},{16,24},{24,16},{1,9},{9,1},{17,25},{25,17},{2,10},{10... | collective-permute-start | bytes 196616 | tf_op jit(solution)/shard_map/ppermute | solution.py:44
  16.9 4.1 %collective-permute-start.5 = (bf16[64,512]{1,0:T(8,128)(2,1)S(1)}, bf16[64,512]{1,0:T(8,128)(2,1)S(1)}, u32[]{:S(2)}, u32[]{:S(2)}) collective-permute-start(bf16[64,512]{1,0:T(8,128)(2,1)S(1)} %shard_map.99.after.terms), channel_id=1, source_target_pairs={{0,24},{8,16},{16,8},{24,0},{1,25},{9,17},{17,9},{25,1},{2,26},{10... | collective-permute-start | bytes 196616 | tf_op jit(solution)/shard_map/ppermute | solution.py:48
  18.2 3.0 %collective-permute-start.7 = (bf16[64,512]{1,0:T(8,128)(2,1)S(1)}, bf16[64,512]{1,0:T(8,128)(2,1)S(1)}, u32[]{:S(2)}, u32[]{:S(2)}) collective-permute-start(bf16[64,512]{1,0:T(8,128)(2,1)S(1)} %shard_map.99.after.terms), channel_id=1, source_target_pairs={{0,8},{8,0},{16,24},{24,16},{1,9},{9,1},{17,25},{25,17},{2,10},{10... | collective-permute-start | bytes 196616 | tf_op jit(solution)/shard_map/ppermute | solution.py:50
  21.0 1.3 %collective-permute-start.6 = (bf16[64,512]{1,0:T(8,128)(2,1)S(1)}, bf16[64,512]{1,0:T(8,128)(2,1)S(1)}, u32[]{:S(2)}, u32[]{:S(2)}) collective-permute-start(bf16[64,512]{1,0:T(8,128)(2,1)S(1)} %shard_map.101.others), channel_id=1, source_target_pairs={{0,8},{8,0},{16,24},{24,16},{1,9},{9,1},{17,25},{25,17},{2,10},{10... | collective-permute-start | bytes 196616 | tf_op jit(solution)/shard_map/ppermute | solution.py:50
  21.7 14.5 %copy-start = (f32[1,2304]{1,0:T(1,128)S(1)}, f32[1,2304]{1,0:T(1,128)}, u32[]{:S(2)}) copy-start(f32[1,2304]{1,0:T(1,128)} %dec_bias.1) | copy-start | bytes 27652
  21.7 14.5 %copy-start.1 = (s32[64]{0:T(128)S(1)}, s32[64]{0:T(128)}, u32[]{:S(2)}) copy-start(s32[64]{0:T(128)} %param.13) | copy-start | bytes 772
  22.8 5.9 %collective-permute-start.8 = (bf16[16,2304]{1,0:T(8,128)(2,1)S(1)}, bf16[16,2304]{1,0:T(8,128)(2,1)S(1)}, u32[]{:S(2)}, u32[]{:S(2)}) collective-permute-start(bf16[16,2304]{1,0:T(8,128)(2,1)S(1)} %get-tuple-element.34), channel_id=1, source_target_pairs={{0,3},{1,2},{2,1},{3,0},{4,7},{5,6},{6,5},{7,4},{8,11},{9,10},{10,... | collective-permute-start | bytes 221192 | tf_op jit(solution)/shard_map/ppermute | solution.py:62
  24.1 4.6 %collective-permute-start.9 = (bf16[16,2304]{1,0:T(8,128)(2,1)S(1)}, bf16[16,2304]{1,0:T(8,128)(2,1)S(1)}, u32[]{:S(2)}, u32[]{:S(2)}) collective-permute-start(bf16[16,2304]{1,0:T(8,128)(2,1)S(1)} %get-tuple-element.35), channel_id=1, source_target_pairs={{0,2},{1,3},{2,0},{3,1},{4,6},{5,7},{6,4},{7,5},{8,10},{9,11},{10,... | collective-permute-start | bytes 221192 | tf_op jit(solution)/shard_map/ppermute | solution.py:62
  24.6 5.1 %collective-permute-start.10 = (bf16[16,2304]{1,0:T(8,128)(2,1)S(1)}, bf16[16,2304]{1,0:T(8,128)(2,1)S(1)}, u32[]{:S(2)}, u32[]{:S(2)}) collective-permute-start(bf16[16,2304]{1,0:T(8,128)(2,1)S(1)} %get-tuple-element.36), channel_id=1, source_target_pairs={{0,1},{1,0},{2,3},{3,2},{4,5},{5,4},{6,7},{7,6},{8,9},{9,8},{10,11... | collective-permute-start | bytes 221192 | tf_op jit(solution)/shard_map/ppermute | solution.py:62
  29.7 6.5 %collective-permute-start.11 = (bf16[16,2304]{1,0:T(8,128)(2,1)S(1)}, bf16[16,2304]{1,0:T(8,128)(2,1)S(1)}, u32[]{:S(2)}, u32[]{:S(2)}) collective-permute-start(bf16[16,2304]{1,0:T(8,128)(2,1)S(1)} %get-tuple-element.38), channel_id=1, source_target_pairs={{0,4},{1,5},{2,6},{3,7},{4,0},{5,1},{6,2},{7,3},{8,12},{9,13},{10,... | collective-permute-start | bytes 221192 | tf_op jit(solution)/shard_map/ppermute | solution.py:68
  36.4 5.3 %collective-permute-start.14 = (bf16[16,2304]{1,0:T(8,128)(2,1)S(1)}, bf16[16,2304]{1,0:T(8,128)(2,1)S(1)}, u32[]{:S(2)}, u32[]{:S(2)}) collective-permute-start(bf16[16,2304]{1,0:T(8,128)(2,1)S(1)} %get-tuple-element.39.rest_0_), channel_id=1, source_target_pairs={{0,3},{1,2},{2,1},{3,0},{4,7},{5,6},{6,5},{7,4},{8,11},{9,10},{10,... | collective-permute-start | bytes 221192 | tf_op jit(solution)/shard_map/ppermute | solution.py:62
  37.0 4.6 %collective-permute-start.13 = (bf16[16,2304]{1,0:T(8,128)(2,1)S(1)}, bf16[16,2304]{1,0:T(8,128)(2,1)S(1)}, u32[]{:S(2)}, u32[]{:S(2)}) collective-permute-start(bf16[16,2304]{1,0:T(8,128)(2,1)S(1)} %get-tuple-element.39.rest_0_), channel_id=1, source_target_pairs={{0,2},{1,3},{2,0},{3,1},{4,6},{5,7},{6,4},{7,5},{8,10},{9,11},{10,... | collective-permute-start | bytes 221192 | tf_op jit(solution)/shard_map/ppermute | solution.py:62
  37.7 4.7 %collective-permute-start.12 = (bf16[16,2304]{1,0:T(8,128)(2,1)S(1)}, bf16[16,2304]{1,0:T(8,128)(2,1)S(1)}, u32[]{:S(2)}, u32[]{:S(2)}) collective-permute-start(bf16[16,2304]{1,0:T(8,128)(2,1)S(1)} %get-tuple-element.39.rest_0_), channel_id=1, source_target_pairs={{0,1},{1,0},{2,3},{3,2},{4,5},{5,4},{6,7},{7,6},{8,9},{9,8},{10,11... | collective-permute-start | bytes 221192 | tf_op jit(solution)/shard_map/ppermute | solution.py:62
  43.0 1.3 %collective-permute-start.15 = (bf16[64,512]{1,0:T(8,128)(2,1)S(1)}, bf16[64,512]{1,0:T(8,128)(2,1)S(1)}, u32[]{:S(2)}, u32[]{:S(2)}) collective-permute-start(bf16[64,512]{1,0:T(8,128)(2,1)S(1)} %shard_map.107.before), channel_id=1, source_target_pairs={{0,8},{8,0},{16,24},{24,16},{1,9},{9,1},{17,25},{25,17},{2,10},{10... | collective-permute-start | bytes 196616 | tf_op jit(solution)/shard_map/ppermute | solution.py:44
  44.3 4.1 %collective-permute-start.17 = (bf16[64,512]{1,0:T(8,128)(2,1)S(1)}, bf16[64,512]{1,0:T(8,128)(2,1)S(1)}, u32[]{:S(2)}, u32[]{:S(2)}) collective-permute-start(bf16[64,512]{1,0:T(8,128)(2,1)S(1)} %shard_map.108.after.terms), channel_id=1, source_target_pairs={{0,24},{8,16},{16,8},{24,0},{1,25},{9,17},{17,9},{25,1},{2,26},{10... | collective-permute-start | bytes 196616 | tf_op jit(solution)/shard_map/ppermute | solution.py:48
  45.6 3.0 %collective-permute-start.16 = (bf16[64,512]{1,0:T(8,128)(2,1)S(1)}, bf16[64,512]{1,0:T(8,128)(2,1)S(1)}, u32[]{:S(2)}, u32[]{:S(2)}) collective-permute-start(bf16[64,512]{1,0:T(8,128)(2,1)S(1)} %shard_map.108.after.terms), channel_id=1, source_target_pairs={{0,8},{8,0},{16,24},{24,16},{1,9},{9,1},{17,25},{25,17},{2,10},{10... | collective-permute-start | bytes 196616 | tf_op jit(solution)/shard_map/ppermute | solution.py:50
  48.4 1.3 %collective-permute-start.18 = (bf16[64,512]{1,0:T(8,128)(2,1)S(1)}, bf16[64,512]{1,0:T(8,128)(2,1)S(1)}, u32[]{:S(2)}, u32[]{:S(2)}) collective-permute-start(bf16[64,512]{1,0:T(8,128)(2,1)S(1)} %shard_map.110.others), channel_id=1, source_target_pairs={{0,8},{8,0},{16,24},{24,16},{1,9},{9,1},{17,25},{25,17},{2,10},{10... | collective-permute-start | bytes 196616 | tf_op jit(solution)/shard_map/ppermute | solution.py:50
  50.3 5.4 %collective-permute-start.19 = (bf16[16,2304]{1,0:T(8,128)(2,1)S(1)}, bf16[16,2304]{1,0:T(8,128)(2,1)S(1)}, u32[]{:S(2)}, u32[]{:S(2)}) collective-permute-start(bf16[16,2304]{1,0:T(8,128)(2,1)S(1)} %get-tuple-element.49), channel_id=1, source_target_pairs={{0,3},{1,2},{2,1},{3,0},{4,7},{5,6},{6,5},{7,4},{8,11},{9,10},{10,... | collective-permute-start | bytes 221192 | tf_op jit(solution)/shard_map/ppermute | solution.py:62
  52.0 5.1 %collective-permute-start.20 = (bf16[16,2304]{1,0:T(8,128)(2,1)S(1)}, bf16[16,2304]{1,0:T(8,128)(2,1)S(1)}, u32[]{:S(2)}, u32[]{:S(2)}) collective-permute-start(bf16[16,2304]{1,0:T(8,128)(2,1)S(1)} %get-tuple-element.50), channel_id=1, source_target_pairs={{0,1},{1,0},{2,3},{3,2},{4,5},{5,4},{6,7},{7,6},{8,9},{9,8},{10,11... | collective-permute-start | bytes 221192 | tf_op jit(solution)/shard_map/ppermute | solution.py:62
  52.8 4.7 %collective-permute-start.21 = (bf16[16,2304]{1,0:T(8,128)(2,1)S(1)}, bf16[16,2304]{1,0:T(8,128)(2,1)S(1)}, u32[]{:S(2)}, u32[]{:S(2)}) collective-permute-start(bf16[16,2304]{1,0:T(8,128)(2,1)S(1)} %get-tuple-element.51), channel_id=1, source_target_pairs={{0,2},{1,3},{2,0},{3,1},{4,6},{5,7},{6,4},{7,5},{8,10},{9,11},{10,... | collective-permute-start | bytes 221192 | tf_op jit(solution)/shard_map/ppermute | solution.py:62
  57.5 4.9 %collective-permute-start.22 = (bf16[8,2304]{1,0:T(8,128)(2,1)S(1)}, bf16[8,2304]{1,0:T(8,128)(2,1)S(1)}, u32[]{:S(2)}, u32[]{:S(2)}) collective-permute-start(bf16[8,2304]{1,0:T(8,128)(2,1)S(1)} %get-tuple-element.53), channel_id=1, source_target_pairs={{0,4},{1,5},{2,6},{3,7},{4,0},{5,1},{6,2},{7,3},{8,12},{9,13},{10,... | collective-permute-start | bytes 110600 | tf_op jit(solution)/shard_map/ppermute | solution.py:68
